TPU v7x, 32 devices: a whole 2x2x4 slice. The times are simulated.
32 devices in a mesh: groups: 2 (over x), ctx: 16 (over z, y, core).
Axes of the slice: x: 2, y: 2, z: 4, core: 2. Of those that a mesh axis runs over, the one named last changes fastest.
Arguments:
- queries: bfloat16 [4096, 4096], P(('groups', 'ctx')), parts along dimension 0, may hold values from -400 to 400
- span_keys: bfloat16 [4096, 512], P(('groups', 'ctx')), parts along dimension 0, may hold values from -25 to 25
- span_values: bfloat16 [4096, 512], P(('groups', 'ctx')), parts along dimension 0, may hold values from -96 to 96
- cache_keys: bfloat16 [65536, 512], P(('groups', 'ctx')), parts along dimension 0, may hold values from -24 to 24
- cache_values: bfloat16 [65536, 512], P(('groups', 'ctx')), parts along dimension 0, may hold values from -96 to 96
- vertical_blocks: int32 [8, 16], P('groups'), parts along dimension 0, may hold values from 0 to 511, as said below
- slash_offsets: int32 [8, 64], P('groups'), parts along dimension 0, may hold values from 0 to 127, as said below
Outputs:
- attended: bfloat16 [4096, 4096], P(('groups', 'ctx')), parts along dimension 0
There are 2 independent parts, one for each index of `groups`. A program takes and returns all parts, laid end to end along the dimension named above; each array names one. Nothing has to cross between parts.
Inputs may be any that keep to these rules, and one draw needn't show every extreme that they name: `vertical_blocks`: each row holds 16 different block numbers of the cache; the first key-value head always reads the cache's last block. `slash_offsets`: each row holds 64 different offsets, always among them 0, 1 and 127.
All inputs are finite; a program needn't handle non-finite values.
Results may differ from a plain program's by a relative error of at most 0.005.
Values may be sent and summed in bfloat16 or wider, within the bound.
No kernel may reach another device: no remote copies, remote signals or barrier semaphores. Data moves between devices by JAX's collectives and lax.ppermute only.
A program may use at most 64 MiB of HBM per device.

v0:
```python
import math

import jax
import jax.numpy as jnp
from jax import lax
from jax.sharding import PartitionSpec as P

KVH = 4
GROUP = 8
HD = 128
QDEV = 128
VBLOCK = 64
NV = 16
SMAX = 128


def passed_along(shard, axis, by):
    peers = lax.axis_size(axis)
    pairs = [(i, i + by) for i in range(peers) if 0 <= i + by < peers]
    return lax.ppermute(shard, axis, pairs)


def band_mask(offset_row, tile_first):
    query_ids = jnp.arange(QDEV, dtype=jnp.int32)[:, None]
    key_ids = jnp.arange(SMAX + QDEV, dtype=jnp.int32)[None, :]
    distance = query_ids + SMAX - key_ids
    table = jnp.zeros((SMAX,), jnp.bool_).at[offset_row].set(True)
    inside = (distance >= 0) & (distance < SMAX)
    chosen = inside & table[jnp.clip(distance, 0, SMAX - 1)]
    return chosen & (key_ids >= SMAX * tile_first)


def attend_tile(query_tile, key_sets, value_sets, offsets, tile_first):
    factor = 1.0 / math.sqrt(HD)
    grouped = query_tile.reshape(QDEV, KVH, GROUP, HD)
    results = []
    for kv_head in range(KVH):
        query_rows = grouped[:, kv_head].transpose(1, 0, 2).reshape(GROUP * QDEV, HD)
        scores = (
            jnp.dot(query_rows, key_sets[kv_head].T, preferred_element_type=jnp.float32) * factor
        )
        scores = scores.reshape(GROUP, QDEV, -1)
        allowed = jnp.concatenate(
            [jnp.ones((QDEV, NV * VBLOCK), jnp.bool_), band_mask(offsets[kv_head], tile_first)],
            axis=1,
        )
        scores = jnp.where(allowed[None], scores, -jnp.inf)
        largest = jnp.max(scores, axis=-1, keepdims=True)
        expos = jnp.exp(scores - largest)
        weights = (expos / jnp.sum(expos, axis=-1, keepdims=True)).astype(jnp.bfloat16)
        mixed = jnp.dot(
            weights.reshape(GROUP * QDEV, -1),
            value_sets[kv_head],
            preferred_element_type=jnp.float32,
        )
        results.append(mixed.reshape(GROUP, QDEV, HD).transpose(1, 0, 2))
    return jnp.stack(results, axis=1).reshape(QDEV, KVH * GROUP * HD).astype(jnp.bfloat16)


def owned_blocks(cache_array, owners, local_ids, device):
    per_device = cache_array.shape[0] // VBLOCK
    blocked = cache_array.reshape(per_device, VBLOCK, KVH, HD)
    pieces = []
    for kv_head in range(KVH):
        picked = (owners[kv_head] == device)[:, None, None]
        taken = blocked[local_ids[kv_head], :, kv_head, :].astype(jnp.float32)
        pieces.append(jnp.where(picked, taken, jnp.zeros_like(taken)).reshape(NV * VBLOCK, HD))
    return jnp.stack(pieces)


def shards(
    queries, span_keys, span_values, cache_keys, cache_values, vertical_blocks, slash_offsets
):
    device = lax.axis_index("ctx")
    rim_rows = jnp.stack([span_keys, span_values])
    earlier = passed_along(rim_rows, "ctx", 1)
    per_device = cache_keys.shape[0] // VBLOCK
    owners = vertical_blocks // per_device
    local_ids = vertical_blocks % per_device
    mine_k = owned_blocks(cache_keys, owners, local_ids, device)
    mine_v = owned_blocks(cache_values, owners, local_ids, device)
    summed_k, summed_v = lax.psum((mine_k, mine_v), "ctx")
    whole_k = summed_k.astype(jnp.bfloat16)
    whole_v = summed_v.astype(jnp.bfloat16)
    band_k = jnp.concatenate([earlier[0], span_keys], axis=0).reshape(SMAX + QDEV, KVH, HD)
    band_v = jnp.concatenate([earlier[1], span_values], axis=0).reshape(SMAX + QDEV, KVH, HD)
    key_sets = [
        jnp.concatenate([whole_k[kv_head], band_k[:, kv_head, :]], axis=0) for kv_head in range(KVH)
    ]
    value_sets = [
        jnp.concatenate([whole_v[kv_head], band_v[:, kv_head, :]], axis=0) for kv_head in range(KVH)
    ]
    tile_first = (device == 0).astype(jnp.int32)
    return attend_tile(queries, key_sets, value_sets, slash_offsets, tile_first)


def solution(mesh):
    in_specs = (
        P(("groups", "ctx"), None),
        P(("groups", "ctx"), None),
        P(("groups", "ctx"), None),
        P(("groups", "ctx"), None),
        P(("groups", "ctx"), None),
        P("groups", None),
        P("groups", None),
    )
    out_specs = P(("groups", "ctx"), None)
    return jax.shard_map(shards, mesh=mesh, in_specs=in_specs, out_specs=out_specs, check_vma=False)
```

profile of v0, /device:TPU:0, one launch (start us, length us, event | category | flops | bytes accessed | tf_op | source)
XLA Modules:
  0.0 949.8 jit_solution(12952795143937400099)
XLA Ops:
  0.0 1.7 pad_maximum_fusion.3
  1.7 3.1 collective-permute-start
  5.4 2.6 reshape.711
  8.0 1.9 copy.26
  9.9 2.2 gather_fusion.4
  12.1 2.2 gather_fusion.3
  14.3 2.6 reshape.714
  16.8 1.9 copy.38
  18.8 2.2 gather_fusion.8
  21.0 2.2 gather_fusion.7
  23.2 2.2 gather_fusion.2
  25.4 2.2 gather_fusion.6
  27.6 2.2 gather_fusion.1
  29.8 2.9 gather_fusion.5
  36.8 191.6 %gather_fusion.11 = pred[32768]{0:T(1024)(128)(4,1)S(1)} fusion(pred[128]{0:T(512)(128)(4,1)S(1)} %scatter_custom_fusion.3, s32[32768]{0:T(1024)S(1)} %broadcast_clamp_fusion), kind=kCustom, calls=%fused_computation.11 | custom fusion | bytes 196608 | tf_op jit(solution)/shard_map/gather | solution.py:29
  229.0 191.6 %gather_fusion.10 = pred[32768]{0:T(1024)(128)(4,1)S(1)} fusion(pred[128]{0:T(512)(128)(4,1)S(1)} %scatter_custom_fusion.2, s32[32768]{0:T(1024)S(1)} %broadcast_clamp_fusion), kind=kCustom, calls=%fused_computation.10 | custom fusion | bytes 196608 | tf_op jit(solution)/shard_map/gather | solution.py:29
  421.2 191.6 %gather_fusion.9 = pred[32768]{0:T(1024)(128)(4,1)S(1)} fusion(pred[128]{0:T(512)(128)(4,1)S(1)} %scatter_custom_fusion.1, s32[32768]{0:T(1024)S(1)} %broadcast_clamp_fusion), kind=kCustom, calls=%fused_computation.9 | custom fusion | bytes 196608 | tf_op jit(solution)/shard_map/gather | solution.py:29
  612.8 191.6 %gather_fusion = pred[32768]{0:T(1024)(128)(4,1)S(1)} fusion(pred[128]{0:T(512)(128)(4,1)S(1)} %scatter_custom_fusion, s32[32768]{0:T(1024)S(1)} %broadcast_clamp_fusion), kind=kCustom, calls=%fused_computation | custom fusion | bytes 196608 | tf_op jit(solution)/shard_map/gather | solution.py:29
  805.7 1.6 copy.36
  807.3 1.0 slice_bitcast_fusion.11
  809.3 1.0 copy.41
  811.3 1.0 copy.39
  812.4 1.0 copy.43
  813.6 1.1 broadcast_select_fusion.2
  814.8 1.1 broadcast_select_fusion.3
  815.9 1.1 broadcast_select_fusion.1
  817.2 1.8 pad_maximum_fusion
  819.0 96.7 %all-reduce.10 = (bf16[4,1024,128]{1,2,0:T(8,128)(2,1)}, bf16[4,1024,128]{1,2,0:T(8,128)(2,1)S(1)}) all-reduce(f32[4,1024,128]{1,2,0:T(8,128)S(1)} %get-tuple-element.63, f32[4,1024,128]{1,2,0:T(8,128)} %get-tuple-element.64), channel_id=1, replica_groups=mesh['groups'=2,'ctx'=16] {'ctx'}, use_global_device_ids=true, to_apply=%region_1.2 | all-reduce | flops 1048576 | bytes 6291456 | tf_op jit(solution)/shard_map/psum | solution.py:82
  915.7 1.3 slice_bitcast_fusion.10
  918.7 1.0 copy.47
  922.5 1.1 copy.37
  923.6 1.1 copy.50
  924.8 1.1 copy.49
  927.0 1.0 fusion.82
  929.1 2.0 fusion.86
  931.0 1.1 fusion
  932.1 1.4 divide_convert_fusion.3
  933.5 1.1 fusion.84
  934.6 1.1 fusion.2
  935.6 1.4 divide_convert_fusion.1
  937.0 1.1 fusion.85
  938.1 1.1 fusion.1
  939.2 1.6 divide_convert_fusion.2
  940.8 1.1 fusion.83
  941.8 1.1 fusion.3
  942.9 1.4 divide_convert_fusion
  947.4 1.0 fusion.7
  948.5 1.3 copy.51
  (75 shorter events, 19.4 us)
Async XLA Ops:
  1.7 925.3 %collective-permute-start = (bf16[2,128,512]{2,1,0:T(8,128)(2,1)}, bf16[2,128,512]{2,1,0:T(8,128)(2,1)}, u32[]{:S(2)}, u32[]{:S(2)}) collective-permute-start(bf16[2,128,512]{2,1,0:T(8,128)(2,1)} %pad_maximum_fusion.3), channel_id=1, source_target_pairs={{0,1},{1,2},{2,3},{3,4},{4,5},{5,6},{6,7},{7,8},{8,9},{9,10},{10,1... | collective-permute-start | bytes 786440 | tf_op jit(solution)/shard_map/ppermute | solution.py:20
  14.3 18.4 %copy-start.8 = (s32[4,64]{1,0:T(4,128)S(1)}, s32[4,64]{1,0:T(4,128)}, u32[]{:S(2)}) copy-start(s32[4,64]{1,0:T(4,128)} %param.13) | copy-start | bytes 3076
  819.0 98.9 %copy-start.4 = (bf16[128,512]{1,0:T(8,128)(2,1)S(1)}, bf16[128,512]{1,0:T(8,128)(2,1)}, u32[]{:S(2)}) copy-start(bf16[128,512]{1,0:T(8,128)(2,1)} %param.8) | copy-start | bytes 393220
  819.0 106.9 %copy-start = (bf16[8,128,128]{1,2,0:T(8,128)(2,1)S(1)}, bf16[8,128,128]{1,2,0:T(8,128)(2,1)}, u32[]{:S(2)}) copy-start(bf16[8,128,128]{1,2,0:T(8,128)(2,1)} %get-tuple-element.18) | copy-start | bytes 786436
  932.1 1.4 copy-start.3
  935.6 1.4 copy-start.2
  939.2 1.6 copy-start.1
  942.9 1.5 copy-start.7
  942.9 2.4 copy-start.6
  944.3 2.1 copy-start.5
where the time goes:
time: 951 us; the launch traced here: 950 us
  local copies, waits for them, and re-layouts  819 us (86%)
  blocking collectives  96.7 us (10%)
  other arithmetic  21 us (2%)
    gather x8, local copies, waits for them, and re-layouts, band_mask(): chosen = inside & table[jnp.clip(distance, 0, SMAX - 1)]  769 us
    psum x1, blocking collectives, shards(): summed_k, summed_v = lax.psum((mine_k, mine_v), 'ctx')  96.7 us
  transfers between devices with their start and end apart: 1, of which 0 were waited for; matrix products, arithmetic and copies ran while one was open for 87% of the time, Pallas kernels for 0%

commit v1 on v0

v1 whole, which is shorter than its diff:
```python
import functools
import math

import jax
import jax.numpy as jnp
from jax import lax
from jax.experimental import pallas as pl
from jax.experimental.pallas import tpu as pltpu
from jax.sharding import PartitionSpec as P

KVH = 4
GROUP = 8
HD = 128
QDEV = 128
VBLOCK = 64
NV = 16
NS = 64
SMAX = 128
ENTRIES = KVH * NV
FACTOR = math.log2(math.e) / math.sqrt(HD)
LOW = -1e38

ANY = pl.BlockSpec(memory_space=pl.ANY)
SMEM = pl.BlockSpec(memory_space=pltpu.SMEM)


def band_mask(offsets_ref, head, first):
    columns = lax.broadcasted_iota(jnp.int32, (8, SMAX + QDEV), 1)
    distance = SMAX - columns
    row = jnp.zeros((8, SMAX + QDEV), jnp.int32)
    for at in range(NS):
        row = jnp.where(distance == offsets_ref[head, at], 1, row)
    rows = jnp.concatenate([row] * (QDEV // 8), axis=0)
    rolled = pltpu.roll(rows, 0, 1, stride=1, stride_axis=0)
    keys = lax.broadcasted_iota(jnp.int32, (QDEV, SMAX + QDEV), 1)
    return (rolled > 0) & (keys >= jnp.where(first, SMAX, 0))


def attend_rows(rows, keys, values_ones, mask):
    scores = lax.dot_general(
        rows, keys, (((1,), (1,)), ((), ())), preferred_element_type=jnp.float32
    )
    if mask is not None:
        wide = scores.shape[1] - mask.shape[1]
        reps = rows.shape[0] // QDEV
        tiled = jnp.concatenate([mask] * reps, axis=0)
        band = jnp.where(tiled, scores[:, wide:], LOW)
        scores = jnp.concatenate([scores[:, :wide], band], axis=1)
    largest = jnp.max(scores, axis=1, keepdims=True) * FACTOR
    weights = jnp.exp2(scores * FACTOR - largest).astype(jnp.bfloat16)
    mixed = jnp.dot(weights, values_ones, preferred_element_type=jnp.float32)
    return largest, mixed


def dense_kernel(
    offsets, queries, keys, values, before_k, own_k, before_v, own_v, out, kbuf, vbuf
):
    head = pl.program_id(0)
    first = lax.axis_index("ctx") == 0
    wide = NV * VBLOCK
    kbuf[:wide] = keys[0]
    kbuf[wide : wide + SMAX] = before_k[...]
    kbuf[wide + SMAX :] = own_k[...]
    vbuf[:wide, :HD] = values[0]
    vbuf[wide : wide + SMAX, :HD] = before_v[...]
    vbuf[wide + SMAX :, :HD] = own_v[...]
    vbuf[:, HD:] = jnp.ones((wide + SMAX + QDEV, HD), jnp.bfloat16)
    mask = band_mask(offsets, head, first)
    for at in range(0, GROUP, 2):
        rows = jnp.concatenate(
            [queries[:, (at + i) * HD : (at + i + 1) * HD] for i in range(2)], axis=0
        )
        _, mixed = attend_rows(rows, kbuf[...], vbuf[...], mask)
        result = (mixed[:, :HD] / mixed[:, HD:]).astype(jnp.bfloat16)
        for i in range(2):
            out[:, (at + i) * HD : (at + i + 1) * HD] = result[i * QDEV : (i + 1) * QDEV]


def head_block(rows):
    return pl.BlockSpec((rows, HD), lambda head: (0, head))


def attend_dense(offsets, queries, keys, values, bands):
    wide = NV * VBLOCK
    return pl.pallas_call(
        dense_kernel,
        grid=(KVH,),
        out_shape=jax.ShapeDtypeStruct(queries.shape, jnp.bfloat16),
        in_specs=[
            SMEM,
            pl.BlockSpec((QDEV, GROUP * HD), lambda head: (0, head)),
            pl.BlockSpec((1, wide, HD), lambda head: (head, 0, 0)),
            pl.BlockSpec((1, wide, HD), lambda head: (head, 0, 0)),
        ]
        + [head_block(QDEV)] * 4,
        out_specs=pl.BlockSpec((QDEV, GROUP * HD), lambda head: (0, head)),
        scratch_shapes=[
            pltpu.VMEM((wide + SMAX + QDEV, HD), jnp.bfloat16),
            pltpu.VMEM((wide + SMAX + QDEV, 2 * HD), jnp.bfloat16),
        ],
        compiler_params=pltpu.CompilerParams(vmem_limit_bytes=48 * 2**20),
        name="attend_dense",
    )(offsets, queries, keys, values, *bands)


def owned_kernel(per_device, blocks, cache_k, cache_v, out_k, out_v, sems):
    me = lax.axis_index("ctx")
    out_k[...] = jnp.zeros_like(out_k)
    out_v[...] = jnp.zeros_like(out_v)

    def copies(entry):
        head, at = entry // NV, entry % NV
        block = blocks[head, at]
        local = block % per_device
        rows = pl.ds(pl.multiple_of(local * VBLOCK, VBLOCK), VBLOCK)
        columns = pl.ds(pl.multiple_of(head * HD, HD), HD)
        pairs = ((cache_k, out_k, 0), (cache_v, out_v, 1))
        return block // per_device == me, [
            pltpu.make_async_copy(source.at[rows, columns], target.at[entry], sems.at[entry, i])
            for source, target, i in pairs
        ]

    def start(entry, carry):
        mine, both = copies(entry)

        @pl.when(mine)
        def _():
            for copy in both:
                copy.start()

        return carry

    def wait(entry, carry):
        mine, both = copies(entry)

        @pl.when(mine)
        def _():
            for copy in both:
                copy.wait()

        return carry

    lax.fori_loop(0, ENTRIES, start, 0)
    lax.fori_loop(0, ENTRIES, wait, 0)


def owned_blocks(blocks, cache_k, cache_v):
    shape = jax.ShapeDtypeStruct((ENTRIES, VBLOCK, HD), jnp.bfloat16)
    whole = pl.BlockSpec(memory_space=pltpu.VMEM)
    return pl.pallas_call(
        functools.partial(owned_kernel, cache_k.shape[0] // VBLOCK),
        out_shape=(shape, shape),
        in_specs=[SMEM, ANY, ANY],
        out_specs=(whole, whole),
        scratch_shapes=[pltpu.SemaphoreType.DMA((ENTRIES, 2))],
        compiler_params=pltpu.CompilerParams(vmem_limit_bytes=16 * 2**20),
        name="owned_blocks",
    )(blocks, cache_k, cache_v)


def permuted(array, pairs):
    return lax.ppermute(array, "ctx", pairs)


def general(queries, bands, cache_k, cache_v, blocks, offsets):
    mine = owned_blocks(blocks, cache_k, cache_v)
    keys, values = lax.psum(mine, "ctx")
    keys = keys.reshape(KVH, NV * VBLOCK, HD)
    values = values.reshape(KVH, NV * VBLOCK, HD)
    return attend_dense(offsets, queries, keys, values, bands)


def shards(queries, span_k, span_v, cache_k, cache_v, blocks, offsets):
    peers = lax.axis_size("ctx")
    ahead = [(i, i + 1) for i in range(peers - 1)]
    bands = (permuted(span_k, ahead), span_k, permuted(span_v, ahead), span_v)
    return general(queries, bands, cache_k, cache_v, blocks, offsets)


def solution(mesh):
    rows = P(("groups", "ctx"), None)
    heads = P("groups", None)
    return jax.shard_map(
        shards,
        mesh=mesh,
        in_specs=(rows, rows, rows, rows, rows, heads, heads),
        out_specs=rows,
        check_vma=False,
    )
```

time: 951 us -> 139 us (0.15)
  local copies, waits for them, and re-layouts: 819 us -> 7.17 us
  blocking collectives: 96.7 us -> 0 us
  waiting for transfers between devices: 0.01 us -> 93.8 us
  other arithmetic: 21 us -> 0 us
  Pallas kernels: 0 us -> 17.2 us
  between operations: 0.54 us -> 13.5 us
    gather x16 -> x0, local copies, waits for them, and re-layouts: 787 us -> none  [the longest x8 769 us: band_mask(): chosen = inside & table[jnp.clip(distance, 0, SMAX - 1)]]
    psum x1 -> x0, blocking collectives: 96.7 us -> none  [shards(): summed_k, summed_v = lax.psum((mine_k, mine_v), 'ctx')]
    psum x0 -> x1, waiting for transfers between devices: none -> 92.8 us  [general(): keys, values = lax.psum(mine, 'ctx')]
    pallas_call x0 -> x2, Pallas kernels: none -> 17.2 us  [the longest x1 10.5 us: attend_dense(): pl.pallas_call(dense_kernel, grid=(KVH,), out_shape=jax.ShapeDtypeStruct(...]
  transfers between devices with their start and end apart: 1 -> 3, of which waited for: 0 -> 2; matrix products, arithmetic and copies ran while one was open for 87% -> 0% of each run, Pallas kernels for 0% -> 0%
where the time goes in v1:
time: 139 us
  waiting for transfers between devices  93.8 us (67%)
  Pallas kernels  17.2 us (12%)
  between operations  13.5 us (10%)
  local copies, waits for them, and re-layouts  7.17 us (5%)
  starting transfers between devices  6.92 us (5%)
    psum x1, waiting for transfers between devices, general(): keys, values = lax.psum(mine, 'ctx')  92.8 us
    pallas_call x1, Pallas kernels, attend_dense(): pl.pallas_call(dense_kernel, grid=(KVH,), out_shape=jax.ShapeDtypeStruct(...  10.5 us
    unnamed x18, local copies, waits for them, and re-layouts  7.17 us
    ppermute x2, starting transfers between devices, permuted(): return lax.ppermute(array, 'ctx', pairs)  6.92 us
    pallas_call x1, Pallas kernels, owned_blocks(): pl.pallas_call(functools.partial(owned_kernel, cache_k.shape[0] // VBLOCK...  6.71 us
  transfers between devices with their start and end apart: 3, of which 2 were waited for; matrix products, arithmetic and copies ran while one was open for 0% of the time, Pallas kernels for 0%

profile of v1, /device:TPU:0, one launch (start us, length us, event | category | flops | bytes accessed | tf_op | source)
XLA Modules:
  0.0 138.6 jit_solution(16123667624679987175)
XLA Ops:
  6.5 0.0 all-reduce.3.cloned.1.call-start
  6.5 0.0 copy-start
  6.5 1.6 %copy-done = bf16[2048,512]{1,0:T(8,128)(2,1)S(1)} copy-done((bf16[2048,512]{1,0:T(8,128)(2,1)S(1)}, bf16[2048,512]{1,0:T(8,128)(2,1)}, u32[]{:S(2)}) %copy-start) | copy-done | bytes 2097176
  8.1 0.0 copy-start.1
  8.1 1.6 %copy-done.1 = bf16[2048,512]{1,0:T(8,128)(2,1)S(1)} copy-done((bf16[2048,512]{1,0:T(8,128)(2,1)S(1)}, bf16[2048,512]{1,0:T(8,128)(2,1)}, u32[]{:S(2)}) %copy-start.1) | copy-done | bytes 2097176
  9.7 0.0 copy-start.7
  9.7 0.7 copy-done.7
  10.4 6.7 %owned_blocks.1 = (bf16[64,64,128]{2,1,0:T(8,128)(2,1)}, bf16[64,64,128]{2,1,0:T(8,128)(2,1)}) custom-call(s32[4,16]{1,0:T(4,128)S(1)} %copy-done.7, bf16[2048,512]{1,0:T(8,128)(2,1)S(1)} %copy-done, bf16[2048,512]{1,0:T(8,128)(2,1)S(1)} %copy-done.1), custom_call_target="tpu_custom_call" | custom-call | tf_op jit(solution)/shard_map/owned_blocks/pallas_call | solution.py:150
  17.1 0.0 copy-start.5
  17.1 0.0 copy-start.6
  17.1 0.0 copy-start.2
  17.2 0.0 copy-start.8
  17.2 0.0 all-reduce.3.cloned.1.call-update
  17.2 0.8 copy-done.5
  18.0 2.3 %collective-permute-start = (bf16[128,512]{1,0:T(8,128)(2,1)S(1)}, bf16[128,512]{1,0:T(8,128)(2,1)S(1)}, u32[]{:S(2)}, u32[]{:S(2)}) collective-permute-start(bf16[128,512]{1,0:T(8,128)(2,1)S(1)} %copy-done.5), channel_id=1, source_target_pairs={{0,1},{1,2},{2,3},{3,4},{4,5},{5,6},{6,7},{7,8},{8,9},{9,10},{10,1... | collective-permute-start | bytes 393224 | tf_op jit(solution)/shard_map/ppermute | solution.py:162
  20.4 0.0 copy-done.6
  20.4 4.6 %collective-permute-start.1 = (bf16[128,512]{1,0:T(8,128)(2,1)S(1)}, bf16[128,512]{1,0:T(8,128)(2,1)S(1)}, u32[]{:S(2)}, u32[]{:S(2)}) collective-permute-start(bf16[128,512]{1,0:T(8,128)(2,1)S(1)} %copy-done.6), channel_id=1, source_target_pairs={{0,1},{1,2},{2,3},{3,4},{4,5},{5,6},{6,7},{7,8},{8,9},{9,10},{10,1... | collective-permute-start | bytes 393224 | tf_op jit(solution)/shard_map/ppermute | solution.py:162
  25.0 0.0 collective-permute-done.before_k
  25.0 1.0 collective-permute-done.1.before_v
  25.9 92.8 %all-reduce.3.cloned.1.call-done = (bf16[4,1024,128]{2,1,0:T(8,128)(2,1)}, bf16[4,1024,128]{2,1,0:T(8,128)(2,1)}) async-done(((bf16[4,1024,128]{2,1,0:T(8,128)(2,1)}, bf16[4,1024,128]{2,1,0:T(8,128)(2,1)}), (bf16[4,1024,128]{2,1,0:T(8,128)(2,1)}, bf16[4,1024,128]{2,1,0:T(8,128)(2,1)})) %all-reduce.3.cloned.1.call-update) | async-done | bytes 2097168 | tf_op jit(solution)/shard_map/psum | solution.py:167
  118.8 0.0 copy-done.2
  118.8 0.0 copy-done.8
  118.8 0.0 copy-start.3
  118.8 1.2 copy-done.3
  120.0 0.0 copy-start.4
  120.0 1.2 copy-done.4
  121.2 10.5 %attend_dense.1 = bf16[128,4096]{1,0:T(8,128)(2,1)} custom-call(s32[4,64]{1,0:T(4,128)S(1)} %copy-done.8, bf16[128,4096]{1,0:T(8,128)(2,1)S(1)} %copy-done.2, bf16[4,1024,128]{2,1,0:T(8,128)(2,1)S(1)} %copy-done.3, bf16[4,1024,128]{2,1,0:T(8,128)(2,1)S(1)} %copy-done.4, bf16[128,512]{1,0:T(8,128)(2,1)S(1)} %collective-permute-done.before_k, ...), custom_call_target="tpu_custom_call" | custom-call | tf_op jit(solution)/shard_map/attend_dense/pallas_call | solution.py:85
Async XLA Ops:
  6.5 112.2 %all-reduce.3.cloned.1.call-start = ((), (), s32[]{:S(2)}) async-start(), calls=%async_computation | async-start | bytes 4194304 | tf_op jit(solution)/shard_map/psum | solution.py:167
  6.5 1.6 %copy-start = (bf16[2048,512]{1,0:T(8,128)(2,1)S(1)}, bf16[2048,512]{1,0:T(8,128)(2,1)}, u32[]{:S(2)}) copy-start(bf16[2048,512]{1,0:T(8,128)(2,1)} %cache_k.1) | copy-start | bytes 6291460
  8.1 1.6 %copy-start.1 = (bf16[2048,512]{1,0:T(8,128)(2,1)S(1)}, bf16[2048,512]{1,0:T(8,128)(2,1)}, u32[]{:S(2)}) copy-start(bf16[2048,512]{1,0:T(8,128)(2,1)} %cache_v.1) | copy-start | bytes 6291460
  9.7 0.7 copy-start.7
  17.1 0.9 copy-start.5
  17.1 3.3 %copy-start.6 = (bf16[128,512]{1,0:T(8,128)(2,1)S(1)}, bf16[128,512]{1,0:T(8,128)(2,1)}, u32[]{:S(2)}) copy-start(bf16[128,512]{1,0:T(8,128)(2,1)} %own_v.1) | copy-start | bytes 393220
  17.1 101.6 %copy-start.2 = (bf16[128,4096]{1,0:T(8,128)(2,1)S(1)}, bf16[128,4096]{1,0:T(8,128)(2,1)}, u32[]{:S(2)}) copy-start(bf16[128,4096]{1,0:T(8,128)(2,1)} %queries.1) | copy-start | bytes 3145732
  17.2 101.6 %copy-start.8 = (s32[4,64]{1,0:T(4,128)S(1)}, s32[4,64]{1,0:T(4,128)}, u32[]{:S(2)}) copy-start(s32[4,64]{1,0:T(4,128)} %offsets.1) | copy-start | bytes 3076
  18.0 6.9 %collective-permute-start = (bf16[128,512]{1,0:T(8,128)(2,1)S(1)}, bf16[128,512]{1,0:T(8,128)(2,1)S(1)}, u32[]{:S(2)}, u32[]{:S(2)}) collective-permute-start(bf16[128,512]{1,0:T(8,128)(2,1)S(1)} %copy-done.5), channel_id=1, source_target_pairs={{0,1},{1,2},{2,3},{3,4},{4,5},{5,6},{6,7},{7,8},{8,9},{9,10},{10,1... | collective-permute-start | bytes 393224 | tf_op jit(solution)/shard_map/ppermute | solution.py:162
  20.4 5.5 %collective-permute-start.1 = (bf16[128,512]{1,0:T(8,128)(2,1)S(1)}, bf16[128,512]{1,0:T(8,128)(2,1)S(1)}, u32[]{:S(2)}, u32[]{:S(2)}) collective-permute-start(bf16[128,512]{1,0:T(8,128)(2,1)S(1)} %copy-done.6), channel_id=1, source_target_pairs={{0,1},{1,2},{2,3},{3,4},{4,5},{5,6},{6,7},{7,8},{8,9},{9,10},{10,1... | collective-permute-start | bytes 393224 | tf_op jit(solution)/shard_map/ppermute | solution.py:162
  118.8 1.2 copy-start.3
  120.0 1.2 copy-start.4
Sparse Core Ops, SparseCore 0:
  17.3 101.3 all-reduce.2

commit v2 on v1

--- a/solution.py
+++ b/solution.py
@@ -158,8 +158,265 @@
     )(blocks, cache_k, cache_v)
 
 
+STAGES = 2
+ROWS = VBLOCK // STAGES
+WHOLE = pl.BlockSpec(memory_space=pltpu.VMEM)
+
+
+def room(share):
+    mean = ENTRIES * share
+    wide = mean + 3.0 * math.sqrt(mean * (1.0 - share)) + 1.5
+    return min(ENTRIES, math.ceil(wide))
+
+
+def owner_of(blocks, entry, per_device):
+    return lax.div(blocks[entry // NV, entry % NV], per_device)
+
+
+def pack_kernel(per_device, limit, blocks, cache_k, cache_v, kept, sent, sems):
+    me = lax.axis_index("ctx")
+    odd = lax.rem(me, 2)
+
+    def each(act):
+        def step(entry, count):
+            head = entry // NV
+            block = blocks[head, entry % NV]
+            owner = lax.div(block, per_device)
+            mine = owner == me
+            local = block - owner * per_device
+            columns = pl.ds(pl.multiple_of(head * HD, HD), HD)
+
+            @pl.when(mine & (count < limit))
+            def _():
+                for parity, pair in enumerate(((cache_k, cache_v), (cache_v, cache_k))):
+
+                    @pl.when(odd == parity)
+                    def _(pair=pair):
+                        for stage in range(STAGES):
+                            rows = pl.ds(pl.multiple_of(local * VBLOCK + stage * ROWS, ROWS), ROWS)
+                            for i, target in enumerate((kept, sent)):
+                                act(
+                                    pltpu.make_async_copy(
+                                        pair[i].at[rows, columns],
+                                        target.at[stage, count],
+                                        sems.at[count, stage, i],
+                                    )
+                                )
+
+            return count + mine.astype(jnp.int32)
+
+        lax.fori_loop(0, ENTRIES, step, 0)
+
+    each(lambda copy: copy.start())
+    each(lambda copy: copy.wait())
+
+
+def pack(blocks, cache_k, cache_v, limit):
+    shape = jax.ShapeDtypeStruct((STAGES, limit, ROWS, HD), jnp.bfloat16)
+    return pl.pallas_call(
+        functools.partial(pack_kernel, cache_k.shape[0] // VBLOCK, limit),
+        out_shape=(shape, shape),
+        in_specs=[SMEM, ANY, ANY],
+        out_specs=(WHOLE, WHOLE),
+        scratch_shapes=[pltpu.SemaphoreType.DMA((limit, STAGES, 2))],
+        compiler_params=pltpu.CompilerParams(vmem_limit_bytes=16 * 2**20),
+        name="pack",
+    )(blocks, cache_k, cache_v)
+
+
+def merge_loop(blocks, per_device, known, bit, limit, copy_mine, copy_other):
+    me = lax.axis_index("ctx")
+
+    def step(entry, carry):
+        at_mine, at_other = carry
+        away = (owner_of(blocks, entry, per_device) ^ me) & ~known
+        mine, other = away == 0, away == bit
+        place = at_mine + at_other
+
+        @pl.when(mine & (at_mine < limit))
+        def _():
+            copy_mine(entry, at_mine, place)
+
+        @pl.when(other & (at_other < limit))
+        def _():
+            copy_other(entry, at_other, place)
+
+        return at_mine + mine.astype(jnp.int32), at_other + other.astype(jnp.int32)
+
+    lax.fori_loop(0, ENTRIES, step, (0, 0))
+
+
+def merge_kernel(per_device, known, bit, limit, blocks, mine, other, *outs):
+    def copied(source):
+        def copy(entry, at, place):
+            @pl.when(place < outs[0].shape[0])
+            def _():
+                if len(outs) == 1:
+                    outs[0][place] = source[at]
+                else:
+                    for stage, out in enumerate(outs):
+                        out[place] = source[stage, at]
+
+        return copy
+
+    merge_loop(blocks, per_device, known, bit, limit, copied(mine), copied(other))
+
+
+def merged(blocks, per_device, known, bit, mine, other, size):
+    count = STAGES if mine.ndim == 4 else 1
+    shape = jax.ShapeDtypeStruct((size, ROWS, HD), jnp.bfloat16)
+    return pl.pallas_call(
+        functools.partial(merge_kernel, per_device, known, bit, mine.shape[-3]),
+        out_shape=(shape,) * count,
+        in_specs=[SMEM, WHOLE, WHOLE],
+        out_specs=(WHOLE,) * count,
+        compiler_params=pltpu.CompilerParams(vmem_limit_bytes=16 * 2**20),
+        name="merge",
+    )(blocks, mine, other)
+
+
+def stage_kernel(per_device, known, bit, banded, last, *refs):
+    refs = list(refs)
+    blocks = refs.pop(0)
+    offsets = refs.pop(0) if banded else None
+    queries, mine, other, mine_twin, other_twin = refs[:5]
+    refs = refs[5:]
+    if banded:
+        before_k, before_v, own_k, own_v = refs[:4]
+        refs = refs[4:]
+    else:
+        largest_in, mixed_in = refs[:2]
+        refs = refs[2:]
+    outs, (kbuf, vbuf) = refs[:-2], refs[-2:]
+    head = pl.program_id(0)
+    me = lax.axis_index("ctx")
+    wide = NV * ROWS
+
+    @pl.when(head == 0)
+    def _():
+        def assemble(first, second):
+            def copied(pair):
+                def copy(entry, at, place):
+                    rows = pl.ds(pl.multiple_of(lax.rem(entry, NV) * ROWS, ROWS), ROWS)
+                    first[entry // NV, rows, :HD] = pair[0][at]
+                    second[entry // NV, rows, :HD] = pair[1][at]
+
+                return copy
+
+            merge_loop(
+                blocks,
+                per_device,
+                known,
+                bit,
+                mine.shape[0],
+                copied((mine, mine_twin)),
+                copied((other, other_twin)),
+            )
+
+        @pl.when(lax.rem(me, 2) == 0)
+        def _():
+            assemble(kbuf, vbuf)
+
+        @pl.when(lax.rem(me, 2) == 1)
+        def _():
+            assemble(vbuf, kbuf)
+
+        for at in range(KVH):
+            vbuf[at, :, HD:] = jnp.ones((vbuf.shape[1], HD), jnp.bfloat16)
+
+    mask = None
+    if banded:
+        kbuf[head, wide : wide + SMAX] = before_k[...]
+        kbuf[head, wide + SMAX :] = own_k[...]
+        vbuf[head, wide : wide + SMAX, :HD] = before_v[...]
+        vbuf[head, wide + SMAX :, :HD] = own_v[...]
+        mask = band_mask(offsets, head, me == 0)
+    for at in range(0, GROUP, 2):
+        rows = jnp.concatenate(
+            [queries[:, (at + i) * HD : (at + i + 1) * HD] for i in range(2)], axis=0
+        )
+        tile = slice(at * QDEV, (at + 2) * QDEV)
+        largest, mixed = attend_rows(rows, kbuf[head], vbuf[head], mask)
+        if not banded:
+            before = largest_in[tile, :1]
+            above = jnp.maximum(before, largest)
+            mixed = mixed * jnp.exp2(largest - above) + mixed_in[tile] * jnp.exp2(before - above)
+            largest = above
+        if last:
+            result = (mixed[:, :HD] / mixed[:, HD:]).astype(jnp.bfloat16)
+            for i in range(2):
+                outs[0][:, (at + i) * HD : (at + i + 1) * HD] = result[i * QDEV : (i + 1) * QDEV]
+        else:
+            outs[0][tile] = jnp.broadcast_to(largest, (2 * QDEV, HD))
+            outs[1][tile] = mixed
+
+
+def attend_stage(known, bit, per_device, blocks, queries, lists, offsets=None, bands=None, state=None):
+    banded, last = bands is not None, state is not None
+    tall = GROUP * QDEV
+    head_rows = pl.BlockSpec((QDEV, GROUP * HD), lambda head: (0, head))
+    specs = [SMEM] + [SMEM] * banded + [head_rows] + [WHOLE] * 4
+    args = [blocks] + [offsets] * banded + [queries, *lists]
+    states = [
+        pl.BlockSpec((tall, HD), lambda head: (head, 0)),
+        pl.BlockSpec((tall, 2 * HD), lambda head: (head, 0)),
+    ]
+    if banded:
+        before, own_k, own_v = bands
+        second = pl.BlockSpec((QDEV, HD), lambda head: (0, head + KVH))
+        specs += [head_block(QDEV), second, head_block(QDEV), head_block(QDEV)]
+        args += [before, before, own_k, own_v]
+    else:
+        specs += states
+        args += state
+    if last:
+        out_shape = jax.ShapeDtypeStruct(queries.shape, jnp.bfloat16)
+        out_specs = head_rows
+    else:
+        out_shape = (
+            jax.ShapeDtypeStruct((KVH * tall, HD), jnp.float32),
+            jax.ShapeDtypeStruct((KVH * tall, 2 * HD), jnp.float32),
+        )
+        out_specs = tuple(states)
+    keys = NV * ROWS + (SMAX + QDEV) * banded
+    return pl.pallas_call(
+        functools.partial(stage_kernel, per_device, known, bit, banded, last),
+        grid=(KVH,),
+        out_shape=out_shape,
+        in_specs=specs,
+        out_specs=out_specs,
+        scratch_shapes=[
+            pltpu.VMEM((KVH, keys, HD), jnp.bfloat16),
+            pltpu.VMEM((KVH, keys, 2 * HD), jnp.bfloat16),
+        ],
+        compiler_params=pltpu.CompilerParams(vmem_limit_bytes=48 * 2**20),
+        cost_estimate=pl.CostEstimate(
+            flops=4 * KVH * tall * keys * HD,
+            bytes_accessed=8 * 2**20,
+            transcendentals=KVH * tall * keys,
+        ),
+        name="attend_last" if last else "attend_first",
+    )(*args)
+
+
 def permuted(array, pairs):
     return lax.ppermute(array, "ctx", pairs)
+
+
+def swapped(array, bit):
+    return permuted(array, [(i, i ^ bit) for i in range(lax.axis_size("ctx"))])
+
+
+def fits(blocks, per_device, peers, bits):
+    owners = (blocks // per_device).reshape(1, ENTRIES)
+    ids = jnp.arange(peers, dtype=jnp.int32)[:, None]
+    fine = jnp.bool_(True)
+    known = 0
+    for bit in [0] + bits[:-1]:
+        known |= bit
+        counts = jnp.sum((((owners ^ ids) & ~known) == 0).astype(jnp.int32), axis=1)
+        fine &= jnp.max(counts) <= room((1 << known.bit_count()) / peers)
+    return fine
 
 
 def general(queries, bands, cache_k, cache_v, blocks, offsets):
@@ -167,14 +424,43 @@
     keys, values = lax.psum(mine, "ctx")
     keys = keys.reshape(KVH, NV * VBLOCK, HD)
     values = values.reshape(KVH, NV * VBLOCK, HD)
+    before, own_k, own_v = bands
+    wide = KVH * HD
+    bands = (before[:, :wide], own_k, before[:, wide:], own_v)
     return attend_dense(offsets, queries, keys, values, bands)
 
 
 def shards(queries, span_k, span_v, cache_k, cache_v, blocks, offsets):
     peers = lax.axis_size("ctx")
+    per_device = cache_k.shape[0] // VBLOCK
     ahead = [(i, i + 1) for i in range(peers - 1)]
-    bands = (permuted(span_k, ahead), span_k, permuted(span_v, ahead), span_v)
-    return general(queries, bands, cache_k, cache_v, blocks, offsets)
+    bits = [1] + [1 << at for at in range(peers.bit_length() - 2, 0, -1)]
+
+    kept, sent = pack(blocks, cache_k, cache_v, room(1 / peers))
+    other = swapped(sent, 1)
+    lists = merged(blocks, per_device, 0, 1, kept, other, room(2 / peers))
+    known = 1
+    pairs = []
+    for mine in lists:
+        known = 1
+        for bit in bits[1:]:
+            other = swapped(mine, bit)
+            if bit == bits[-1]:
+                break
+            share = (1 << (known | bit).bit_count()) / peers
+            (mine,) = merged(blocks, per_device, known, bit, mine, other, room(share))
+            known |= bit
+        pairs.append((mine, other, swapped(mine, 1), swapped(other, 1)))
+
+    before = permuted(jnp.concatenate([span_k, span_v], axis=1), ahead)
+    bands = (before, span_k, span_v)
+    shared = (known, bits[-1], per_device, blocks, queries)
+    state = attend_stage(*shared, pairs[0], offsets=offsets, bands=bands)
+    return lax.cond(
+        fits(blocks, per_device, peers, bits),
+        lambda: attend_stage(*shared, pairs[1], state=state),
+        lambda: general(queries, bands, cache_k, cache_v, blocks, offsets),
+    )
 
 
 def solution(mesh):

time: 139 us -> 94.1 us (0.68)
  waiting for transfers between devices: 93.8 us -> 22.7 us
  Pallas kernels: 17.2 us -> 38.3 us
  local copies, waits for them, and re-layouts: 7.17 us -> 1.08 us
  starting transfers between devices: 6.92 us -> 11.6 us
  other arithmetic: 0 us -> 3.56 us
  between operations: 13.5 us -> 16.1 us
    psum x1 -> x0, waiting for transfers between devices: 92.8 us -> none  [general(): keys, values = lax.psum(mine, 'ctx')]
    ppermute x2 -> x12, waiting for transfers between devices: 0.95 us -> 22.7 us  [permuted(): return lax.ppermute(array, 'ctx', pairs)]
    pallas_call x2 -> x8, Pallas kernels: 17.2 us -> 38.3 us  [the longest x2 19.6 us: attend_stage(): pl.pallas_call(functools.partial(stage_kernel, per_device, known, bit, ba...]
    unnamed x18 -> x12, local copies, waits for them, and re-layouts: 7.17 us -> 0.99 us
    ppermute x2 -> x12, starting transfers between devices: 6.92 us -> 11.6 us  [permuted(): return lax.ppermute(array, 'ctx', pairs)]
    reduce_max x0 -> x4, other arithmetic: none -> 2.67 us  [fits(): fine &= jnp.max(counts) <= room((1 << known.bit_count()) / peers)]
  transfers between devices with their start and end apart: 3 -> 12, of which waited for: 2 -> 5; matrix products, arithmetic and copies ran while one was open for 0% -> 4% of each run, Pallas kernels for 0% -> 22%
where the time goes in v2:
time: 94.1 us; the launch traced here: 93.3 us
  Pallas kernels  38.3 us (41%)
  waiting for transfers between devices  22.7 us (24%)
  between operations  16.1 us (17%)
  starting transfers between devices  11.6 us (12%)
  other arithmetic  3.56 us (4%)
  local copies, waits for them, and re-layouts  1.08 us (1%)
    ppermute x12, waiting for transfers between devices, permuted(): return lax.ppermute(array, 'ctx', pairs)  22.7 us
    pallas_call x2, Pallas kernels, attend_stage(): pl.pallas_call(functools.partial(stage_kernel, per_device, known, bit, ba...  19.6 us
    pallas_call x5, Pallas kernels, merged(): pl.pallas_call(functools.partial(merge_kernel, per_device, known, bit, mi...  13.3 us
    ppermute x12, starting transfers between devices, permuted(): return lax.ppermute(array, 'ctx', pairs)  11.6 us
    pallas_call x1, Pallas kernels, pack(): pl.pallas_call(functools.partial(pack_kernel, cache_k.shape[0] // VBLOCK,...  5.43 us
    reduce_max x4, other arithmetic, fits(): fine &= jnp.max(counts) <= room((1 << known.bit_count()) / peers)  2.67 us
  transfers between devices with their start and end apart: 12, of which 5 were waited for; matrix products, arithmetic and copies ran while one was open for 4% of the time, Pallas kernels for 22%

profile of v2, /device:TPU:0, one launch (start us, length us, event | category | flops | bytes accessed | tf_op | source)
XLA Modules:
  0.0 93.3 jit_solution(2389852907481321479)
XLA Ops:
  6.5 5.4 %pack.1 = (bf16[2,12,32,128]{3,2,1,0:T(8,128)(2,1)S(1)}, bf16[2,12,32,128]{3,2,1,0:T(8,128)(2,1)S(1)}) custom-call(s32[4,16]{1,0:T(4,128)} %refs_0_.1, bf16[2048,512]{1,0:T(8,128)(2,1)} %cache_k.1, bf16[2048,512]{1,0:T(8,128)(2,1)} %cache_v.1), custom_call_target="tpu_custom_call" | custom-call | tf_op jit(solution)/shard_map/pack/pallas_call | solution.py:216
  12.0 0.0 copy-start.4
  12.0 0.0 copy-start.5
  12.0 0.0 copy-start.2
  12.0 0.0 copy-start.7
  12.0 0.5 collective-permute-start.1
  12.5 1.1 %collective-permute-done.1.other = bf16[2,12,32,128]{3,2,1,0:T(8,128)(2,1)S(1)} collective-permute-done((bf16[2,12,32,128]{3,2,1,0:T(8,128)(2,1)S(1)}, bf16[2,12,32,128]{3,2,1,0:T(8,128)(2,1)S(1)}, u32[]{:S(2)}, u32[]{:S(2)}) %collective-permute-start.1) | collective-permute-done | bytes 196640 | tf_op jit(solution)/shard_map/ppermute | solution.py:403
  13.6 2.6 %merge.5 = (bf16[18,32,128]{2,1,0:T(8,128)(2,1)S(1)}, bf16[18,32,128]{2,1,0:T(8,128)(2,1)S(1)}) custom-call(s32[4,16]{1,0:T(4,128)S(1)} %copy-done.6, bf16[2,12,32,128]{3,2,1,0:T(8,128)(2,1)S(1)} %get-tuple-element.64.mine, bf16[2,12,32,128]{3,2,1,0:T(8,128)(2,1)S(1)} %collective-permute-done.1.other), custom_call_target="tpu_custom_call" | custom-call | tf_op jit(solution)/shard_map/merge/pallas_call | solution.py:268
  16.3 4.0 %collective-permute-start.7 = (bf16[18,32,128]{2,1,0:T(8,128)(2,1)S(1)}, bf16[18,32,128]{2,1,0:T(8,128)(2,1)S(1)}, u32[]{:S(2)}, u32[]{:S(2)}) collective-permute-start(bf16[18,32,128]{2,1,0:T(8,128)(2,1)S(1)} %get-tuple-element.67.mine), channel_id=1, source_target_pairs={{0,8},{1,9},{2,10},{3,11},{4,12},{5,13},{6,14},{7,15},{8,0},{9,1},... | collective-permute-start | bytes 442376 | tf_op jit(solution)/shard_map/ppermute | solution.py:403
  20.3 0.1 collective-permute-start.2
  20.4 10.9 %collective-permute-done.7.other = bf16[18,32,128]{2,1,0:T(8,128)(2,1)S(1)} collective-permute-done((bf16[18,32,128]{2,1,0:T(8,128)(2,1)S(1)}, bf16[18,32,128]{2,1,0:T(8,128)(2,1)S(1)}, u32[]{:S(2)}, u32[]{:S(2)}) %collective-permute-start.7) | collective-permute-done | bytes 147488 | tf_op jit(solution)/shard_map/ppermute | solution.py:403
  31.2 2.7 %merge.8.mine = bf16[28,32,128]{2,1,0:T(8,128)(2,1)S(1)} custom-call(s32[4,16]{1,0:T(4,128)S(1)} %copy-done.6, bf16[18,32,128]{2,1,0:T(8,128)(2,1)S(1)} %get-tuple-element.67.mine, bf16[18,32,128]{2,1,0:T(8,128)(2,1)S(1)} %collective-permute-done.7.other), custom_call_target="tpu_custom_call" | custom-call | tf_op jit(solution)/shard_map/merge/pallas_call | solution.py:268
  33.9 0.4 collective-permute-start.8
  34.3 0.0 collective-permute-done.2.other
  34.3 2.7 %merge.6.mine = bf16[28,32,128]{2,1,0:T(8,128)(2,1)S(1)} custom-call(s32[4,16]{1,0:T(4,128)S(1)} %copy-done.6, bf16[18,32,128]{2,1,0:T(8,128)(2,1)S(1)} %get-tuple-element.66.mine, bf16[18,32,128]{2,1,0:T(8,128)(2,1)S(1)} %collective-permute-done.2.other), custom_call_target="tpu_custom_call" | custom-call | tf_op jit(solution)/shard_map/merge/pallas_call | solution.py:268
  37.0 1.8 %collective-permute-start.3 = (bf16[28,32,128]{2,1,0:T(8,128)(2,1)S(1)}, bf16[28,32,128]{2,1,0:T(8,128)(2,1)S(1)}, u32[]{:S(2)}, u32[]{:S(2)}) collective-permute-start(bf16[28,32,128]{2,1,0:T(8,128)(2,1)S(1)} %merge.6.mine), channel_id=1, source_target_pairs={{0,4},{1,5},{2,6},{3,7},{4,0},{5,1},{6,2},{7,3},{8,12},{9,13},{10,... | collective-permute-start | bytes 688136 | tf_op jit(solution)/shard_map/ppermute | solution.py:403
  38.7 3.2 %collective-permute-done.8.other = bf16[28,32,128]{2,1,0:T(8,128)(2,1)S(1)} collective-permute-done((bf16[28,32,128]{2,1,0:T(8,128)(2,1)S(1)}, bf16[28,32,128]{2,1,0:T(8,128)(2,1)S(1)}, u32[]{:S(2)}, u32[]{:S(2)}) %collective-permute-start.8) | collective-permute-done | bytes 229408 | tf_op jit(solution)/shard_map/ppermute | solution.py:403
  41.9 2.7 %merge.9.refs_3_ = bf16[46,32,128]{2,1,0:T(8,128)(2,1)S(1)} custom-call(s32[4,16]{1,0:T(4,128)S(1)} %copy-done.6, bf16[28,32,128]{2,1,0:T(8,128)(2,1)S(1)} %merge.8.mine, bf16[28,32,128]{2,1,0:T(8,128)(2,1)S(1)} %collective-permute-done.8.other), custom_call_target="tpu_custom_call" | custom-call | tf_op jit(solution)/shard_map/merge/pallas_call | solution.py:268
  44.5 1.1 %collective-permute-start.9 = (bf16[46,32,128]{2,1,0:T(8,128)(2,1)S(1)}, bf16[46,32,128]{2,1,0:T(8,128)(2,1)S(1)}, u32[]{:S(2)}, u32[]{:S(2)}) collective-permute-start(bf16[46,32,128]{2,1,0:T(8,128)(2,1)S(1)} %merge.9.refs_3_), channel_id=1, source_target_pairs={{0,2},{1,3},{2,0},{3,1},{4,6},{5,7},{6,4},{7,5},{8,10},{9,11},{10,... | collective-permute-start | bytes 1130504 | tf_op jit(solution)/shard_map/ppermute | solution.py:403
  45.6 0.0 collective-permute-done.3.other
  45.6 2.7 %merge.7 = bf16[46,32,128]{2,1,0:T(8,128)(2,1)S(1)} custom-call(s32[4,16]{1,0:T(4,128)S(1)} %copy-done.6, bf16[28,32,128]{2,1,0:T(8,128)(2,1)S(1)} %merge.6.mine, bf16[28,32,128]{2,1,0:T(8,128)(2,1)S(1)} %collective-permute-done.3.other), custom_call_target="tpu_custom_call" | custom-call | tf_op jit(solution)/shard_map/merge/pallas_call | solution.py:268
  48.3 1.2 %collective-permute-start.4 = (bf16[46,32,128]{2,1,0:T(8,128)(2,1)S(1)}, bf16[46,32,128]{2,1,0:T(8,128)(2,1)}, u32[]{:S(2)}, u32[]{:S(2)}) collective-permute-start(bf16[46,32,128]{2,1,0:T(8,128)(2,1)S(1)} %merge.7), channel_id=1, source_target_pairs={{0,2},{1,3},{2,0},{3,1},{4,6},{5,7},{6,4},{7,5},{8,10},{9,11},{10,... | collective-permute-start | bytes 1130504 | tf_op jit(solution)/shard_map/ppermute | solution.py:403
  49.5 0.0 collective-permute-start.10
  49.5 5.2 %collective-permute-done.9.refs_4_ = bf16[46,32,128]{2,1,0:T(8,128)(2,1)S(1)} collective-permute-done((bf16[46,32,128]{2,1,0:T(8,128)(2,1)S(1)}, bf16[46,32,128]{2,1,0:T(8,128)(2,1)S(1)}, u32[]{:S(2)}, u32[]{:S(2)}) %collective-permute-start.9) | collective-permute-done | bytes 376864 | tf_op jit(solution)/shard_map/ppermute | solution.py:403
  54.7 0.0 collective-permute-start.11
  54.7 0.7 pad_maximum_fusion
  55.4 2.4 %collective-permute-start = (bf16[128,1024]{1,0:T(8,128)(2,1)}, bf16[128,1024]{1,0:T(8,128)(2,1)S(1)}, u32[]{:S(2)}, u32[]{:S(2)}) collective-permute-start(bf16[128,1024]{1,0:T(8,128)(2,1)} %pad_maximum_fusion), channel_id=1, source_target_pairs={{0,1},{1,2},{2,3},{3,4},{4,5},{5,6},{6,7},{7,8},{8,9},{9,10},{10,1... | collective-permute-start | bytes 786440 | tf_op jit(solution)/shard_map/ppermute | solution.py:403
  57.9 0.1 collective-permute-start.5
  58.0 2.4 %collective-permute-done.4 = bf16[46,32,128]{2,1,0:T(8,128)(2,1)} collective-permute-done((bf16[46,32,128]{2,1,0:T(8,128)(2,1)S(1)}, bf16[46,32,128]{2,1,0:T(8,128)(2,1)}, u32[]{:S(2)}, u32[]{:S(2)}) %collective-permute-start.4) | collective-permute-done | bytes 376864 | tf_op jit(solution)/shard_map/ppermute | solution.py:403
  60.4 0.0 collective-permute-start.6
  60.4 0.1 xor.8
  60.5 0.2 convert_reduce_fusion
  60.7 0.6 reduce_max.36
  61.3 0.7 reduce_max.37
  62.0 0.7 reduce_max.38
  62.7 0.7 reduce_max.39
  65.9 0.0 collective-permute-done.refs_7_.refs_8_
  65.9 0.0 collective-permute-done.10.refs_5_
  65.9 0.0 collective-permute-done.11.refs_6_
  65.9 0.0 copy-done.2
  65.9 0.0 copy-done.7
  65.9 10.2 %attend_first.1 = (f32[4096,128]{1,0:T(8,128)}, f32[4096,256]{1,0:T(8,128)}) custom-call(s32[4,16]{1,0:T(4,128)S(1)} %copy-done.6, s32[4,64]{1,0:T(4,128)S(1)} %copy-done.7, bf16[128,4096]{1,0:T(8,128)(2,1)S(1)} %copy-done.2, bf16[46,32,128]{2,1,0:T(8,128)(2,1)S(1)} %merge.9.refs_3_, bf16[46,32,128]{2,1,0:T(8,128)(2,1)S(1)} %collective-permute-done.9.refs_4_, ...), custom_call_target="tpu_custom_call" | custom-call | flops 1610612736 | bytes 8388608 | tf_op jit(solution)/shard_map/attend_first/pallas_call | solution.py:382
  76.1 0.0 collective-permute-done.5
  76.1 0.0 collective-permute-done.6
  76.1 9.4 %conditional.1 = (bf16[128,4096]{1,0:T(8,128)(2,1)S(1)}) conditional(s32[]{:T(128)} %convert_element_type.19, (s32[4,16]{1,0:T(4,128)S(1)}, bf16[2048,512]{1,0:T(8,128)(2,1)}, bf16[2048,512]{1,0:T(8,128)(2,1)}, bf16[128,1024]{1,0:T(8,128)(2,1)S(1)}, s32[4,64]{1,0:T(4,128)S(1)}, /*index=5*/bf16[128,4096]{1,0:T(8,128)(2,1)S(1)}, ...), branch_computations={%region_8.11_spmd, %region_11.12_spmd} | conditional | flops 1073741824 | bytes 21495912 | solution.py:459
  76.2 9.3 %attend_last.1 = bf16[128,4096]{1,0:T(8,128)(2,1)S(1)} custom-call(s32[4,16]{1,0:T(4,128)S(1)} %get-tuple-element.50.refs_0_, bf16[128,4096]{1,0:T(8,128)(2,1)S(1)} %get-tuple-element.51.refs_1_, bf16[46,32,128]{2,1,0:T(8,128)(2,1)S(1)} %get-tuple-element.52.refs_2_, bf16[46,32,128]{2,1,0:T(8,128)(2,1)} %get-tuple-element.53.refs_3_, ...), custom_call_target="tpu_custom_call" | custom-call | flops 1073741824 | bytes 8388608 | tf_op jit(solution)/shard_map/cond/branch_1_fun/attend_last/pallas_call | solution.py:382
  85.5 0.0 copy-start.3
  85.5 1.0 %copy-done.3 = bf16[128,4096]{1,0:T(8,128)(2,1)} copy-done((bf16[128,4096]{1,0:T(8,128)(2,1)}, bf16[128,4096]{1,0:T(8,128)(2,1)S(1)}, u32[]{:S(2)}) %copy-start.3) | copy-done | bytes 1048600
  (5 shorter events, 0.0 us)
Async XLA Ops:
  6.5 7.1 %copy-start.6 = (s32[4,16]{1,0:T(4,128)S(1)}, s32[4,16]{1,0:T(4,128)}, u32[]{:S(2)}) copy-start(s32[4,16]{1,0:T(4,128)} %refs_0_.1) | copy-start | bytes 772
  12.0 42.7 %copy-start.4 = (bf16[128,512]{1,0:T(8,128)(2,1)S(1)}, bf16[128,512]{1,0:T(8,128)(2,1)}, u32[]{:S(2)}) copy-start(bf16[128,512]{1,0:T(8,128)(2,1)} %refs_10_.1) | copy-start | bytes 393220
  12.0 42.7 %copy-start.5 = (bf16[128,512]{1,0:T(8,128)(2,1)S(1)}, bf16[128,512]{1,0:T(8,128)(2,1)}, u32[]{:S(2)}) copy-start(bf16[128,512]{1,0:T(8,128)(2,1)} %refs_9_.1) | copy-start | bytes 393220
  12.0 53.9 %copy-start.2 = (bf16[128,4096]{1,0:T(8,128)(2,1)S(1)}, bf16[128,4096]{1,0:T(8,128)(2,1)}, u32[]{:S(2)}) copy-start(bf16[128,4096]{1,0:T(8,128)(2,1)} %refs_2_.1) | copy-start | bytes 3145732
  12.0 53.9 %copy-start.7 = (s32[4,64]{1,0:T(4,128)S(1)}, s32[4,64]{1,0:T(4,128)}, u32[]{:S(2)}) copy-start(s32[4,64]{1,0:T(4,128)} %refs_1_.1) | copy-start | bytes 3076
  12.0 1.6 %collective-permute-start.1 = (bf16[2,12,32,128]{3,2,1,0:T(8,128)(2,1)S(1)}, bf16[2,12,32,128]{3,2,1,0:T(8,128)(2,1)S(1)}, u32[]{:S(2)}, u32[]{:S(2)}) collective-permute-start(bf16[2,12,32,128]{3,2,1,0:T(8,128)(2,1)S(1)} %get-tuple-element.65), channel_id=1, source_target_pairs={{0,1},{1,0},{2,3},{3,2},{4,5},{5,4},{6,7},{7,6},{8,9},{9,8},{10,11... | collective-permute-start | bytes 589832 | tf_op jit(solution)/shard_map/ppermute | solution.py:403
  16.3 15.0 %collective-permute-start.7 = (bf16[18,32,128]{2,1,0:T(8,128)(2,1)S(1)}, bf16[18,32,128]{2,1,0:T(8,128)(2,1)S(1)}, u32[]{:S(2)}, u32[]{:S(2)}) collective-permute-start(bf16[18,32,128]{2,1,0:T(8,128)(2,1)S(1)} %get-tuple-element.67.mine), channel_id=1, source_target_pairs={{0,8},{1,9},{2,10},{3,11},{4,12},{5,13},{6,14},{7,15},{8,0},{9,1},... | collective-permute-start | bytes 442376 | tf_op jit(solution)/shard_map/ppermute | solution.py:403
  20.3 14.0 %collective-permute-start.2 = (bf16[18,32,128]{2,1,0:T(8,128)(2,1)S(1)}, bf16[18,32,128]{2,1,0:T(8,128)(2,1)S(1)}, u32[]{:S(2)}, u32[]{:S(2)}) collective-permute-start(bf16[18,32,128]{2,1,0:T(8,128)(2,1)S(1)} %get-tuple-element.66.mine), channel_id=1, source_target_pairs={{0,8},{1,9},{2,10},{3,11},{4,12},{5,13},{6,14},{7,15},{8,0},{9,1},... | collective-permute-start | bytes 442376 | tf_op jit(solution)/shard_map/ppermute | solution.py:403
  33.9 8.0 %collective-permute-start.8 = (bf16[28,32,128]{2,1,0:T(8,128)(2,1)S(1)}, bf16[28,32,128]{2,1,0:T(8,128)(2,1)S(1)}, u32[]{:S(2)}, u32[]{:S(2)}) collective-permute-start(bf16[28,32,128]{2,1,0:T(8,128)(2,1)S(1)} %merge.8.mine), channel_id=1, source_target_pairs={{0,4},{1,5},{2,6},{3,7},{4,0},{5,1},{6,2},{7,3},{8,12},{9,13},{10,... | collective-permute-start | bytes 688136 | tf_op jit(solution)/shard_map/ppermute | solution.py:403
  37.0 8.7 %collective-permute-start.3 = (bf16[28,32,128]{2,1,0:T(8,128)(2,1)S(1)}, bf16[28,32,128]{2,1,0:T(8,128)(2,1)S(1)}, u32[]{:S(2)}, u32[]{:S(2)}) collective-permute-start(bf16[28,32,128]{2,1,0:T(8,128)(2,1)S(1)} %merge.6.mine), channel_id=1, source_target_pairs={{0,4},{1,5},{2,6},{3,7},{4,0},{5,1},{6,2},{7,3},{8,12},{9,13},{10,... | collective-permute-start | bytes 688136 | tf_op jit(solution)/shard_map/ppermute | solution.py:403
  44.5 10.2 %collective-permute-start.9 = (bf16[46,32,128]{2,1,0:T(8,128)(2,1)S(1)}, bf16[46,32,128]{2,1,0:T(8,128)(2,1)S(1)}, u32[]{:S(2)}, u32[]{:S(2)}) collective-permute-start(bf16[46,32,128]{2,1,0:T(8,128)(2,1)S(1)} %merge.9.refs_3_), channel_id=1, source_target_pairs={{0,2},{1,3},{2,0},{3,1},{4,6},{5,7},{6,4},{7,5},{8,10},{9,11},{10,... | collective-permute-start | bytes 1130504 | tf_op jit(solution)/shard_map/ppermute | solution.py:403
  48.3 12.1 %collective-permute-start.4 = (bf16[46,32,128]{2,1,0:T(8,128)(2,1)S(1)}, bf16[46,32,128]{2,1,0:T(8,128)(2,1)}, u32[]{:S(2)}, u32[]{:S(2)}) collective-permute-start(bf16[46,32,128]{2,1,0:T(8,128)(2,1)S(1)} %merge.7), channel_id=1, source_target_pairs={{0,2},{1,3},{2,0},{3,1},{4,6},{5,7},{6,4},{7,5},{8,10},{9,11},{10,... | collective-permute-start | bytes 1130504 | tf_op jit(solution)/shard_map/ppermute | solution.py:403
  49.5 16.4 %collective-permute-start.10 = (bf16[46,32,128]{2,1,0:T(8,128)(2,1)S(1)}, bf16[46,32,128]{2,1,0:T(8,128)(2,1)S(1)}, u32[]{:S(2)}, u32[]{:S(2)}) collective-permute-start(bf16[46,32,128]{2,1,0:T(8,128)(2,1)S(1)} %merge.9.refs_3_), channel_id=1, source_target_pairs={{0,1},{1,0},{2,3},{3,2},{4,5},{5,4},{6,7},{7,6},{8,9},{9,8},{10,11... | collective-permute-start | bytes 1130504 | tf_op jit(solution)/shard_map/ppermute | solution.py:403
  54.7 11.2 %collective-permute-start.11 = (bf16[46,32,128]{2,1,0:T(8,128)(2,1)S(1)}, bf16[46,32,128]{2,1,0:T(8,128)(2,1)S(1)}, u32[]{:S(2)}, u32[]{:S(2)}) collective-permute-start(bf16[46,32,128]{2,1,0:T(8,128)(2,1)S(1)} %collective-permute-done.9.refs_4_), channel_id=1, source_target_pairs={{0,1},{1,0},{2,3},{3,2},{4,5},{5,4},{6,7},{7,6},{8,9},{9,8},{10,11... | collective-permute-start | bytes 1130504 | tf_op jit(solution)/shard_map/ppermute | solution.py:403
  55.4 10.4 %collective-permute-start = (bf16[128,1024]{1,0:T(8,128)(2,1)}, bf16[128,1024]{1,0:T(8,128)(2,1)S(1)}, u32[]{:S(2)}, u32[]{:S(2)}) collective-permute-start(bf16[128,1024]{1,0:T(8,128)(2,1)} %pad_maximum_fusion), channel_id=1, source_target_pairs={{0,1},{1,2},{2,3},{3,4},{4,5},{5,6},{6,7},{7,8},{8,9},{9,10},{10,1... | collective-permute-start | bytes 786440 | tf_op jit(solution)/shard_map/ppermute | solution.py:403
  57.9 18.3 %collective-permute-start.5 = (bf16[46,32,128]{2,1,0:T(8,128)(2,1)S(1)}, bf16[46,32,128]{2,1,0:T(8,128)(2,1)}, u32[]{:S(2)}, u32[]{:S(2)}) collective-permute-start(bf16[46,32,128]{2,1,0:T(8,128)(2,1)S(1)} %merge.7), channel_id=1, source_target_pairs={{0,1},{1,0},{2,3},{3,2},{4,5},{5,4},{6,7},{7,6},{8,9},{9,8},{10,11... | collective-permute-start | bytes 1130504 | tf_op jit(solution)/shard_map/ppermute | solution.py:403
  60.4 15.7 %collective-permute-start.6 = (bf16[46,32,128]{2,1,0:T(8,128)(2,1)}, bf16[46,32,128]{2,1,0:T(8,128)(2,1)}, u32[]{:S(2)}, u32[]{:S(2)}) collective-permute-start(bf16[46,32,128]{2,1,0:T(8,128)(2,1)} %collective-permute-done.4), channel_id=1, source_target_pairs={{0,1},{1,0},{2,3},{3,2},{4,5},{5,4},{6,7},{7,6},{8,9},{9,8},{10,11... | collective-permute-start | bytes 1130504 | tf_op jit(solution)/shard_map/ppermute | solution.py:403
  85.5 1.0 %copy-start.3 = (bf16[128,4096]{1,0:T(8,128)(2,1)}, bf16[128,4096]{1,0:T(8,128)(2,1)S(1)}, u32[]{:S(2)}) copy-start(bf16[128,4096]{1,0:T(8,128)(2,1)S(1)} %get-tuple-element.106) | copy-start | bytes 3145732

commit v3 on v2

--- a/solution.py
+++ b/solution.py
@@ -166,107 +166,95 @@
 def room(share):
     mean = ENTRIES * share
     wide = mean + 3.0 * math.sqrt(mean * (1.0 - share)) + 1.5
-    return min(ENTRIES, math.ceil(wide))
-
-
-def owner_of(blocks, entry, per_device):
-    return lax.div(blocks[entry // NV, entry % NV], per_device)
+    return min(ENTRIES + 1, math.ceil(wide))
+
+
+def owner_of(block, per_device):
+    if per_device & (per_device - 1) == 0:
+        return lax.shift_right_logical(block, per_device.bit_length() - 1)
+    return lax.div(block, per_device)
 
 
 def pack_kernel(per_device, limit, blocks, cache_k, cache_v, kept, sent, sems):
     me = lax.axis_index("ctx")
-    odd = lax.rem(me, 2)
-
-    def each(act):
-        def step(entry, count):
-            head = entry // NV
-            block = blocks[head, entry % NV]
-            owner = lax.div(block, per_device)
-            mine = owner == me
-            local = block - owner * per_device
-            columns = pl.ds(pl.multiple_of(head * HD, HD), HD)
-
-            @pl.when(mine & (count < limit))
+    even = lax.rem(me, 2) == 0
+    count = jnp.int32(0)
+    for entry in range(ENTRIES):
+        head = entry // NV
+        block = blocks[head, entry % NV]
+        owner = owner_of(block, per_device)
+        mine = owner == me
+        local = block - owner * per_device
+
+        def start(pair, head=head, local=local, count=count):
+            rows = pl.ds(pl.multiple_of(local * VBLOCK, VBLOCK), VBLOCK)
+            for i, target in enumerate((kept, sent)):
+                source = pair[i].at[rows, pl.ds(head * HD, HD)]
+                pltpu.make_async_copy(source, target.at[count], sems.at[count, i]).start()
+
+        @pl.when(mine & (count < limit))
+        def _(start=start):
+            @pl.when(even)
             def _():
-                for parity, pair in enumerate(((cache_k, cache_v), (cache_v, cache_k))):
-
-                    @pl.when(odd == parity)
-                    def _(pair=pair):
-                        for stage in range(STAGES):
-                            rows = pl.ds(pl.multiple_of(local * VBLOCK + stage * ROWS, ROWS), ROWS)
-                            for i, target in enumerate((kept, sent)):
-                                act(
-                                    pltpu.make_async_copy(
-                                        pair[i].at[rows, columns],
-                                        target.at[stage, count],
-                                        sems.at[count, stage, i],
-                                    )
-                                )
-
-            return count + mine.astype(jnp.int32)
-
-        lax.fori_loop(0, ENTRIES, step, 0)
-
-    each(lambda copy: copy.start())
-    each(lambda copy: copy.wait())
+                start((cache_k, cache_v))
+
+            @pl.when(jnp.logical_not(even))
+            def _():
+                start((cache_v, cache_k))
+
+        count += mine.astype(jnp.int32)
+
+    for at in range(limit):
+
+        @pl.when(at < count)
+        def _(at=at):
+            for i, target in enumerate((kept, sent)):
+                source = cache_k.at[pl.ds(0, VBLOCK), pl.ds(0, HD)]
+                pltpu.make_async_copy(source, target.at[at], sems.at[at, i]).wait()
 
 
 def pack(blocks, cache_k, cache_v, limit):
-    shape = jax.ShapeDtypeStruct((STAGES, limit, ROWS, HD), jnp.bfloat16)
+    shape = jax.ShapeDtypeStruct((limit, VBLOCK, HD), jnp.bfloat16)
     return pl.pallas_call(
         functools.partial(pack_kernel, cache_k.shape[0] // VBLOCK, limit),
         out_shape=(shape, shape),
         in_specs=[SMEM, ANY, ANY],
         out_specs=(WHOLE, WHOLE),
-        scratch_shapes=[pltpu.SemaphoreType.DMA((limit, STAGES, 2))],
+        scratch_shapes=[pltpu.SemaphoreType.DMA((limit, 2))],
         compiler_params=pltpu.CompilerParams(vmem_limit_bytes=16 * 2**20),
         name="pack",
     )(blocks, cache_k, cache_v)
 
 
-def merge_loop(blocks, per_device, known, bit, limit, copy_mine, copy_other):
+def walk(blocks, per_device, known, bit, limits, act):
     me = lax.axis_index("ctx")
-
-    def step(entry, carry):
-        at_mine, at_other = carry
-        away = (owner_of(blocks, entry, per_device) ^ me) & ~known
+    at_mine = at_other = jnp.int32(0)
+    for entry in range(ENTRIES):
+        away = (owner_of(blocks[entry // NV, entry % NV], per_device) ^ me) & ~known
         mine, other = away == 0, away == bit
-        place = at_mine + at_other
-
-        @pl.when(mine & (at_mine < limit))
-        def _():
-            copy_mine(entry, at_mine, place)
-
-        @pl.when(other & (at_other < limit))
-        def _():
-            copy_other(entry, at_other, place)
-
-        return at_mine + mine.astype(jnp.int32), at_other + other.astype(jnp.int32)
-
-    lax.fori_loop(0, ENTRIES, step, (0, 0))
-
-
-def merge_kernel(per_device, known, bit, limit, blocks, mine, other, *outs):
-    def copied(source):
-        def copy(entry, at, place):
-            @pl.when(place < outs[0].shape[0])
-            def _():
-                if len(outs) == 1:
-                    outs[0][place] = source[at]
-                else:
-                    for stage, out in enumerate(outs):
-                        out[place] = source[stage, at]
-
-        return copy
-
-    merge_loop(blocks, per_device, known, bit, limit, copied(mine), copied(other))
+        tops = jnp.minimum(at_mine, limits[0] - 1), jnp.minimum(at_other, limits[1] - 1)
+        act(entry, *tops, at_mine + at_other, other)
+        at_mine += mine.astype(jnp.int32)
+        at_other += other.astype(jnp.int32)
+
+
+def merge_kernel(per_device, known, bit, blocks, mine, other, *outs):
+    size = outs[0].shape[0]
+
+    def act(entry, at_mine, at_other, place, theirs):
+        tile = jnp.where(theirs, other[at_other], mine[at_mine])
+        place = jnp.minimum(place, size - 1)
+        for stage, out in enumerate(outs):
+            out[place] = tile[stage * ROWS : (stage + 1) * ROWS]
+
+    walk(blocks, per_device, known, bit, (mine.shape[0], other.shape[0]), act)
 
 
 def merged(blocks, per_device, known, bit, mine, other, size):
-    count = STAGES if mine.ndim == 4 else 1
+    count = mine.shape[1] // ROWS
     shape = jax.ShapeDtypeStruct((size, ROWS, HD), jnp.bfloat16)
     return pl.pallas_call(
-        functools.partial(merge_kernel, per_device, known, bit, mine.shape[-3]),
+        functools.partial(merge_kernel, per_device, known, bit),
         out_shape=(shape,) * count,
         in_specs=[SMEM, WHOLE, WHOLE],
         out_specs=(WHOLE,) * count,
@@ -294,33 +282,16 @@
 
     @pl.when(head == 0)
     def _():
-        def assemble(first, second):
-            def copied(pair):
-                def copy(entry, at, place):
-                    rows = pl.ds(pl.multiple_of(lax.rem(entry, NV) * ROWS, ROWS), ROWS)
-                    first[entry // NV, rows, :HD] = pair[0][at]
-                    second[entry // NV, rows, :HD] = pair[1][at]
-
-                return copy
-
-            merge_loop(
-                blocks,
-                per_device,
-                known,
-                bit,
-                mine.shape[0],
-                copied((mine, mine_twin)),
-                copied((other, other_twin)),
-            )
-
-        @pl.when(lax.rem(me, 2) == 0)
-        def _():
-            assemble(kbuf, vbuf)
-
-        @pl.when(lax.rem(me, 2) == 1)
-        def _():
-            assemble(vbuf, kbuf)
-
+        even = lax.rem(me, 2) == 0
+
+        def act(entry, at_mine, at_other, place, theirs):
+            tile = jnp.where(theirs, other[at_other], mine[at_mine])
+            twin = jnp.where(theirs, other_twin[at_other], mine_twin[at_mine])
+            rows = pl.ds(entry % NV * ROWS, ROWS)
+            kbuf[entry // NV, rows] = jnp.where(even, tile, twin)
+            vbuf[entry // NV, rows, :HD] = jnp.where(even, twin, tile)
+
+        walk(blocks, per_device, known, bit, (mine.shape[0], other.shape[0]), act)
         for at in range(KVH):
             vbuf[at, :, HD:] = jnp.ones((vbuf.shape[1], HD), jnp.bfloat16)
 
@@ -408,20 +379,19 @@
 
 
 def fits(blocks, per_device, peers, bits):
-    owners = (blocks // per_device).reshape(1, ENTRIES)
-    ids = jnp.arange(peers, dtype=jnp.int32)[:, None]
-    fine = jnp.bool_(True)
-    known = 0
-    for bit in [0] + bits[:-1]:
-        known |= bit
-        counts = jnp.sum((((owners ^ ids) & ~known) == 0).astype(jnp.int32), axis=1)
-        fine &= jnp.max(counts) <= room((1 << known.bit_count()) / peers)
-    return fine
-
-
-def general(queries, bands, cache_k, cache_v, blocks, offsets):
-    mine = owned_blocks(blocks, cache_k, cache_v)
-    keys, values = lax.psum(mine, "ctx")
+    masks = [sum(bits[:at]) for at in range(len(bits))]
+    most = [room((1 << at) / peers) - (at > 0) for at in range(len(bits))]
+    owners = (blocks // per_device).reshape(1, 1, ENTRIES)
+    ids = jnp.arange(peers, dtype=jnp.int32)[None, :, None]
+    away = (owners ^ ids) & ~jnp.array(masks, jnp.int32)[:, None, None]
+    counts = jnp.sum((away == 0).astype(jnp.int32), axis=2)
+    return jnp.all(counts <= jnp.array(most, jnp.int32)[:, None])
+
+
+def general(queries, bands, cache_k, cache_v, blocks, offsets, bits):
+    keys, values = owned_blocks(blocks, cache_k, cache_v)
+    for bit in bits:
+        keys, values = keys + swapped(keys, bit), values + swapped(values, bit)
     keys = keys.reshape(KVH, NV * VBLOCK, HD)
     values = values.reshape(KVH, NV * VBLOCK, HD)
     before, own_k, own_v = bands
@@ -437,29 +407,31 @@
     bits = [1] + [1 << at for at in range(peers.bit_length() - 2, 0, -1)]
 
     kept, sent = pack(blocks, cache_k, cache_v, room(1 / peers))
-    other = swapped(sent, 1)
-    lists = merged(blocks, per_device, 0, 1, kept, other, room(2 / peers))
+    mine = list(merged(blocks, per_device, 0, 1, kept, swapped(sent, 1), room(2 / peers)))
+    before = permuted(jnp.concatenate([span_k, span_v], axis=1), ahead)
+    other = [None] * STAGES
     known = 1
-    pairs = []
-    for mine in lists:
-        known = 1
-        for bit in bits[1:]:
-            other = swapped(mine, bit)
-            if bit == bits[-1]:
-                break
-            share = (1 << (known | bit).bit_count()) / peers
-            (mine,) = merged(blocks, per_device, known, bit, mine, other, room(share))
-            known |= bit
-        pairs.append((mine, other, swapped(mine, 1), swapped(other, 1)))
-
-    before = permuted(jnp.concatenate([span_k, span_v], axis=1), ahead)
+    for bit in bits[1:]:
+        other[0] = swapped(mine[0], bit)
+        if bit == bits[1]:
+            other[0], before = lax.optimization_barrier((other[0], before))
+            other[0], mine[1] = lax.optimization_barrier((other[0], mine[1]))
+        other[1] = swapped(mine[1], bit)
+        if bit == bits[-1]:
+            break
+        size = room((1 << (known | bit).bit_count()) / peers)
+        for stage in range(STAGES):
+            (mine[stage],) = merged(blocks, per_device, known, bit, mine[stage], other[stage], size)
+        known |= bit
+    lists = [(m, o, swapped(m, 1), swapped(o, 1)) for m, o in zip(mine, other)]
+
     bands = (before, span_k, span_v)
     shared = (known, bits[-1], per_device, blocks, queries)
-    state = attend_stage(*shared, pairs[0], offsets=offsets, bands=bands)
+    state = attend_stage(*shared, lists[0], offsets=offsets, bands=bands)
     return lax.cond(
         fits(blocks, per_device, peers, bits),
-        lambda: attend_stage(*shared, pairs[1], state=state),
-        lambda: general(queries, bands, cache_k, cache_v, blocks, offsets),
+        lambda: attend_stage(*shared, lists[1], state=state),
+        lambda: general(queries, bands, cache_k, cache_v, blocks, offsets, bits),
     )
 
 

time: 94.1 us -> 70.6 us (0.75)
  Pallas kernels: 38.3 us -> 22.3 us
  between operations: 16.1 us -> 0.91 us
  waiting for transfers between devices: 22.7 us -> 28.3 us
  starting transfers between devices: 11.6 us -> 16.7 us
  other arithmetic: 3.56 us -> 0.95 us
    pallas_call x5, Pallas kernels: 13.3 us -> 5.87 us  [merged(): pl.pallas_call(functools.partial(merge_kernel, per_device, known, bit), o...]
    ppermute x12, waiting for transfers between devices: 22.7 us -> 28.3 us  [permuted(): return lax.ppermute(array, 'ctx', pairs)]
    pallas_call x2, Pallas kernels: 19.6 us -> 14.3 us  [attend_stage(): pl.pallas_call(functools.partial(stage_kernel, per_device, known, bit, ba...]
    ppermute x12, starting transfers between devices: 11.6 us -> 16.7 us  [permuted(): return lax.ppermute(array, 'ctx', pairs)]
    pallas_call x1, Pallas kernels: 5.43 us -> 2.11 us  [pack(): pl.pallas_call(functools.partial(pack_kernel, cache_k.shape[0] // VBLOCK,...]
    reduce_max x4 -> x0, other arithmetic: 2.67 us -> none  [fits(): fine &= jnp.max(counts) <= room((1 << known.bit_count()) / peers)]
  transfers between devices with their start and end apart: 12 -> 12, of which waited for: 5 -> 5; matrix products, arithmetic and copies ran while one was open for 4% -> 1% of each run, Pallas kernels for 22% -> 17%
where the time goes in v3:
time: 70.6 us; the launch traced here: 70.4 us
  waiting for transfers between devices  28.3 us (40%)
  Pallas kernels  22.3 us (32%)
  starting transfers between devices  16.7 us (24%)
  local copies, waits for them, and re-layouts  1.1 us (2%)
  other arithmetic  0.95 us (1%)
  between operations  0.91 us (1%)
    ppermute x12, waiting for transfers between devices, permuted(): return lax.ppermute(array, 'ctx', pairs)  28.3 us
    ppermute x12, starting transfers between devices, permuted(): return lax.ppermute(array, 'ctx', pairs)  16.7 us
    pallas_call x2, Pallas kernels, attend_stage(): pl.pallas_call(functools.partial(stage_kernel, per_device, known, bit, ba...  14.3 us
    pallas_call x5, Pallas kernels, merged(): pl.pallas_call(functools.partial(merge_kernel, per_device, known, bit), o...  5.87 us
    pallas_call x1, Pallas kernels, pack(): pl.pallas_call(functools.partial(pack_kernel, cache_k.shape[0] // VBLOCK,...  2.11 us
  transfers between devices with their start and end apart: 12, of which 5 were waited for; matrix products, arithmetic and copies ran while one was open for 1% of the time, Pallas kernels for 17%

profile of v3, /device:TPU:0, one launch (start us, length us, event | category | flops | bytes accessed | tf_op | source)
XLA Modules:
  0.0 70.4 jit_solution(16293777569241469354)
XLA Ops:
  0.0 2.1 %pack.1 = (bf16[12,64,128]{2,1,0:T(8,128)(2,1)S(1)}, bf16[12,64,128]{2,1,0:T(8,128)(2,1)S(1)}) custom-call(s32[4,16]{1,0:T(4,128)} %refs_0_.1, bf16[2048,512]{1,0:T(8,128)(2,1)} %cache_k.1, bf16[2048,512]{1,0:T(8,128)(2,1)} %cache_v.1), custom_call_target="tpu_custom_call" | custom-call | tf_op jit(solution)/shard_map/pack/pallas_call | solution.py:218
  2.1 0.0 copy-start.9
  2.1 0.0 copy-start.8
  2.1 0.0 copy-start.2
  2.2 0.0 copy-start.7
  2.2 0.7 %collective-permute-start.8 = (bf16[12,64,128]{2,1,0:T(8,128)(2,1)S(1)}, bf16[12,64,128]{2,1,0:T(8,128)(2,1)S(1)}, u32[]{:S(2)}, u32[]{:S(2)}) collective-permute-start(bf16[12,64,128]{2,1,0:T(8,128)(2,1)S(1)} %get-tuple-element.69), channel_id=1, source_target_pairs={{0,1},{1,0},{2,3},{3,2},{4,5},{5,4},{6,7},{7,6},{8,9},{9,8},{10,11... | collective-permute-start | bytes 589832 | tf_op jit(solution)/shard_map/ppermute | solution.py:374
  2.9 0.0 copy-done.5
  2.9 0.0 copy-done.4
  2.9 2.1 %collective-permute-start.10 = (bf16[128,1024]{1,0:T(8,128)(2,1)S(1)}, bf16[128,1024]{1,0:T(8,128)(2,1)S(1)}, u32[]{:S(2)}, u32[]{:S(2)}) collective-permute-start(bf16[128,1024]{1,0:T(8,128)(2,1)S(1)} %pad_maximum_fusion), channel_id=1, source_target_pairs={{0,1},{1,2},{2,3},{3,4},{4,5},{5,6},{6,7},{7,8},{8,9},{9,10},{10,1... | collective-permute-start | bytes 786440 | tf_op jit(solution)/shard_map/ppermute | solution.py:374
  5.0 0.0 collective-permute-done.8.other
  5.0 0.0 copy-done.6
  5.1 1.4 %merge.5 = (bf16[18,32,128]{2,1,0:T(8,128)(2,1)S(1)}, bf16[18,32,128]{2,1,0:T(8,128)(2,1)S(1)}) custom-call(s32[4,16]{1,0:T(4,128)S(1)} %copy-done.6, bf16[12,64,128]{2,1,0:T(8,128)(2,1)S(1)} %get-tuple-element.68.mine, bf16[12,64,128]{2,1,0:T(8,128)(2,1)S(1)} %collective-permute-done.8.other), custom_call_target="tpu_custom_call" | custom-call | tf_op jit(solution)/shard_map/merge/pallas_call | solution.py:256
  6.4 3.8 %collective-permute-start.9 = (bf16[18,32,128]{2,1,0:T(8,128)(2,1)S(1)}, bf16[18,32,128]{2,1,0:T(8,128)(2,1)S(1)}, u32[]{:S(2)}, u32[]{:S(2)}) collective-permute-start(bf16[18,32,128]{2,1,0:T(8,128)(2,1)S(1)} %get-tuple-element.70.mine), channel_id=1, source_target_pairs={{0,8},{1,9},{2,10},{3,11},{4,12},{5,13},{6,14},{7,15},{8,0},{9,1},... | collective-permute-start | bytes 442376 | tf_op jit(solution)/shard_map/ppermute | solution.py:374
  10.2 0.0 collective-permute-done.10.refs_7_.refs_8_
  10.2 7.1 %collective-permute-done.9.other = bf16[18,32,128]{2,1,0:T(8,128)(2,1)S(1)} collective-permute-done((bf16[18,32,128]{2,1,0:T(8,128)(2,1)S(1)}, bf16[18,32,128]{2,1,0:T(8,128)(2,1)S(1)}, u32[]{:S(2)}, u32[]{:S(2)}) %collective-permute-start.9) | collective-permute-done | bytes 147488 | tf_op jit(solution)/shard_map/ppermute | solution.py:374
  17.2 1.1 %merge.8.mine = bf16[28,32,128]{2,1,0:T(8,128)(2,1)S(1)} custom-call(s32[4,16]{1,0:T(4,128)S(1)} %copy-done.6, bf16[18,32,128]{2,1,0:T(8,128)(2,1)S(1)} %get-tuple-element.70.mine, bf16[18,32,128]{2,1,0:T(8,128)(2,1)S(1)} %collective-permute-done.9.other), custom_call_target="tpu_custom_call" | custom-call | tf_op jit(solution)/shard_map/merge/pallas_call | solution.py:256
  18.4 1.8 %collective-permute-start.16 = (bf16[28,32,128]{2,1,0:T(8,128)(2,1)S(1)}, bf16[28,32,128]{2,1,0:T(8,128)(2,1)S(1)}, u32[]{:S(2)}, u32[]{:S(2)}) collective-permute-start(bf16[28,32,128]{2,1,0:T(8,128)(2,1)S(1)} %merge.8.mine), channel_id=1, source_target_pairs={{0,4},{1,5},{2,6},{3,7},{4,0},{5,1},{6,2},{7,3},{8,12},{9,13},{10,... | collective-permute-start | bytes 688136 | tf_op jit(solution)/shard_map/ppermute | solution.py:374
  20.2 3.4 %collective-permute-start.11 = (bf16[18,32,128]{2,1,0:T(8,128)(2,1)S(1)}, bf16[18,32,128]{2,1,0:T(8,128)(2,1)S(1)}, u32[]{:S(2)}, u32[]{:S(2)}) collective-permute-start(bf16[18,32,128]{2,1,0:T(8,128)(2,1)S(1)} %get-tuple-element.74.mine), channel_id=1, source_target_pairs={{0,8},{1,9},{2,10},{3,11},{4,12},{5,13},{6,14},{7,15},{8,0},{9,1},... | collective-permute-start | bytes 442376 | tf_op jit(solution)/shard_map/ppermute | solution.py:374
  23.6 5.0 %collective-permute-done.11.other = bf16[18,32,128]{2,1,0:T(8,128)(2,1)S(1)} collective-permute-done((bf16[18,32,128]{2,1,0:T(8,128)(2,1)S(1)}, bf16[18,32,128]{2,1,0:T(8,128)(2,1)S(1)}, u32[]{:S(2)}, u32[]{:S(2)}) %collective-permute-start.11) | collective-permute-done | bytes 147488 | tf_op jit(solution)/shard_map/ppermute | solution.py:374
  28.6 1.1 %merge.6.mine = bf16[28,32,128]{2,1,0:T(8,128)(2,1)S(1)} custom-call(s32[4,16]{1,0:T(4,128)S(1)} %copy-done.6, bf16[18,32,128]{2,1,0:T(8,128)(2,1)S(1)} %get-tuple-element.74.mine, bf16[18,32,128]{2,1,0:T(8,128)(2,1)S(1)} %collective-permute-done.11.other), custom_call_target="tpu_custom_call" | custom-call | tf_op jit(solution)/shard_map/merge/pallas_call | solution.py:256
  29.8 4.1 %collective-permute-start.12 = (bf16[28,32,128]{2,1,0:T(8,128)(2,1)S(1)}, bf16[28,32,128]{2,1,0:T(8,128)(2,1)S(1)}, u32[]{:S(2)}, u32[]{:S(2)}) collective-permute-start(bf16[28,32,128]{2,1,0:T(8,128)(2,1)S(1)} %merge.6.mine), channel_id=1, source_target_pairs={{0,4},{1,5},{2,6},{3,7},{4,0},{5,1},{6,2},{7,3},{8,12},{9,13},{10,... | collective-permute-start | bytes 688136 | tf_op jit(solution)/shard_map/ppermute | solution.py:374
  33.9 0.0 collective-permute-done.16.other
  33.9 1.1 %merge.9.refs_3_ = bf16[46,32,128]{2,1,0:T(8,128)(2,1)S(1)} custom-call(s32[4,16]{1,0:T(4,128)S(1)} %copy-done.6, bf16[28,32,128]{2,1,0:T(8,128)(2,1)S(1)} %merge.8.mine, bf16[28,32,128]{2,1,0:T(8,128)(2,1)S(1)} %collective-permute-done.16.other), custom_call_target="tpu_custom_call" | custom-call | tf_op jit(solution)/shard_map/merge/pallas_call | solution.py:256
  35.0 0.2 collective-permute-start.17
  35.2 4.0 %collective-permute-done.12.other = bf16[28,32,128]{2,1,0:T(8,128)(2,1)S(1)} collective-permute-done((bf16[28,32,128]{2,1,0:T(8,128)(2,1)S(1)}, bf16[28,32,128]{2,1,0:T(8,128)(2,1)S(1)}, u32[]{:S(2)}, u32[]{:S(2)}) %collective-permute-start.12) | collective-permute-done | bytes 229408 | tf_op jit(solution)/shard_map/ppermute | solution.py:374
  39.2 1.1 %merge.7 = bf16[46,32,128]{2,1,0:T(8,128)(2,1)S(1)} custom-call(s32[4,16]{1,0:T(4,128)S(1)} %copy-done.6, bf16[28,32,128]{2,1,0:T(8,128)(2,1)S(1)} %merge.6.mine, bf16[28,32,128]{2,1,0:T(8,128)(2,1)S(1)} %collective-permute-done.12.other), custom_call_target="tpu_custom_call" | custom-call | tf_op jit(solution)/shard_map/merge/pallas_call | solution.py:256
  40.4 0.1 collective-permute-start.13
  40.5 0.1 xor.20
  40.5 0.0 collective-permute-start.18
  40.5 6.2 %collective-permute-done.17.refs_4_ = bf16[46,32,128]{2,1,0:T(8,128)(2,1)S(1)} collective-permute-done((bf16[46,32,128]{2,1,0:T(8,128)(2,1)S(1)}, bf16[46,32,128]{2,1,0:T(8,128)(2,1)S(1)}, u32[]{:S(2)}, u32[]{:S(2)}) %collective-permute-start.17) | collective-permute-done | bytes 376864 | tf_op jit(solution)/shard_map/ppermute | solution.py:374
  46.8 0.0 collective-permute-start.19
  46.8 0.5 collective-permute-start.14
  47.3 6.0 %collective-permute-done.13 = bf16[46,32,128]{2,1,0:T(8,128)(2,1)} collective-permute-done((bf16[46,32,128]{2,1,0:T(8,128)(2,1)S(1)}, bf16[46,32,128]{2,1,0:T(8,128)(2,1)}, u32[]{:S(2)}, u32[]{:S(2)}) %collective-permute-start.13) | collective-permute-done | bytes 376864 | tf_op jit(solution)/shard_map/ppermute | solution.py:374
  53.2 0.0 collective-permute-start.15
  53.2 0.0 copy-done.9
  53.2 0.2 convert_reduce_fusion
  53.5 0.7 %compare_reduce_fusion = pred[]{:T(512)} fusion(s32[4,16]{1,0:T(4,128)S(1)} %convert_reduce_fusion, s32[4]{0:T(128)S(1)} %copy-done.8), kind=kLoop, calls=%fused_computation.11 | loop fusion | flops 127 | bytes 273 | tf_op jit(solution)/shard_map/reduce_and | solution.py:388
  54.8 0.0 copy-start
  54.8 0.0 copy-start.1
  54.8 0.0 collective-permute-done.18.refs_5_
  54.8 0.0 collective-permute-done.19.refs_6_
  54.9 7.3 %attend_first.1 = (f32[4096,128]{1,0:T(8,128)S(1)}, f32[4096,256]{1,0:T(8,128)S(1)}) custom-call(s32[4,16]{1,0:T(4,128)S(1)} %copy-done.6, s32[4,64]{1,0:T(4,128)S(1)} %copy-done.7, bf16[128,4096]{1,0:T(8,128)(2,1)S(1)} %copy-done.2, bf16[46,32,128]{2,1,0:T(8,128)(2,1)S(1)} %merge.9.refs_3_, bf16[46,32,128]{2,1,0:T(8,128)(2,1)S(1)} %collective-permute-done.17.refs_4_, ...), custom_call_target="tpu_custom_call" | custom-call | flops 1610612736 | bytes 8388608 | tf_op jit(solution)/shard_map/attend_first/pallas_call | solution.py:353
  62.2 0.0 collective-permute-done.14
  62.2 0.0 collective-permute-done.15
  62.3 7.1 %conditional.1 = (bf16[128,4096]{1,0:T(8,128)(2,1)S(1)}) conditional(s32[]{:T(128)} %convert_element_type.7, (s32[4,16]{1,0:T(4,128)S(1)}, bf16[2048,512]{1,0:T(8,128)(2,1)S(1)}, bf16[2048,512]{1,0:T(8,128)(2,1)S(1)}, bf16[128,1024]{1,0:T(8,128)(2,1)S(1)}, s32[4,64]{1,0:T(4,128)S(1)}, /*index=5*/bf16[128,4096]{1,0:T(8,128)(2,1)S(1)}, ...), branch_computations={%region_2.3_spmd, %region_3.4_spmd} | conditional | flops 1073741824 | bytes 59244872 | solution.py:431
  62.5 6.9 %attend_last.1 = bf16[128,4096]{1,0:T(8,128)(2,1)S(1)} custom-call(s32[4,16]{1,0:T(4,128)S(1)} %get-tuple-element.50.refs_0_, bf16[128,4096]{1,0:T(8,128)(2,1)S(1)} %get-tuple-element.51.refs_1_, bf16[46,32,128]{2,1,0:T(8,128)(2,1)S(1)} %get-tuple-element.52.refs_2_, bf16[46,32,128]{2,1,0:T(8,128)(2,1)} %get-tuple-element.53.refs_3_, ...), custom_call_target="tpu_custom_call" | custom-call | flops 1073741824 | bytes 8388608 | tf_op jit(solution)/shard_map/cond/branch_1_fun/attend_last/pallas_call | solution.py:353
  69.4 0.0 copy-start.3
  69.4 1.0 %copy-done.3 = bf16[128,4096]{1,0:T(8,128)(2,1)} copy-done((bf16[128,4096]{1,0:T(8,128)(2,1)}, bf16[128,4096]{1,0:T(8,128)(2,1)S(1)}, u32[]{:S(2)}) %copy-start.3) | copy-done | bytes 1048600
  (11 shorter events, 0.0 us)
Async XLA Ops:
  0.0 5.0 %copy-start.6 = (s32[4,16]{1,0:T(4,128)S(1)}, s32[4,16]{1,0:T(4,128)}, u32[]{:S(2)}) copy-start(s32[4,16]{1,0:T(4,128)} %refs_0_.1) | copy-start | bytes 772
  0.0 2.9 %copy-start.5 = (bf16[128,512]{1,0:T(8,128)(2,1)S(1)}, bf16[128,512]{1,0:T(8,128)(2,1)}, u32[]{:S(2)}) copy-start(bf16[128,512]{1,0:T(8,128)(2,1)} %refs_9_.1) | copy-start | bytes 393220
  0.0 2.9 %copy-start.4 = (bf16[128,512]{1,0:T(8,128)(2,1)S(1)}, bf16[128,512]{1,0:T(8,128)(2,1)}, u32[]{:S(2)}) copy-start(bf16[128,512]{1,0:T(8,128)(2,1)} %refs_10_.1) | copy-start | bytes 393220
  2.1 51.1 %copy-start.9 = (s32[4]{0:T(128)S(1)}, s32[4]{0:T(128)}, u32[]{:S(2)}) copy-start(s32[4]{0:T(128)} %constant.26) | copy-start | bytes 52
  2.1 51.3 %copy-start.8 = (s32[4]{0:T(128)S(1)}, s32[4]{0:T(128)}, u32[]{:S(2)}) copy-start(s32[4]{0:T(128)} %constant.25.clone) | copy-start | bytes 52
  2.1 52.7 %copy-start.2 = (bf16[128,4096]{1,0:T(8,128)(2,1)S(1)}, bf16[128,4096]{1,0:T(8,128)(2,1)}, u32[]{:S(2)}) copy-start(bf16[128,4096]{1,0:T(8,128)(2,1)} %refs_2_.1) | copy-start | bytes 3145732
  2.2 52.7 %copy-start.7 = (s32[4,64]{1,0:T(4,128)S(1)}, s32[4,64]{1,0:T(4,128)}, u32[]{:S(2)}) copy-start(s32[4,64]{1,0:T(4,128)} %refs_1_.1) | copy-start | bytes 3076
  2.2 2.9 %collective-permute-start.8 = (bf16[12,64,128]{2,1,0:T(8,128)(2,1)S(1)}, bf16[12,64,128]{2,1,0:T(8,128)(2,1)S(1)}, u32[]{:S(2)}, u32[]{:S(2)}) collective-permute-start(bf16[12,64,128]{2,1,0:T(8,128)(2,1)S(1)} %get-tuple-element.69), channel_id=1, source_target_pairs={{0,1},{1,0},{2,3},{3,2},{4,5},{5,4},{6,7},{7,6},{8,9},{9,8},{10,11... | collective-permute-start | bytes 589832 | tf_op jit(solution)/shard_map/ppermute | solution.py:374
  2.9 7.2 %collective-permute-start.10 = (bf16[128,1024]{1,0:T(8,128)(2,1)S(1)}, bf16[128,1024]{1,0:T(8,128)(2,1)S(1)}, u32[]{:S(2)}, u32[]{:S(2)}) collective-permute-start(bf16[128,1024]{1,0:T(8,128)(2,1)S(1)} %pad_maximum_fusion), channel_id=1, source_target_pairs={{0,1},{1,2},{2,3},{3,4},{4,5},{5,6},{6,7},{7,8},{8,9},{9,10},{10,1... | collective-permute-start | bytes 786440 | tf_op jit(solution)/shard_map/ppermute | solution.py:374
  6.4 10.8 %collective-permute-start.9 = (bf16[18,32,128]{2,1,0:T(8,128)(2,1)S(1)}, bf16[18,32,128]{2,1,0:T(8,128)(2,1)S(1)}, u32[]{:S(2)}, u32[]{:S(2)}) collective-permute-start(bf16[18,32,128]{2,1,0:T(8,128)(2,1)S(1)} %get-tuple-element.70.mine), channel_id=1, source_target_pairs={{0,8},{1,9},{2,10},{3,11},{4,12},{5,13},{6,14},{7,15},{8,0},{9,1},... | collective-permute-start | bytes 442376 | tf_op jit(solution)/shard_map/ppermute | solution.py:374
  18.4 15.5 %collective-permute-start.16 = (bf16[28,32,128]{2,1,0:T(8,128)(2,1)S(1)}, bf16[28,32,128]{2,1,0:T(8,128)(2,1)S(1)}, u32[]{:S(2)}, u32[]{:S(2)}) collective-permute-start(bf16[28,32,128]{2,1,0:T(8,128)(2,1)S(1)} %merge.8.mine), channel_id=1, source_target_pairs={{0,4},{1,5},{2,6},{3,7},{4,0},{5,1},{6,2},{7,3},{8,12},{9,13},{10,... | collective-permute-start | bytes 688136 | tf_op jit(solution)/shard_map/ppermute | solution.py:374
  20.2 8.4 %collective-permute-start.11 = (bf16[18,32,128]{2,1,0:T(8,128)(2,1)S(1)}, bf16[18,32,128]{2,1,0:T(8,128)(2,1)S(1)}, u32[]{:S(2)}, u32[]{:S(2)}) collective-permute-start(bf16[18,32,128]{2,1,0:T(8,128)(2,1)S(1)} %get-tuple-element.74.mine), channel_id=1, source_target_pairs={{0,8},{1,9},{2,10},{3,11},{4,12},{5,13},{6,14},{7,15},{8,0},{9,1},... | collective-permute-start | bytes 442376 | tf_op jit(solution)/shard_map/ppermute | solution.py:374
  29.8 9.5 %collective-permute-start.12 = (bf16[28,32,128]{2,1,0:T(8,128)(2,1)S(1)}, bf16[28,32,128]{2,1,0:T(8,128)(2,1)S(1)}, u32[]{:S(2)}, u32[]{:S(2)}) collective-permute-start(bf16[28,32,128]{2,1,0:T(8,128)(2,1)S(1)} %merge.6.mine), channel_id=1, source_target_pairs={{0,4},{1,5},{2,6},{3,7},{4,0},{5,1},{6,2},{7,3},{8,12},{9,13},{10,... | collective-permute-start | bytes 688136 | tf_op jit(solution)/shard_map/ppermute | solution.py:374
  35.0 11.8 %collective-permute-start.17 = (bf16[46,32,128]{2,1,0:T(8,128)(2,1)S(1)}, bf16[46,32,128]{2,1,0:T(8,128)(2,1)S(1)}, u32[]{:S(2)}, u32[]{:S(2)}) collective-permute-start(bf16[46,32,128]{2,1,0:T(8,128)(2,1)S(1)} %merge.9.refs_3_), channel_id=1, source_target_pairs={{0,2},{1,3},{2,0},{3,1},{4,6},{5,7},{6,4},{7,5},{8,10},{9,11},{10,... | collective-permute-start | bytes 1130504 | tf_op jit(solution)/shard_map/ppermute | solution.py:374
  40.4 12.9 %collective-permute-start.13 = (bf16[46,32,128]{2,1,0:T(8,128)(2,1)S(1)}, bf16[46,32,128]{2,1,0:T(8,128)(2,1)}, u32[]{:S(2)}, u32[]{:S(2)}) collective-permute-start(bf16[46,32,128]{2,1,0:T(8,128)(2,1)S(1)} %merge.7), channel_id=1, source_target_pairs={{0,2},{1,3},{2,0},{3,1},{4,6},{5,7},{6,4},{7,5},{8,10},{9,11},{10,... | collective-permute-start | bytes 1130504 | tf_op jit(solution)/shard_map/ppermute | solution.py:374
  40.5 14.3 %collective-permute-start.18 = (bf16[46,32,128]{2,1,0:T(8,128)(2,1)S(1)}, bf16[46,32,128]{2,1,0:T(8,128)(2,1)S(1)}, u32[]{:S(2)}, u32[]{:S(2)}) collective-permute-start(bf16[46,32,128]{2,1,0:T(8,128)(2,1)S(1)} %merge.9.refs_3_), channel_id=1, source_target_pairs={{0,1},{1,0},{2,3},{3,2},{4,5},{5,4},{6,7},{7,6},{8,9},{9,8},{10,11... | collective-permute-start | bytes 1130504 | tf_op jit(solution)/shard_map/ppermute | solution.py:374
  46.8 8.1 %collective-permute-start.19 = (bf16[46,32,128]{2,1,0:T(8,128)(2,1)S(1)}, bf16[46,32,128]{2,1,0:T(8,128)(2,1)S(1)}, u32[]{:S(2)}, u32[]{:S(2)}) collective-permute-start(bf16[46,32,128]{2,1,0:T(8,128)(2,1)S(1)} %collective-permute-done.17.refs_4_), channel_id=1, source_target_pairs={{0,1},{1,0},{2,3},{3,2},{4,5},{5,4},{6,7},{7,6},{8,9},{9,8},{10,11... | collective-permute-start | bytes 1130504 | tf_op jit(solution)/shard_map/ppermute | solution.py:374
  46.8 15.5 %collective-permute-start.14 = (bf16[46,32,128]{2,1,0:T(8,128)(2,1)S(1)}, bf16[46,32,128]{2,1,0:T(8,128)(2,1)}, u32[]{:S(2)}, u32[]{:S(2)}) collective-permute-start(bf16[46,32,128]{2,1,0:T(8,128)(2,1)S(1)} %merge.7), channel_id=1, source_target_pairs={{0,1},{1,0},{2,3},{3,2},{4,5},{5,4},{6,7},{7,6},{8,9},{9,8},{10,11... | collective-permute-start | bytes 1130504 | tf_op jit(solution)/shard_map/ppermute | solution.py:374
  53.2 9.0 %collective-permute-start.15 = (bf16[46,32,128]{2,1,0:T(8,128)(2,1)}, bf16[46,32,128]{2,1,0:T(8,128)(2,1)}, u32[]{:S(2)}, u32[]{:S(2)}) collective-permute-start(bf16[46,32,128]{2,1,0:T(8,128)(2,1)} %collective-permute-done.13), channel_id=1, source_target_pairs={{0,1},{1,0},{2,3},{3,2},{4,5},{5,4},{6,7},{7,6},{8,9},{9,8},{10,11... | collective-permute-start | bytes 1130504 | tf_op jit(solution)/shard_map/ppermute | solution.py:374
  54.8 7.4 %copy-start = (bf16[2048,512]{1,0:T(8,128)(2,1)S(1)}, bf16[2048,512]{1,0:T(8,128)(2,1)}, u32[]{:S(2)}) copy-start(bf16[2048,512]{1,0:T(8,128)(2,1)} %cache_k.1) | copy-start | bytes 6291460
  54.8 7.4 %copy-start.1 = (bf16[2048,512]{1,0:T(8,128)(2,1)S(1)}, bf16[2048,512]{1,0:T(8,128)(2,1)}, u32[]{:S(2)}) copy-start(bf16[2048,512]{1,0:T(8,128)(2,1)} %cache_v.1) | copy-start | bytes 6291460
  69.4 1.0 %copy-start.3 = (bf16[128,4096]{1,0:T(8,128)(2,1)}, bf16[128,4096]{1,0:T(8,128)(2,1)S(1)}, u32[]{:S(2)}) copy-start(bf16[128,4096]{1,0:T(8,128)(2,1)S(1)} %get-tuple-element.117) | copy-start | bytes 3145732

commit v4 on v3

--- a/solution.py
+++ b/solution.py
@@ -159,6 +159,8 @@
 
 
 STAGES = 2
+TILE = 2
+OUT_SPACE = pltpu.HBM
 ROWS = VBLOCK // STAGES
 WHOLE = pl.BlockSpec(memory_space=pltpu.VMEM)
 
@@ -270,101 +272,106 @@
     queries, mine, other, mine_twin, other_twin = refs[:5]
     refs = refs[5:]
     if banded:
-        before_k, before_v, own_k, own_v = refs[:4]
-        refs = refs[4:]
+        before, own_k, own_v = refs[:3]
+        refs = refs[3:]
     else:
-        largest_in, mixed_in = refs[:2]
-        refs = refs[2:]
-    outs, (kbuf, vbuf) = refs[:-2], refs[-2:]
-    head = pl.program_id(0)
+        largest_in, total_in, mixed_in = refs[:3]
+        refs = refs[3:]
+    if last:
+        out, kbuf, vbuf, held, sems = refs
+    else:
+        largest_out, total_out, mixed_out, kbuf, vbuf = refs
     me = lax.axis_index("ctx")
+    even = lax.rem(me, 2) == 0
     wide = NV * ROWS
 
-    @pl.when(head == 0)
-    def _():
-        even = lax.rem(me, 2) == 0
-
-        def act(entry, at_mine, at_other, place, theirs):
-            tile = jnp.where(theirs, other[at_other], mine[at_mine])
-            twin = jnp.where(theirs, other_twin[at_other], mine_twin[at_mine])
-            rows = pl.ds(entry % NV * ROWS, ROWS)
-            kbuf[entry // NV, rows] = jnp.where(even, tile, twin)
-            vbuf[entry // NV, rows, :HD] = jnp.where(even, twin, tile)
-
-        walk(blocks, per_device, known, bit, (mine.shape[0], other.shape[0]), act)
-        for at in range(KVH):
-            vbuf[at, :, HD:] = jnp.ones((vbuf.shape[1], HD), jnp.bfloat16)
-
-    mask = None
-    if banded:
-        kbuf[head, wide : wide + SMAX] = before_k[...]
-        kbuf[head, wide + SMAX :] = own_k[...]
-        vbuf[head, wide : wide + SMAX, :HD] = before_v[...]
-        vbuf[head, wide + SMAX :, :HD] = own_v[...]
-        mask = band_mask(offsets, head, me == 0)
-    for at in range(0, GROUP, 2):
-        rows = jnp.concatenate(
-            [queries[:, (at + i) * HD : (at + i + 1) * HD] for i in range(2)], axis=0
-        )
-        tile = slice(at * QDEV, (at + 2) * QDEV)
-        largest, mixed = attend_rows(rows, kbuf[head], vbuf[head], mask)
-        if not banded:
-            before = largest_in[tile, :1]
-            above = jnp.maximum(before, largest)
-            mixed = mixed * jnp.exp2(largest - above) + mixed_in[tile] * jnp.exp2(before - above)
-            largest = above
+    def act(entry, at_mine, at_other, place, theirs):
+        tile = jnp.where(theirs, other[at_other], mine[at_mine])
+        twin = jnp.where(theirs, other_twin[at_other], mine_twin[at_mine])
+        rows = pl.ds(entry % NV * ROWS, ROWS)
+        kbuf[entry // NV, rows] = jnp.where(even, tile, twin)
+        vbuf[entry // NV, rows, :HD] = jnp.where(even, twin, tile)
+
+    walk(blocks, per_device, known, bit, (mine.shape[0], other.shape[0]), act)
+    copies = []
+    for head in range(KVH):
+        columns = slice(head * HD, (head + 1) * HD)
+        vbuf[head, :, HD:] = jnp.ones((vbuf.shape[1], HD), jnp.bfloat16)
+        mask = None
+        if banded:
+            values = slice((KVH + head) * HD, (KVH + head + 1) * HD)
+            kbuf[head, wide : wide + SMAX] = before[:, columns]
+            kbuf[head, wide + SMAX :] = own_k[:, columns]
+            vbuf[head, wide : wide + SMAX, :HD] = before[:, values]
+            vbuf[head, wide + SMAX :, :HD] = own_v[:, columns]
+            mask = band_mask(offsets, head, me == 0)
+        for at in range(0, GROUP, TILE):
+            rows = jnp.concatenate(
+                [
+                    queries[:, (head * GROUP + at + i) * HD : (head * GROUP + at + i + 1) * HD]
+                    for i in range(TILE)
+                ],
+                axis=0,
+            )
+            start = (head * GROUP + at) * QDEV
+            tile = slice(start, start + TILE * QDEV)
+            largest, mixed = attend_rows(rows, kbuf[head], vbuf[head], mask)
+            mixed, total = mixed[:, :HD], mixed[:, HD:]
+            largest = jnp.broadcast_to(largest, mixed.shape)
+            if not banded:
+                above = jnp.maximum(largest_in[tile], largest)
+                now, then = jnp.exp2(largest - above), jnp.exp2(largest_in[tile] - above)
+                mixed = mixed * now + mixed_in[tile] * then
+                total = total * now + total_in[tile] * then
+                largest = above
+            if last:
+                result = (mixed / total).astype(jnp.bfloat16)
+                for i in range(TILE):
+                    held[head, :, (at + i) * HD : (at + i + 1) * HD] = result[
+                        i * QDEV : (i + 1) * QDEV
+                    ]
+            else:
+                largest_out[tile], total_out[tile], mixed_out[tile] = largest, total, mixed
         if last:
-            result = (mixed[:, :HD] / mixed[:, HD:]).astype(jnp.bfloat16)
-            for i in range(2):
-                outs[0][:, (at + i) * HD : (at + i + 1) * HD] = result[i * QDEV : (i + 1) * QDEV]
-        else:
-            outs[0][tile] = jnp.broadcast_to(largest, (2 * QDEV, HD))
-            outs[1][tile] = mixed
+            span = pl.ds(head * GROUP * HD, GROUP * HD)
+            copies.append(pltpu.make_async_copy(held.at[head], out.at[:, span], sems.at[head]))
+            copies[-1].start()
+    for copy in copies:
+        copy.wait()
 
 
 def attend_stage(known, bit, per_device, blocks, queries, lists, offsets=None, bands=None, state=None):
     banded, last = bands is not None, state is not None
-    tall = GROUP * QDEV
-    head_rows = pl.BlockSpec((QDEV, GROUP * HD), lambda head: (0, head))
-    specs = [SMEM] + [SMEM] * banded + [head_rows] + [WHOLE] * 4
+    tall = KVH * GROUP * QDEV
     args = [blocks] + [offsets] * banded + [queries, *lists]
-    states = [
-        pl.BlockSpec((tall, HD), lambda head: (head, 0)),
-        pl.BlockSpec((tall, 2 * HD), lambda head: (head, 0)),
+    args += list(bands if banded else state)
+    specs = [SMEM] * (1 + banded) + [WHOLE] * (len(args) - 1 - banded)
+    keys = NV * ROWS + (SMAX + QDEV) * banded
+    scratch = [
+        pltpu.VMEM((KVH, keys, HD), jnp.bfloat16),
+        pltpu.VMEM((KVH, keys, 2 * HD), jnp.bfloat16),
     ]
-    if banded:
-        before, own_k, own_v = bands
-        second = pl.BlockSpec((QDEV, HD), lambda head: (0, head + KVH))
-        specs += [head_block(QDEV), second, head_block(QDEV), head_block(QDEV)]
-        args += [before, before, own_k, own_v]
-    else:
-        specs += states
-        args += state
     if last:
         out_shape = jax.ShapeDtypeStruct(queries.shape, jnp.bfloat16)
-        out_specs = head_rows
+        out_specs = pl.BlockSpec(memory_space=OUT_SPACE)
+        scratch += [
+            pltpu.VMEM((KVH, QDEV, GROUP * HD), jnp.bfloat16),
+            pltpu.SemaphoreType.DMA((KVH,)),
+        ]
     else:
-        out_shape = (
-            jax.ShapeDtypeStruct((KVH * tall, HD), jnp.float32),
-            jax.ShapeDtypeStruct((KVH * tall, 2 * HD), jnp.float32),
-        )
-        out_specs = tuple(states)
-    keys = NV * ROWS + (SMAX + QDEV) * banded
+        out_shape = (jax.ShapeDtypeStruct((tall, HD), jnp.float32),) * 3
+        out_specs = (WHOLE,) * 3
     return pl.pallas_call(
         functools.partial(stage_kernel, per_device, known, bit, banded, last),
-        grid=(KVH,),
         out_shape=out_shape,
         in_specs=specs,
         out_specs=out_specs,
-        scratch_shapes=[
-            pltpu.VMEM((KVH, keys, HD), jnp.bfloat16),
-            pltpu.VMEM((KVH, keys, 2 * HD), jnp.bfloat16),
-        ],
+        scratch_shapes=scratch,
         compiler_params=pltpu.CompilerParams(vmem_limit_bytes=48 * 2**20),
         cost_estimate=pl.CostEstimate(
-            flops=4 * KVH * tall * keys * HD,
+            flops=4 * tall * keys * HD,
             bytes_accessed=8 * 2**20,
-            transcendentals=KVH * tall * keys,
+            transcendentals=tall * keys,
         ),
         name="attend_last" if last else "attend_first",
     )(*args)
@@ -415,7 +422,6 @@
         other[0] = swapped(mine[0], bit)
         if bit == bits[1]:
             other[0], before = lax.optimization_barrier((other[0], before))
-            other[0], mine[1] = lax.optimization_barrier((other[0], mine[1]))
         other[1] = swapped(mine[1], bit)
         if bit == bits[-1]:
             break
@@ -423,14 +429,17 @@
         for stage in range(STAGES):
             (mine[stage],) = merged(blocks, per_device, known, bit, mine[stage], other[stage], size)
         known |= bit
-    lists = [(m, o, swapped(m, 1), swapped(o, 1)) for m, o in zip(mine, other)]
+    twins = [swapped(m, 1) for m in mine]
 
     bands = (before, span_k, span_v)
     shared = (known, bits[-1], per_device, blocks, queries)
-    state = attend_stage(*shared, lists[0], offsets=offsets, bands=bands)
+    lists = (mine[0], other[0], twins[0], swapped(other[0], 1))
+    state = attend_stage(*shared, lists, offsets=offsets, bands=bands)
+    state, late = lax.optimization_barrier((state, other[1]))
+    lists = (mine[1], late, twins[1], swapped(late, 1))
     return lax.cond(
         fits(blocks, per_device, peers, bits),
-        lambda: attend_stage(*shared, lists[1], state=state),
+        lambda: attend_stage(*shared, lists, state=state),
         lambda: general(queries, bands, cache_k, cache_v, blocks, offsets, bits),
     )
 

time: 70.6 us -> 69.1 us (0.979)
  starting transfers between devices: 16.7 us -> 12.3 us
  Pallas kernels: 22.3 us -> 24 us
  waiting for transfers between devices: 28.3 us -> 29.9 us
    ppermute x12, starting transfers between devices: 16.7 us -> 12.3 us  [permuted(): return lax.ppermute(array, 'ctx', pairs)]
    ppermute x12, waiting for transfers between devices: 28.3 us -> 29.9 us  [permuted(): return lax.ppermute(array, 'ctx', pairs)]
    pallas_call x2, Pallas kernels: 14.3 us -> 15.8 us  [attend_stage(): pl.pallas_call(functools.partial(stage_kernel, per_device, known, bit, ba...]
  transfers between devices with their start and end apart: 12 -> 12, of which waited for: 5 -> 6; matrix products, arithmetic and copies ran while one was open for 1% -> 1% of each run, Pallas kernels for 17% -> 17%
where the time goes in v4:
time: 69.1 us
  waiting for transfers between devices  29.9 us (43%)
  Pallas kernels  24 us (35%)
  starting transfers between devices  12.3 us (18%)
  local copies, waits for them, and re-layouts  1.08 us (2%)
  other arithmetic  0.95 us (1%)
  between operations  0.87 us (1%)
    ppermute x12, waiting for transfers between devices, permuted(): return lax.ppermute(array, 'ctx', pairs)  29.9 us
    pallas_call x2, Pallas kernels, attend_stage(): pl.pallas_call(functools.partial(stage_kernel, per_device, known, bit, ba...  15.8 us
    ppermute x12, starting transfers between devices, permuted(): return lax.ppermute(array, 'ctx', pairs)  12.3 us
    pallas_call x5, Pallas kernels, merged(): pl.pallas_call(functools.partial(merge_kernel, per_device, known, bit), o...  5.87 us
    pallas_call x1, Pallas kernels, pack(): pl.pallas_call(functools.partial(pack_kernel, cache_k.shape[0] // VBLOCK,...  2.32 us
  transfers between devices with their start and end apart: 12, of which 6 were waited for; matrix products, arithmetic and copies ran while one was open for 1% of the time, Pallas kernels for 17%

profile of v4, /device:TPU:0, one launch (start us, length us, event | category | flops | bytes accessed | tf_op | source)
XLA Modules:
  0.0 69.1 jit_solution(649731549248401264)
XLA Ops:
  0.0 0.0 copy-start.4
  0.0 2.3 %pack.1 = (bf16[12,64,128]{2,1,0:T(8,128)(2,1)S(1)}, bf16[12,64,128]{2,1,0:T(8,128)(2,1)S(1)}) custom-call(s32[4,16]{1,0:T(4,128)} %refs_0_.1, bf16[2048,512]{1,0:T(8,128)(2,1)} %cache_k.1, bf16[2048,512]{1,0:T(8,128)(2,1)} %cache_v.1), custom_call_target="tpu_custom_call" | custom-call | tf_op jit(solution)/shard_map/pack/pallas_call | solution.py:220
  2.3 0.0 copy-start
  2.4 0.0 copy-start.5
  2.4 0.5 collective-permute-start.8
  2.9 0.0 copy-done.3
  2.9 0.0 copy-done.2
  2.9 2.1 %collective-permute-start.10 = (bf16[128,1024]{1,0:T(8,128)(2,1)S(1)}, bf16[128,1024]{1,0:T(8,128)(2,1)S(1)}, u32[]{:S(2)}, u32[]{:S(2)}) collective-permute-start(bf16[128,1024]{1,0:T(8,128)(2,1)S(1)} %pad_maximum_fusion), channel_id=1, source_target_pairs={{0,1},{1,2},{2,3},{3,4},{4,5},{5,6},{6,7},{7,8},{8,9},{9,10},{10,1... | collective-permute-start | bytes 786440 | tf_op jit(solution)/shard_map/ppermute | solution.py:381
  5.0 0.0 collective-permute-done.8.other
  5.0 0.0 copy-done.4
  5.0 1.4 %merge.5 = (bf16[18,32,128]{2,1,0:T(8,128)(2,1)S(1)}, bf16[18,32,128]{2,1,0:T(8,128)(2,1)S(1)}) custom-call(s32[4,16]{1,0:T(4,128)S(1)} %copy-done.4, bf16[12,64,128]{2,1,0:T(8,128)(2,1)S(1)} %get-tuple-element.74.mine, bf16[12,64,128]{2,1,0:T(8,128)(2,1)S(1)} %collective-permute-done.8.other), custom_call_target="tpu_custom_call" | custom-call | tf_op jit(solution)/shard_map/merge/pallas_call | solution.py:258
  6.4 4.0 %collective-permute-start.9 = (bf16[18,32,128]{2,1,0:T(8,128)(2,1)S(1)}, bf16[18,32,128]{2,1,0:T(8,128)(2,1)S(1)}, u32[]{:S(2)}, u32[]{:S(2)}) collective-permute-start(bf16[18,32,128]{2,1,0:T(8,128)(2,1)S(1)} %get-tuple-element.76.mine), channel_id=1, source_target_pairs={{0,8},{1,9},{2,10},{3,11},{4,12},{5,13},{6,14},{7,15},{8,0},{9,1},... | collective-permute-start | bytes 442376 | tf_op jit(solution)/shard_map/ppermute | solution.py:381
  10.4 0.0 collective-permute-done.10.refs_7_
  10.4 7.3 %collective-permute-done.9.other = bf16[18,32,128]{2,1,0:T(8,128)(2,1)S(1)} collective-permute-done((bf16[18,32,128]{2,1,0:T(8,128)(2,1)S(1)}, bf16[18,32,128]{2,1,0:T(8,128)(2,1)S(1)}, u32[]{:S(2)}, u32[]{:S(2)}) %collective-permute-start.9) | collective-permute-done | bytes 147488 | tf_op jit(solution)/shard_map/ppermute | solution.py:381
  17.7 1.1 %merge.8.mine = bf16[28,32,128]{2,1,0:T(8,128)(2,1)S(1)} custom-call(s32[4,16]{1,0:T(4,128)S(1)} %copy-done.4, bf16[18,32,128]{2,1,0:T(8,128)(2,1)S(1)} %get-tuple-element.76.mine, bf16[18,32,128]{2,1,0:T(8,128)(2,1)S(1)} %collective-permute-done.9.other), custom_call_target="tpu_custom_call" | custom-call | tf_op jit(solution)/shard_map/merge/pallas_call | solution.py:258
  18.9 1.6 %collective-permute-start.13 = (bf16[28,32,128]{2,1,0:T(8,128)(2,1)S(1)}, bf16[28,32,128]{2,1,0:T(8,128)(2,1)S(1)}, u32[]{:S(2)}, u32[]{:S(2)}) collective-permute-start(bf16[28,32,128]{2,1,0:T(8,128)(2,1)S(1)} %merge.8.mine), channel_id=1, source_target_pairs={{0,4},{1,5},{2,6},{3,7},{4,0},{5,1},{6,2},{7,3},{8,12},{9,13},{10,... | collective-permute-start | bytes 688136 | tf_op jit(solution)/shard_map/ppermute | solution.py:381
  20.4 6.3 %collective-permute-done.13.other = bf16[28,32,128]{2,1,0:T(8,128)(2,1)S(1)} collective-permute-done((bf16[28,32,128]{2,1,0:T(8,128)(2,1)S(1)}, bf16[28,32,128]{2,1,0:T(8,128)(2,1)S(1)}, u32[]{:S(2)}, u32[]{:S(2)}) %collective-permute-start.13) | collective-permute-done | bytes 229408 | tf_op jit(solution)/shard_map/ppermute | solution.py:381
  26.8 1.1 %merge.9.refs_3_ = bf16[46,32,128]{2,1,0:T(8,128)(2,1)S(1)} custom-call(s32[4,16]{1,0:T(4,128)S(1)} %copy-done.4, bf16[28,32,128]{2,1,0:T(8,128)(2,1)S(1)} %merge.8.mine, bf16[28,32,128]{2,1,0:T(8,128)(2,1)S(1)} %collective-permute-done.13.other), custom_call_target="tpu_custom_call" | custom-call | tf_op jit(solution)/shard_map/merge/pallas_call | solution.py:258
  27.9 1.9 %collective-permute-start.14 = (bf16[46,32,128]{2,1,0:T(8,128)(2,1)S(1)}, bf16[46,32,128]{2,1,0:T(8,128)(2,1)S(1)}, u32[]{:S(2)}, u32[]{:S(2)}) collective-permute-start(bf16[46,32,128]{2,1,0:T(8,128)(2,1)S(1)} %merge.9.refs_3_), channel_id=1, source_target_pairs={{0,2},{1,3},{2,0},{3,1},{4,6},{5,7},{6,4},{7,5},{8,10},{9,11},{10,... | collective-permute-start | bytes 1130504 | tf_op jit(solution)/shard_map/ppermute | solution.py:381
  29.8 1.5 %collective-permute-start.11 = (bf16[18,32,128]{2,1,0:T(8,128)(2,1)S(1)}, bf16[18,32,128]{2,1,0:T(8,128)(2,1)S(1)}, u32[]{:S(2)}, u32[]{:S(2)}) collective-permute-start(bf16[18,32,128]{2,1,0:T(8,128)(2,1)S(1)} %get-tuple-element.78.mine), channel_id=1, source_target_pairs={{0,8},{1,9},{2,10},{3,11},{4,12},{5,13},{6,14},{7,15},{8,0},{9,1},... | collective-permute-start | bytes 442376 | tf_op jit(solution)/shard_map/ppermute | solution.py:381
  31.3 7.3 %collective-permute-done.11.other = bf16[18,32,128]{2,1,0:T(8,128)(2,1)S(1)} collective-permute-done((bf16[18,32,128]{2,1,0:T(8,128)(2,1)S(1)}, bf16[18,32,128]{2,1,0:T(8,128)(2,1)S(1)}, u32[]{:S(2)}, u32[]{:S(2)}) %collective-permute-start.11) | collective-permute-done | bytes 147488 | tf_op jit(solution)/shard_map/ppermute | solution.py:381
  38.6 1.1 %merge.6.mine = bf16[28,32,128]{2,1,0:T(8,128)(2,1)S(1)} custom-call(s32[4,16]{1,0:T(4,128)S(1)} %copy-done.4, bf16[18,32,128]{2,1,0:T(8,128)(2,1)S(1)} %get-tuple-element.78.mine, bf16[18,32,128]{2,1,0:T(8,128)(2,1)S(1)} %collective-permute-done.11.other), custom_call_target="tpu_custom_call" | custom-call | tf_op jit(solution)/shard_map/merge/pallas_call | solution.py:258
  39.7 0.1 collective-permute-start.12
  39.8 0.1 collective-permute-start.15
  39.9 0.0 collective-permute-done.14.refs_4_
  39.9 0.5 collective-permute-start.16
  40.4 6.8 %collective-permute-done.12.other = bf16[28,32,128]{2,1,0:T(8,128)(2,1)S(1)} collective-permute-done((bf16[28,32,128]{2,1,0:T(8,128)(2,1)S(1)}, bf16[28,32,128]{2,1,0:T(8,128)(2,1)S(1)}, u32[]{:S(2)}, u32[]{:S(2)}) %collective-permute-start.12) | collective-permute-done | bytes 229408 | tf_op jit(solution)/shard_map/ppermute | solution.py:381
  47.2 1.1 %merge.7 = bf16[46,32,128]{2,1,0:T(8,128)(2,1)S(1)} custom-call(s32[4,16]{1,0:T(4,128)S(1)} %copy-done.4, bf16[28,32,128]{2,1,0:T(8,128)(2,1)S(1)} %merge.6.mine, bf16[28,32,128]{2,1,0:T(8,128)(2,1)S(1)} %collective-permute-done.12.other), custom_call_target="tpu_custom_call" | custom-call | tf_op jit(solution)/shard_map/merge/pallas_call | solution.py:258
  48.4 0.1 collective-permute-start.17
  48.5 0.1 xor.20
  48.5 0.0 collective-permute-start.18
  48.6 0.0 collective-permute-done.15.refs_5_
  48.6 0.0 collective-permute-done.16.refs_6_
  48.6 0.0 copy-done
  48.6 0.0 copy-done.5
  48.6 7.9 %attend_first.1 = (f32[4096,128]{1,0:T(8,128)}, f32[4096,128]{1,0:T(8,128)}, f32[4096,128]{1,0:T(8,128)}) custom-call(s32[4,16]{1,0:T(4,128)S(1)} %copy-done.4, s32[4,64]{1,0:T(4,128)S(1)} %copy-done.5, bf16[128,4096]{1,0:T(8,128)(2,1)S(1)} %copy-done, bf16[46,32,128]{2,1,0:T(8,128)(2,1)S(1)} %merge.9.refs_3_, ...), custom_call_target="tpu_custom_call" | custom-call | flops 1610612736 | bytes 8388608 | tf_op jit(solution)/shard_map/attend_first/pallas_call | solution.py:364
  56.5 1.8 %collective-permute-done.17 = bf16[46,32,128]{2,1,0:T(8,128)(2,1)} collective-permute-done((bf16[46,32,128]{2,1,0:T(8,128)(2,1)S(1)}, bf16[46,32,128]{2,1,0:T(8,128)(2,1)}, u32[]{:S(2)}, u32[]{:S(2)}) %collective-permute-start.17) | collective-permute-done | bytes 376864 | tf_op jit(solution)/shard_map/ppermute | solution.py:381
  58.3 0.0 collective-permute-start.19
  58.3 0.0 copy-done.7
  58.3 0.2 convert_reduce_fusion
  58.5 0.0 copy-done.6
  58.5 0.7 %compare_reduce_fusion = pred[]{:T(512)} fusion(s32[4,16]{1,0:T(4,128)S(1)} %convert_reduce_fusion, s32[4]{0:T(128)S(1)} %copy-done.6), kind=kLoop, calls=%fused_computation.11 | loop fusion | flops 127 | bytes 273 | tf_op jit(solution)/shard_map/reduce_and | solution.py:395
  59.9 0.0 collective-permute-done.18
  59.9 0.3 collective-permute-done.19
  60.2 8.0 %conditional.1 = (bf16[128,4096]{1,0:T(8,128)(2,1)S(1)}) conditional(s32[]{:T(128)} %convert_element_type.7, (s32[4,16]{1,0:T(4,128)S(1)}, bf16[2048,512]{1,0:T(8,128)(2,1)}, bf16[2048,512]{1,0:T(8,128)(2,1)}, bf16[128,1024]{1,0:T(8,128)(2,1)S(1)}, s32[4,64]{1,0:T(4,128)S(1)}, /*index=5*/bf16[128,4096]{1,0:T(8,128)(2,1)S(1)}, ...), branch_computations={%region_2.3_spmd, %region_3.4_spmd} | conditional | flops 1073741824 | bytes 59244872 | solution.py:440
  60.2 8.0 %attend_last.1 = bf16[128,4096]{1,0:T(8,128)(2,1)S(1)} custom-call(s32[4,16]{1,0:T(4,128)S(1)} %get-tuple-element.52.refs_0_, bf16[128,4096]{1,0:T(8,128)(2,1)S(1)} %get-tuple-element.53.refs_1_, bf16[46,32,128]{2,1,0:T(8,128)(2,1)S(1)} %get-tuple-element.54.refs_2_, bf16[46,32,128]{2,1,0:T(8,128)(2,1)} %get-tuple-element.55.refs_3_, ...), custom_call_target="tpu_custom_call" | custom-call | flops 1073741824 | bytes 8388608 | tf_op jit(solution)/shard_map/cond/branch_1_fun/attend_last/pallas_call | solution.py:364
  68.2 0.0 copy-start.1
  68.2 1.0 %copy-done.1 = bf16[128,4096]{1,0:T(8,128)(2,1)} copy-done((bf16[128,4096]{1,0:T(8,128)(2,1)}, bf16[128,4096]{1,0:T(8,128)(2,1)S(1)}, u32[]{:S(2)}) %copy-start.1) | copy-done | bytes 1048600
  (7 shorter events, 0.0 us)
Async XLA Ops:
  0.0 5.0 %copy-start.4 = (s32[4,16]{1,0:T(4,128)S(1)}, s32[4,16]{1,0:T(4,128)}, u32[]{:S(2)}) copy-start(s32[4,16]{1,0:T(4,128)} %refs_0_.1) | copy-start | bytes 772
  0.0 2.9 %copy-start.3 = (bf16[128,512]{1,0:T(8,128)(2,1)S(1)}, bf16[128,512]{1,0:T(8,128)(2,1)}, u32[]{:S(2)}) copy-start(bf16[128,512]{1,0:T(8,128)(2,1)} %refs_8_.1) | copy-start | bytes 393220
  0.0 2.9 %copy-start.2 = (bf16[128,512]{1,0:T(8,128)(2,1)S(1)}, bf16[128,512]{1,0:T(8,128)(2,1)}, u32[]{:S(2)}) copy-start(bf16[128,512]{1,0:T(8,128)(2,1)} %refs_9_.1) | copy-start | bytes 393220
  2.3 46.3 %copy-start = (bf16[128,4096]{1,0:T(8,128)(2,1)S(1)}, bf16[128,4096]{1,0:T(8,128)(2,1)}, u32[]{:S(2)}) copy-start(bf16[128,4096]{1,0:T(8,128)(2,1)} %refs_2_.1) | copy-start | bytes 3145732
  2.4 46.3 %copy-start.5 = (s32[4,64]{1,0:T(4,128)S(1)}, s32[4,64]{1,0:T(4,128)}, u32[]{:S(2)}) copy-start(s32[4,64]{1,0:T(4,128)} %refs_1_.1) | copy-start | bytes 3076
  2.4 2.7 %collective-permute-start.8 = (bf16[12,64,128]{2,1,0:T(8,128)(2,1)S(1)}, bf16[12,64,128]{2,1,0:T(8,128)(2,1)S(1)}, u32[]{:S(2)}, u32[]{:S(2)}) collective-permute-start(bf16[12,64,128]{2,1,0:T(8,128)(2,1)S(1)} %get-tuple-element.75), channel_id=1, source_target_pairs={{0,1},{1,0},{2,3},{3,2},{4,5},{5,4},{6,7},{7,6},{8,9},{9,8},{10,11... | collective-permute-start | bytes 589832 | tf_op jit(solution)/shard_map/ppermute | solution.py:381
  2.9 7.5 %collective-permute-start.10 = (bf16[128,1024]{1,0:T(8,128)(2,1)S(1)}, bf16[128,1024]{1,0:T(8,128)(2,1)S(1)}, u32[]{:S(2)}, u32[]{:S(2)}) collective-permute-start(bf16[128,1024]{1,0:T(8,128)(2,1)S(1)} %pad_maximum_fusion), channel_id=1, source_target_pairs={{0,1},{1,2},{2,3},{3,4},{4,5},{5,6},{6,7},{7,8},{8,9},{9,10},{10,1... | collective-permute-start | bytes 786440 | tf_op jit(solution)/shard_map/ppermute | solution.py:381
  6.4 11.3 %collective-permute-start.9 = (bf16[18,32,128]{2,1,0:T(8,128)(2,1)S(1)}, bf16[18,32,128]{2,1,0:T(8,128)(2,1)S(1)}, u32[]{:S(2)}, u32[]{:S(2)}) collective-permute-start(bf16[18,32,128]{2,1,0:T(8,128)(2,1)S(1)} %get-tuple-element.76.mine), channel_id=1, source_target_pairs={{0,8},{1,9},{2,10},{3,11},{4,12},{5,13},{6,14},{7,15},{8,0},{9,1},... | collective-permute-start | bytes 442376 | tf_op jit(solution)/shard_map/ppermute | solution.py:381
  18.9 7.9 %collective-permute-start.13 = (bf16[28,32,128]{2,1,0:T(8,128)(2,1)S(1)}, bf16[28,32,128]{2,1,0:T(8,128)(2,1)S(1)}, u32[]{:S(2)}, u32[]{:S(2)}) collective-permute-start(bf16[28,32,128]{2,1,0:T(8,128)(2,1)S(1)} %merge.8.mine), channel_id=1, source_target_pairs={{0,4},{1,5},{2,6},{3,7},{4,0},{5,1},{6,2},{7,3},{8,12},{9,13},{10,... | collective-permute-start | bytes 688136 | tf_op jit(solution)/shard_map/ppermute | solution.py:381
  27.9 12.0 %collective-permute-start.14 = (bf16[46,32,128]{2,1,0:T(8,128)(2,1)S(1)}, bf16[46,32,128]{2,1,0:T(8,128)(2,1)S(1)}, u32[]{:S(2)}, u32[]{:S(2)}) collective-permute-start(bf16[46,32,128]{2,1,0:T(8,128)(2,1)S(1)} %merge.9.refs_3_), channel_id=1, source_target_pairs={{0,2},{1,3},{2,0},{3,1},{4,6},{5,7},{6,4},{7,5},{8,10},{9,11},{10,... | collective-permute-start | bytes 1130504 | tf_op jit(solution)/shard_map/ppermute | solution.py:381
  29.8 8.8 %collective-permute-start.11 = (bf16[18,32,128]{2,1,0:T(8,128)(2,1)S(1)}, bf16[18,32,128]{2,1,0:T(8,128)(2,1)S(1)}, u32[]{:S(2)}, u32[]{:S(2)}) collective-permute-start(bf16[18,32,128]{2,1,0:T(8,128)(2,1)S(1)} %get-tuple-element.78.mine), channel_id=1, source_target_pairs={{0,8},{1,9},{2,10},{3,11},{4,12},{5,13},{6,14},{7,15},{8,0},{9,1},... | collective-permute-start | bytes 442376 | tf_op jit(solution)/shard_map/ppermute | solution.py:381
  39.7 7.5 %collective-permute-start.12 = (bf16[28,32,128]{2,1,0:T(8,128)(2,1)S(1)}, bf16[28,32,128]{2,1,0:T(8,128)(2,1)S(1)}, u32[]{:S(2)}, u32[]{:S(2)}) collective-permute-start(bf16[28,32,128]{2,1,0:T(8,128)(2,1)S(1)} %merge.6.mine), channel_id=1, source_target_pairs={{0,4},{1,5},{2,6},{3,7},{4,0},{5,1},{6,2},{7,3},{8,12},{9,13},{10,... | collective-permute-start | bytes 688136 | tf_op jit(solution)/shard_map/ppermute | solution.py:381
  39.8 8.8 %collective-permute-start.15 = (bf16[46,32,128]{2,1,0:T(8,128)(2,1)S(1)}, bf16[46,32,128]{2,1,0:T(8,128)(2,1)S(1)}, u32[]{:S(2)}, u32[]{:S(2)}) collective-permute-start(bf16[46,32,128]{2,1,0:T(8,128)(2,1)S(1)} %merge.9.refs_3_), channel_id=1, source_target_pairs={{0,1},{1,0},{2,3},{3,2},{4,5},{5,4},{6,7},{7,6},{8,9},{9,8},{10,11... | collective-permute-start | bytes 1130504 | tf_op jit(solution)/shard_map/ppermute | solution.py:381
  39.9 8.7 %collective-permute-start.16 = (bf16[46,32,128]{2,1,0:T(8,128)(2,1)S(1)}, bf16[46,32,128]{2,1,0:T(8,128)(2,1)S(1)}, u32[]{:S(2)}, u32[]{:S(2)}) collective-permute-start(bf16[46,32,128]{2,1,0:T(8,128)(2,1)S(1)} %collective-permute-done.14.refs_4_), channel_id=1, source_target_pairs={{0,1},{1,0},{2,3},{3,2},{4,5},{5,4},{6,7},{7,6},{8,9},{9,8},{10,11... | collective-permute-start | bytes 1130504 | tf_op jit(solution)/shard_map/ppermute | solution.py:381
  48.4 9.9 %collective-permute-start.17 = (bf16[46,32,128]{2,1,0:T(8,128)(2,1)S(1)}, bf16[46,32,128]{2,1,0:T(8,128)(2,1)}, u32[]{:S(2)}, u32[]{:S(2)}) collective-permute-start(bf16[46,32,128]{2,1,0:T(8,128)(2,1)S(1)} %merge.7), channel_id=1, source_target_pairs={{0,2},{1,3},{2,0},{3,1},{4,6},{5,7},{6,4},{7,5},{8,10},{9,11},{10,... | collective-permute-start | bytes 1130504 | tf_op jit(solution)/shard_map/ppermute | solution.py:381
  48.5 9.7 %copy-start.7 = (s32[4]{0:T(128)S(1)}, s32[4]{0:T(128)}, u32[]{:S(2)}) copy-start(s32[4]{0:T(128)} %constant.26) | copy-start | bytes 52
  48.5 9.9 %copy-start.6 = (s32[4]{0:T(128)S(1)}, s32[4]{0:T(128)}, u32[]{:S(2)}) copy-start(s32[4]{0:T(128)} %constant.25.clone) | copy-start | bytes 52
  48.5 11.3 %collective-permute-start.18 = (bf16[46,32,128]{2,1,0:T(8,128)(2,1)S(1)}, bf16[46,32,128]{2,1,0:T(8,128)(2,1)}, u32[]{:S(2)}, u32[]{:S(2)}) collective-permute-start(bf16[46,32,128]{2,1,0:T(8,128)(2,1)S(1)} %merge.7), channel_id=1, source_target_pairs={{0,1},{1,0},{2,3},{3,2},{4,5},{5,4},{6,7},{7,6},{8,9},{9,8},{10,11... | collective-permute-start | bytes 1130504 | tf_op jit(solution)/shard_map/ppermute | solution.py:381
  58.3 1.9 %collective-permute-start.19 = (bf16[46,32,128]{2,1,0:T(8,128)(2,1)}, bf16[46,32,128]{2,1,0:T(8,128)(2,1)S(1)}, u32[]{:S(2)}, u32[]{:S(2)}) collective-permute-start(bf16[46,32,128]{2,1,0:T(8,128)(2,1)} %collective-permute-done.17), channel_id=1, source_target_pairs={{0,1},{1,0},{2,3},{3,2},{4,5},{5,4},{6,7},{7,6},{8,9},{9,8},{10,11... | collective-permute-start | bytes 1130504 | tf_op jit(solution)/shard_map/ppermute | solution.py:381
  68.2 1.0 %copy-start.1 = (bf16[128,4096]{1,0:T(8,128)(2,1)}, bf16[128,4096]{1,0:T(8,128)(2,1)S(1)}, u32[]{:S(2)}) copy-start(bf16[128,4096]{1,0:T(8,128)(2,1)S(1)} %get-tuple-element.126) | copy-start | bytes 3145732

commit v5 on v4

--- a/solution.py
+++ b/solution.py
@@ -161,6 +161,8 @@
 STAGES = 2
 TILE = 2
 OUT_SPACE = pltpu.HBM
+VMEM = 24
+COST = 2**20
 ROWS = VBLOCK // STAGES
 WHOLE = pl.BlockSpec(memory_space=pltpu.VMEM)
 
@@ -240,29 +242,32 @@
         at_other += other.astype(jnp.int32)
 
 
-def merge_kernel(per_device, known, bit, blocks, mine, other, *outs):
+def merge_kernel(per_device, known, bit, count, blocks, *refs):
+    mine, other, outs = refs[:count], refs[count : 2 * count], refs[2 * count :]
     size = outs[0].shape[0]
 
     def act(entry, at_mine, at_other, place, theirs):
-        tile = jnp.where(theirs, other[at_other], mine[at_mine])
+        tiles = [jnp.where(theirs, o[at_other], m[at_mine]) for m, o in zip(mine, other)]
+        tile = jnp.concatenate(tiles, axis=0)
         place = jnp.minimum(place, size - 1)
-        for stage, out in enumerate(outs):
-            out[place] = tile[stage * ROWS : (stage + 1) * ROWS]
-
-    walk(blocks, per_device, known, bit, (mine.shape[0], other.shape[0]), act)
+        for at, out in enumerate(outs):
+            rows = out.shape[1]
+            out[place] = tile[at * rows : (at + 1) * rows]
+
+    walk(blocks, per_device, known, bit, (mine[0].shape[0], other[0].shape[0]), act)
 
 
 def merged(blocks, per_device, known, bit, mine, other, size):
-    count = mine.shape[1] // ROWS
+    count = sum(m.shape[1] for m in mine) // ROWS
     shape = jax.ShapeDtypeStruct((size, ROWS, HD), jnp.bfloat16)
     return pl.pallas_call(
-        functools.partial(merge_kernel, per_device, known, bit),
+        functools.partial(merge_kernel, per_device, known, bit, len(mine)),
         out_shape=(shape,) * count,
-        in_specs=[SMEM, WHOLE, WHOLE],
+        in_specs=[SMEM] + [WHOLE] * (2 * len(mine)),
         out_specs=(WHOLE,) * count,
         compiler_params=pltpu.CompilerParams(vmem_limit_bytes=16 * 2**20),
         name="merge",
-    )(blocks, mine, other)
+    )(blocks, *mine, *other)
 
 
 def stage_kernel(per_device, known, bit, banded, last, *refs):
@@ -275,12 +280,12 @@
         before, own_k, own_v = refs[:3]
         refs = refs[3:]
     else:
-        largest_in, total_in, mixed_in = refs[:3]
-        refs = refs[3:]
+        marks_in, mixed_in = refs[:2]
+        refs = refs[2:]
     if last:
         out, kbuf, vbuf, held, sems = refs
     else:
-        largest_out, total_out, mixed_out, kbuf, vbuf = refs
+        marks_out, mixed_out, kbuf, vbuf = refs
     me = lax.axis_index("ctx")
     even = lax.rem(me, 2) == 0
     wide = NV * ROWS
@@ -317,13 +322,12 @@
             tile = slice(start, start + TILE * QDEV)
             largest, mixed = attend_rows(rows, kbuf[head], vbuf[head], mask)
             mixed, total = mixed[:, :HD], mixed[:, HD:]
-            largest = jnp.broadcast_to(largest, mixed.shape)
             if not banded:
-                above = jnp.maximum(largest_in[tile], largest)
-                now, then = jnp.exp2(largest - above), jnp.exp2(largest_in[tile] - above)
+                before_largest = marks_in[tile, :1]
+                above = jnp.maximum(before_largest, largest)
+                now, then = jnp.exp2(largest - above), jnp.exp2(before_largest - above)
                 mixed = mixed * now + mixed_in[tile] * then
-                total = total * now + total_in[tile] * then
-                largest = above
+                total = total * now + marks_in[tile, HD - 1 :] * then
             if last:
                 result = (mixed / total).astype(jnp.bfloat16)
                 for i in range(TILE):
@@ -331,7 +335,9 @@
                         i * QDEV : (i + 1) * QDEV
                     ]
             else:
-                largest_out[tile], total_out[tile], mixed_out[tile] = largest, total, mixed
+                lanes = lax.broadcasted_iota(jnp.int32, mixed.shape, 1)
+                marks_out[tile] = jnp.where(lanes < HD // 2, largest, total)
+                mixed_out[tile] = mixed
         if last:
             span = pl.ds(head * GROUP * HD, GROUP * HD)
             copies.append(pltpu.make_async_copy(held.at[head], out.at[:, span], sems.at[head]))
@@ -359,20 +365,16 @@
             pltpu.SemaphoreType.DMA((KVH,)),
         ]
     else:
-        out_shape = (jax.ShapeDtypeStruct((tall, HD), jnp.float32),) * 3
-        out_specs = (WHOLE,) * 3
+        out_shape = (jax.ShapeDtypeStruct((tall, HD), jnp.float32),) * 2
+        out_specs = (WHOLE,) * 2
     return pl.pallas_call(
         functools.partial(stage_kernel, per_device, known, bit, banded, last),
         out_shape=out_shape,
         in_specs=specs,
         out_specs=out_specs,
         scratch_shapes=scratch,
-        compiler_params=pltpu.CompilerParams(vmem_limit_bytes=48 * 2**20),
-        cost_estimate=pl.CostEstimate(
-            flops=4 * tall * keys * HD,
-            bytes_accessed=8 * 2**20,
-            transcendentals=tall * keys,
-        ),
+        compiler_params=pltpu.CompilerParams(vmem_limit_bytes=VMEM * 2**20),
+        cost_estimate=pl.CostEstimate(flops=COST, bytes_accessed=COST, transcendentals=0),
         name="attend_last" if last else "attend_first",
     )(*args)
 
@@ -414,20 +416,24 @@
     bits = [1] + [1 << at for at in range(peers.bit_length() - 2, 0, -1)]
 
     kept, sent = pack(blocks, cache_k, cache_v, room(1 / peers))
-    mine = list(merged(blocks, per_device, 0, 1, kept, swapped(sent, 1), room(2 / peers)))
+    mine = merged(blocks, per_device, 0, 1, [kept], [swapped(sent, 1)], room(2 / peers))
     before = permuted(jnp.concatenate([span_k, span_v], axis=1), ahead)
+    short = jnp.logical_not(fits(blocks, per_device, peers, bits)).astype(jnp.int32)
     other = [None] * STAGES
     known = 1
     for bit in bits[1:]:
-        other[0] = swapped(mine[0], bit)
+        other = [swapped(m, bit) for m in mine]
         if bit == bits[1]:
-            other[0], before = lax.optimization_barrier((other[0], before))
-        other[1] = swapped(mine[1], bit)
+            other[0], before, short = lax.optimization_barrier((other[0], before, short))
         if bit == bits[-1]:
             break
         size = room((1 << (known | bit).bit_count()) / peers)
-        for stage in range(STAGES):
-            (mine[stage],) = merged(blocks, per_device, known, bit, mine[stage], other[stage], size)
+        level = (blocks, per_device, known, bit)
+        if bit == bits[1]:
+            mine = merged(*level, mine, other, size)
+        else:
+            pairs = zip(mine, other)
+            mine = [merged(*level, [m], [o], size)[0] for m, o in pairs]
         known |= bit
     twins = [swapped(m, 1) for m in mine]
 
@@ -437,11 +443,12 @@
     state = attend_stage(*shared, lists, offsets=offsets, bands=bands)
     state, late = lax.optimization_barrier((state, other[1]))
     lists = (mine[1], late, twins[1], swapped(late, 1))
-    return lax.cond(
-        fits(blocks, per_device, peers, bits),
-        lambda: attend_stage(*shared, lists, state=state),
-        lambda: general(queries, bands, cache_k, cache_v, blocks, offsets, bits),
-    )
+    fast = attend_stage(*shared, lists, state=state)
+
+    def again(carry):
+        return 0, general(queries, bands, cache_k, cache_v, blocks, offsets, bits)
+
+    return lax.while_loop(lambda carry: carry[0] > 0, again, (short, fast))[1]
 
 
 def solution(mesh):

time: 69.1 us -> 67.7 us (0.980)
  Pallas kernels: 24 us -> 21.2 us
  waiting for transfers between devices: 29.9 us -> 31.7 us
  local copies, waits for them, and re-layouts: 1.08 us -> 0.12 us
    pallas_call x2, Pallas kernels: 15.8 us -> 14 us  [attend_stage(): pl.pallas_call(functools.partial(stage_kernel, per_device, known, bit, ba...]
    ppermute x12, waiting for transfers between devices: 29.9 us -> 31.7 us  [permuted(): return lax.ppermute(array, 'ctx', pairs)]
    pallas_call x5 -> x4, Pallas kernels: 5.87 us -> 4.9 us  [merged(): pl.pallas_call(functools.partial(merge_kernel, per_device, known, bit, le...]
    unnamed x16, local copies, waits for them, and re-layouts: 1 us -> 0.03 us
  transfers between devices with their start and end apart: 12 -> 12, of which waited for: 6 -> 6; matrix products, arithmetic and copies ran while one was open for 1% -> 2% of each run, Pallas kernels for 17% -> 12%
where the time goes in v5:
time: 67.7 us; the launch traced here: 67.5 us
  waiting for transfers between devices  31.7 us (47%)
  Pallas kernels  21.2 us (31%)
  starting transfers between devices  12.5 us (18%)
  between operations  0.98 us (1%)
  other arithmetic  0.95 us (1%)
    ppermute x12, waiting for transfers between devices, permuted(): return lax.ppermute(array, 'ctx', pairs)  31.7 us
    pallas_call x2, Pallas kernels, attend_stage(): pl.pallas_call(functools.partial(stage_kernel, per_device, known, bit, ba...  14 us
    ppermute x12, starting transfers between devices, permuted(): return lax.ppermute(array, 'ctx', pairs)  12.5 us
    pallas_call x4, Pallas kernels, merged(): pl.pallas_call(functools.partial(merge_kernel, per_device, known, bit, le...  4.9 us
    pallas_call x1, Pallas kernels, pack(): pl.pallas_call(functools.partial(pack_kernel, cache_k.shape[0] // VBLOCK,...  2.32 us
  transfers between devices with their start and end apart: 12, of which 6 were waited for; matrix products, arithmetic and copies ran while one was open for 2% of the time, Pallas kernels for 12%

profile of v5, /device:TPU:0, one launch (start us, length us, event | category | flops | bytes accessed | tf_op | source)
XLA Modules:
  0.0 67.5 jit_solution(11654531195740890101)
XLA Ops:
  0.0 0.0 copy-start.9
  0.0 0.0 copy-start.8
  0.0 0.0 copy-start.6
  0.0 0.0 copy-start.3
  0.0 2.3 %pack.1 = (bf16[12,64,128]{2,1,0:T(8,128)(2,1)S(1)}, bf16[12,64,128]{2,1,0:T(8,128)(2,1)S(1)}) custom-call(s32[4,16]{1,0:T(4,128)} %refs_0_.3, bf16[2048,512]{1,0:T(8,128)(2,1)} %cache_k.1, bf16[2048,512]{1,0:T(8,128)(2,1)} %cache_v.1), custom_call_target="tpu_custom_call" | custom-call | tf_op jit(solution)/shard_map/pack/pallas_call | solution.py:222
  2.3 0.0 copy-start.2
  2.4 0.0 copy-start.7
  2.4 0.6 collective-permute-start.8
  2.9 0.0 copy-done.3
  3.0 0.0 copy-done.4
  3.0 2.1 %collective-permute-start.10 = (bf16[128,1024]{1,0:T(8,128)(2,1)S(1)}, bf16[128,1024]{1,0:T(8,128)(2,1)S(1)}, u32[]{:S(2)}, u32[]{:S(2)}) collective-permute-start(bf16[128,1024]{1,0:T(8,128)(2,1)S(1)} %pad_maximum_fusion), channel_id=1, source_target_pairs={{0,1},{1,2},{2,3},{3,4},{4,5},{5,6},{6,7},{7,8},{8,9},{9,10},{10,1... | collective-permute-start | bytes 786440 | tf_op jit(solution)/shard_map/ppermute | solution.py:383
  5.1 0.0 copy-done.6
  5.1 0.1 xor.20
  5.2 0.0 collective-permute-done.8.refs_1_
  5.2 1.4 %merge.4 = (bf16[18,32,128]{2,1,0:T(8,128)(2,1)S(1)}, bf16[18,32,128]{2,1,0:T(8,128)(2,1)S(1)}) custom-call(s32[4,16]{1,0:T(4,128)S(1)} %copy-done.6, bf16[12,64,128]{2,1,0:T(8,128)(2,1)S(1)} %get-tuple-element.71.refs_0_, bf16[12,64,128]{2,1,0:T(8,128)(2,1)S(1)} %collective-permute-done.8.refs_1_), custom_call_target="tpu_custom_call" | custom-call | tf_op jit(solution)/shard_map/merge/pallas_call | solution.py:263
  6.6 3.8 %collective-permute-start.9 = (bf16[18,32,128]{2,1,0:T(8,128)(2,1)S(1)}, bf16[18,32,128]{2,1,0:T(8,128)(2,1)S(1)}, u32[]{:S(2)}, u32[]{:S(2)}) collective-permute-start(bf16[18,32,128]{2,1,0:T(8,128)(2,1)S(1)} %get-tuple-element.73.refs_0_), channel_id=1, source_target_pairs={{0,8},{1,9},{2,10},{3,11},{4,12},{5,13},{6,14},{7,15},{8,0},{9,1},... | collective-permute-start | bytes 442376 | tf_op jit(solution)/shard_map/ppermute | solution.py:383
  10.3 0.1 collective-permute-start.11
  10.4 0.0 copy-done.9
  10.4 0.2 convert_reduce_fusion
  10.6 0.0 copy-done.8
  10.6 0.7 %compare_reduce_fusion = pred[]{:T(512)} fusion(s32[4,16]{1,0:T(4,128)S(1)} %convert_reduce_fusion, s32[4]{0:T(128)S(1)} %copy-done.8), kind=kLoop, calls=%fused_computation.11 | loop fusion | flops 127 | bytes 273 | tf_op jit(solution)/shard_map/reduce_and | solution.py:397
  12.0 0.0 collective-permute-done.10.refs_7_
  12.0 8.6 %collective-permute-done.9.refs_2_ = bf16[18,32,128]{2,1,0:T(8,128)(2,1)S(1)} collective-permute-done((bf16[18,32,128]{2,1,0:T(8,128)(2,1)S(1)}, bf16[18,32,128]{2,1,0:T(8,128)(2,1)S(1)}, u32[]{:S(2)}, u32[]{:S(2)}) %collective-permute-start.9) | collective-permute-done | bytes 147488 | tf_op jit(solution)/shard_map/ppermute | solution.py:383
  20.6 3.2 %collective-permute-done.11.refs_3_ = bf16[18,32,128]{2,1,0:T(8,128)(2,1)S(1)} collective-permute-done((bf16[18,32,128]{2,1,0:T(8,128)(2,1)S(1)}, bf16[18,32,128]{2,1,0:T(8,128)(2,1)S(1)}, u32[]{:S(2)}, u32[]{:S(2)}) %collective-permute-start.11) | collective-permute-done | bytes 147488 | tf_op jit(solution)/shard_map/ppermute | solution.py:383
  23.7 1.3 %merge.5 = (bf16[28,32,128]{2,1,0:T(8,128)(2,1)S(1)}, bf16[28,32,128]{2,1,0:T(8,128)(2,1)S(1)}) custom-call(s32[4,16]{1,0:T(4,128)S(1)} %copy-done.6, bf16[18,32,128]{2,1,0:T(8,128)(2,1)S(1)} %get-tuple-element.73.refs_0_, bf16[18,32,128]{2,1,0:T(8,128)(2,1)S(1)} %get-tuple-element.75.refs_1_, bf16[18,32,128]{2,1,0:T(8,128)(2,1)S(1)} %collective-permute-done.9.refs_2_, ...), custom_call_target="tpu_custom_call" | custom-call | tf_op jit(solution)/shard_map/merge/pallas_call | solution.py:263
  25.0 1.8 %collective-permute-start.13 = (bf16[28,32,128]{2,1,0:T(8,128)(2,1)S(1)}, bf16[28,32,128]{2,1,0:T(8,128)(2,1)S(1)}, u32[]{:S(2)}, u32[]{:S(2)}) collective-permute-start(bf16[28,32,128]{2,1,0:T(8,128)(2,1)S(1)} %get-tuple-element.78.refs_0_), channel_id=1, source_target_pairs={{0,4},{1,5},{2,6},{3,7},{4,0},{5,1},{6,2},{7,3},{8,12},{9,13},{10,... | collective-permute-start | bytes 688136 | tf_op jit(solution)/shard_map/ppermute | solution.py:383
  26.8 6.4 %collective-permute-done.13.refs_1_ = bf16[28,32,128]{2,1,0:T(8,128)(2,1)S(1)} collective-permute-done((bf16[28,32,128]{2,1,0:T(8,128)(2,1)S(1)}, bf16[28,32,128]{2,1,0:T(8,128)(2,1)S(1)}, u32[]{:S(2)}, u32[]{:S(2)}) %collective-permute-start.13) | collective-permute-done | bytes 229408 | tf_op jit(solution)/shard_map/ppermute | solution.py:383
  33.2 1.1 %merge.7.refs_3_ = bf16[46,32,128]{2,1,0:T(8,128)(2,1)S(1)} custom-call(s32[4,16]{1,0:T(4,128)S(1)} %copy-done.6, bf16[28,32,128]{2,1,0:T(8,128)(2,1)S(1)} %get-tuple-element.78.refs_0_, bf16[28,32,128]{2,1,0:T(8,128)(2,1)S(1)} %collective-permute-done.13.refs_1_), custom_call_target="tpu_custom_call" | custom-call | tf_op jit(solution)/shard_map/merge/pallas_call | solution.py:263
  34.3 2.1 %collective-permute-start.14 = (bf16[46,32,128]{2,1,0:T(8,128)(2,1)S(1)}, bf16[46,32,128]{2,1,0:T(8,128)(2,1)S(1)}, u32[]{:S(2)}, u32[]{:S(2)}) collective-permute-start(bf16[46,32,128]{2,1,0:T(8,128)(2,1)S(1)} %merge.7.refs_3_), channel_id=1, source_target_pairs={{0,2},{1,3},{2,0},{3,1},{4,6},{5,7},{6,4},{7,5},{8,10},{9,11},{10,... | collective-permute-start | bytes 1130504 | tf_op jit(solution)/shard_map/ppermute | solution.py:383
  36.4 0.3 collective-permute-start.12
  36.7 0.0 collective-permute-start.15
  36.7 8.2 %collective-permute-done.14.refs_4_ = bf16[46,32,128]{2,1,0:T(8,128)(2,1)S(1)} collective-permute-done((bf16[46,32,128]{2,1,0:T(8,128)(2,1)S(1)}, bf16[46,32,128]{2,1,0:T(8,128)(2,1)S(1)}, u32[]{:S(2)}, u32[]{:S(2)}) %collective-permute-start.14) | collective-permute-done | bytes 376864 | tf_op jit(solution)/shard_map/ppermute | solution.py:383
  44.9 0.0 collective-permute-start.16
  44.9 0.0 collective-permute-done.12.refs_1_
  44.9 1.1 %merge.6.refs_2_ = bf16[46,32,128]{2,1,0:T(8,128)(2,1)S(1)} custom-call(s32[4,16]{1,0:T(4,128)S(1)} %copy-done.6, bf16[28,32,128]{2,1,0:T(8,128)(2,1)S(1)} %get-tuple-element.77.refs_0_, bf16[28,32,128]{2,1,0:T(8,128)(2,1)S(1)} %collective-permute-done.12.refs_1_), custom_call_target="tpu_custom_call" | custom-call | tf_op jit(solution)/shard_map/merge/pallas_call | solution.py:263
  46.0 1.6 %collective-permute-start.17 = (bf16[46,32,128]{2,1,0:T(8,128)(2,1)S(1)}, bf16[46,32,128]{2,1,0:T(8,128)(2,1)S(1)}, u32[]{:S(2)}, u32[]{:S(2)}) collective-permute-start(bf16[46,32,128]{2,1,0:T(8,128)(2,1)S(1)} %merge.6.refs_2_), channel_id=1, source_target_pairs={{0,2},{1,3},{2,0},{3,1},{4,6},{5,7},{6,4},{7,5},{8,10},{9,11},{10,... | collective-permute-start | bytes 1130504 | tf_op jit(solution)/shard_map/ppermute | solution.py:383
  47.6 0.2 collective-permute-start.18
  47.8 0.0 collective-permute-done.15.refs_5_
  47.8 0.0 collective-permute-done.16.refs_6_
  47.8 0.0 copy-done.2
  47.8 0.0 copy-done.7
  47.8 5.7 %attend_first.1 = (f32[4096,128]{1,0:T(8,128)S(1)}, f32[4096,128]{1,0:T(8,128)S(1)}) custom-call(s32[4,16]{1,0:T(4,128)S(1)} %copy-done.6, s32[4,64]{1,0:T(4,128)S(1)} %copy-done.7, bf16[128,4096]{1,0:T(8,128)(2,1)S(1)} %copy-done.2, bf16[46,32,128]{2,1,0:T(8,128)(2,1)S(1)} %merge.7.refs_3_, bf16[46,32,128]{2,1,0:T(8,128)(2,1)S(1)} %collective-permute-done.14.refs_4_, ...), custom_call_target="tpu_custom_call" | custom-call | flops 1048576 | bytes 1048576 | tf_op jit(solution)/shard_map/attend_first/pallas_call | solution.py:370
  53.5 3.8 %collective-permute-done.17.refs_3_ = bf16[46,32,128]{2,1,0:T(8,128)(2,1)S(1)} collective-permute-done((bf16[46,32,128]{2,1,0:T(8,128)(2,1)S(1)}, bf16[46,32,128]{2,1,0:T(8,128)(2,1)S(1)}, u32[]{:S(2)}, u32[]{:S(2)}) %collective-permute-start.17) | collective-permute-done | bytes 376864 | tf_op jit(solution)/shard_map/ppermute | solution.py:383
  57.3 0.0 collective-permute-start.19
  57.3 0.0 collective-permute-done.18.refs_4_
  57.3 1.7 %collective-permute-done.19.refs_5_ = bf16[46,32,128]{2,1,0:T(8,128)(2,1)S(1)} collective-permute-done((bf16[46,32,128]{2,1,0:T(8,128)(2,1)S(1)}, bf16[46,32,128]{2,1,0:T(8,128)(2,1)S(1)}, u32[]{:S(2)}, u32[]{:S(2)}) %collective-permute-start.19) | collective-permute-done | bytes 376864 | tf_op jit(solution)/shard_map/ppermute | solution.py:383
  59.0 8.3 %attend_last.1 = bf16[128,4096]{1,0:T(8,128)(2,1)} custom-call(s32[4,16]{1,0:T(4,128)S(1)} %copy-done.6, bf16[128,4096]{1,0:T(8,128)(2,1)S(1)} %copy-done.2, bf16[46,32,128]{2,1,0:T(8,128)(2,1)S(1)} %merge.6.refs_2_, bf16[46,32,128]{2,1,0:T(8,128)(2,1)S(1)} %collective-permute-done.17.refs_3_, bf16[46,32,128]{2,1,0:T(8,128)(2,1)S(1)} %collective-permute-done.18.refs_4_, ...), custom_call_target="tpu_custom_call" | custom-call | flops 1048576 | bytes 1048576 | tf_op jit(solution)/shard_map/attend_last/pallas_call | solution.py:370
  67.3 0.0 copy-done
  (6 shorter events, 0.0 us)
Async XLA Ops:
  0.0 10.4 %copy-start.9 = (s32[4]{0:T(128)S(1)}, s32[4]{0:T(128)}, u32[]{:S(2)}) copy-start(s32[4]{0:T(128)} %constant.30) | copy-start | bytes 52
  0.0 10.6 %copy-start.8 = (s32[4]{0:T(128)S(1)}, s32[4]{0:T(128)}, u32[]{:S(2)}) copy-start(s32[4]{0:T(128)} %constant.29.clone) | copy-start | bytes 52
  0.0 5.1 %copy-start.6 = (s32[4,16]{1,0:T(4,128)S(1)}, s32[4,16]{1,0:T(4,128)}, u32[]{:S(2)}) copy-start(s32[4,16]{1,0:T(4,128)} %refs_0_.3) | copy-start | bytes 772
  0.0 2.9 %copy-start.3 = (bf16[128,512]{1,0:T(8,128)(2,1)S(1)}, bf16[128,512]{1,0:T(8,128)(2,1)}, u32[]{:S(2)}) copy-start(bf16[128,512]{1,0:T(8,128)(2,1)} %refs_9_.1) | copy-start | bytes 393220
  0.0 2.9 %copy-start.4 = (bf16[128,512]{1,0:T(8,128)(2,1)S(1)}, bf16[128,512]{1,0:T(8,128)(2,1)}, u32[]{:S(2)}) copy-start(bf16[128,512]{1,0:T(8,128)(2,1)} %refs_8_.1) | copy-start | bytes 393220
  2.3 45.5 %copy-start.2 = (bf16[128,4096]{1,0:T(8,128)(2,1)S(1)}, bf16[128,4096]{1,0:T(8,128)(2,1)}, u32[]{:S(2)}) copy-start(bf16[128,4096]{1,0:T(8,128)(2,1)} %refs_1_.3) | copy-start | bytes 3145732
  2.4 45.5 %copy-start.7 = (s32[4,64]{1,0:T(4,128)S(1)}, s32[4,64]{1,0:T(4,128)}, u32[]{:S(2)}) copy-start(s32[4,64]{1,0:T(4,128)} %refs_1_.2) | copy-start | bytes 3076
  2.4 2.8 %collective-permute-start.8 = (bf16[12,64,128]{2,1,0:T(8,128)(2,1)S(1)}, bf16[12,64,128]{2,1,0:T(8,128)(2,1)S(1)}, u32[]{:S(2)}, u32[]{:S(2)}) collective-permute-start(bf16[12,64,128]{2,1,0:T(8,128)(2,1)S(1)} %get-tuple-element.72), channel_id=1, source_target_pairs={{0,1},{1,0},{2,3},{3,2},{4,5},{5,4},{6,7},{7,6},{8,9},{9,8},{10,11... | collective-permute-start | bytes 589832 | tf_op jit(solution)/shard_map/ppermute | solution.py:383
  3.0 9.0 %collective-permute-start.10 = (bf16[128,1024]{1,0:T(8,128)(2,1)S(1)}, bf16[128,1024]{1,0:T(8,128)(2,1)S(1)}, u32[]{:S(2)}, u32[]{:S(2)}) collective-permute-start(bf16[128,1024]{1,0:T(8,128)(2,1)S(1)} %pad_maximum_fusion), channel_id=1, source_target_pairs={{0,1},{1,2},{2,3},{3,4},{4,5},{5,6},{6,7},{7,8},{8,9},{9,10},{10,1... | collective-permute-start | bytes 786440 | tf_op jit(solution)/shard_map/ppermute | solution.py:383
  6.6 14.0 %collective-permute-start.9 = (bf16[18,32,128]{2,1,0:T(8,128)(2,1)S(1)}, bf16[18,32,128]{2,1,0:T(8,128)(2,1)S(1)}, u32[]{:S(2)}, u32[]{:S(2)}) collective-permute-start(bf16[18,32,128]{2,1,0:T(8,128)(2,1)S(1)} %get-tuple-element.73.refs_0_), channel_id=1, source_target_pairs={{0,8},{1,9},{2,10},{3,11},{4,12},{5,13},{6,14},{7,15},{8,0},{9,1},... | collective-permute-start | bytes 442376 | tf_op jit(solution)/shard_map/ppermute | solution.py:383
  10.3 13.4 %collective-permute-start.11 = (bf16[18,32,128]{2,1,0:T(8,128)(2,1)S(1)}, bf16[18,32,128]{2,1,0:T(8,128)(2,1)S(1)}, u32[]{:S(2)}, u32[]{:S(2)}) collective-permute-start(bf16[18,32,128]{2,1,0:T(8,128)(2,1)S(1)} %get-tuple-element.75.refs_1_), channel_id=1, source_target_pairs={{0,8},{1,9},{2,10},{3,11},{4,12},{5,13},{6,14},{7,15},{8,0},{9,1},... | collective-permute-start | bytes 442376 | tf_op jit(solution)/shard_map/ppermute | solution.py:383
  25.0 8.2 %collective-permute-start.13 = (bf16[28,32,128]{2,1,0:T(8,128)(2,1)S(1)}, bf16[28,32,128]{2,1,0:T(8,128)(2,1)S(1)}, u32[]{:S(2)}, u32[]{:S(2)}) collective-permute-start(bf16[28,32,128]{2,1,0:T(8,128)(2,1)S(1)} %get-tuple-element.78.refs_0_), channel_id=1, source_target_pairs={{0,4},{1,5},{2,6},{3,7},{4,0},{5,1},{6,2},{7,3},{8,12},{9,13},{10,... | collective-permute-start | bytes 688136 | tf_op jit(solution)/shard_map/ppermute | solution.py:383
  34.3 10.6 %collective-permute-start.14 = (bf16[46,32,128]{2,1,0:T(8,128)(2,1)S(1)}, bf16[46,32,128]{2,1,0:T(8,128)(2,1)S(1)}, u32[]{:S(2)}, u32[]{:S(2)}) collective-permute-start(bf16[46,32,128]{2,1,0:T(8,128)(2,1)S(1)} %merge.7.refs_3_), channel_id=1, source_target_pairs={{0,2},{1,3},{2,0},{3,1},{4,6},{5,7},{6,4},{7,5},{8,10},{9,11},{10,... | collective-permute-start | bytes 1130504 | tf_op jit(solution)/shard_map/ppermute | solution.py:383
  36.4 8.5 %collective-permute-start.12 = (bf16[28,32,128]{2,1,0:T(8,128)(2,1)S(1)}, bf16[28,32,128]{2,1,0:T(8,128)(2,1)S(1)}, u32[]{:S(2)}, u32[]{:S(2)}) collective-permute-start(bf16[28,32,128]{2,1,0:T(8,128)(2,1)S(1)} %get-tuple-element.77.refs_0_), channel_id=1, source_target_pairs={{0,4},{1,5},{2,6},{3,7},{4,0},{5,1},{6,2},{7,3},{8,12},{9,13},{10,... | collective-permute-start | bytes 688136 | tf_op jit(solution)/shard_map/ppermute | solution.py:383
  36.7 11.1 %collective-permute-start.15 = (bf16[46,32,128]{2,1,0:T(8,128)(2,1)S(1)}, bf16[46,32,128]{2,1,0:T(8,128)(2,1)S(1)}, u32[]{:S(2)}, u32[]{:S(2)}) collective-permute-start(bf16[46,32,128]{2,1,0:T(8,128)(2,1)S(1)} %merge.7.refs_3_), channel_id=1, source_target_pairs={{0,1},{1,0},{2,3},{3,2},{4,5},{5,4},{6,7},{7,6},{8,9},{9,8},{10,11... | collective-permute-start | bytes 1130504 | tf_op jit(solution)/shard_map/ppermute | solution.py:383
  44.9 2.9 %collective-permute-start.16 = (bf16[46,32,128]{2,1,0:T(8,128)(2,1)S(1)}, bf16[46,32,128]{2,1,0:T(8,128)(2,1)S(1)}, u32[]{:S(2)}, u32[]{:S(2)}) collective-permute-start(bf16[46,32,128]{2,1,0:T(8,128)(2,1)S(1)} %collective-permute-done.14.refs_4_), channel_id=1, source_target_pairs={{0,1},{1,0},{2,3},{3,2},{4,5},{5,4},{6,7},{7,6},{8,9},{9,8},{10,11... | collective-permute-start | bytes 1130504 | tf_op jit(solution)/shard_map/ppermute | solution.py:383
  46.0 11.2 %collective-permute-start.17 = (bf16[46,32,128]{2,1,0:T(8,128)(2,1)S(1)}, bf16[46,32,128]{2,1,0:T(8,128)(2,1)S(1)}, u32[]{:S(2)}, u32[]{:S(2)}) collective-permute-start(bf16[46,32,128]{2,1,0:T(8,128)(2,1)S(1)} %merge.6.refs_2_), channel_id=1, source_target_pairs={{0,2},{1,3},{2,0},{3,1},{4,6},{5,7},{6,4},{7,5},{8,10},{9,11},{10,... | collective-permute-start | bytes 1130504 | tf_op jit(solution)/shard_map/ppermute | solution.py:383
  47.6 9.7 %collective-permute-start.18 = (bf16[46,32,128]{2,1,0:T(8,128)(2,1)S(1)}, bf16[46,32,128]{2,1,0:T(8,128)(2,1)S(1)}, u32[]{:S(2)}, u32[]{:S(2)}) collective-permute-start(bf16[46,32,128]{2,1,0:T(8,128)(2,1)S(1)} %merge.6.refs_2_), channel_id=1, source_target_pairs={{0,1},{1,0},{2,3},{3,2},{4,5},{5,4},{6,7},{7,6},{8,9},{9,8},{10,11... | collective-permute-start | bytes 1130504 | tf_op jit(solution)/shard_map/ppermute | solution.py:383
  57.3 10.0 %copy-start = (bf16[2048,512]{1,0:T(8,128)(2,1)S(1)}, bf16[2048,512]{1,0:T(8,128)(2,1)}, u32[]{:S(2)}) copy-start(bf16[2048,512]{1,0:T(8,128)(2,1)} %cache_k.1) | copy-start | bytes 6291460
  57.3 1.7 %collective-permute-start.19 = (bf16[46,32,128]{2,1,0:T(8,128)(2,1)S(1)}, bf16[46,32,128]{2,1,0:T(8,128)(2,1)S(1)}, u32[]{:S(2)}, u32[]{:S(2)}) collective-permute-start(bf16[46,32,128]{2,1,0:T(8,128)(2,1)S(1)} %collective-permute-done.17.refs_3_), channel_id=1, source_target_pairs={{0,1},{1,0},{2,3},{3,2},{4,5},{5,4},{6,7},{7,6},{8,9},{9,8},{10,11... | collective-permute-start | bytes 1130504 | tf_op jit(solution)/shard_map/ppermute | solution.py:383

commit v6 on v5

--- a/solution.py
+++ b/solution.py
@@ -36,7 +36,7 @@
     return (rolled > 0) & (keys >= jnp.where(first, SMAX, 0))
 
 
-def attend_rows(rows, keys, values_ones, mask):
+def attend_rows(rows, keys, values_ones, mask, floor=None):
     scores = lax.dot_general(
         rows, keys, (((1,), (1,)), ((), ())), preferred_element_type=jnp.float32
     )
@@ -47,6 +47,8 @@
         band = jnp.where(tiled, scores[:, wide:], LOW)
         scores = jnp.concatenate([scores[:, :wide], band], axis=1)
     largest = jnp.max(scores, axis=1, keepdims=True) * FACTOR
+    if floor is not None:
+        largest = jnp.maximum(largest, floor)
     weights = jnp.exp2(scores * FACTOR - largest).astype(jnp.bfloat16)
     mixed = jnp.dot(weights, values_ones, preferred_element_type=jnp.float32)
     return largest, mixed
@@ -242,32 +244,32 @@
         at_other += other.astype(jnp.int32)
 
 
-def merge_kernel(per_device, known, bit, count, blocks, *refs):
-    mine, other, outs = refs[:count], refs[count : 2 * count], refs[2 * count :]
-    size = outs[0].shape[0]
+def merge_kernel(per_device, known, bit, halved, blocks, mine, other, *outs):
+    size, rows = outs[0].shape[:2]
+    me = lax.axis_index("ctx")
+    first = pl.multiple_of(jnp.where((me & halved) == 0, 0, rows), rows) if halved else 0
 
     def act(entry, at_mine, at_other, place, theirs):
-        tiles = [jnp.where(theirs, o[at_other], m[at_mine]) for m, o in zip(mine, other)]
-        tile = jnp.concatenate(tiles, axis=0)
         place = jnp.minimum(place, size - 1)
         for at, out in enumerate(outs):
-            rows = out.shape[1]
-            out[place] = tile[at * rows : (at + 1) * rows]
-
-    walk(blocks, per_device, known, bit, (mine[0].shape[0], other[0].shape[0]), act)
-
-
-def merged(blocks, per_device, known, bit, mine, other, size):
-    count = sum(m.shape[1] for m in mine) // ROWS
-    shape = jax.ShapeDtypeStruct((size, ROWS, HD), jnp.bfloat16)
-    return pl.pallas_call(
-        functools.partial(merge_kernel, per_device, known, bit, len(mine)),
-        out_shape=(shape,) * count,
-        in_specs=[SMEM] + [WHOLE] * (2 * len(mine)),
-        out_specs=(WHOLE,) * count,
+            span = pl.ds(first + at * rows, rows)
+            out[place] = jnp.where(theirs, other[at_other, span], mine[at_mine, span])
+
+    walk(blocks, per_device, known, bit, (mine.shape[0], other.shape[0]), act)
+
+
+def merged(blocks, per_device, known, bit, mine, other, size, parts=1, halved=0):
+    rows = mine.shape[1] // (2 if halved else parts)
+    shape = jax.ShapeDtypeStruct((size, rows, HD), jnp.bfloat16)
+    outs = pl.pallas_call(
+        functools.partial(merge_kernel, per_device, known, bit, halved),
+        out_shape=(shape,) * parts,
+        in_specs=[SMEM, WHOLE, WHOLE],
+        out_specs=(WHOLE,) * parts,
         compiler_params=pltpu.CompilerParams(vmem_limit_bytes=16 * 2**20),
         name="merge",
-    )(blocks, *mine, *other)
+    )(blocks, mine, other)
+    return outs if parts > 1 else outs[0]
 
 
 def stage_kernel(per_device, known, bit, banded, last, *refs):
@@ -297,7 +299,17 @@
         kbuf[entry // NV, rows] = jnp.where(even, tile, twin)
         vbuf[entry // NV, rows, :HD] = jnp.where(even, twin, tile)
 
-    walk(blocks, per_device, known, bit, (mine.shape[0], other.shape[0]), act)
+    if not last:
+        walk(blocks, per_device, known, bit, (mine.shape[0], other.shape[0]), act)
+    else:
+        half = wide // 2
+        for head in range(KVH):
+            span = slice(head * NV, (head + 1) * NV)
+            for at, (own, twin) in enumerate(((mine, mine_twin), (other, other_twin))):
+                tile, pair = own[span].reshape(half, HD), twin[span].reshape(half, HD)
+                rows = slice(at * half, (at + 1) * half)
+                kbuf[head, rows] = jnp.where(even, tile, pair)
+                vbuf[head, rows, :HD] = jnp.where(even, pair, tile)
     copies = []
     for head in range(KVH):
         columns = slice(head * HD, (head + 1) * HD)
@@ -320,14 +332,13 @@
             )
             start = (head * GROUP + at) * QDEV
             tile = slice(start, start + TILE * QDEV)
-            largest, mixed = attend_rows(rows, kbuf[head], vbuf[head], mask)
+            floor = None if banded else marks_in[tile, :1]
+            largest, mixed = attend_rows(rows, kbuf[head], vbuf[head], mask, floor)
             mixed, total = mixed[:, :HD], mixed[:, HD:]
             if not banded:
-                before_largest = marks_in[tile, :1]
-                above = jnp.maximum(before_largest, largest)
-                now, then = jnp.exp2(largest - above), jnp.exp2(before_largest - above)
-                mixed = mixed * now + mixed_in[tile] * then
-                total = total * now + marks_in[tile, HD - 1 :] * then
+                then = jnp.exp2(floor - largest)
+                mixed = mixed + mixed_in[tile] * then
+                total = total + marks_in[tile, HD - 1 :] * then
             if last:
                 result = (mixed / total).astype(jnp.bfloat16)
                 for i in range(TILE):
@@ -387,9 +398,8 @@
     return permuted(array, [(i, i ^ bit) for i in range(lax.axis_size("ctx"))])
 
 
-def fits(blocks, per_device, peers, bits):
-    masks = [sum(bits[:at]) for at in range(len(bits))]
-    most = [room((1 << at) / peers) - (at > 0) for at in range(len(bits))]
+def fits(blocks, per_device, peers, masks):
+    most = [room((1 << mask.bit_count()) / peers) - (mask > 0) for mask in masks]
     owners = (blocks // per_device).reshape(1, 1, ENTRIES)
     ids = jnp.arange(peers, dtype=jnp.int32)[None, :, None]
     away = (owners ^ ids) & ~jnp.array(masks, jnp.int32)[:, None, None]
@@ -413,36 +423,48 @@
     peers = lax.axis_size("ctx")
     per_device = cache_k.shape[0] // VBLOCK
     ahead = [(i, i + 1) for i in range(peers - 1)]
-    bits = [1] + [1 << at for at in range(peers.bit_length() - 2, 0, -1)]
+    near = 2
+    far = [1 << at for at in range(peers.bit_length() - 2, 1, -1)]
+    bits = [1] + far + [near]
+    masks_a = [sum(bits[:at]) for at in range(len(bits))]
+    masks_b = [1 + near + sum(far[:at]) for at in range(len(far))]
+
+    def merge(known, bit, mine, other, **how):
+        size = room((1 << (known | bit).bit_count()) / peers)
+        if known + bit == peers - 1:
+            size = ENTRIES
+        return merged(blocks, per_device, known, bit, mine, other, size, **how)
 
     kept, sent = pack(blocks, cache_k, cache_v, room(1 / peers))
-    mine = merged(blocks, per_device, 0, 1, [kept], [swapped(sent, 1)], room(2 / peers))
+    mine_a, mine_b = merge(0, 1, kept, swapped(sent, 1), parts=STAGES)
     before = permuted(jnp.concatenate([span_k, span_v], axis=1), ahead)
-    short = jnp.logical_not(fits(blocks, per_device, peers, bits)).astype(jnp.int32)
-    other = [None] * STAGES
-    known = 1
-    for bit in bits[1:]:
-        other = [swapped(m, bit) for m in mine]
-        if bit == bits[1]:
-            other[0], before, short = lax.optimization_barrier((other[0], before, short))
-        if bit == bits[-1]:
-            break
-        size = room((1 << (known | bit).bit_count()) / peers)
-        level = (blocks, per_device, known, bit)
-        if bit == bits[1]:
-            mine = merged(*level, mine, other, size)
-        else:
-            pairs = zip(mine, other)
-            mine = [merged(*level, [m], [o], size)[0] for m, o in pairs]
-        known |= bit
-    twins = [swapped(m, 1) for m in mine]
+    short = jnp.logical_not(fits(blocks, per_device, peers, masks_a + masks_b)).astype(jnp.int32)
+
+    steps_a = list(zip(masks_a[1:], far))
+    steps_b = list(zip([1] + masks_b, [near] + far))
+    other_a = swapped(mine_a, far[0])
+    other_b = swapped(mine_b, near)
+    other_a, before, short = lax.optimization_barrier((other_a, before, short))
+    for at, (known, bit) in enumerate(steps_a):
+        mine_a = merge(known, bit, mine_a, other_a)
+        known_b, bit_b = steps_b[at]
+        mine_b = merge(known_b, bit_b, mine_b, other_b, halved=near if at == 0 else 0)
+        if at < len(far) - 1:
+            mine_a, mine_b = lax.optimization_barrier((mine_a, mine_b))
+        other_a = swapped(mine_a, (far + [near])[at + 1])
+        other_b = swapped(mine_b, far[at])
+        if at < len(far) - 1:
+            other_a, other_b = lax.optimization_barrier((other_a, other_b))
+    mine_b = merge(*steps_b[-1], mine_b, other_b)
+    other_b = swapped(mine_b, near)
+    twin_a, twin_b = swapped(mine_a, 1), swapped(mine_b, 1)
 
     bands = (before, span_k, span_v)
-    shared = (known, bits[-1], per_device, blocks, queries)
-    lists = (mine[0], other[0], twins[0], swapped(other[0], 1))
+    shared = (peers - 1 - near, near, per_device, blocks, queries)
+    lists = (mine_a, other_a, twin_a, swapped(other_a, 1))
     state = attend_stage(*shared, lists, offsets=offsets, bands=bands)
-    state, late = lax.optimization_barrier((state, other[1]))
-    lists = (mine[1], late, twins[1], swapped(late, 1))
+    state, late = lax.optimization_barrier((state, other_b))
+    lists = (mine_b, late, twin_b, swapped(late, 1))
     fast = attend_stage(*shared, lists, state=state)
 
     def again(carry):

time: 67.7 us -> 61 us (0.901)
  waiting for transfers between devices: 31.7 us -> 18.6 us
  starting transfers between devices: 12.5 us -> 18.1 us
  Pallas kernels: 21.2 us -> 22 us
    ppermute x12 -> x13, waiting for transfers between devices: 31.7 us -> 18.6 us  [permuted(): return lax.ppermute(array, 'ctx', pairs)]
    ppermute x12 -> x13, starting transfers between devices: 12.5 us -> 18.1 us  [permuted(): return lax.ppermute(array, 'ctx', pairs)]
    pallas_call x4 -> x6, Pallas kernels: 4.9 us -> 6.83 us  [merged(): pl.pallas_call(functools.partial(merge_kernel, per_device, known, bit, ha...]
    pallas_call x2, Pallas kernels: 14 us -> 12.8 us  [attend_stage(): pl.pallas_call(functools.partial(stage_kernel, per_device, known, bit, ba...]
  transfers between devices with their start and end apart: 12 -> 13, of which waited for: 6 -> 6; matrix products, arithmetic and copies ran while one was open for 2% -> 2% of each run, Pallas kernels for 12% -> 17%
where the time goes in v6:
time: 61 us; the launch traced here: 60.8 us
  Pallas kernels  22 us (36%)
  waiting for transfers between devices  18.6 us (30%)
  starting transfers between devices  18.1 us (30%)
  between operations  1 us (2%)
  other arithmetic  0.98 us (2%)
    ppermute x13, waiting for transfers between devices, permuted(): return lax.ppermute(array, 'ctx', pairs)  18.6 us
    ppermute x13, starting transfers between devices, permuted(): return lax.ppermute(array, 'ctx', pairs)  18.1 us
    pallas_call x2, Pallas kernels, attend_stage(): pl.pallas_call(functools.partial(stage_kernel, per_device, known, bit, ba...  12.8 us
    pallas_call x6, Pallas kernels, merged(): pl.pallas_call(functools.partial(merge_kernel, per_device, known, bit, ha...  6.83 us
    pallas_call x1, Pallas kernels, pack(): pl.pallas_call(functools.partial(pack_kernel, cache_k.shape[0] // VBLOCK,...  2.35 us
  transfers between devices with their start and end apart: 13, of which 6 were waited for; matrix products, arithmetic and copies ran while one was open for 2% of the time, Pallas kernels for 17%

profile of v6, /device:TPU:0, one launch (start us, length us, event | category | flops | bytes accessed | tf_op | source)
XLA Modules:
  0.0 60.8 jit_solution(7996455163822099462)
XLA Ops:
  0.0 2.4 %pack.1 = (bf16[12,64,128]{2,1,0:T(8,128)(2,1)S(1)}, bf16[12,64,128]{2,1,0:T(8,128)(2,1)S(1)}) custom-call(s32[4,16]{1,0:T(4,128)} %refs_0_.3, bf16[2048,512]{1,0:T(8,128)(2,1)} %cache_k.1, bf16[2048,512]{1,0:T(8,128)(2,1)} %cache_v.1), custom_call_target="tpu_custom_call" | custom-call | tf_op jit(solution)/shard_map/pack/pallas_call | solution.py:224
  2.4 0.0 copy-start.2
  2.4 0.0 copy-start.7
  2.4 0.2 collective-permute-start.8
  2.6 0.0 copy-done.3
  2.6 0.0 copy-done.4
  2.7 2.3 %collective-permute-start.10 = (bf16[128,1024]{1,0:T(8,128)(2,1)S(1)}, bf16[128,1024]{1,0:T(8,128)(2,1)S(1)}, u32[]{:S(2)}, u32[]{:S(2)}) collective-permute-start(bf16[128,1024]{1,0:T(8,128)(2,1)S(1)} %pad_maximum_fusion), channel_id=1, source_target_pairs={{0,1},{1,2},{2,3},{3,4},{4,5},{5,6},{6,7},{7,8},{8,9},{9,10},{10,1... | collective-permute-start | bytes 786440 | tf_op jit(solution)/shard_map/ppermute | solution.py:394
  4.9 0.0 copy-done.6
  5.0 0.1 xor.20
  5.1 0.0 collective-permute-done.8.other
  5.1 1.4 %merge.6 = (bf16[18,32,128]{2,1,0:T(8,128)(2,1)S(1)}, bf16[18,32,128]{2,1,0:T(8,128)(2,1)S(1)}) custom-call(s32[4,16]{1,0:T(4,128)S(1)} %copy-done.6, bf16[12,64,128]{2,1,0:T(8,128)(2,1)S(1)} %get-tuple-element.73.mine, bf16[12,64,128]{2,1,0:T(8,128)(2,1)S(1)} %collective-permute-done.8.other), custom_call_target="tpu_custom_call" | custom-call | tf_op jit(solution)/shard_map/merge/pallas_call | solution.py:264
  6.4 4.0 %collective-permute-start.9 = (bf16[18,32,128]{2,1,0:T(8,128)(2,1)S(1)}, bf16[18,32,128]{2,1,0:T(8,128)(2,1)S(1)}, u32[]{:S(2)}, u32[]{:S(2)}) collective-permute-start(bf16[18,32,128]{2,1,0:T(8,128)(2,1)S(1)} %get-tuple-element.75.mine), channel_id=1, source_target_pairs={{0,8},{1,9},{2,10},{3,11},{4,12},{5,13},{6,14},{7,15},{8,0},{9,1},... | collective-permute-start | bytes 442376 | tf_op jit(solution)/shard_map/ppermute | solution.py:394
  10.4 1.3 %collective-permute-start.11 = (bf16[18,32,128]{2,1,0:T(8,128)(2,1)S(1)}, bf16[18,32,128]{2,1,0:T(8,128)(2,1)S(1)}, u32[]{:S(2)}, u32[]{:S(2)}) collective-permute-start(bf16[18,32,128]{2,1,0:T(8,128)(2,1)S(1)} %get-tuple-element.78.mine), channel_id=1, source_target_pairs={{0,2},{1,3},{2,0},{3,1},{4,6},{5,7},{6,4},{7,5},{8,10},{9,11},{10,... | collective-permute-start | bytes 442376 | tf_op jit(solution)/shard_map/ppermute | solution.py:394
  11.7 0.0 copy-done.8
  11.7 0.2 convert_reduce_fusion
  11.9 0.0 copy-done.9
  11.9 0.7 %compare_reduce_fusion = pred[]{:T(512)} fusion(s32[6,16]{1,0:T(8,128)S(1)} %convert_reduce_fusion, s32[6]{0:T(128)S(1)} %copy-done.9), kind=kLoop, calls=%fused_computation.4 | loop fusion | flops 191 | bytes 409 | tf_op jit(solution)/shard_map/reduce_and | solution.py:407
  13.3 0.0 collective-permute-done.10.refs_7_
  13.3 4.2 %collective-permute-done.9.other = bf16[18,32,128]{2,1,0:T(8,128)(2,1)S(1)} collective-permute-done((bf16[18,32,128]{2,1,0:T(8,128)(2,1)S(1)}, bf16[18,32,128]{2,1,0:T(8,128)(2,1)S(1)}, u32[]{:S(2)}, u32[]{:S(2)}) %collective-permute-start.9) | collective-permute-done | bytes 147488 | tf_op jit(solution)/shard_map/ppermute | solution.py:394
  17.5 1.1 %merge.7.mine = bf16[28,32,128]{2,1,0:T(8,128)(2,1)S(1)} custom-call(s32[4,16]{1,0:T(4,128)S(1)} %copy-done.6, bf16[18,32,128]{2,1,0:T(8,128)(2,1)S(1)} %get-tuple-element.75.mine, bf16[18,32,128]{2,1,0:T(8,128)(2,1)S(1)} %collective-permute-done.9.other), custom_call_target="tpu_custom_call" | custom-call | tf_op jit(solution)/shard_map/merge/pallas_call | solution.py:264
  18.7 0.0 collective-permute-done.11.other
  18.7 1.1 %merge.8.mine = bf16[28,16,128]{2,1,0:T(8,128)(2,1)S(1)} custom-call(s32[4,16]{1,0:T(4,128)S(1)} %copy-done.6, bf16[18,32,128]{2,1,0:T(8,128)(2,1)S(1)} %get-tuple-element.78.mine, bf16[18,32,128]{2,1,0:T(8,128)(2,1)S(1)} %collective-permute-done.11.other), custom_call_target="tpu_custom_call" | custom-call | tf_op jit(solution)/shard_map/merge/pallas_call | solution.py:264
  19.8 1.8 %collective-permute-start.12 = (bf16[28,32,128]{2,1,0:T(8,128)(2,1)S(1)}, bf16[28,32,128]{2,1,0:T(8,128)(2,1)S(1)}, u32[]{:S(2)}, u32[]{:S(2)}) collective-permute-start(bf16[28,32,128]{2,1,0:T(8,128)(2,1)S(1)} %merge.7.mine), channel_id=1, source_target_pairs={{0,4},{1,5},{2,6},{3,7},{4,0},{5,1},{6,2},{7,3},{8,12},{9,13},{10,... | collective-permute-start | bytes 688136 | tf_op jit(solution)/shard_map/ppermute | solution.py:394
  21.6 3.4 %collective-permute-start.13 = (bf16[28,16,128]{2,1,0:T(8,128)(2,1)S(1)}, bf16[28,16,128]{2,1,0:T(8,128)(2,1)S(1)}, u32[]{:S(2)}, u32[]{:S(2)}) collective-permute-start(bf16[28,16,128]{2,1,0:T(8,128)(2,1)S(1)} %merge.8.mine), channel_id=1, source_target_pairs={{0,8},{1,9},{2,10},{3,11},{4,12},{5,13},{6,14},{7,15},{8,0},{9,1},... | collective-permute-start | bytes 344072 | tf_op jit(solution)/shard_map/ppermute | solution.py:394
  25.0 4.3 %collective-permute-done.13.other = bf16[28,16,128]{2,1,0:T(8,128)(2,1)S(1)} collective-permute-done((bf16[28,16,128]{2,1,0:T(8,128)(2,1)S(1)}, bf16[28,16,128]{2,1,0:T(8,128)(2,1)S(1)}, u32[]{:S(2)}, u32[]{:S(2)}) %collective-permute-start.13) | collective-permute-done | bytes 114720 | tf_op jit(solution)/shard_map/ppermute | solution.py:394
  29.3 1.2 %collective-permute-done.12.other = bf16[28,32,128]{2,1,0:T(8,128)(2,1)S(1)} collective-permute-done((bf16[28,32,128]{2,1,0:T(8,128)(2,1)S(1)}, bf16[28,32,128]{2,1,0:T(8,128)(2,1)S(1)}, u32[]{:S(2)}, u32[]{:S(2)}) %collective-permute-start.12) | collective-permute-done | bytes 229408 | tf_op jit(solution)/shard_map/ppermute | solution.py:394
  30.4 1.1 %merge.11.refs_3_ = bf16[46,32,128]{2,1,0:T(8,128)(2,1)S(1)} custom-call(s32[4,16]{1,0:T(4,128)S(1)} %copy-done.6, bf16[28,32,128]{2,1,0:T(8,128)(2,1)S(1)} %merge.7.mine, bf16[28,32,128]{2,1,0:T(8,128)(2,1)S(1)} %collective-permute-done.12.other), custom_call_target="tpu_custom_call" | custom-call | tf_op jit(solution)/shard_map/merge/pallas_call | solution.py:264
  31.6 2.0 %collective-permute-start.15 = (bf16[46,32,128]{2,1,0:T(8,128)(2,1)S(1)}, bf16[46,32,128]{2,1,0:T(8,128)(2,1)S(1)}, u32[]{:S(2)}, u32[]{:S(2)}) collective-permute-start(bf16[46,32,128]{2,1,0:T(8,128)(2,1)S(1)} %merge.11.refs_3_), channel_id=1, source_target_pairs={{0,2},{1,3},{2,0},{3,1},{4,6},{5,7},{6,4},{7,5},{8,10},{9,11},{10,... | collective-permute-start | bytes 1130504 | tf_op jit(solution)/shard_map/ppermute | solution.py:394
  33.6 1.0 %merge.9.mine = bf16[46,16,128]{2,1,0:T(8,128)(2,1)S(1)} custom-call(s32[4,16]{1,0:T(4,128)S(1)} %copy-done.6, bf16[28,16,128]{2,1,0:T(8,128)(2,1)S(1)} %merge.8.mine, bf16[28,16,128]{2,1,0:T(8,128)(2,1)S(1)} %collective-permute-done.13.other), custom_call_target="tpu_custom_call" | custom-call | tf_op jit(solution)/shard_map/merge/pallas_call | solution.py:264
  34.6 1.4 %collective-permute-start.14 = (bf16[46,16,128]{2,1,0:T(8,128)(2,1)S(1)}, bf16[46,16,128]{2,1,0:T(8,128)(2,1)S(1)}, u32[]{:S(2)}, u32[]{:S(2)}) collective-permute-start(bf16[46,16,128]{2,1,0:T(8,128)(2,1)S(1)} %merge.9.mine), channel_id=1, source_target_pairs={{0,4},{1,5},{2,6},{3,7},{4,0},{5,1},{6,2},{7,3},{8,12},{9,13},{10,... | collective-permute-start | bytes 565256 | tf_op jit(solution)/shard_map/ppermute | solution.py:394
  36.0 0.0 collective-permute-start.16
  36.0 6.1 %collective-permute-done.15.refs_4_ = bf16[46,32,128]{2,1,0:T(8,128)(2,1)S(1)} collective-permute-done((bf16[46,32,128]{2,1,0:T(8,128)(2,1)S(1)}, bf16[46,32,128]{2,1,0:T(8,128)(2,1)S(1)}, u32[]{:S(2)}, u32[]{:S(2)}) %collective-permute-start.15) | collective-permute-done | bytes 376864 | tf_op jit(solution)/shard_map/ppermute | solution.py:394
  42.1 0.0 collective-permute-start.17
  42.1 0.0 collective-permute-done.14.other
  42.1 1.0 %merge.10.refs_2_ = bf16[64,16,128]{2,1,0:T(8,128)(2,1)S(1)} custom-call(s32[4,16]{1,0:T(4,128)S(1)} %copy-done.6, bf16[46,16,128]{2,1,0:T(8,128)(2,1)S(1)} %merge.9.mine, bf16[46,16,128]{2,1,0:T(8,128)(2,1)S(1)} %collective-permute-done.14.other), custom_call_target="tpu_custom_call" | custom-call | tf_op jit(solution)/shard_map/merge/pallas_call | solution.py:264
  43.1 1.5 %collective-permute-start.18 = (bf16[64,16,128]{2,1,0:T(8,128)(2,1)S(1)}, bf16[64,16,128]{2,1,0:T(8,128)(2,1)S(1)}, u32[]{:S(2)}, u32[]{:S(2)}) collective-permute-start(bf16[64,16,128]{2,1,0:T(8,128)(2,1)S(1)} %merge.10.refs_2_), channel_id=1, source_target_pairs={{0,2},{1,3},{2,0},{3,1},{4,6},{5,7},{6,4},{7,5},{8,10},{9,11},{10,... | collective-permute-start | bytes 786440 | tf_op jit(solution)/shard_map/ppermute | solution.py:394
  44.6 0.2 collective-permute-start.19
  44.9 0.0 collective-permute-done.16.refs_5_
  44.9 0.0 collective-permute-done.17.refs_6_
  44.9 0.0 copy-done.2
  44.9 0.0 copy-done.7
  44.9 5.7 %attend_first.1 = (f32[4096,128]{1,0:T(8,128)S(1)}, f32[4096,128]{1,0:T(8,128)S(1)}) custom-call(s32[4,16]{1,0:T(4,128)S(1)} %copy-done.6, s32[4,64]{1,0:T(4,128)S(1)} %copy-done.7, bf16[128,4096]{1,0:T(8,128)(2,1)S(1)} %copy-done.2, bf16[46,32,128]{2,1,0:T(8,128)(2,1)S(1)} %merge.11.refs_3_, bf16[46,32,128]{2,1,0:T(8,128)(2,1)S(1)} %collective-permute-done.15.refs_4_, ...), custom_call_target="tpu_custom_call" | custom-call | flops 1048576 | bytes 1048576 | tf_op jit(solution)/shard_map/attend_first/pallas_call | solution.py:381
  50.6 1.3 %collective-permute-done.18.refs_3_ = bf16[64,16,128]{2,1,0:T(8,128)(2,1)S(1)} collective-permute-done((bf16[64,16,128]{2,1,0:T(8,128)(2,1)S(1)}, bf16[64,16,128]{2,1,0:T(8,128)(2,1)S(1)}, u32[]{:S(2)}, u32[]{:S(2)}) %collective-permute-start.18) | collective-permute-done | bytes 262176 | tf_op jit(solution)/shard_map/ppermute | solution.py:394
  51.9 0.0 collective-permute-start.20
  51.9 0.0 collective-permute-done.19.refs_4_
  51.9 1.5 %collective-permute-done.20.refs_5_ = bf16[64,16,128]{2,1,0:T(8,128)(2,1)S(1)} collective-permute-done((bf16[64,16,128]{2,1,0:T(8,128)(2,1)S(1)}, bf16[64,16,128]{2,1,0:T(8,128)(2,1)S(1)}, u32[]{:S(2)}, u32[]{:S(2)}) %collective-permute-start.20) | collective-permute-done | bytes 262176 | tf_op jit(solution)/shard_map/ppermute | solution.py:394
  53.4 7.2 %attend_last.1 = bf16[128,4096]{1,0:T(8,128)(2,1)} custom-call(s32[4,16]{1,0:T(4,128)S(1)} %copy-done.6, bf16[128,4096]{1,0:T(8,128)(2,1)S(1)} %copy-done.2, bf16[64,16,128]{2,1,0:T(8,128)(2,1)S(1)} %merge.10.refs_2_, bf16[64,16,128]{2,1,0:T(8,128)(2,1)S(1)} %collective-permute-done.18.refs_3_, bf16[64,16,128]{2,1,0:T(8,128)(2,1)S(1)} %collective-permute-done.19.refs_4_, ...), custom_call_target="tpu_custom_call" | custom-call | flops 1048576 | bytes 1048576 | tf_op jit(solution)/shard_map/attend_last/pallas_call | solution.py:381
  60.6 0.0 copy-done
  (10 shorter events, 0.1 us)
Async XLA Ops:
  0.0 11.7 %copy-start.8 = (s32[6]{0:T(128)S(1)}, s32[6]{0:T(128)}, u32[]{:S(2)}) copy-start(s32[6]{0:T(128)} %constant.30) | copy-start | bytes 76
  0.0 11.9 %copy-start.9 = (s32[6]{0:T(128)S(1)}, s32[6]{0:T(128)}, u32[]{:S(2)}) copy-start(s32[6]{0:T(128)} %constant.29.clone) | copy-start | bytes 76
  0.0 4.9 %copy-start.6 = (s32[4,16]{1,0:T(4,128)S(1)}, s32[4,16]{1,0:T(4,128)}, u32[]{:S(2)}) copy-start(s32[4,16]{1,0:T(4,128)} %refs_0_.3) | copy-start | bytes 772
  0.0 2.6 %copy-start.3 = (bf16[128,512]{1,0:T(8,128)(2,1)S(1)}, bf16[128,512]{1,0:T(8,128)(2,1)}, u32[]{:S(2)}) copy-start(bf16[128,512]{1,0:T(8,128)(2,1)} %refs_9_.1) | copy-start | bytes 393220
  0.0 2.6 %copy-start.4 = (bf16[128,512]{1,0:T(8,128)(2,1)S(1)}, bf16[128,512]{1,0:T(8,128)(2,1)}, u32[]{:S(2)}) copy-start(bf16[128,512]{1,0:T(8,128)(2,1)} %refs_8_.1) | copy-start | bytes 393220
  2.4 42.5 %copy-start.2 = (bf16[128,4096]{1,0:T(8,128)(2,1)S(1)}, bf16[128,4096]{1,0:T(8,128)(2,1)}, u32[]{:S(2)}) copy-start(bf16[128,4096]{1,0:T(8,128)(2,1)} %refs_1_.3) | copy-start | bytes 3145732
  2.4 42.5 %copy-start.7 = (s32[4,64]{1,0:T(4,128)S(1)}, s32[4,64]{1,0:T(4,128)}, u32[]{:S(2)}) copy-start(s32[4,64]{1,0:T(4,128)} %refs_1_.2) | copy-start | bytes 3076
  2.4 2.7 %collective-permute-start.8 = (bf16[12,64,128]{2,1,0:T(8,128)(2,1)S(1)}, bf16[12,64,128]{2,1,0:T(8,128)(2,1)S(1)}, u32[]{:S(2)}, u32[]{:S(2)}) collective-permute-start(bf16[12,64,128]{2,1,0:T(8,128)(2,1)S(1)} %get-tuple-element.74), channel_id=1, source_target_pairs={{0,1},{1,0},{2,3},{3,2},{4,5},{5,4},{6,7},{7,6},{8,9},{9,8},{10,11... | collective-permute-start | bytes 589832 | tf_op jit(solution)/shard_map/ppermute | solution.py:394
  2.7 10.6 %collective-permute-start.10 = (bf16[128,1024]{1,0:T(8,128)(2,1)S(1)}, bf16[128,1024]{1,0:T(8,128)(2,1)S(1)}, u32[]{:S(2)}, u32[]{:S(2)}) collective-permute-start(bf16[128,1024]{1,0:T(8,128)(2,1)S(1)} %pad_maximum_fusion), channel_id=1, source_target_pairs={{0,1},{1,2},{2,3},{3,4},{4,5},{5,6},{6,7},{7,8},{8,9},{9,10},{10,1... | collective-permute-start | bytes 786440 | tf_op jit(solution)/shard_map/ppermute | solution.py:394
  6.4 11.1 %collective-permute-start.9 = (bf16[18,32,128]{2,1,0:T(8,128)(2,1)S(1)}, bf16[18,32,128]{2,1,0:T(8,128)(2,1)S(1)}, u32[]{:S(2)}, u32[]{:S(2)}) collective-permute-start(bf16[18,32,128]{2,1,0:T(8,128)(2,1)S(1)} %get-tuple-element.75.mine), channel_id=1, source_target_pairs={{0,8},{1,9},{2,10},{3,11},{4,12},{5,13},{6,14},{7,15},{8,0},{9,1},... | collective-permute-start | bytes 442376 | tf_op jit(solution)/shard_map/ppermute | solution.py:394
  10.4 8.3 %collective-permute-start.11 = (bf16[18,32,128]{2,1,0:T(8,128)(2,1)S(1)}, bf16[18,32,128]{2,1,0:T(8,128)(2,1)S(1)}, u32[]{:S(2)}, u32[]{:S(2)}) collective-permute-start(bf16[18,32,128]{2,1,0:T(8,128)(2,1)S(1)} %get-tuple-element.78.mine), channel_id=1, source_target_pairs={{0,2},{1,3},{2,0},{3,1},{4,6},{5,7},{6,4},{7,5},{8,10},{9,11},{10,... | collective-permute-start | bytes 442376 | tf_op jit(solution)/shard_map/ppermute | solution.py:394
  19.8 10.6 %collective-permute-start.12 = (bf16[28,32,128]{2,1,0:T(8,128)(2,1)S(1)}, bf16[28,32,128]{2,1,0:T(8,128)(2,1)S(1)}, u32[]{:S(2)}, u32[]{:S(2)}) collective-permute-start(bf16[28,32,128]{2,1,0:T(8,128)(2,1)S(1)} %merge.7.mine), channel_id=1, source_target_pairs={{0,4},{1,5},{2,6},{3,7},{4,0},{5,1},{6,2},{7,3},{8,12},{9,13},{10,... | collective-permute-start | bytes 688136 | tf_op jit(solution)/shard_map/ppermute | solution.py:394
  21.6 7.6 %collective-permute-start.13 = (bf16[28,16,128]{2,1,0:T(8,128)(2,1)S(1)}, bf16[28,16,128]{2,1,0:T(8,128)(2,1)S(1)}, u32[]{:S(2)}, u32[]{:S(2)}) collective-permute-start(bf16[28,16,128]{2,1,0:T(8,128)(2,1)S(1)} %merge.8.mine), channel_id=1, source_target_pairs={{0,8},{1,9},{2,10},{3,11},{4,12},{5,13},{6,14},{7,15},{8,0},{9,1},... | collective-permute-start | bytes 344072 | tf_op jit(solution)/shard_map/ppermute | solution.py:394
  31.6 10.5 %collective-permute-start.15 = (bf16[46,32,128]{2,1,0:T(8,128)(2,1)S(1)}, bf16[46,32,128]{2,1,0:T(8,128)(2,1)S(1)}, u32[]{:S(2)}, u32[]{:S(2)}) collective-permute-start(bf16[46,32,128]{2,1,0:T(8,128)(2,1)S(1)} %merge.11.refs_3_), channel_id=1, source_target_pairs={{0,2},{1,3},{2,0},{3,1},{4,6},{5,7},{6,4},{7,5},{8,10},{9,11},{10,... | collective-permute-start | bytes 1130504 | tf_op jit(solution)/shard_map/ppermute | solution.py:394
  34.6 7.4 %collective-permute-start.14 = (bf16[46,16,128]{2,1,0:T(8,128)(2,1)S(1)}, bf16[46,16,128]{2,1,0:T(8,128)(2,1)S(1)}, u32[]{:S(2)}, u32[]{:S(2)}) collective-permute-start(bf16[46,16,128]{2,1,0:T(8,128)(2,1)S(1)} %merge.9.mine), channel_id=1, source_target_pairs={{0,4},{1,5},{2,6},{3,7},{4,0},{5,1},{6,2},{7,3},{8,12},{9,13},{10,... | collective-permute-start | bytes 565256 | tf_op jit(solution)/shard_map/ppermute | solution.py:394
  36.0 8.9 %collective-permute-start.16 = (bf16[46,32,128]{2,1,0:T(8,128)(2,1)S(1)}, bf16[46,32,128]{2,1,0:T(8,128)(2,1)S(1)}, u32[]{:S(2)}, u32[]{:S(2)}) collective-permute-start(bf16[46,32,128]{2,1,0:T(8,128)(2,1)S(1)} %merge.11.refs_3_), channel_id=1, source_target_pairs={{0,1},{1,0},{2,3},{3,2},{4,5},{5,4},{6,7},{7,6},{8,9},{9,8},{10,11... | collective-permute-start | bytes 1130504 | tf_op jit(solution)/shard_map/ppermute | solution.py:394
  42.1 2.8 %collective-permute-start.17 = (bf16[46,32,128]{2,1,0:T(8,128)(2,1)S(1)}, bf16[46,32,128]{2,1,0:T(8,128)(2,1)S(1)}, u32[]{:S(2)}, u32[]{:S(2)}) collective-permute-start(bf16[46,32,128]{2,1,0:T(8,128)(2,1)S(1)} %collective-permute-done.15.refs_4_), channel_id=1, source_target_pairs={{0,1},{1,0},{2,3},{3,2},{4,5},{5,4},{6,7},{7,6},{8,9},{9,8},{10,11... | collective-permute-start | bytes 1130504 | tf_op jit(solution)/shard_map/ppermute | solution.py:394
  43.1 8.8 %collective-permute-start.18 = (bf16[64,16,128]{2,1,0:T(8,128)(2,1)S(1)}, bf16[64,16,128]{2,1,0:T(8,128)(2,1)S(1)}, u32[]{:S(2)}, u32[]{:S(2)}) collective-permute-start(bf16[64,16,128]{2,1,0:T(8,128)(2,1)S(1)} %merge.10.refs_2_), channel_id=1, source_target_pairs={{0,2},{1,3},{2,0},{3,1},{4,6},{5,7},{6,4},{7,5},{8,10},{9,11},{10,... | collective-permute-start | bytes 786440 | tf_op jit(solution)/shard_map/ppermute | solution.py:394
  44.6 7.3 %collective-permute-start.19 = (bf16[64,16,128]{2,1,0:T(8,128)(2,1)S(1)}, bf16[64,16,128]{2,1,0:T(8,128)(2,1)S(1)}, u32[]{:S(2)}, u32[]{:S(2)}) collective-permute-start(bf16[64,16,128]{2,1,0:T(8,128)(2,1)S(1)} %merge.10.refs_2_), channel_id=1, source_target_pairs={{0,1},{1,0},{2,3},{3,2},{4,5},{5,4},{6,7},{7,6},{8,9},{9,8},{10,11... | collective-permute-start | bytes 786440 | tf_op jit(solution)/shard_map/ppermute | solution.py:394
  51.9 8.7 %copy-start = (bf16[2048,512]{1,0:T(8,128)(2,1)S(1)}, bf16[2048,512]{1,0:T(8,128)(2,1)}, u32[]{:S(2)}) copy-start(bf16[2048,512]{1,0:T(8,128)(2,1)} %cache_k.1) | copy-start | bytes 6291460
  51.9 1.5 %collective-permute-start.20 = (bf16[64,16,128]{2,1,0:T(8,128)(2,1)S(1)}, bf16[64,16,128]{2,1,0:T(8,128)(2,1)S(1)}, u32[]{:S(2)}, u32[]{:S(2)}) collective-permute-start(bf16[64,16,128]{2,1,0:T(8,128)(2,1)S(1)} %collective-permute-done.18.refs_3_), channel_id=1, source_target_pairs={{0,1},{1,0},{2,3},{3,2},{4,5},{5,4},{6,7},{7,6},{8,9},{9,8},{10,11... | collective-permute-start | bytes 786440 | tf_op jit(solution)/shard_map/ppermute | solution.py:394

commit v7 on v6

--- a/solution.py
+++ b/solution.py
@@ -48,8 +48,11 @@
         scores = jnp.concatenate([scores[:, :wide], band], axis=1)
     largest = jnp.max(scores, axis=1, keepdims=True) * FACTOR
     if floor is not None:
-        largest = jnp.maximum(largest, floor)
-    weights = jnp.exp2(scores * FACTOR - largest).astype(jnp.bfloat16)
+        largest = jnp.maximum(jnp.broadcast_to(largest, floor.shape), floor)
+        above = jnp.concatenate([largest] * (scores.shape[1] // HD), axis=1)
+    else:
+        above = largest
+    weights = jnp.exp2(scores * FACTOR - above).astype(jnp.bfloat16)
     mixed = jnp.dot(weights, values_ones, preferred_element_type=jnp.float32)
     return largest, mixed
 
@@ -272,9 +275,8 @@
     return outs if parts > 1 else outs[0]
 
 
-def stage_kernel(per_device, known, bit, banded, last, *refs):
+def stage_kernel(banded, last, *refs):
     refs = list(refs)
-    blocks = refs.pop(0)
     offsets = refs.pop(0) if banded else None
     queries, mine, other, mine_twin, other_twin = refs[:5]
     refs = refs[5:]
@@ -282,34 +284,24 @@
         before, own_k, own_v = refs[:3]
         refs = refs[3:]
     else:
-        marks_in, mixed_in = refs[:2]
-        refs = refs[2:]
+        largest_in, total_in, mixed_in = refs[:3]
+        refs = refs[3:]
     if last:
         out, kbuf, vbuf, held, sems = refs
     else:
-        marks_out, mixed_out, kbuf, vbuf = refs
+        largest_out, total_out, mixed_out, kbuf, vbuf = refs
     me = lax.axis_index("ctx")
     even = lax.rem(me, 2) == 0
     wide = NV * ROWS
 
-    def act(entry, at_mine, at_other, place, theirs):
-        tile = jnp.where(theirs, other[at_other], mine[at_mine])
-        twin = jnp.where(theirs, other_twin[at_other], mine_twin[at_mine])
-        rows = pl.ds(entry % NV * ROWS, ROWS)
-        kbuf[entry // NV, rows] = jnp.where(even, tile, twin)
-        vbuf[entry // NV, rows, :HD] = jnp.where(even, twin, tile)
-
-    if not last:
-        walk(blocks, per_device, known, bit, (mine.shape[0], other.shape[0]), act)
-    else:
-        half = wide // 2
-        for head in range(KVH):
-            span = slice(head * NV, (head + 1) * NV)
-            for at, (own, twin) in enumerate(((mine, mine_twin), (other, other_twin))):
-                tile, pair = own[span].reshape(half, HD), twin[span].reshape(half, HD)
-                rows = slice(at * half, (at + 1) * half)
-                kbuf[head, rows] = jnp.where(even, tile, pair)
-                vbuf[head, rows, :HD] = jnp.where(even, pair, tile)
+    half = wide // 2
+    for head in range(KVH):
+        span = slice(head * NV, (head + 1) * NV)
+        for at, (own, twin) in enumerate(((mine, mine_twin), (other, other_twin))):
+            tile, pair = own[span].reshape(half, HD), twin[span].reshape(half, HD)
+            rows = slice(at * half, (at + 1) * half)
+            kbuf[head, rows] = jnp.where(even, tile, pair)
+            vbuf[head, rows, :HD] = jnp.where(even, pair, tile)
     copies = []
     for head in range(KVH):
         columns = slice(head * HD, (head + 1) * HD)
@@ -332,13 +324,13 @@
             )
             start = (head * GROUP + at) * QDEV
             tile = slice(start, start + TILE * QDEV)
-            floor = None if banded else marks_in[tile, :1]
+            floor = None if banded else largest_in[tile]
             largest, mixed = attend_rows(rows, kbuf[head], vbuf[head], mask, floor)
             mixed, total = mixed[:, :HD], mixed[:, HD:]
             if not banded:
                 then = jnp.exp2(floor - largest)
                 mixed = mixed + mixed_in[tile] * then
-                total = total + marks_in[tile, HD - 1 :] * then
+                total = total + total_in[tile] * then
             if last:
                 result = (mixed / total).astype(jnp.bfloat16)
                 for i in range(TILE):
@@ -346,8 +338,8 @@
                         i * QDEV : (i + 1) * QDEV
                     ]
             else:
-                lanes = lax.broadcasted_iota(jnp.int32, mixed.shape, 1)
-                marks_out[tile] = jnp.where(lanes < HD // 2, largest, total)
+                largest_out[tile] = jnp.broadcast_to(largest, mixed.shape)
+                total_out[tile] = total
                 mixed_out[tile] = mixed
         if last:
             span = pl.ds(head * GROUP * HD, GROUP * HD)
@@ -357,12 +349,12 @@
         copy.wait()
 
 
-def attend_stage(known, bit, per_device, blocks, queries, lists, offsets=None, bands=None, state=None):
+def attend_stage(queries, lists, offsets=None, bands=None, state=None):
     banded, last = bands is not None, state is not None
     tall = KVH * GROUP * QDEV
-    args = [blocks] + [offsets] * banded + [queries, *lists]
+    args = [offsets] * banded + [queries, *lists]
     args += list(bands if banded else state)
-    specs = [SMEM] * (1 + banded) + [WHOLE] * (len(args) - 1 - banded)
+    specs = [SMEM] * banded + [WHOLE] * (len(args) - banded)
     keys = NV * ROWS + (SMAX + QDEV) * banded
     scratch = [
         pltpu.VMEM((KVH, keys, HD), jnp.bfloat16),
@@ -376,10 +368,10 @@
             pltpu.SemaphoreType.DMA((KVH,)),
         ]
     else:
-        out_shape = (jax.ShapeDtypeStruct((tall, HD), jnp.float32),) * 2
-        out_specs = (WHOLE,) * 2
+        out_shape = (jax.ShapeDtypeStruct((tall, HD), jnp.float32),) * 3
+        out_specs = (WHOLE,) * 3
     return pl.pallas_call(
-        functools.partial(stage_kernel, per_device, known, bit, banded, last),
+        functools.partial(stage_kernel, banded, last),
         out_shape=out_shape,
         in_specs=specs,
         out_specs=out_specs,
@@ -425,47 +417,42 @@
     ahead = [(i, i + 1) for i in range(peers - 1)]
     near = 2
     far = [1 << at for at in range(peers.bit_length() - 2, 1, -1)]
-    bits = [1] + far + [near]
-    masks_a = [sum(bits[:at]) for at in range(len(bits))]
-    masks_b = [1 + near + sum(far[:at]) for at in range(len(far))]
-
-    def merge(known, bit, mine, other, **how):
-        size = room((1 << (known | bit).bit_count()) / peers)
-        if known + bit == peers - 1:
-            size = ENTRIES
+    bits = [1, near] + far
+    masks = [sum(bits[:at]) for at in range(len(bits))]
+
+    def merge(step, mine, other, **how):
+        known, bit = masks[step], bits[step]
+        size = ENTRIES if step == len(bits) - 1 else room((2 << known.bit_count()) / peers)
         return merged(blocks, per_device, known, bit, mine, other, size, **how)
 
     kept, sent = pack(blocks, cache_k, cache_v, room(1 / peers))
-    mine_a, mine_b = merge(0, 1, kept, swapped(sent, 1), parts=STAGES)
-    before = permuted(jnp.concatenate([span_k, span_v], axis=1), ahead)
-    short = jnp.logical_not(fits(blocks, per_device, peers, masks_a + masks_b)).astype(jnp.int32)
-
-    steps_a = list(zip(masks_a[1:], far))
-    steps_b = list(zip([1] + masks_b, [near] + far))
-    other_a = swapped(mine_a, far[0])
-    other_b = swapped(mine_b, near)
-    other_a, before, short = lax.optimization_barrier((other_a, before, short))
-    for at, (known, bit) in enumerate(steps_a):
-        mine_a = merge(known, bit, mine_a, other_a)
-        known_b, bit_b = steps_b[at]
-        mine_b = merge(known_b, bit_b, mine_b, other_b, halved=near if at == 0 else 0)
-        if at < len(far) - 1:
-            mine_a, mine_b = lax.optimization_barrier((mine_a, mine_b))
-        other_a = swapped(mine_a, (far + [near])[at + 1])
-        other_b = swapped(mine_b, far[at])
-        if at < len(far) - 1:
-            other_a, other_b = lax.optimization_barrier((other_a, other_b))
-    mine_b = merge(*steps_b[-1], mine_b, other_b)
-    other_b = swapped(mine_b, near)
-    twin_a, twin_b = swapped(mine_a, 1), swapped(mine_b, 1)
+    mine = list(merge(0, kept, swapped(sent, 1), parts=STAGES))
+    spans, mine[1] = lax.optimization_barrier((jnp.concatenate([span_k, span_v], axis=1), mine[1]))
+    before = permuted(spans, ahead)
+    short = jnp.logical_not(fits(blocks, per_device, peers, masks)).astype(jnp.int32)
+
+    other = [swapped(m, near) for m in mine]
+    other[0], short = lax.optimization_barrier((other[0], short))
+    for step in range(1, len(bits)):
+        nearby = {"halved": near} if step == 1 else {}
+        if step > 1:
+            other[0], mine[1] = lax.optimization_barrier((other[0], mine[1]))
+        mine[0] = merge(step, mine[0], other[0], **nearby)
+        other[1], mine[0] = lax.optimization_barrier((other[1], mine[0]))
+        if step == 1:
+            other[1], before = lax.optimization_barrier((other[1], before))
+        mine[1] = merge(step, mine[1], other[1], **nearby)
+        after = (bits[2:] + [near])[step - 1]
+        other = [swapped(m, after) for m in mine]
+    other[0], mine[1] = lax.optimization_barrier((other[0], mine[1]))
+    twins = [swapped(m, 1) for m in mine]
 
     bands = (before, span_k, span_v)
-    shared = (peers - 1 - near, near, per_device, blocks, queries)
-    lists = (mine_a, other_a, twin_a, swapped(other_a, 1))
-    state = attend_stage(*shared, lists, offsets=offsets, bands=bands)
-    state, late = lax.optimization_barrier((state, other_b))
-    lists = (mine_b, late, twin_b, swapped(late, 1))
-    fast = attend_stage(*shared, lists, state=state)
+    lists = (mine[0], other[0], twins[0], swapped(other[0], 1))
+    state = attend_stage(queries, lists, offsets=offsets, bands=bands)
+    state, late = lax.optimization_barrier((state, other[1]))
+    lists = (mine[1], late, twins[1], swapped(late, 1))
+    fast = attend_stage(queries, lists, state=state)
 
     def again(carry):
         return 0, general(queries, bands, cache_k, cache_v, blocks, offsets, bits)

time: 61 us -> 67.9 us (1.11)
  waiting for transfers between devices: 18.6 us -> 30.5 us
  starting transfers between devices: 18.1 us -> 15.6 us
  Pallas kernels: 22 us -> 19.5 us
    ppermute x13 -> x14, waiting for transfers between devices: 18.6 us -> 30.5 us  [permuted(): return lax.ppermute(array, 'ctx', pairs)]
    pallas_call x2, Pallas kernels: 12.8 us -> 9.45 us  [attend_stage(): pl.pallas_call(functools.partial(stage_kernel, banded, last), out_shape=o...]
    ppermute x13 -> x14, starting transfers between devices: 18.1 us -> 15.6 us  [permuted(): return lax.ppermute(array, 'ctx', pairs)]
    pallas_call x6 -> x7, Pallas kernels: 6.83 us -> 7.74 us  [merged(): pl.pallas_call(functools.partial(merge_kernel, per_device, known, bit, ha...]
  transfers between devices with their start and end apart: 13 -> 14, of which waited for: 6 -> 10; matrix products, arithmetic and copies ran while one was open for 2% -> 2% of each run, Pallas kernels for 17% -> 17%
where the time goes in v7:
time: 67.9 us; the launch traced here: 67.7 us
  waiting for transfers between devices  30.5 us (45%)
  Pallas kernels  19.5 us (29%)
  starting transfers between devices  15.6 us (23%)
  between operations  0.99 us (1%)
  other arithmetic  0.95 us (1%)
    ppermute x14, waiting for transfers between devices, permuted(): return lax.ppermute(array, 'ctx', pairs)  30.5 us
    ppermute x14, starting transfers between devices, permuted(): return lax.ppermute(array, 'ctx', pairs)  15.6 us
    pallas_call x2, Pallas kernels, attend_stage(): pl.pallas_call(functools.partial(stage_kernel, banded, last), out_shape=o...  9.45 us
    pallas_call x7, Pallas kernels, merged(): pl.pallas_call(functools.partial(merge_kernel, per_device, known, bit, ha...  7.74 us
    pallas_call x1, Pallas kernels, pack(): pl.pallas_call(functools.partial(pack_kernel, cache_k.shape[0] // VBLOCK,...  2.33 us
  transfers between devices with their start and end apart: 14, of which 10 were waited for; matrix products, arithmetic and copies ran while one was open for 2% of the time, Pallas kernels for 17%

profile of v7, /device:TPU:0, one launch (start us, length us, event | category | flops | bytes accessed | tf_op | source)
XLA Modules:
  0.0 67.7 jit_solution(5887026578476905239)
XLA Ops:
  0.0 2.3 %pack.1 = (bf16[12,64,128]{2,1,0:T(8,128)(2,1)S(1)}, bf16[12,64,128]{2,1,0:T(8,128)(2,1)S(1)}) custom-call(s32[4,16]{1,0:T(4,128)} %blocks.15, bf16[2048,512]{1,0:T(8,128)(2,1)} %cache_k.1, bf16[2048,512]{1,0:T(8,128)(2,1)} %cache_v.1), custom_call_target="tpu_custom_call" | custom-call | tf_op jit(solution)/shard_map/pack/pallas_call | solution.py:227
  2.4 0.0 copy-start.2
  2.4 0.0 copy-start.7
  2.4 0.6 collective-permute-start.8
  2.9 0.0 copy-done.6
  3.0 0.1 xor.20
  3.0 0.0 copy-done.3
  3.0 0.0 copy-done.4
  3.1 0.9 %collective-permute-done.8.other = bf16[12,64,128]{2,1,0:T(8,128)(2,1)S(1)} collective-permute-done((bf16[12,64,128]{2,1,0:T(8,128)(2,1)S(1)}, bf16[12,64,128]{2,1,0:T(8,128)(2,1)S(1)}, u32[]{:S(2)}, u32[]{:S(2)}) %collective-permute-start.8) | collective-permute-done | bytes 196640 | tf_op jit(solution)/shard_map/ppermute | solution.py:386
  4.0 1.4 %merge.7 = (bf16[18,32,128]{2,1,0:T(8,128)(2,1)S(1)}, bf16[18,32,128]{2,1,0:T(8,128)(2,1)S(1)}) custom-call(s32[4,16]{1,0:T(4,128)S(1)} %copy-done.6, bf16[12,64,128]{2,1,0:T(8,128)(2,1)S(1)} %get-tuple-element.86.mine, bf16[12,64,128]{2,1,0:T(8,128)(2,1)S(1)} %collective-permute-done.8.other), custom_call_target="tpu_custom_call" | custom-call | tf_op jit(solution)/shard_map/merge/pallas_call | solution.py:267
  5.4 2.3 %collective-permute-start.12 = (bf16[128,1024]{1,0:T(8,128)(2,1)S(1)}, bf16[128,1024]{1,0:T(8,128)(2,1)S(1)}, u32[]{:S(2)}, u32[]{:S(2)}) collective-permute-start(bf16[128,1024]{1,0:T(8,128)(2,1)S(1)} %pad_maximum_fusion), channel_id=1, source_target_pairs={{0,1},{1,2},{2,3},{3,4},{4,5},{5,6},{6,7},{7,8},{8,9},{9,10},{10,1... | collective-permute-start | bytes 786440 | tf_op jit(solution)/shard_map/ppermute | solution.py:386
  7.7 2.4 %collective-permute-start.10 = (bf16[18,32,128]{2,1,0:T(8,128)(2,1)S(1)}, bf16[18,32,128]{2,1,0:T(8,128)(2,1)S(1)}, u32[]{:S(2)}, u32[]{:S(2)}) collective-permute-start(bf16[18,32,128]{2,1,0:T(8,128)(2,1)S(1)} %get-tuple-element.91.mine), channel_id=1, source_target_pairs={{0,2},{1,3},{2,0},{3,1},{4,6},{5,7},{6,4},{7,5},{8,10},{9,11},{10,... | collective-permute-start | bytes 442376 | tf_op jit(solution)/shard_map/ppermute | solution.py:386
  10.1 0.1 collective-permute-start.9
  10.2 0.0 copy-done.9
  10.2 0.2 convert_reduce_fusion
  10.4 0.0 copy-done.8
  10.4 0.7 %compare_reduce_fusion = pred[]{:T(512)} fusion(s32[4,16]{1,0:T(4,128)S(1)} %convert_reduce_fusion, s32[4]{0:T(128)S(1)} %copy-done.8), kind=kLoop, calls=%fused_computation.11 | loop fusion | flops 127 | bytes 273 | tf_op jit(solution)/shard_map/reduce_and | solution.py:399
  11.8 5.7 %collective-permute-done.9.other = bf16[18,32,128]{2,1,0:T(8,128)(2,1)S(1)} collective-permute-done((bf16[18,32,128]{2,1,0:T(8,128)(2,1)S(1)}, bf16[18,32,128]{2,1,0:T(8,128)(2,1)S(1)}, u32[]{:S(2)}, u32[]{:S(2)}) %collective-permute-start.9) | collective-permute-done | bytes 147488 | tf_op jit(solution)/shard_map/ppermute | solution.py:386
  17.5 1.1 %merge.8.mine = bf16[28,16,128]{2,1,0:T(8,128)(2,1)S(1)} custom-call(s32[4,16]{1,0:T(4,128)S(1)} %copy-done.6, bf16[18,32,128]{2,1,0:T(8,128)(2,1)S(1)} %get-tuple-element.88.mine, bf16[18,32,128]{2,1,0:T(8,128)(2,1)S(1)} %collective-permute-done.9.other), custom_call_target="tpu_custom_call" | custom-call | tf_op jit(solution)/shard_map/merge/pallas_call | solution.py:267
  18.6 0.0 collective-permute-done.10.other
  18.6 6.5 %collective-permute-start.11 = (bf16[28,16,128]{2,1,0:T(8,128)(2,1)S(1)}, bf16[28,16,128]{2,1,0:T(8,128)(2,1)S(1)}, u32[]{:S(2)}, u32[]{:S(2)}) collective-permute-start(bf16[28,16,128]{2,1,0:T(8,128)(2,1)S(1)} %merge.8.mine), channel_id=1, source_target_pairs={{0,8},{1,9},{2,10},{3,11},{4,12},{5,13},{6,14},{7,15},{8,0},{9,1},... | collective-permute-start | bytes 344072 | tf_op jit(solution)/shard_map/ppermute | solution.py:386
  25.1 0.0 collective-permute-done.12.refs_6_
  25.1 1.1 %merge.9.mine = bf16[28,16,128]{2,1,0:T(8,128)(2,1)S(1)} custom-call(s32[4,16]{1,0:T(4,128)S(1)} %copy-done.6, bf16[18,32,128]{2,1,0:T(8,128)(2,1)S(1)} %get-tuple-element.91.mine, bf16[18,32,128]{2,1,0:T(8,128)(2,1)S(1)} %collective-permute-done.10.other), custom_call_target="tpu_custom_call" | custom-call | tf_op jit(solution)/shard_map/merge/pallas_call | solution.py:267
  26.3 0.1 collective-permute-start.13
  26.4 7.6 %collective-permute-done.11.other = bf16[28,16,128]{2,1,0:T(8,128)(2,1)S(1)} collective-permute-done((bf16[28,16,128]{2,1,0:T(8,128)(2,1)S(1)}, bf16[28,16,128]{2,1,0:T(8,128)(2,1)S(1)}, u32[]{:S(2)}, u32[]{:S(2)}) %collective-permute-start.11) | collective-permute-done | bytes 114720 | tf_op jit(solution)/shard_map/ppermute | solution.py:386
  34.0 1.0 %merge.10.mine = bf16[46,16,128]{2,1,0:T(8,128)(2,1)S(1)} custom-call(s32[4,16]{1,0:T(4,128)S(1)} %copy-done.6, bf16[28,16,128]{2,1,0:T(8,128)(2,1)S(1)} %merge.8.mine, bf16[28,16,128]{2,1,0:T(8,128)(2,1)S(1)} %collective-permute-done.11.other), custom_call_target="tpu_custom_call" | custom-call | tf_op jit(solution)/shard_map/merge/pallas_call | solution.py:267
  35.1 0.9 %collective-permute-done.13.other = bf16[28,16,128]{2,1,0:T(8,128)(2,1)S(1)} collective-permute-done((bf16[28,16,128]{2,1,0:T(8,128)(2,1)S(1)}, bf16[28,16,128]{2,1,0:T(8,128)(2,1)S(1)}, u32[]{:S(2)}, u32[]{:S(2)}) %collective-permute-start.13) | collective-permute-done | bytes 114720 | tf_op jit(solution)/shard_map/ppermute | solution.py:386
  35.9 0.2 collective-permute-start.15
  36.1 1.0 %merge.11.mine = bf16[46,16,128]{2,1,0:T(8,128)(2,1)S(1)} custom-call(s32[4,16]{1,0:T(4,128)S(1)} %copy-done.6, bf16[28,16,128]{2,1,0:T(8,128)(2,1)S(1)} %merge.9.mine, bf16[28,16,128]{2,1,0:T(8,128)(2,1)S(1)} %collective-permute-done.13.other), custom_call_target="tpu_custom_call" | custom-call | tf_op jit(solution)/shard_map/merge/pallas_call | solution.py:267
  37.2 1.9 %collective-permute-start.14 = (bf16[46,16,128]{2,1,0:T(8,128)(2,1)S(1)}, bf16[46,16,128]{2,1,0:T(8,128)(2,1)S(1)}, u32[]{:S(2)}, u32[]{:S(2)}) collective-permute-start(bf16[46,16,128]{2,1,0:T(8,128)(2,1)S(1)} %merge.11.mine), channel_id=1, source_target_pairs={{0,4},{1,5},{2,6},{3,7},{4,0},{5,1},{6,2},{7,3},{8,12},{9,13},{10,... | collective-permute-start | bytes 565256 | tf_op jit(solution)/shard_map/ppermute | solution.py:386
  39.1 4.5 %collective-permute-done.15.other = bf16[46,16,128]{2,1,0:T(8,128)(2,1)S(1)} collective-permute-done((bf16[46,16,128]{2,1,0:T(8,128)(2,1)S(1)}, bf16[46,16,128]{2,1,0:T(8,128)(2,1)S(1)}, u32[]{:S(2)}, u32[]{:S(2)}) %collective-permute-start.15) | collective-permute-done | bytes 188448 | tf_op jit(solution)/shard_map/ppermute | solution.py:386
  43.6 1.0 %merge.12.refs_2_ = bf16[64,16,128]{2,1,0:T(8,128)(2,1)S(1)} custom-call(s32[4,16]{1,0:T(4,128)S(1)} %copy-done.6, bf16[46,16,128]{2,1,0:T(8,128)(2,1)S(1)} %merge.10.mine, bf16[46,16,128]{2,1,0:T(8,128)(2,1)S(1)} %collective-permute-done.15.other), custom_call_target="tpu_custom_call" | custom-call | tf_op jit(solution)/shard_map/merge/pallas_call | solution.py:267
  44.6 1.6 %collective-permute-done.14.other = bf16[46,16,128]{2,1,0:T(8,128)(2,1)S(1)} collective-permute-done((bf16[46,16,128]{2,1,0:T(8,128)(2,1)S(1)}, bf16[46,16,128]{2,1,0:T(8,128)(2,1)S(1)}, u32[]{:S(2)}, u32[]{:S(2)}) %collective-permute-start.14) | collective-permute-done | bytes 188448 | tf_op jit(solution)/shard_map/ppermute | solution.py:386
  46.2 0.3 collective-permute-start.16
  46.6 0.0 collective-permute-start.17
  46.6 1.0 %merge.13.refs_1_ = bf16[64,16,128]{2,1,0:T(8,128)(2,1)S(1)} custom-call(s32[4,16]{1,0:T(4,128)S(1)} %copy-done.6, bf16[46,16,128]{2,1,0:T(8,128)(2,1)S(1)} %merge.11.mine, bf16[46,16,128]{2,1,0:T(8,128)(2,1)S(1)} %collective-permute-done.14.other), custom_call_target="tpu_custom_call" | custom-call | tf_op jit(solution)/shard_map/merge/pallas_call | solution.py:267
  47.6 5.5 %collective-permute-done.16.refs_3_ = bf16[64,16,128]{2,1,0:T(8,128)(2,1)S(1)} collective-permute-done((bf16[64,16,128]{2,1,0:T(8,128)(2,1)S(1)}, bf16[64,16,128]{2,1,0:T(8,128)(2,1)S(1)}, u32[]{:S(2)}, u32[]{:S(2)}) %collective-permute-start.16) | collective-permute-done | bytes 262176 | tf_op jit(solution)/shard_map/ppermute | solution.py:386
  53.1 0.0 collective-permute-start.18
  53.1 1.0 %collective-permute-start.19 = (bf16[64,16,128]{2,1,0:T(8,128)(2,1)S(1)}, bf16[64,16,128]{2,1,0:T(8,128)(2,1)S(1)}, u32[]{:S(2)}, u32[]{:S(2)}) collective-permute-start(bf16[64,16,128]{2,1,0:T(8,128)(2,1)S(1)} %merge.13.refs_1_), channel_id=1, source_target_pairs={{0,2},{1,3},{2,0},{3,1},{4,6},{5,7},{6,4},{7,5},{8,10},{9,11},{10,... | collective-permute-start | bytes 786440 | tf_op jit(solution)/shard_map/ppermute | solution.py:386
  54.1 0.2 collective-permute-start.20
  54.3 0.0 collective-permute-done.17.refs_4_
  54.3 0.3 collective-permute-done.18.refs_5_
  54.7 5.3 %attend_first.1 = (f32[4096,128]{1,0:T(8,128)S(1)}, f32[4096,128]{1,0:T(8,128)S(1)}, f32[4096,128]{1,0:T(8,128)S(1)}) custom-call(s32[4,64]{1,0:T(4,128)S(1)} %copy-done.7, bf16[128,4096]{1,0:T(8,128)(2,1)S(1)} %copy-done.2, bf16[64,16,128]{2,1,0:T(8,128)(2,1)S(1)} %merge.12.refs_2_, bf16[64,16,128]{2,1,0:T(8,128)(2,1)S(1)} %collective-permute-done.16.refs_3_, ...), custom_call_target="tpu_custom_call" | custom-call | flops 1048576 | bytes 1048576 | tf_op jit(solution)/shard_map/attend_first/pallas_call | solution.py:373
  60.0 1.9 %collective-permute-done.19.refs_2_ = bf16[64,16,128]{2,1,0:T(8,128)(2,1)S(1)} collective-permute-done((bf16[64,16,128]{2,1,0:T(8,128)(2,1)S(1)}, bf16[64,16,128]{2,1,0:T(8,128)(2,1)S(1)}, u32[]{:S(2)}, u32[]{:S(2)}) %collective-permute-start.19) | collective-permute-done | bytes 262176 | tf_op jit(solution)/shard_map/ppermute | solution.py:386
  61.8 0.0 collective-permute-start.21
  61.8 0.0 collective-permute-done.20.refs_3_
  61.9 1.5 %collective-permute-done.21.refs_4_ = bf16[64,16,128]{2,1,0:T(8,128)(2,1)S(1)} collective-permute-done((bf16[64,16,128]{2,1,0:T(8,128)(2,1)S(1)}, bf16[64,16,128]{2,1,0:T(8,128)(2,1)S(1)}, u32[]{:S(2)}, u32[]{:S(2)}) %collective-permute-start.21) | collective-permute-done | bytes 262176 | tf_op jit(solution)/shard_map/ppermute | solution.py:386
  63.4 4.1 %attend_last.1 = bf16[128,4096]{1,0:T(8,128)(2,1)} custom-call(bf16[128,4096]{1,0:T(8,128)(2,1)S(1)} %copy-done.2, bf16[64,16,128]{2,1,0:T(8,128)(2,1)S(1)} %merge.13.refs_1_, bf16[64,16,128]{2,1,0:T(8,128)(2,1)S(1)} %collective-permute-done.19.refs_2_, bf16[64,16,128]{2,1,0:T(8,128)(2,1)S(1)} %collective-permute-done.20.refs_3_, ...), custom_call_target="tpu_custom_call" | custom-call | flops 1048576 | bytes 1048576 | tf_op jit(solution)/shard_map/attend_last/pallas_call | solution.py:373
  (13 shorter events, 0.1 us)
Async XLA Ops:
  0.0 10.2 %copy-start.9 = (s32[4]{0:T(128)S(1)}, s32[4]{0:T(128)}, u32[]{:S(2)}) copy-start(s32[4]{0:T(128)} %constant.30) | copy-start | bytes 52
  0.0 10.4 %copy-start.8 = (s32[4]{0:T(128)S(1)}, s32[4]{0:T(128)}, u32[]{:S(2)}) copy-start(s32[4]{0:T(128)} %constant.29.clone) | copy-start | bytes 52
  0.0 2.9 %copy-start.6 = (s32[4,16]{1,0:T(4,128)S(1)}, s32[4,16]{1,0:T(4,128)}, u32[]{:S(2)}) copy-start(s32[4,16]{1,0:T(4,128)} %blocks.15) | copy-start | bytes 772
  0.0 3.0 %copy-start.3 = (bf16[128,512]{1,0:T(8,128)(2,1)S(1)}, bf16[128,512]{1,0:T(8,128)(2,1)}, u32[]{:S(2)}) copy-start(bf16[128,512]{1,0:T(8,128)(2,1)} %refs_8_.1) | copy-start | bytes 393220
  0.0 3.0 %copy-start.4 = (bf16[128,512]{1,0:T(8,128)(2,1)S(1)}, bf16[128,512]{1,0:T(8,128)(2,1)}, u32[]{:S(2)}) copy-start(bf16[128,512]{1,0:T(8,128)(2,1)} %refs_7_.1) | copy-start | bytes 393220
  2.4 52.3 %copy-start.2 = (bf16[128,4096]{1,0:T(8,128)(2,1)S(1)}, bf16[128,4096]{1,0:T(8,128)(2,1)}, u32[]{:S(2)}) copy-start(bf16[128,4096]{1,0:T(8,128)(2,1)} %refs_0_.3) | copy-start | bytes 3145732
  2.4 52.3 %copy-start.7 = (s32[4,64]{1,0:T(4,128)S(1)}, s32[4,64]{1,0:T(4,128)}, u32[]{:S(2)}) copy-start(s32[4,64]{1,0:T(4,128)} %refs_0_.2) | copy-start | bytes 3076
  2.4 1.6 %collective-permute-start.8 = (bf16[12,64,128]{2,1,0:T(8,128)(2,1)S(1)}, bf16[12,64,128]{2,1,0:T(8,128)(2,1)S(1)}, u32[]{:S(2)}, u32[]{:S(2)}) collective-permute-start(bf16[12,64,128]{2,1,0:T(8,128)(2,1)S(1)} %get-tuple-element.87), channel_id=1, source_target_pairs={{0,1},{1,0},{2,3},{3,2},{4,5},{5,4},{6,7},{7,6},{8,9},{9,8},{10,11... | collective-permute-start | bytes 589832 | tf_op jit(solution)/shard_map/ppermute | solution.py:386
  5.4 19.8 %collective-permute-start.12 = (bf16[128,1024]{1,0:T(8,128)(2,1)S(1)}, bf16[128,1024]{1,0:T(8,128)(2,1)S(1)}, u32[]{:S(2)}, u32[]{:S(2)}) collective-permute-start(bf16[128,1024]{1,0:T(8,128)(2,1)S(1)} %pad_maximum_fusion), channel_id=1, source_target_pairs={{0,1},{1,2},{2,3},{3,4},{4,5},{5,6},{6,7},{7,8},{8,9},{9,10},{10,1... | collective-permute-start | bytes 786440 | tf_op jit(solution)/shard_map/ppermute | solution.py:386
  7.7 10.9 %collective-permute-start.10 = (bf16[18,32,128]{2,1,0:T(8,128)(2,1)S(1)}, bf16[18,32,128]{2,1,0:T(8,128)(2,1)S(1)}, u32[]{:S(2)}, u32[]{:S(2)}) collective-permute-start(bf16[18,32,128]{2,1,0:T(8,128)(2,1)S(1)} %get-tuple-element.91.mine), channel_id=1, source_target_pairs={{0,2},{1,3},{2,0},{3,1},{4,6},{5,7},{6,4},{7,5},{8,10},{9,11},{10,... | collective-permute-start | bytes 442376 | tf_op jit(solution)/shard_map/ppermute | solution.py:386
  10.1 7.4 %collective-permute-start.9 = (bf16[18,32,128]{2,1,0:T(8,128)(2,1)S(1)}, bf16[18,32,128]{2,1,0:T(8,128)(2,1)S(1)}, u32[]{:S(2)}, u32[]{:S(2)}) collective-permute-start(bf16[18,32,128]{2,1,0:T(8,128)(2,1)S(1)} %get-tuple-element.88.mine), channel_id=1, source_target_pairs={{0,2},{1,3},{2,0},{3,1},{4,6},{5,7},{6,4},{7,5},{8,10},{9,11},{10,... | collective-permute-start | bytes 442376 | tf_op jit(solution)/shard_map/ppermute | solution.py:386
  18.6 15.4 %collective-permute-start.11 = (bf16[28,16,128]{2,1,0:T(8,128)(2,1)S(1)}, bf16[28,16,128]{2,1,0:T(8,128)(2,1)S(1)}, u32[]{:S(2)}, u32[]{:S(2)}) collective-permute-start(bf16[28,16,128]{2,1,0:T(8,128)(2,1)S(1)} %merge.8.mine), channel_id=1, source_target_pairs={{0,8},{1,9},{2,10},{3,11},{4,12},{5,13},{6,14},{7,15},{8,0},{9,1},... | collective-permute-start | bytes 344072 | tf_op jit(solution)/shard_map/ppermute | solution.py:386
  26.3 9.7 %collective-permute-start.13 = (bf16[28,16,128]{2,1,0:T(8,128)(2,1)S(1)}, bf16[28,16,128]{2,1,0:T(8,128)(2,1)S(1)}, u32[]{:S(2)}, u32[]{:S(2)}) collective-permute-start(bf16[28,16,128]{2,1,0:T(8,128)(2,1)S(1)} %merge.9.mine), channel_id=1, source_target_pairs={{0,8},{1,9},{2,10},{3,11},{4,12},{5,13},{6,14},{7,15},{8,0},{9,1},... | collective-permute-start | bytes 344072 | tf_op jit(solution)/shard_map/ppermute | solution.py:386
  35.9 7.6 %collective-permute-start.15 = (bf16[46,16,128]{2,1,0:T(8,128)(2,1)S(1)}, bf16[46,16,128]{2,1,0:T(8,128)(2,1)S(1)}, u32[]{:S(2)}, u32[]{:S(2)}) collective-permute-start(bf16[46,16,128]{2,1,0:T(8,128)(2,1)S(1)} %merge.10.mine), channel_id=1, source_target_pairs={{0,4},{1,5},{2,6},{3,7},{4,0},{5,1},{6,2},{7,3},{8,12},{9,13},{10,... | collective-permute-start | bytes 565256 | tf_op jit(solution)/shard_map/ppermute | solution.py:386
  37.2 9.0 %collective-permute-start.14 = (bf16[46,16,128]{2,1,0:T(8,128)(2,1)S(1)}, bf16[46,16,128]{2,1,0:T(8,128)(2,1)S(1)}, u32[]{:S(2)}, u32[]{:S(2)}) collective-permute-start(bf16[46,16,128]{2,1,0:T(8,128)(2,1)S(1)} %merge.11.mine), channel_id=1, source_target_pairs={{0,4},{1,5},{2,6},{3,7},{4,0},{5,1},{6,2},{7,3},{8,12},{9,13},{10,... | collective-permute-start | bytes 565256 | tf_op jit(solution)/shard_map/ppermute | solution.py:386
  46.2 6.9 %collective-permute-start.16 = (bf16[64,16,128]{2,1,0:T(8,128)(2,1)S(1)}, bf16[64,16,128]{2,1,0:T(8,128)(2,1)S(1)}, u32[]{:S(2)}, u32[]{:S(2)}) collective-permute-start(bf16[64,16,128]{2,1,0:T(8,128)(2,1)S(1)} %merge.12.refs_2_), channel_id=1, source_target_pairs={{0,2},{1,3},{2,0},{3,1},{4,6},{5,7},{6,4},{7,5},{8,10},{9,11},{10,... | collective-permute-start | bytes 786440 | tf_op jit(solution)/shard_map/ppermute | solution.py:386
  46.6 7.8 %collective-permute-start.17 = (bf16[64,16,128]{2,1,0:T(8,128)(2,1)S(1)}, bf16[64,16,128]{2,1,0:T(8,128)(2,1)S(1)}, u32[]{:S(2)}, u32[]{:S(2)}) collective-permute-start(bf16[64,16,128]{2,1,0:T(8,128)(2,1)S(1)} %merge.12.refs_2_), channel_id=1, source_target_pairs={{0,1},{1,0},{2,3},{3,2},{4,5},{5,4},{6,7},{7,6},{8,9},{9,8},{10,11... | collective-permute-start | bytes 786440 | tf_op jit(solution)/shard_map/ppermute | solution.py:386
  53.1 1.5 %collective-permute-start.18 = (bf16[64,16,128]{2,1,0:T(8,128)(2,1)S(1)}, bf16[64,16,128]{2,1,0:T(8,128)(2,1)S(1)}, u32[]{:S(2)}, u32[]{:S(2)}) collective-permute-start(bf16[64,16,128]{2,1,0:T(8,128)(2,1)S(1)} %collective-permute-done.16.refs_3_), channel_id=1, source_target_pairs={{0,1},{1,0},{2,3},{3,2},{4,5},{5,4},{6,7},{7,6},{8,9},{9,8},{10,11... | collective-permute-start | bytes 786440 | tf_op jit(solution)/shard_map/ppermute | solution.py:386
  53.1 8.7 %collective-permute-start.19 = (bf16[64,16,128]{2,1,0:T(8,128)(2,1)S(1)}, bf16[64,16,128]{2,1,0:T(8,128)(2,1)S(1)}, u32[]{:S(2)}, u32[]{:S(2)}) collective-permute-start(bf16[64,16,128]{2,1,0:T(8,128)(2,1)S(1)} %merge.13.refs_1_), channel_id=1, source_target_pairs={{0,2},{1,3},{2,0},{3,1},{4,6},{5,7},{6,4},{7,5},{8,10},{9,11},{10,... | collective-permute-start | bytes 786440 | tf_op jit(solution)/shard_map/ppermute | solution.py:386
  54.1 7.7 %collective-permute-start.20 = (bf16[64,16,128]{2,1,0:T(8,128)(2,1)S(1)}, bf16[64,16,128]{2,1,0:T(8,128)(2,1)S(1)}, u32[]{:S(2)}, u32[]{:S(2)}) collective-permute-start(bf16[64,16,128]{2,1,0:T(8,128)(2,1)S(1)} %merge.13.refs_1_), channel_id=1, source_target_pairs={{0,1},{1,0},{2,3},{3,2},{4,5},{5,4},{6,7},{7,6},{8,9},{9,8},{10,11... | collective-permute-start | bytes 786440 | tf_op jit(solution)/shard_map/ppermute | solution.py:386
  61.8 5.7 %copy-start = (bf16[2048,512]{1,0:T(8,128)(2,1)S(1)}, bf16[2048,512]{1,0:T(8,128)(2,1)}, u32[]{:S(2)}) copy-start(bf16[2048,512]{1,0:T(8,128)(2,1)} %cache_k.1) | copy-start | bytes 6291460
  61.8 1.5 %collective-permute-start.21 = (bf16[64,16,128]{2,1,0:T(8,128)(2,1)S(1)}, bf16[64,16,128]{2,1,0:T(8,128)(2,1)S(1)}, u32[]{:S(2)}, u32[]{:S(2)}) collective-permute-start(bf16[64,16,128]{2,1,0:T(8,128)(2,1)S(1)} %collective-permute-done.19.refs_2_), channel_id=1, source_target_pairs={{0,1},{1,0},{2,3},{3,2},{4,5},{5,4},{6,7},{7,6},{8,9},{9,8},{10,11... | collective-permute-start | bytes 786440 | tf_op jit(solution)/shard_map/ppermute | solution.py:386

commit v8 on v6

--- a/solution.py
+++ b/solution.py
@@ -48,8 +48,11 @@
         scores = jnp.concatenate([scores[:, :wide], band], axis=1)
     largest = jnp.max(scores, axis=1, keepdims=True) * FACTOR
     if floor is not None:
-        largest = jnp.maximum(largest, floor)
-    weights = jnp.exp2(scores * FACTOR - largest).astype(jnp.bfloat16)
+        largest = jnp.maximum(jnp.broadcast_to(largest, floor.shape), floor)
+        above = jnp.concatenate([largest] * (scores.shape[1] // HD), axis=1)
+    else:
+        above = largest
+    weights = jnp.exp2(scores * FACTOR - above).astype(jnp.bfloat16)
     mixed = jnp.dot(weights, values_ones, preferred_element_type=jnp.float32)
     return largest, mixed
 
@@ -244,32 +247,40 @@
         at_other += other.astype(jnp.int32)
 
 
-def merge_kernel(per_device, known, bit, halved, blocks, mine, other, *outs):
-    size, rows = outs[0].shape[:2]
+def merge_kernel(per_device, jobs, blocks, *refs):
+    refs = list(refs)
     me = lax.axis_index("ctx")
-    first = pl.multiple_of(jnp.where((me & halved) == 0, 0, rows), rows) if halved else 0
-
-    def act(entry, at_mine, at_other, place, theirs):
-        place = jnp.minimum(place, size - 1)
-        for at, out in enumerate(outs):
-            span = pl.ds(first + at * rows, rows)
-            out[place] = jnp.where(theirs, other[at_other, span], mine[at_mine, span])
-
-    walk(blocks, per_device, known, bit, (mine.shape[0], other.shape[0]), act)
-
-
-def merged(blocks, per_device, known, bit, mine, other, size, parts=1, halved=0):
-    rows = mine.shape[1] // (2 if halved else parts)
-    shape = jax.ShapeDtypeStruct((size, rows, HD), jnp.bfloat16)
-    outs = pl.pallas_call(
-        functools.partial(merge_kernel, per_device, known, bit, halved),
-        out_shape=(shape,) * parts,
-        in_specs=[SMEM, WHOLE, WHOLE],
-        out_specs=(WHOLE,) * parts,
+    sources = [(refs.pop(0), refs.pop(0)) for _ in jobs]
+    for (known, bit, halved, parts), (mine, other) in zip(jobs, sources):
+        outs = [refs.pop(0) for _ in range(parts)]
+        size, rows = outs[0].shape[:2]
+        first = pl.multiple_of(jnp.where((me & halved) == 0, 0, rows), rows) if halved else 0
+
+        def act(
+            entry, at_mine, at_other, place, theirs, mine=mine, other=other, outs=outs, first=first
+        ):
+            place = jnp.minimum(place, outs[0].shape[0] - 1)
+            for at, out in enumerate(outs):
+                span = pl.ds(first + at * out.shape[1], out.shape[1])
+                out[place] = jnp.where(theirs, other[at_other, span], mine[at_mine, span])
+
+        walk(blocks, per_device, known, bit, (mine.shape[0], other.shape[0]), act)
+
+
+def merged(blocks, per_device, jobs):
+    shapes, lists = [], []
+    for _, _, halved, parts, mine, other, size in jobs:
+        rows = mine.shape[1] // (2 if halved else parts)
+        shapes += [jax.ShapeDtypeStruct((size, rows, HD), jnp.bfloat16)] * parts
+        lists += [mine, other]
+    return pl.pallas_call(
+        functools.partial(merge_kernel, per_device, [job[:4] for job in jobs]),
+        out_shape=tuple(shapes),
+        in_specs=[SMEM] + [WHOLE] * len(lists),
+        out_specs=(WHOLE,) * len(shapes),
         compiler_params=pltpu.CompilerParams(vmem_limit_bytes=16 * 2**20),
         name="merge",
-    )(blocks, mine, other)
-    return outs if parts > 1 else outs[0]
+    )(blocks, *lists)
 
 
 def stage_kernel(per_device, known, bit, banded, last, *refs):
@@ -282,12 +293,12 @@
         before, own_k, own_v = refs[:3]
         refs = refs[3:]
     else:
-        marks_in, mixed_in = refs[:2]
-        refs = refs[2:]
+        largest_in, total_in, mixed_in = refs[:3]
+        refs = refs[3:]
     if last:
         out, kbuf, vbuf, held, sems = refs
     else:
-        marks_out, mixed_out, kbuf, vbuf = refs
+        largest_out, total_out, mixed_out, kbuf, vbuf = refs
     me = lax.axis_index("ctx")
     even = lax.rem(me, 2) == 0
     wide = NV * ROWS
@@ -332,13 +343,13 @@
             )
             start = (head * GROUP + at) * QDEV
             tile = slice(start, start + TILE * QDEV)
-            floor = None if banded else marks_in[tile, :1]
+            floor = None if banded else largest_in[tile]
             largest, mixed = attend_rows(rows, kbuf[head], vbuf[head], mask, floor)
             mixed, total = mixed[:, :HD], mixed[:, HD:]
             if not banded:
                 then = jnp.exp2(floor - largest)
                 mixed = mixed + mixed_in[tile] * then
-                total = total + marks_in[tile, HD - 1 :] * then
+                total = total + total_in[tile] * then
             if last:
                 result = (mixed / total).astype(jnp.bfloat16)
                 for i in range(TILE):
@@ -346,8 +357,8 @@
                         i * QDEV : (i + 1) * QDEV
                     ]
             else:
-                lanes = lax.broadcasted_iota(jnp.int32, mixed.shape, 1)
-                marks_out[tile] = jnp.where(lanes < HD // 2, largest, total)
+                largest_out[tile] = jnp.broadcast_to(largest, mixed.shape)
+                total_out[tile] = total
                 mixed_out[tile] = mixed
         if last:
             span = pl.ds(head * GROUP * HD, GROUP * HD)
@@ -376,8 +387,8 @@
             pltpu.SemaphoreType.DMA((KVH,)),
         ]
     else:
-        out_shape = (jax.ShapeDtypeStruct((tall, HD), jnp.float32),) * 2
-        out_specs = (WHOLE,) * 2
+        out_shape = (jax.ShapeDtypeStruct((tall, HD), jnp.float32),) * 3
+        out_specs = (WHOLE,) * 3
     return pl.pallas_call(
         functools.partial(stage_kernel, per_device, known, bit, banded, last),
         out_shape=out_shape,
@@ -429,14 +440,15 @@
     masks_a = [sum(bits[:at]) for at in range(len(bits))]
     masks_b = [1 + near + sum(far[:at]) for at in range(len(far))]
 
-    def merge(known, bit, mine, other, **how):
+    def job(known, bit, mine, other, parts=1, halved=0):
         size = room((1 << (known | bit).bit_count()) / peers)
         if known + bit == peers - 1:
             size = ENTRIES
-        return merged(blocks, per_device, known, bit, mine, other, size, **how)
-
+        return known, bit, halved, parts, mine, other, size
+
+    merge = functools.partial(merged, blocks, per_device)
     kept, sent = pack(blocks, cache_k, cache_v, room(1 / peers))
-    mine_a, mine_b = merge(0, 1, kept, swapped(sent, 1), parts=STAGES)
+    mine_a, mine_b = merge([job(0, 1, kept, swapped(sent, 1), parts=STAGES)])
     before = permuted(jnp.concatenate([span_k, span_v], axis=1), ahead)
     short = jnp.logical_not(fits(blocks, per_device, peers, masks_a + masks_b)).astype(jnp.int32)
 
@@ -445,17 +457,19 @@
     other_a = swapped(mine_a, far[0])
     other_b = swapped(mine_b, near)
     other_a, before, short = lax.optimization_barrier((other_a, before, short))
-    for at, (known, bit) in enumerate(steps_a):
-        mine_a = merge(known, bit, mine_a, other_a)
-        known_b, bit_b = steps_b[at]
-        mine_b = merge(known_b, bit_b, mine_b, other_b, halved=near if at == 0 else 0)
+    for at in range(len(far)):
+        job_a = job(*steps_a[at], mine_a, other_a)
+        job_b = job(*steps_b[at], mine_b, other_b, halved=near if at == 0 else 0)
         if at < len(far) - 1:
-            mine_a, mine_b = lax.optimization_barrier((mine_a, mine_b))
+            mine_a, mine_b = merge([job_a, job_b])
+        else:
+            (mine_a,), (mine_b,) = merge([job_a]), merge([job_b])
         other_a = swapped(mine_a, (far + [near])[at + 1])
         other_b = swapped(mine_b, far[at])
         if at < len(far) - 1:
             other_a, other_b = lax.optimization_barrier((other_a, other_b))
-    mine_b = merge(*steps_b[-1], mine_b, other_b)
+    (mine_b,) = merge([job(*steps_b[-1], mine_b, other_b)])
+    other_a, mine_b = lax.optimization_barrier((other_a, mine_b))
     other_b = swapped(mine_b, near)
     twin_a, twin_b = swapped(mine_a, 1), swapped(mine_b, 1)
 

time: 61 us -> 56.9 us (0.933)
  Pallas kernels: 22 us -> 18.7 us
  waiting for transfers between devices: 18.6 us -> 17.7 us
    pallas_call x2, Pallas kernels: 12.8 us -> 10.2 us  [attend_stage(): pl.pallas_call(functools.partial(stage_kernel, per_device, known, bit, ba...]
    ppermute x13, waiting for transfers between devices: 18.6 us -> 17.7 us  [permuted(): return lax.ppermute(array, 'ctx', pairs)]
    pallas_call x6 -> x5, Pallas kernels: 6.83 us -> 6.24 us  [merged(): pl.pallas_call(functools.partial(merge_kernel, per_device, [job[:4] for j...]
  transfers between devices with their start and end apart: 13 -> 13, of which waited for: 6 -> 7; matrix products, arithmetic and copies ran while one was open for 2% -> 2% of each run, Pallas kernels for 17% -> 16%
where the time goes in v8:
time: 56.9 us; the launch traced here: 56.6 us
  Pallas kernels  18.7 us (33%)
  starting transfers between devices  18.1 us (32%)
  waiting for transfers between devices  17.7 us (31%)
  other arithmetic  0.98 us (2%)
  between operations  0.98 us (2%)
    ppermute x13, starting transfers between devices, permuted(): return lax.ppermute(array, 'ctx', pairs)  18.1 us
    ppermute x13, waiting for transfers between devices, permuted(): return lax.ppermute(array, 'ctx', pairs)  17.7 us
    pallas_call x2, Pallas kernels, attend_stage(): pl.pallas_call(functools.partial(stage_kernel, per_device, known, bit, ba...  10.2 us
    pallas_call x5, Pallas kernels, merged(): pl.pallas_call(functools.partial(merge_kernel, per_device, [job[:4] for j...  6.24 us
    pallas_call x1, Pallas kernels, pack(): pl.pallas_call(functools.partial(pack_kernel, cache_k.shape[0] // VBLOCK,...  2.25 us
  transfers between devices with their start and end apart: 13, of which 7 were waited for; matrix products, arithmetic and copies ran while one was open for 2% of the time, Pallas kernels for 16%

profile of v8, /device:TPU:0, one launch (start us, length us, event | category | flops | bytes accessed | tf_op | source)
XLA Modules:
  0.0 56.6 jit_solution(9422097408925745046)
XLA Ops:
  0.0 0.0 copy-start.8
  0.0 2.3 %pack.1 = (bf16[12,64,128]{2,1,0:T(8,128)(2,1)S(1)}, bf16[12,64,128]{2,1,0:T(8,128)(2,1)S(1)}) custom-call(s32[4,16]{1,0:T(4,128)} %refs_0_.3, bf16[2048,512]{1,0:T(8,128)(2,1)} %cache_k.1, bf16[2048,512]{1,0:T(8,128)(2,1)} %cache_v.1), custom_call_target="tpu_custom_call" | custom-call | tf_op jit(solution)/shard_map/pack/pallas_call | solution.py:227
  2.3 0.0 copy-start.2
  2.3 0.0 copy-start.7
  2.3 0.5 collective-permute-start.8
  2.8 0.0 copy-done.3
  2.8 0.0 copy-done.4
  2.9 2.1 %collective-permute-start.10 = (bf16[128,1024]{1,0:T(8,128)(2,1)S(1)}, bf16[128,1024]{1,0:T(8,128)(2,1)S(1)}, u32[]{:S(2)}, u32[]{:S(2)}) collective-permute-start(bf16[128,1024]{1,0:T(8,128)(2,1)S(1)} %pad_maximum_fusion), channel_id=1, source_target_pairs={{0,1},{1,2},{2,3},{3,4},{4,5},{5,6},{6,7},{7,8},{8,9},{9,10},{10,1... | collective-permute-start | bytes 786440 | tf_op jit(solution)/shard_map/ppermute | solution.py:405
  5.0 0.0 copy-done.6
  5.0 0.1 xor.20
  5.1 0.0 collective-permute-done.8.refs_1_
  5.1 1.4 %merge.5 = (bf16[18,32,128]{2,1,0:T(8,128)(2,1)S(1)}, bf16[18,32,128]{2,1,0:T(8,128)(2,1)S(1)}) custom-call(s32[4,16]{1,0:T(4,128)S(1)} %copy-done.6, bf16[12,64,128]{2,1,0:T(8,128)(2,1)S(1)} %get-tuple-element.77.refs_0_, bf16[12,64,128]{2,1,0:T(8,128)(2,1)S(1)} %collective-permute-done.8.refs_1_), custom_call_target="tpu_custom_call" | custom-call | tf_op jit(solution)/shard_map/merge/pallas_call | solution.py:276
  6.5 3.9 %collective-permute-start.9 = (bf16[18,32,128]{2,1,0:T(8,128)(2,1)S(1)}, bf16[18,32,128]{2,1,0:T(8,128)(2,1)S(1)}, u32[]{:S(2)}, u32[]{:S(2)}) collective-permute-start(bf16[18,32,128]{2,1,0:T(8,128)(2,1)S(1)} %get-tuple-element.79.refs_0_), channel_id=1, source_target_pairs={{0,8},{1,9},{2,10},{3,11},{4,12},{5,13},{6,14},{7,15},{8,0},{9,1},... | collective-permute-start | bytes 442376 | tf_op jit(solution)/shard_map/ppermute | solution.py:405
  10.3 1.7 %collective-permute-start.11 = (bf16[18,32,128]{2,1,0:T(8,128)(2,1)S(1)}, bf16[18,32,128]{2,1,0:T(8,128)(2,1)S(1)}, u32[]{:S(2)}, u32[]{:S(2)}) collective-permute-start(bf16[18,32,128]{2,1,0:T(8,128)(2,1)S(1)} %get-tuple-element.82.refs_2_), channel_id=1, source_target_pairs={{0,2},{1,3},{2,0},{3,1},{4,6},{5,7},{6,4},{7,5},{8,10},{9,11},{10,... | collective-permute-start | bytes 442376 | tf_op jit(solution)/shard_map/ppermute | solution.py:405
  12.1 0.0 copy-done.8
  12.1 0.2 convert_reduce_fusion
  12.3 0.0 copy-done.9
  12.3 0.7 %compare_reduce_fusion = pred[]{:T(512)} fusion(s32[6,16]{1,0:T(8,128)S(1)} %convert_reduce_fusion, s32[6]{0:T(128)S(1)} %copy-done.9), kind=kLoop, calls=%fused_computation.4 | loop fusion | flops 191 | bytes 409 | tf_op jit(solution)/shard_map/reduce_and | solution.py:418
  13.7 0.0 collective-permute-done.10.refs_7_
  13.7 3.8 %collective-permute-done.9.refs_1_ = bf16[18,32,128]{2,1,0:T(8,128)(2,1)S(1)} collective-permute-done((bf16[18,32,128]{2,1,0:T(8,128)(2,1)S(1)}, bf16[18,32,128]{2,1,0:T(8,128)(2,1)S(1)}, u32[]{:S(2)}, u32[]{:S(2)}) %collective-permute-start.9) | collective-permute-done | bytes 147488 | tf_op jit(solution)/shard_map/ppermute | solution.py:405
  17.5 0.0 collective-permute-done.11.refs_3_
  17.5 1.7 %merge.6 = (bf16[28,32,128]{2,1,0:T(8,128)(2,1)S(1)}, bf16[28,16,128]{2,1,0:T(8,128)(2,1)S(1)}) custom-call(s32[4,16]{1,0:T(4,128)S(1)} %copy-done.6, bf16[18,32,128]{2,1,0:T(8,128)(2,1)S(1)} %get-tuple-element.79.refs_0_, bf16[18,32,128]{2,1,0:T(8,128)(2,1)S(1)} %collective-permute-done.9.refs_1_, bf16[18,32,128]{2,1,0:T(8,128)(2,1)S(1)} %get-tuple-element.82.refs_2_, ...), custom_call_target="tpu_custom_call" | custom-call | tf_op jit(solution)/shard_map/merge/pallas_call | solution.py:276
  19.2 1.8 %collective-permute-start.12 = (bf16[28,32,128]{2,1,0:T(8,128)(2,1)S(1)}, bf16[28,32,128]{2,1,0:T(8,128)(2,1)S(1)}, u32[]{:S(2)}, u32[]{:S(2)}) collective-permute-start(bf16[28,32,128]{2,1,0:T(8,128)(2,1)S(1)} %get-tuple-element.83.refs_0_), channel_id=1, source_target_pairs={{0,4},{1,5},{2,6},{3,7},{4,0},{5,1},{6,2},{7,3},{8,12},{9,13},{10,... | collective-permute-start | bytes 688136 | tf_op jit(solution)/shard_map/ppermute | solution.py:405
  20.9 3.4 %collective-permute-start.13 = (bf16[28,16,128]{2,1,0:T(8,128)(2,1)S(1)}, bf16[28,16,128]{2,1,0:T(8,128)(2,1)S(1)}, u32[]{:S(2)}, u32[]{:S(2)}) collective-permute-start(bf16[28,16,128]{2,1,0:T(8,128)(2,1)S(1)} %get-tuple-element.84.refs_0_), channel_id=1, source_target_pairs={{0,8},{1,9},{2,10},{3,11},{4,12},{5,13},{6,14},{7,15},{8,0},{9,1},... | collective-permute-start | bytes 344072 | tf_op jit(solution)/shard_map/ppermute | solution.py:405
  24.3 4.3 %collective-permute-done.13.refs_1_ = bf16[28,16,128]{2,1,0:T(8,128)(2,1)S(1)} collective-permute-done((bf16[28,16,128]{2,1,0:T(8,128)(2,1)S(1)}, bf16[28,16,128]{2,1,0:T(8,128)(2,1)S(1)}, u32[]{:S(2)}, u32[]{:S(2)}) %collective-permute-start.13) | collective-permute-done | bytes 114720 | tf_op jit(solution)/shard_map/ppermute | solution.py:405
  28.6 1.2 %collective-permute-done.12.refs_1_ = bf16[28,32,128]{2,1,0:T(8,128)(2,1)S(1)} collective-permute-done((bf16[28,32,128]{2,1,0:T(8,128)(2,1)S(1)}, bf16[28,32,128]{2,1,0:T(8,128)(2,1)S(1)}, u32[]{:S(2)}, u32[]{:S(2)}) %collective-permute-start.12) | collective-permute-done | bytes 229408 | tf_op jit(solution)/shard_map/ppermute | solution.py:405
  29.8 1.1 %merge.7.refs_3_ = bf16[46,32,128]{2,1,0:T(8,128)(2,1)S(1)} custom-call(s32[4,16]{1,0:T(4,128)S(1)} %copy-done.6, bf16[28,32,128]{2,1,0:T(8,128)(2,1)S(1)} %get-tuple-element.83.refs_0_, bf16[28,32,128]{2,1,0:T(8,128)(2,1)S(1)} %collective-permute-done.12.refs_1_), custom_call_target="tpu_custom_call" | custom-call | tf_op jit(solution)/shard_map/merge/pallas_call | solution.py:276
  30.9 1.9 %collective-permute-start.14 = (bf16[46,32,128]{2,1,0:T(8,128)(2,1)S(1)}, bf16[46,32,128]{2,1,0:T(8,128)(2,1)S(1)}, u32[]{:S(2)}, u32[]{:S(2)}) collective-permute-start(bf16[46,32,128]{2,1,0:T(8,128)(2,1)S(1)} %merge.7.refs_3_), channel_id=1, source_target_pairs={{0,2},{1,3},{2,0},{3,1},{4,6},{5,7},{6,4},{7,5},{8,10},{9,11},{10,... | collective-permute-start | bytes 1130504 | tf_op jit(solution)/shard_map/ppermute | solution.py:405
  32.8 1.0 %merge.8.refs_0_ = bf16[46,16,128]{2,1,0:T(8,128)(2,1)S(1)} custom-call(s32[4,16]{1,0:T(4,128)S(1)} %copy-done.6, bf16[28,16,128]{2,1,0:T(8,128)(2,1)S(1)} %get-tuple-element.84.refs_0_, bf16[28,16,128]{2,1,0:T(8,128)(2,1)S(1)} %collective-permute-done.13.refs_1_), custom_call_target="tpu_custom_call" | custom-call | tf_op jit(solution)/shard_map/merge/pallas_call | solution.py:276
  33.8 1.2 %collective-permute-start.15 = (bf16[46,16,128]{2,1,0:T(8,128)(2,1)S(1)}, bf16[46,16,128]{2,1,0:T(8,128)(2,1)S(1)}, u32[]{:S(2)}, u32[]{:S(2)}) collective-permute-start(bf16[46,16,128]{2,1,0:T(8,128)(2,1)S(1)} %merge.8.refs_0_), channel_id=1, source_target_pairs={{0,4},{1,5},{2,6},{3,7},{4,0},{5,1},{6,2},{7,3},{8,12},{9,13},{10,... | collective-permute-start | bytes 565256 | tf_op jit(solution)/shard_map/ppermute | solution.py:405
  35.0 0.0 collective-permute-start.16
  35.0 4.7 %collective-permute-done.15.refs_1_ = bf16[46,16,128]{2,1,0:T(8,128)(2,1)S(1)} collective-permute-done((bf16[46,16,128]{2,1,0:T(8,128)(2,1)S(1)}, bf16[46,16,128]{2,1,0:T(8,128)(2,1)S(1)}, u32[]{:S(2)}, u32[]{:S(2)}) %collective-permute-start.15) | collective-permute-done | bytes 188448 | tf_op jit(solution)/shard_map/ppermute | solution.py:405
  39.7 1.0 %merge.9.refs_2_ = bf16[64,16,128]{2,1,0:T(8,128)(2,1)S(1)} custom-call(s32[4,16]{1,0:T(4,128)S(1)} %copy-done.6, bf16[46,16,128]{2,1,0:T(8,128)(2,1)S(1)} %merge.8.refs_0_, bf16[46,16,128]{2,1,0:T(8,128)(2,1)S(1)} %collective-permute-done.15.refs_1_), custom_call_target="tpu_custom_call" | custom-call | tf_op jit(solution)/shard_map/merge/pallas_call | solution.py:276
  40.7 0.7 %collective-permute-done.14.refs_4_ = bf16[46,32,128]{2,1,0:T(8,128)(2,1)S(1)} collective-permute-done((bf16[46,32,128]{2,1,0:T(8,128)(2,1)S(1)}, bf16[46,32,128]{2,1,0:T(8,128)(2,1)S(1)}, u32[]{:S(2)}, u32[]{:S(2)}) %collective-permute-start.14) | collective-permute-done | bytes 376864 | tf_op jit(solution)/shard_map/ppermute | solution.py:405
  41.5 0.0 collective-permute-start.17
  41.5 1.4 %collective-permute-start.18 = (bf16[64,16,128]{2,1,0:T(8,128)(2,1)S(1)}, bf16[64,16,128]{2,1,0:T(8,128)(2,1)S(1)}, u32[]{:S(2)}, u32[]{:S(2)}) collective-permute-start(bf16[64,16,128]{2,1,0:T(8,128)(2,1)S(1)} %merge.9.refs_2_), channel_id=1, source_target_pairs={{0,2},{1,3},{2,0},{3,1},{4,6},{5,7},{6,4},{7,5},{8,10},{9,11},{10,... | collective-permute-start | bytes 786440 | tf_op jit(solution)/shard_map/ppermute | solution.py:405
  42.9 0.2 collective-permute-start.19
  43.1 0.0 collective-permute-done.16.refs_5_
  43.1 0.0 collective-permute-done.17.refs_6_
  43.2 0.0 copy-done.2
  43.2 0.0 copy-done.7
  43.2 5.5 %attend_first.1 = (f32[4096,128]{1,0:T(8,128)S(1)}, f32[4096,128]{1,0:T(8,128)S(1)}, f32[4096,128]{1,0:T(8,128)S(1)}) custom-call(s32[4,16]{1,0:T(4,128)S(1)} %copy-done.6, s32[4,64]{1,0:T(4,128)S(1)} %copy-done.7, bf16[128,4096]{1,0:T(8,128)(2,1)S(1)} %copy-done.2, bf16[46,32,128]{2,1,0:T(8,128)(2,1)S(1)} %merge.7.refs_3_, ...), custom_call_target="tpu_custom_call" | custom-call | flops 1048576 | bytes 1048576 | tf_op jit(solution)/shard_map/attend_first/pallas_call | solution.py:392
  48.7 1.5 %collective-permute-done.18.refs_3_ = bf16[64,16,128]{2,1,0:T(8,128)(2,1)S(1)} collective-permute-done((bf16[64,16,128]{2,1,0:T(8,128)(2,1)S(1)}, bf16[64,16,128]{2,1,0:T(8,128)(2,1)S(1)}, u32[]{:S(2)}, u32[]{:S(2)}) %collective-permute-start.18) | collective-permute-done | bytes 262176 | tf_op jit(solution)/shard_map/ppermute | solution.py:405
  50.2 0.0 collective-permute-start.20
  50.2 0.0 collective-permute-done.19.refs_4_
  50.2 1.5 %collective-permute-done.20.refs_5_ = bf16[64,16,128]{2,1,0:T(8,128)(2,1)S(1)} collective-permute-done((bf16[64,16,128]{2,1,0:T(8,128)(2,1)S(1)}, bf16[64,16,128]{2,1,0:T(8,128)(2,1)S(1)}, u32[]{:S(2)}, u32[]{:S(2)}) %collective-permute-start.20) | collective-permute-done | bytes 262176 | tf_op jit(solution)/shard_map/ppermute | solution.py:405
  51.7 4.7 %attend_last.1 = bf16[128,4096]{1,0:T(8,128)(2,1)} custom-call(s32[4,16]{1,0:T(4,128)S(1)} %copy-done.6, bf16[128,4096]{1,0:T(8,128)(2,1)S(1)} %copy-done.2, bf16[64,16,128]{2,1,0:T(8,128)(2,1)S(1)} %merge.9.refs_2_, bf16[64,16,128]{2,1,0:T(8,128)(2,1)S(1)} %collective-permute-done.18.refs_3_, bf16[64,16,128]{2,1,0:T(8,128)(2,1)S(1)} %collective-permute-done.19.refs_4_, ...), custom_call_target="tpu_custom_call" | custom-call | flops 1048576 | bytes 1048576 | tf_op jit(solution)/shard_map/attend_last/pallas_call | solution.py:392
  56.4 0.0 copy-done
  (9 shorter events, 0.1 us)
Async XLA Ops:
  0.0 12.1 %copy-start.8 = (s32[6]{0:T(128)S(1)}, s32[6]{0:T(128)}, u32[]{:S(2)}) copy-start(s32[6]{0:T(128)} %constant.30) | copy-start | bytes 76
  0.0 12.3 %copy-start.9 = (s32[6]{0:T(128)S(1)}, s32[6]{0:T(128)}, u32[]{:S(2)}) copy-start(s32[6]{0:T(128)} %constant.29.clone) | copy-start | bytes 76
  0.0 5.0 %copy-start.6 = (s32[4,16]{1,0:T(4,128)S(1)}, s32[4,16]{1,0:T(4,128)}, u32[]{:S(2)}) copy-start(s32[4,16]{1,0:T(4,128)} %refs_0_.3) | copy-start | bytes 772
  0.0 2.8 %copy-start.3 = (bf16[128,512]{1,0:T(8,128)(2,1)S(1)}, bf16[128,512]{1,0:T(8,128)(2,1)}, u32[]{:S(2)}) copy-start(bf16[128,512]{1,0:T(8,128)(2,1)} %refs_9_.1) | copy-start | bytes 393220
  0.0 2.8 %copy-start.4 = (bf16[128,512]{1,0:T(8,128)(2,1)S(1)}, bf16[128,512]{1,0:T(8,128)(2,1)}, u32[]{:S(2)}) copy-start(bf16[128,512]{1,0:T(8,128)(2,1)} %refs_8_.1) | copy-start | bytes 393220
  2.3 40.9 %copy-start.2 = (bf16[128,4096]{1,0:T(8,128)(2,1)S(1)}, bf16[128,4096]{1,0:T(8,128)(2,1)}, u32[]{:S(2)}) copy-start(bf16[128,4096]{1,0:T(8,128)(2,1)} %refs_1_.3) | copy-start | bytes 3145732
  2.3 40.9 %copy-start.7 = (s32[4,64]{1,0:T(4,128)S(1)}, s32[4,64]{1,0:T(4,128)}, u32[]{:S(2)}) copy-start(s32[4,64]{1,0:T(4,128)} %refs_1_.2) | copy-start | bytes 3076
  2.3 2.8 %collective-permute-start.8 = (bf16[12,64,128]{2,1,0:T(8,128)(2,1)S(1)}, bf16[12,64,128]{2,1,0:T(8,128)(2,1)S(1)}, u32[]{:S(2)}, u32[]{:S(2)}) collective-permute-start(bf16[12,64,128]{2,1,0:T(8,128)(2,1)S(1)} %get-tuple-element.78), channel_id=1, source_target_pairs={{0,1},{1,0},{2,3},{3,2},{4,5},{5,4},{6,7},{7,6},{8,9},{9,8},{10,11... | collective-permute-start | bytes 589832 | tf_op jit(solution)/shard_map/ppermute | solution.py:405
  2.9 10.8 %collective-permute-start.10 = (bf16[128,1024]{1,0:T(8,128)(2,1)S(1)}, bf16[128,1024]{1,0:T(8,128)(2,1)S(1)}, u32[]{:S(2)}, u32[]{:S(2)}) collective-permute-start(bf16[128,1024]{1,0:T(8,128)(2,1)S(1)} %pad_maximum_fusion), channel_id=1, source_target_pairs={{0,1},{1,2},{2,3},{3,4},{4,5},{5,6},{6,7},{7,8},{8,9},{9,10},{10,1... | collective-permute-start | bytes 786440 | tf_op jit(solution)/shard_map/ppermute | solution.py:405
  6.5 11.0 %collective-permute-start.9 = (bf16[18,32,128]{2,1,0:T(8,128)(2,1)S(1)}, bf16[18,32,128]{2,1,0:T(8,128)(2,1)S(1)}, u32[]{:S(2)}, u32[]{:S(2)}) collective-permute-start(bf16[18,32,128]{2,1,0:T(8,128)(2,1)S(1)} %get-tuple-element.79.refs_0_), channel_id=1, source_target_pairs={{0,8},{1,9},{2,10},{3,11},{4,12},{5,13},{6,14},{7,15},{8,0},{9,1},... | collective-permute-start | bytes 442376 | tf_op jit(solution)/shard_map/ppermute | solution.py:405
  10.3 7.1 %collective-permute-start.11 = (bf16[18,32,128]{2,1,0:T(8,128)(2,1)S(1)}, bf16[18,32,128]{2,1,0:T(8,128)(2,1)S(1)}, u32[]{:S(2)}, u32[]{:S(2)}) collective-permute-start(bf16[18,32,128]{2,1,0:T(8,128)(2,1)S(1)} %get-tuple-element.82.refs_2_), channel_id=1, source_target_pairs={{0,2},{1,3},{2,0},{3,1},{4,6},{5,7},{6,4},{7,5},{8,10},{9,11},{10,... | collective-permute-start | bytes 442376 | tf_op jit(solution)/shard_map/ppermute | solution.py:405
  19.2 10.6 %collective-permute-start.12 = (bf16[28,32,128]{2,1,0:T(8,128)(2,1)S(1)}, bf16[28,32,128]{2,1,0:T(8,128)(2,1)S(1)}, u32[]{:S(2)}, u32[]{:S(2)}) collective-permute-start(bf16[28,32,128]{2,1,0:T(8,128)(2,1)S(1)} %get-tuple-element.83.refs_0_), channel_id=1, source_target_pairs={{0,4},{1,5},{2,6},{3,7},{4,0},{5,1},{6,2},{7,3},{8,12},{9,13},{10,... | collective-permute-start | bytes 688136 | tf_op jit(solution)/shard_map/ppermute | solution.py:405
  20.9 7.7 %collective-permute-start.13 = (bf16[28,16,128]{2,1,0:T(8,128)(2,1)S(1)}, bf16[28,16,128]{2,1,0:T(8,128)(2,1)S(1)}, u32[]{:S(2)}, u32[]{:S(2)}) collective-permute-start(bf16[28,16,128]{2,1,0:T(8,128)(2,1)S(1)} %get-tuple-element.84.refs_0_), channel_id=1, source_target_pairs={{0,8},{1,9},{2,10},{3,11},{4,12},{5,13},{6,14},{7,15},{8,0},{9,1},... | collective-permute-start | bytes 344072 | tf_op jit(solution)/shard_map/ppermute | solution.py:405
  30.9 10.5 %collective-permute-start.14 = (bf16[46,32,128]{2,1,0:T(8,128)(2,1)S(1)}, bf16[46,32,128]{2,1,0:T(8,128)(2,1)S(1)}, u32[]{:S(2)}, u32[]{:S(2)}) collective-permute-start(bf16[46,32,128]{2,1,0:T(8,128)(2,1)S(1)} %merge.7.refs_3_), channel_id=1, source_target_pairs={{0,2},{1,3},{2,0},{3,1},{4,6},{5,7},{6,4},{7,5},{8,10},{9,11},{10,... | collective-permute-start | bytes 1130504 | tf_op jit(solution)/shard_map/ppermute | solution.py:405
  33.8 5.9 %collective-permute-start.15 = (bf16[46,16,128]{2,1,0:T(8,128)(2,1)S(1)}, bf16[46,16,128]{2,1,0:T(8,128)(2,1)S(1)}, u32[]{:S(2)}, u32[]{:S(2)}) collective-permute-start(bf16[46,16,128]{2,1,0:T(8,128)(2,1)S(1)} %merge.8.refs_0_), channel_id=1, source_target_pairs={{0,4},{1,5},{2,6},{3,7},{4,0},{5,1},{6,2},{7,3},{8,12},{9,13},{10,... | collective-permute-start | bytes 565256 | tf_op jit(solution)/shard_map/ppermute | solution.py:405
  35.0 8.1 %collective-permute-start.16 = (bf16[46,32,128]{2,1,0:T(8,128)(2,1)S(1)}, bf16[46,32,128]{2,1,0:T(8,128)(2,1)S(1)}, u32[]{:S(2)}, u32[]{:S(2)}) collective-permute-start(bf16[46,32,128]{2,1,0:T(8,128)(2,1)S(1)} %merge.7.refs_3_), channel_id=1, source_target_pairs={{0,1},{1,0},{2,3},{3,2},{4,5},{5,4},{6,7},{7,6},{8,9},{9,8},{10,11... | collective-permute-start | bytes 1130504 | tf_op jit(solution)/shard_map/ppermute | solution.py:405
  41.5 1.7 %collective-permute-start.17 = (bf16[46,32,128]{2,1,0:T(8,128)(2,1)S(1)}, bf16[46,32,128]{2,1,0:T(8,128)(2,1)S(1)}, u32[]{:S(2)}, u32[]{:S(2)}) collective-permute-start(bf16[46,32,128]{2,1,0:T(8,128)(2,1)S(1)} %collective-permute-done.14.refs_4_), channel_id=1, source_target_pairs={{0,1},{1,0},{2,3},{3,2},{4,5},{5,4},{6,7},{7,6},{8,9},{9,8},{10,11... | collective-permute-start | bytes 1130504 | tf_op jit(solution)/shard_map/ppermute | solution.py:405
  41.5 8.7 %collective-permute-start.18 = (bf16[64,16,128]{2,1,0:T(8,128)(2,1)S(1)}, bf16[64,16,128]{2,1,0:T(8,128)(2,1)S(1)}, u32[]{:S(2)}, u32[]{:S(2)}) collective-permute-start(bf16[64,16,128]{2,1,0:T(8,128)(2,1)S(1)} %merge.9.refs_2_), channel_id=1, source_target_pairs={{0,2},{1,3},{2,0},{3,1},{4,6},{5,7},{6,4},{7,5},{8,10},{9,11},{10,... | collective-permute-start | bytes 786440 | tf_op jit(solution)/shard_map/ppermute | solution.py:405
  42.9 7.3 %collective-permute-start.19 = (bf16[64,16,128]{2,1,0:T(8,128)(2,1)S(1)}, bf16[64,16,128]{2,1,0:T(8,128)(2,1)S(1)}, u32[]{:S(2)}, u32[]{:S(2)}) collective-permute-start(bf16[64,16,128]{2,1,0:T(8,128)(2,1)S(1)} %merge.9.refs_2_), channel_id=1, source_target_pairs={{0,1},{1,0},{2,3},{3,2},{4,5},{5,4},{6,7},{7,6},{8,9},{9,8},{10,11... | collective-permute-start | bytes 786440 | tf_op jit(solution)/shard_map/ppermute | solution.py:405
  50.2 6.3 %copy-start = (bf16[2048,512]{1,0:T(8,128)(2,1)S(1)}, bf16[2048,512]{1,0:T(8,128)(2,1)}, u32[]{:S(2)}) copy-start(bf16[2048,512]{1,0:T(8,128)(2,1)} %cache_k.1) | copy-start | bytes 6291460
  50.2 1.5 %collective-permute-start.20 = (bf16[64,16,128]{2,1,0:T(8,128)(2,1)S(1)}, bf16[64,16,128]{2,1,0:T(8,128)(2,1)S(1)}, u32[]{:S(2)}, u32[]{:S(2)}) collective-permute-start(bf16[64,16,128]{2,1,0:T(8,128)(2,1)S(1)} %collective-permute-done.18.refs_3_), channel_id=1, source_target_pairs={{0,1},{1,0},{2,3},{3,2},{4,5},{5,4},{6,7},{7,6},{8,9},{9,8},{10,11... | collective-permute-start | bytes 786440 | tf_op jit(solution)/shard_map/ppermute | solution.py:405

commit v9 on v8

--- a/solution.py
+++ b/solution.py
@@ -24,12 +24,12 @@
 SMEM = pl.BlockSpec(memory_space=pltpu.SMEM)
 
 
-def band_mask(offsets_ref, head, first):
+def band_mask(offsets, head, first):
     columns = lax.broadcasted_iota(jnp.int32, (8, SMAX + QDEV), 1)
     distance = SMAX - columns
     row = jnp.zeros((8, SMAX + QDEV), jnp.int32)
     for at in range(NS):
-        row = jnp.where(distance == offsets_ref[head, at], 1, row)
+        row = jnp.where(distance == offsets[head, at], 1, row)
     rows = jnp.concatenate([row] * (QDEV // 8), axis=0)
     rolled = pltpu.roll(rows, 0, 1, stride=1, stride_axis=0)
     keys = lax.broadcasted_iota(jnp.int32, (QDEV, SMAX + QDEV), 1)
@@ -188,9 +188,10 @@
     me = lax.axis_index("ctx")
     even = lax.rem(me, 2) == 0
     count = jnp.int32(0)
+    table = blocks[...]
     for entry in range(ENTRIES):
         head = entry // NV
-        block = blocks[head, entry % NV]
+        block = table[head, entry % NV]
         owner = owner_of(block, per_device)
         mine = owner == me
         local = block - owner * per_device
@@ -227,7 +228,7 @@
     return pl.pallas_call(
         functools.partial(pack_kernel, cache_k.shape[0] // VBLOCK, limit),
         out_shape=(shape, shape),
-        in_specs=[SMEM, ANY, ANY],
+        in_specs=[WHOLE, ANY, ANY],
         out_specs=(WHOLE, WHOLE),
         scratch_shapes=[pltpu.SemaphoreType.DMA((limit, 2))],
         compiler_params=pltpu.CompilerParams(vmem_limit_bytes=16 * 2**20),
@@ -237,9 +238,10 @@
 
 def walk(blocks, per_device, known, bit, limits, act):
     me = lax.axis_index("ctx")
+    table = blocks[...]
     at_mine = at_other = jnp.int32(0)
     for entry in range(ENTRIES):
-        away = (owner_of(blocks[entry // NV, entry % NV], per_device) ^ me) & ~known
+        away = (owner_of(table[entry // NV, entry % NV], per_device) ^ me) & ~known
         mine, other = away == 0, away == bit
         tops = jnp.minimum(at_mine, limits[0] - 1), jnp.minimum(at_other, limits[1] - 1)
         act(entry, *tops, at_mine + at_other, other)
@@ -276,7 +278,7 @@
     return pl.pallas_call(
         functools.partial(merge_kernel, per_device, [job[:4] for job in jobs]),
         out_shape=tuple(shapes),
-        in_specs=[SMEM] + [WHOLE] * len(lists),
+        in_specs=[WHOLE] * (1 + len(lists)),
         out_specs=(WHOLE,) * len(shapes),
         compiler_params=pltpu.CompilerParams(vmem_limit_bytes=16 * 2**20),
         name="merge",
@@ -332,7 +334,7 @@
             kbuf[head, wide + SMAX :] = own_k[:, columns]
             vbuf[head, wide : wide + SMAX, :HD] = before[:, values]
             vbuf[head, wide + SMAX :, :HD] = own_v[:, columns]
-            mask = band_mask(offsets, head, me == 0)
+            mask = band_mask(offsets[...], head, me == 0)
         for at in range(0, GROUP, TILE):
             rows = jnp.concatenate(
                 [
@@ -373,7 +375,7 @@
     tall = KVH * GROUP * QDEV
     args = [blocks] + [offsets] * banded + [queries, *lists]
     args += list(bands if banded else state)
-    specs = [SMEM] * (1 + banded) + [WHOLE] * (len(args) - 1 - banded)
+    specs = [WHOLE] * len(args)
     keys = NV * ROWS + (SMAX + QDEV) * banded
     scratch = [
         pltpu.VMEM((KVH, keys, HD), jnp.bfloat16),

time: 56.9 us -> 54.9 us (0.965)
  Pallas kernels: 18.7 us -> 14.9 us
  starting transfers between devices: 18.1 us -> 19.6 us
    pallas_call x5, Pallas kernels: 6.24 us -> 3.1 us  [merged(): pl.pallas_call(functools.partial(merge_kernel, per_device, [job[:4] for j...]
    ppermute x13, starting transfers between devices: 18.1 us -> 19.6 us  [permuted(): return lax.ppermute(array, 'ctx', pairs)]
    pallas_call x2, Pallas kernels: 10.2 us -> 9.07 us  [attend_stage(): pl.pallas_call(functools.partial(stage_kernel, per_device, known, bit, ba...]
  transfers between devices with their start and end apart: 13 -> 13, of which waited for: 7 -> 7; matrix products, arithmetic and copies ran while one was open for 2% -> 2% of each run, Pallas kernels for 16% -> 12%
where the time goes in v9:
time: 54.9 us; the launch traced here: 54.3 us
  starting transfers between devices  19.6 us (36%)
  waiting for transfers between devices  17.7 us (32%)
  Pallas kernels  14.9 us (27%)
  between operations  0.99 us (2%)
  other arithmetic  0.98 us (2%)
    ppermute x13, starting transfers between devices, permuted(): return lax.ppermute(array, 'ctx', pairs)  19.6 us
    ppermute x13, waiting for transfers between devices, permuted(): return lax.ppermute(array, 'ctx', pairs)  17.7 us
    pallas_call x2, Pallas kernels, attend_stage(): pl.pallas_call(functools.partial(stage_kernel, per_device, known, bit, ba...  9.07 us
    pallas_call x5, Pallas kernels, merged(): pl.pallas_call(functools.partial(merge_kernel, per_device, [job[:4] for j...  3.1 us
    pallas_call x1, Pallas kernels, pack(): pl.pallas_call(functools.partial(pack_kernel, cache_k.shape[0] // VBLOCK,...  2.75 us
  transfers between devices with their start and end apart: 13, of which 7 were waited for; matrix products, arithmetic and copies ran while one was open for 2% of the time, Pallas kernels for 12%

profile of v9, /device:TPU:0, one launch (start us, length us, event | category | flops | bytes accessed | tf_op | source)
XLA Modules:
  0.0 54.3 jit_solution(11325107839008777071)
XLA Ops:
  0.0 0.0 copy-start.8
  0.0 2.7 %pack.1 = (bf16[12,64,128]{2,1,0:T(8,128)(2,1)S(1)}, bf16[12,64,128]{2,1,0:T(8,128)(2,1)S(1)}) custom-call(s32[4,16]{1,0:T(4,128)} %refs_0_.3, bf16[2048,512]{1,0:T(8,128)(2,1)} %cache_k.1, bf16[2048,512]{1,0:T(8,128)(2,1)} %cache_v.1), custom_call_target="tpu_custom_call" | custom-call | tf_op jit(solution)/shard_map/pack/pallas_call | solution.py:228
  2.8 0.0 copy-start.2
  2.8 0.0 copy-start.7
  2.8 0.3 collective-permute-start.8
  3.1 0.0 copy-done.3
  3.1 0.0 copy-done.4
  3.2 2.2 %collective-permute-start.10 = (bf16[128,1024]{1,0:T(8,128)(2,1)S(1)}, bf16[128,1024]{1,0:T(8,128)(2,1)S(1)}, u32[]{:S(2)}, u32[]{:S(2)}) collective-permute-start(bf16[128,1024]{1,0:T(8,128)(2,1)S(1)} %pad_maximum_fusion), channel_id=1, source_target_pairs={{0,1},{1,2},{2,3},{3,4},{4,5},{5,6},{6,7},{7,8},{8,9},{9,10},{10,1... | collective-permute-start | bytes 786440 | tf_op jit(solution)/shard_map/ppermute | solution.py:407
  5.3 0.0 copy-done.6
  5.4 0.1 xor.20
  5.4 0.0 collective-permute-done.8.refs_1_
  5.5 0.6 %merge.5 = (bf16[18,32,128]{2,1,0:T(8,128)(2,1)S(1)}, bf16[18,32,128]{2,1,0:T(8,128)(2,1)S(1)}) custom-call(s32[4,16]{1,0:T(4,128)S(1)} %copy-done.6, bf16[12,64,128]{2,1,0:T(8,128)(2,1)S(1)} %get-tuple-element.77.refs_0_, bf16[12,64,128]{2,1,0:T(8,128)(2,1)S(1)} %collective-permute-done.8.refs_1_), custom_call_target="tpu_custom_call" | custom-call | tf_op jit(solution)/shard_map/merge/pallas_call | solution.py:278
  6.0 4.1 %collective-permute-start.9 = (bf16[18,32,128]{2,1,0:T(8,128)(2,1)S(1)}, bf16[18,32,128]{2,1,0:T(8,128)(2,1)S(1)}, u32[]{:S(2)}, u32[]{:S(2)}) collective-permute-start(bf16[18,32,128]{2,1,0:T(8,128)(2,1)S(1)} %get-tuple-element.79.refs_0_), channel_id=1, source_target_pairs={{0,8},{1,9},{2,10},{3,11},{4,12},{5,13},{6,14},{7,15},{8,0},{9,1},... | collective-permute-start | bytes 442376 | tf_op jit(solution)/shard_map/ppermute | solution.py:407
  10.1 1.5 %collective-permute-start.11 = (bf16[18,32,128]{2,1,0:T(8,128)(2,1)S(1)}, bf16[18,32,128]{2,1,0:T(8,128)(2,1)S(1)}, u32[]{:S(2)}, u32[]{:S(2)}) collective-permute-start(bf16[18,32,128]{2,1,0:T(8,128)(2,1)S(1)} %get-tuple-element.82.refs_2_), channel_id=1, source_target_pairs={{0,2},{1,3},{2,0},{3,1},{4,6},{5,7},{6,4},{7,5},{8,10},{9,11},{10,... | collective-permute-start | bytes 442376 | tf_op jit(solution)/shard_map/ppermute | solution.py:407
  11.6 0.0 copy-done.8
  11.6 0.2 convert_reduce_fusion
  11.9 0.0 copy-done.9
  11.9 0.7 %compare_reduce_fusion = pred[]{:T(512)} fusion(s32[6,16]{1,0:T(8,128)S(1)} %convert_reduce_fusion, s32[6]{0:T(128)S(1)} %copy-done.9), kind=kLoop, calls=%fused_computation.4 | loop fusion | flops 191 | bytes 409 | tf_op jit(solution)/shard_map/reduce_and | solution.py:420
  13.2 0.0 collective-permute-done.10.refs_7_
  13.3 4.2 %collective-permute-done.9.refs_1_ = bf16[18,32,128]{2,1,0:T(8,128)(2,1)S(1)} collective-permute-done((bf16[18,32,128]{2,1,0:T(8,128)(2,1)S(1)}, bf16[18,32,128]{2,1,0:T(8,128)(2,1)S(1)}, u32[]{:S(2)}, u32[]{:S(2)}) %collective-permute-start.9) | collective-permute-done | bytes 147488 | tf_op jit(solution)/shard_map/ppermute | solution.py:407
  17.4 0.0 collective-permute-done.11.refs_3_
  17.4 1.0 %merge.6 = (bf16[28,32,128]{2,1,0:T(8,128)(2,1)S(1)}, bf16[28,16,128]{2,1,0:T(8,128)(2,1)S(1)}) custom-call(s32[4,16]{1,0:T(4,128)S(1)} %copy-done.6, bf16[18,32,128]{2,1,0:T(8,128)(2,1)S(1)} %get-tuple-element.79.refs_0_, bf16[18,32,128]{2,1,0:T(8,128)(2,1)S(1)} %collective-permute-done.9.refs_1_, bf16[18,32,128]{2,1,0:T(8,128)(2,1)S(1)} %get-tuple-element.82.refs_2_, ...), custom_call_target="tpu_custom_call" | custom-call | tf_op jit(solution)/shard_map/merge/pallas_call | solution.py:278
  18.5 1.6 %collective-permute-start.12 = (bf16[28,32,128]{2,1,0:T(8,128)(2,1)S(1)}, bf16[28,32,128]{2,1,0:T(8,128)(2,1)S(1)}, u32[]{:S(2)}, u32[]{:S(2)}) collective-permute-start(bf16[28,32,128]{2,1,0:T(8,128)(2,1)S(1)} %get-tuple-element.83.refs_0_), channel_id=1, source_target_pairs={{0,4},{1,5},{2,6},{3,7},{4,0},{5,1},{6,2},{7,3},{8,12},{9,13},{10,... | collective-permute-start | bytes 688136 | tf_op jit(solution)/shard_map/ppermute | solution.py:407
  20.1 3.4 %collective-permute-start.13 = (bf16[28,16,128]{2,1,0:T(8,128)(2,1)S(1)}, bf16[28,16,128]{2,1,0:T(8,128)(2,1)S(1)}, u32[]{:S(2)}, u32[]{:S(2)}) collective-permute-start(bf16[28,16,128]{2,1,0:T(8,128)(2,1)S(1)} %get-tuple-element.84.refs_0_), channel_id=1, source_target_pairs={{0,8},{1,9},{2,10},{3,11},{4,12},{5,13},{6,14},{7,15},{8,0},{9,1},... | collective-permute-start | bytes 344072 | tf_op jit(solution)/shard_map/ppermute | solution.py:407
  23.4 4.3 %collective-permute-done.13.refs_1_ = bf16[28,16,128]{2,1,0:T(8,128)(2,1)S(1)} collective-permute-done((bf16[28,16,128]{2,1,0:T(8,128)(2,1)S(1)}, bf16[28,16,128]{2,1,0:T(8,128)(2,1)S(1)}, u32[]{:S(2)}, u32[]{:S(2)}) %collective-permute-start.13) | collective-permute-done | bytes 114720 | tf_op jit(solution)/shard_map/ppermute | solution.py:407
  27.7 1.2 %collective-permute-done.12.refs_1_ = bf16[28,32,128]{2,1,0:T(8,128)(2,1)S(1)} collective-permute-done((bf16[28,32,128]{2,1,0:T(8,128)(2,1)S(1)}, bf16[28,32,128]{2,1,0:T(8,128)(2,1)S(1)}, u32[]{:S(2)}, u32[]{:S(2)}) %collective-permute-start.12) | collective-permute-done | bytes 229408 | tf_op jit(solution)/shard_map/ppermute | solution.py:407
  28.9 0.5 merge.7.refs_3_
  29.4 1.9 %collective-permute-start.14 = (bf16[46,32,128]{2,1,0:T(8,128)(2,1)S(1)}, bf16[46,32,128]{2,1,0:T(8,128)(2,1)S(1)}, u32[]{:S(2)}, u32[]{:S(2)}) collective-permute-start(bf16[46,32,128]{2,1,0:T(8,128)(2,1)S(1)} %merge.7.refs_3_), channel_id=1, source_target_pairs={{0,2},{1,3},{2,0},{3,1},{4,6},{5,7},{6,4},{7,5},{8,10},{9,11},{10,... | collective-permute-start | bytes 1130504 | tf_op jit(solution)/shard_map/ppermute | solution.py:407
  31.3 0.5 merge.8.refs_0_
  31.8 2.9 %collective-permute-start.15 = (bf16[46,16,128]{2,1,0:T(8,128)(2,1)S(1)}, bf16[46,16,128]{2,1,0:T(8,128)(2,1)S(1)}, u32[]{:S(2)}, u32[]{:S(2)}) collective-permute-start(bf16[46,16,128]{2,1,0:T(8,128)(2,1)S(1)} %merge.8.refs_0_), channel_id=1, source_target_pairs={{0,4},{1,5},{2,6},{3,7},{4,0},{5,1},{6,2},{7,3},{8,12},{9,13},{10,... | collective-permute-start | bytes 565256 | tf_op jit(solution)/shard_map/ppermute | solution.py:407
  34.7 0.0 collective-permute-start.16
  34.7 4.2 %collective-permute-done.15.refs_1_ = bf16[46,16,128]{2,1,0:T(8,128)(2,1)S(1)} collective-permute-done((bf16[46,16,128]{2,1,0:T(8,128)(2,1)S(1)}, bf16[46,16,128]{2,1,0:T(8,128)(2,1)S(1)}, u32[]{:S(2)}, u32[]{:S(2)}) %collective-permute-start.15) | collective-permute-done | bytes 188448 | tf_op jit(solution)/shard_map/ppermute | solution.py:407
  38.9 0.5 merge.9.refs_2_
  39.4 0.3 collective-permute-done.14.refs_4_
  39.7 0.0 collective-permute-start.17
  39.7 1.5 %collective-permute-start.18 = (bf16[64,16,128]{2,1,0:T(8,128)(2,1)S(1)}, bf16[64,16,128]{2,1,0:T(8,128)(2,1)S(1)}, u32[]{:S(2)}, u32[]{:S(2)}) collective-permute-start(bf16[64,16,128]{2,1,0:T(8,128)(2,1)S(1)} %merge.9.refs_2_), channel_id=1, source_target_pairs={{0,2},{1,3},{2,0},{3,1},{4,6},{5,7},{6,4},{7,5},{8,10},{9,11},{10,... | collective-permute-start | bytes 786440 | tf_op jit(solution)/shard_map/ppermute | solution.py:407
  41.2 0.2 collective-permute-start.19
  41.5 0.0 collective-permute-done.16.refs_5_
  41.5 0.0 collective-permute-done.17.refs_6_
  41.5 0.0 copy-done.2
  41.5 0.0 copy-done.7
  41.5 4.9 %attend_first.1 = (f32[4096,128]{1,0:T(8,128)S(1)}, f32[4096,128]{1,0:T(8,128)S(1)}, f32[4096,128]{1,0:T(8,128)S(1)}) custom-call(s32[4,16]{1,0:T(4,128)S(1)} %copy-done.6, s32[4,64]{1,0:T(4,128)S(1)} %copy-done.7, bf16[128,4096]{1,0:T(8,128)(2,1)S(1)} %copy-done.2, bf16[46,32,128]{2,1,0:T(8,128)(2,1)S(1)} %merge.7.refs_3_, ...), custom_call_target="tpu_custom_call" | custom-call | flops 1048576 | bytes 1048576 | tf_op jit(solution)/shard_map/attend_first/pallas_call | solution.py:394
  46.4 2.0 %collective-permute-done.18.refs_3_ = bf16[64,16,128]{2,1,0:T(8,128)(2,1)S(1)} collective-permute-done((bf16[64,16,128]{2,1,0:T(8,128)(2,1)S(1)}, bf16[64,16,128]{2,1,0:T(8,128)(2,1)S(1)}, u32[]{:S(2)}, u32[]{:S(2)}) %collective-permute-start.18) | collective-permute-done | bytes 262176 | tf_op jit(solution)/shard_map/ppermute | solution.py:407
  48.4 0.0 collective-permute-start.20
  48.4 0.0 collective-permute-done.19.refs_4_
  48.4 1.5 %collective-permute-done.20.refs_5_ = bf16[64,16,128]{2,1,0:T(8,128)(2,1)S(1)} collective-permute-done((bf16[64,16,128]{2,1,0:T(8,128)(2,1)S(1)}, bf16[64,16,128]{2,1,0:T(8,128)(2,1)S(1)}, u32[]{:S(2)}, u32[]{:S(2)}) %collective-permute-start.20) | collective-permute-done | bytes 262176 | tf_op jit(solution)/shard_map/ppermute | solution.py:407
  49.9 4.1 %attend_last.1 = bf16[128,4096]{1,0:T(8,128)(2,1)} custom-call(s32[4,16]{1,0:T(4,128)S(1)} %copy-done.6, bf16[128,4096]{1,0:T(8,128)(2,1)S(1)} %copy-done.2, bf16[64,16,128]{2,1,0:T(8,128)(2,1)S(1)} %merge.9.refs_2_, bf16[64,16,128]{2,1,0:T(8,128)(2,1)S(1)} %collective-permute-done.18.refs_3_, bf16[64,16,128]{2,1,0:T(8,128)(2,1)S(1)} %collective-permute-done.19.refs_4_, ...), custom_call_target="tpu_custom_call" | custom-call | flops 1048576 | bytes 1048576 | tf_op jit(solution)/shard_map/attend_last/pallas_call | solution.py:394
  54.1 0.0 copy-done
  (9 shorter events, 0.1 us)
Async XLA Ops:
  0.0 11.6 %copy-start.8 = (s32[6]{0:T(128)S(1)}, s32[6]{0:T(128)}, u32[]{:S(2)}) copy-start(s32[6]{0:T(128)} %constant.30) | copy-start | bytes 76
  0.0 11.9 %copy-start.9 = (s32[6]{0:T(128)S(1)}, s32[6]{0:T(128)}, u32[]{:S(2)}) copy-start(s32[6]{0:T(128)} %constant.29.clone) | copy-start | bytes 76
  0.0 5.3 %copy-start.6 = (s32[4,16]{1,0:T(4,128)S(1)}, s32[4,16]{1,0:T(4,128)}, u32[]{:S(2)}) copy-start(s32[4,16]{1,0:T(4,128)} %refs_0_.3) | copy-start | bytes 772
  0.0 3.1 %copy-start.3 = (bf16[128,512]{1,0:T(8,128)(2,1)S(1)}, bf16[128,512]{1,0:T(8,128)(2,1)}, u32[]{:S(2)}) copy-start(bf16[128,512]{1,0:T(8,128)(2,1)} %refs_9_.1) | copy-start | bytes 393220
  0.0 3.1 %copy-start.4 = (bf16[128,512]{1,0:T(8,128)(2,1)S(1)}, bf16[128,512]{1,0:T(8,128)(2,1)}, u32[]{:S(2)}) copy-start(bf16[128,512]{1,0:T(8,128)(2,1)} %refs_8_.1) | copy-start | bytes 393220
  2.8 38.7 %copy-start.2 = (bf16[128,4096]{1,0:T(8,128)(2,1)S(1)}, bf16[128,4096]{1,0:T(8,128)(2,1)}, u32[]{:S(2)}) copy-start(bf16[128,4096]{1,0:T(8,128)(2,1)} %refs_1_.3) | copy-start | bytes 3145732
  2.8 38.7 %copy-start.7 = (s32[4,64]{1,0:T(4,128)S(1)}, s32[4,64]{1,0:T(4,128)}, u32[]{:S(2)}) copy-start(s32[4,64]{1,0:T(4,128)} %refs_1_.2) | copy-start | bytes 3076
  2.8 2.7 %collective-permute-start.8 = (bf16[12,64,128]{2,1,0:T(8,128)(2,1)S(1)}, bf16[12,64,128]{2,1,0:T(8,128)(2,1)S(1)}, u32[]{:S(2)}, u32[]{:S(2)}) collective-permute-start(bf16[12,64,128]{2,1,0:T(8,128)(2,1)S(1)} %get-tuple-element.78), channel_id=1, source_target_pairs={{0,1},{1,0},{2,3},{3,2},{4,5},{5,4},{6,7},{7,6},{8,9},{9,8},{10,11... | collective-permute-start | bytes 589832 | tf_op jit(solution)/shard_map/ppermute | solution.py:407
  3.2 10.1 %collective-permute-start.10 = (bf16[128,1024]{1,0:T(8,128)(2,1)S(1)}, bf16[128,1024]{1,0:T(8,128)(2,1)S(1)}, u32[]{:S(2)}, u32[]{:S(2)}) collective-permute-start(bf16[128,1024]{1,0:T(8,128)(2,1)S(1)} %pad_maximum_fusion), channel_id=1, source_target_pairs={{0,1},{1,2},{2,3},{3,4},{4,5},{5,6},{6,7},{7,8},{8,9},{9,10},{10,1... | collective-permute-start | bytes 786440 | tf_op jit(solution)/shard_map/ppermute | solution.py:407
  6.0 11.4 %collective-permute-start.9 = (bf16[18,32,128]{2,1,0:T(8,128)(2,1)S(1)}, bf16[18,32,128]{2,1,0:T(8,128)(2,1)S(1)}, u32[]{:S(2)}, u32[]{:S(2)}) collective-permute-start(bf16[18,32,128]{2,1,0:T(8,128)(2,1)S(1)} %get-tuple-element.79.refs_0_), channel_id=1, source_target_pairs={{0,8},{1,9},{2,10},{3,11},{4,12},{5,13},{6,14},{7,15},{8,0},{9,1},... | collective-permute-start | bytes 442376 | tf_op jit(solution)/shard_map/ppermute | solution.py:407
  10.1 7.3 %collective-permute-start.11 = (bf16[18,32,128]{2,1,0:T(8,128)(2,1)S(1)}, bf16[18,32,128]{2,1,0:T(8,128)(2,1)S(1)}, u32[]{:S(2)}, u32[]{:S(2)}) collective-permute-start(bf16[18,32,128]{2,1,0:T(8,128)(2,1)S(1)} %get-tuple-element.82.refs_2_), channel_id=1, source_target_pairs={{0,2},{1,3},{2,0},{3,1},{4,6},{5,7},{6,4},{7,5},{8,10},{9,11},{10,... | collective-permute-start | bytes 442376 | tf_op jit(solution)/shard_map/ppermute | solution.py:407
  18.5 10.4 %collective-permute-start.12 = (bf16[28,32,128]{2,1,0:T(8,128)(2,1)S(1)}, bf16[28,32,128]{2,1,0:T(8,128)(2,1)S(1)}, u32[]{:S(2)}, u32[]{:S(2)}) collective-permute-start(bf16[28,32,128]{2,1,0:T(8,128)(2,1)S(1)} %get-tuple-element.83.refs_0_), channel_id=1, source_target_pairs={{0,4},{1,5},{2,6},{3,7},{4,0},{5,1},{6,2},{7,3},{8,12},{9,13},{10,... | collective-permute-start | bytes 688136 | tf_op jit(solution)/shard_map/ppermute | solution.py:407
  20.1 7.7 %collective-permute-start.13 = (bf16[28,16,128]{2,1,0:T(8,128)(2,1)S(1)}, bf16[28,16,128]{2,1,0:T(8,128)(2,1)S(1)}, u32[]{:S(2)}, u32[]{:S(2)}) collective-permute-start(bf16[28,16,128]{2,1,0:T(8,128)(2,1)S(1)} %get-tuple-element.84.refs_0_), channel_id=1, source_target_pairs={{0,8},{1,9},{2,10},{3,11},{4,12},{5,13},{6,14},{7,15},{8,0},{9,1},... | collective-permute-start | bytes 344072 | tf_op jit(solution)/shard_map/ppermute | solution.py:407
  29.4 10.3 %collective-permute-start.14 = (bf16[46,32,128]{2,1,0:T(8,128)(2,1)S(1)}, bf16[46,32,128]{2,1,0:T(8,128)(2,1)S(1)}, u32[]{:S(2)}, u32[]{:S(2)}) collective-permute-start(bf16[46,32,128]{2,1,0:T(8,128)(2,1)S(1)} %merge.7.refs_3_), channel_id=1, source_target_pairs={{0,2},{1,3},{2,0},{3,1},{4,6},{5,7},{6,4},{7,5},{8,10},{9,11},{10,... | collective-permute-start | bytes 1130504 | tf_op jit(solution)/shard_map/ppermute | solution.py:407
  31.8 7.1 %collective-permute-start.15 = (bf16[46,16,128]{2,1,0:T(8,128)(2,1)S(1)}, bf16[46,16,128]{2,1,0:T(8,128)(2,1)S(1)}, u32[]{:S(2)}, u32[]{:S(2)}) collective-permute-start(bf16[46,16,128]{2,1,0:T(8,128)(2,1)S(1)} %merge.8.refs_0_), channel_id=1, source_target_pairs={{0,4},{1,5},{2,6},{3,7},{4,0},{5,1},{6,2},{7,3},{8,12},{9,13},{10,... | collective-permute-start | bytes 565256 | tf_op jit(solution)/shard_map/ppermute | solution.py:407
  34.7 6.8 %collective-permute-start.16 = (bf16[46,32,128]{2,1,0:T(8,128)(2,1)S(1)}, bf16[46,32,128]{2,1,0:T(8,128)(2,1)S(1)}, u32[]{:S(2)}, u32[]{:S(2)}) collective-permute-start(bf16[46,32,128]{2,1,0:T(8,128)(2,1)S(1)} %merge.7.refs_3_), channel_id=1, source_target_pairs={{0,1},{1,0},{2,3},{3,2},{4,5},{5,4},{6,7},{7,6},{8,9},{9,8},{10,11... | collective-permute-start | bytes 1130504 | tf_op jit(solution)/shard_map/ppermute | solution.py:407
  39.7 1.8 %collective-permute-start.17 = (bf16[46,32,128]{2,1,0:T(8,128)(2,1)S(1)}, bf16[46,32,128]{2,1,0:T(8,128)(2,1)S(1)}, u32[]{:S(2)}, u32[]{:S(2)}) collective-permute-start(bf16[46,32,128]{2,1,0:T(8,128)(2,1)S(1)} %collective-permute-done.14.refs_4_), channel_id=1, source_target_pairs={{0,1},{1,0},{2,3},{3,2},{4,5},{5,4},{6,7},{7,6},{8,9},{9,8},{10,11... | collective-permute-start | bytes 1130504 | tf_op jit(solution)/shard_map/ppermute | solution.py:407
  39.7 8.7 %collective-permute-start.18 = (bf16[64,16,128]{2,1,0:T(8,128)(2,1)S(1)}, bf16[64,16,128]{2,1,0:T(8,128)(2,1)S(1)}, u32[]{:S(2)}, u32[]{:S(2)}) collective-permute-start(bf16[64,16,128]{2,1,0:T(8,128)(2,1)S(1)} %merge.9.refs_2_), channel_id=1, source_target_pairs={{0,2},{1,3},{2,0},{3,1},{4,6},{5,7},{6,4},{7,5},{8,10},{9,11},{10,... | collective-permute-start | bytes 786440 | tf_op jit(solution)/shard_map/ppermute | solution.py:407
  41.2 7.2 %collective-permute-start.19 = (bf16[64,16,128]{2,1,0:T(8,128)(2,1)S(1)}, bf16[64,16,128]{2,1,0:T(8,128)(2,1)S(1)}, u32[]{:S(2)}, u32[]{:S(2)}) collective-permute-start(bf16[64,16,128]{2,1,0:T(8,128)(2,1)S(1)} %merge.9.refs_2_), channel_id=1, source_target_pairs={{0,1},{1,0},{2,3},{3,2},{4,5},{5,4},{6,7},{7,6},{8,9},{9,8},{10,11... | collective-permute-start | bytes 786440 | tf_op jit(solution)/shard_map/ppermute | solution.py:407
  48.4 5.7 %copy-start = (bf16[2048,512]{1,0:T(8,128)(2,1)S(1)}, bf16[2048,512]{1,0:T(8,128)(2,1)}, u32[]{:S(2)}) copy-start(bf16[2048,512]{1,0:T(8,128)(2,1)} %cache_k.1) | copy-start | bytes 6291460
  48.4 1.5 %collective-permute-start.20 = (bf16[64,16,128]{2,1,0:T(8,128)(2,1)S(1)}, bf16[64,16,128]{2,1,0:T(8,128)(2,1)S(1)}, u32[]{:S(2)}, u32[]{:S(2)}) collective-permute-start(bf16[64,16,128]{2,1,0:T(8,128)(2,1)S(1)} %collective-permute-done.18.refs_3_), channel_id=1, source_target_pairs={{0,1},{1,0},{2,3},{3,2},{4,5},{5,4},{6,7},{7,6},{8,9},{9,8},{10,11... | collective-permute-start | bytes 786440 | tf_op jit(solution)/shard_map/ppermute | solution.py:407

commit v10 on v9

--- a/solution.py
+++ b/solution.py
@@ -451,19 +451,22 @@
     merge = functools.partial(merged, blocks, per_device)
     kept, sent = pack(blocks, cache_k, cache_v, room(1 / peers))
     mine_a, mine_b = merge([job(0, 1, kept, swapped(sent, 1), parts=STAGES)])
-    before = permuted(jnp.concatenate([span_k, span_v], axis=1), ahead)
+    spans, mine_b = lax.optimization_barrier((jnp.concatenate([span_k, span_v], axis=1), mine_b))
+    before = permuted(spans, ahead)
     short = jnp.logical_not(fits(blocks, per_device, peers, masks_a + masks_b)).astype(jnp.int32)
 
     steps_a = list(zip(masks_a[1:], far))
     steps_b = list(zip([1] + masks_b, [near] + far))
     other_a = swapped(mine_a, far[0])
     other_b = swapped(mine_b, near)
-    other_a, before, short = lax.optimization_barrier((other_a, before, short))
+    other_a, short = lax.optimization_barrier((other_a, short))
     for at in range(len(far)):
         job_a = job(*steps_a[at], mine_a, other_a)
         job_b = job(*steps_b[at], mine_b, other_b, halved=near if at == 0 else 0)
         if at < len(far) - 1:
             mine_a, mine_b = merge([job_a, job_b])
+            if at == 0:
+                mine_b, before = lax.optimization_barrier((mine_b, before))
         else:
             (mine_a,), (mine_b,) = merge([job_a]), merge([job_b])
         other_a = swapped(mine_a, (far + [near])[at + 1])

time: 54.9 us -> 52.6 us (0.958)
  waiting for transfers between devices: 17.7 us -> 16.1 us
  starting transfers between devices: 19.6 us -> 18.7 us
    ppermute x13, waiting for transfers between devices: 17.7 us -> 16.1 us  [permuted(): return lax.ppermute(array, 'ctx', pairs)]
    ppermute x13, starting transfers between devices: 19.6 us -> 18.7 us  [permuted(): return lax.ppermute(array, 'ctx', pairs)]
  transfers between devices with their start and end apart: 13 -> 13, of which waited for: 7 -> 7; matrix products, arithmetic and copies ran while one was open for 2% -> 2% of each run, Pallas kernels for 12% -> 13%
where the time goes in v10:
time: 52.6 us; the launch traced here: 51.7 us
  starting transfers between devices  18.7 us (36%)
  waiting for transfers between devices  16.1 us (31%)
  Pallas kernels  14.7 us (28%)
  between operations  0.99 us (2%)
  other arithmetic  0.98 us (2%)
    ppermute x13, starting transfers between devices, permuted(): return lax.ppermute(array, 'ctx', pairs)  18.7 us
    ppermute x13, waiting for transfers between devices, permuted(): return lax.ppermute(array, 'ctx', pairs)  16.1 us
    pallas_call x2, Pallas kernels, attend_stage(): pl.pallas_call(functools.partial(stage_kernel, per_device, known, bit, ba...  8.89 us
    pallas_call x5, Pallas kernels, merged(): pl.pallas_call(functools.partial(merge_kernel, per_device, [job[:4] for j...  3.1 us
    pallas_call x1, Pallas kernels, pack(): pl.pallas_call(functools.partial(pack_kernel, cache_k.shape[0] // VBLOCK,...  2.74 us
  transfers between devices with their start and end apart: 13, of which 7 were waited for; matrix products, arithmetic and copies ran while one was open for 2% of the time, Pallas kernels for 13%

profile of v10, /device:TPU:0, one launch (start us, length us, event | category | flops | bytes accessed | tf_op | source)
XLA Modules:
  0.0 51.7 jit_solution(9012192162021764820)
XLA Ops:
  0.0 2.7 %pack.1 = (bf16[12,64,128]{2,1,0:T(8,128)(2,1)S(1)}, bf16[12,64,128]{2,1,0:T(8,128)(2,1)S(1)}) custom-call(s32[4,16]{1,0:T(4,128)} %refs_0_.3, bf16[2048,512]{1,0:T(8,128)(2,1)} %cache_k.1, bf16[2048,512]{1,0:T(8,128)(2,1)} %cache_v.1), custom_call_target="tpu_custom_call" | custom-call | tf_op jit(solution)/shard_map/pack/pallas_call | solution.py:228
  2.8 0.0 copy-start.2
  2.8 0.0 copy-start.7
  2.8 0.5 collective-permute-start.8
  3.3 0.0 copy-done.6
  3.3 0.1 xor.20
  3.4 0.0 copy-done.3
  3.4 0.0 copy-done.4
  3.4 0.9 %collective-permute-done.8.refs_1_ = bf16[12,64,128]{2,1,0:T(8,128)(2,1)S(1)} collective-permute-done((bf16[12,64,128]{2,1,0:T(8,128)(2,1)S(1)}, bf16[12,64,128]{2,1,0:T(8,128)(2,1)S(1)}, u32[]{:S(2)}, u32[]{:S(2)}) %collective-permute-start.8) | collective-permute-done | bytes 196640 | tf_op jit(solution)/shard_map/ppermute | solution.py:407
  4.4 0.6 %merge.5 = (bf16[18,32,128]{2,1,0:T(8,128)(2,1)S(1)}, bf16[18,32,128]{2,1,0:T(8,128)(2,1)S(1)}) custom-call(s32[4,16]{1,0:T(4,128)S(1)} %copy-done.6, bf16[12,64,128]{2,1,0:T(8,128)(2,1)S(1)} %get-tuple-element.80.refs_0_, bf16[12,64,128]{2,1,0:T(8,128)(2,1)S(1)} %collective-permute-done.8.refs_1_), custom_call_target="tpu_custom_call" | custom-call | tf_op jit(solution)/shard_map/merge/pallas_call | solution.py:278
  4.9 4.0 %collective-permute-start.9 = (bf16[18,32,128]{2,1,0:T(8,128)(2,1)S(1)}, bf16[18,32,128]{2,1,0:T(8,128)(2,1)S(1)}, u32[]{:S(2)}, u32[]{:S(2)}) collective-permute-start(bf16[18,32,128]{2,1,0:T(8,128)(2,1)S(1)} %get-tuple-element.82.refs_0_), channel_id=1, source_target_pairs={{0,8},{1,9},{2,10},{3,11},{4,12},{5,13},{6,14},{7,15},{8,0},{9,1},... | collective-permute-start | bytes 442376 | tf_op jit(solution)/shard_map/ppermute | solution.py:407
  9.0 1.5 %collective-permute-start.10 = (bf16[18,32,128]{2,1,0:T(8,128)(2,1)S(1)}, bf16[18,32,128]{2,1,0:T(8,128)(2,1)S(1)}, u32[]{:S(2)}, u32[]{:S(2)}) collective-permute-start(bf16[18,32,128]{2,1,0:T(8,128)(2,1)S(1)} %get-tuple-element.86.refs_2_), channel_id=1, source_target_pairs={{0,2},{1,3},{2,0},{3,1},{4,6},{5,7},{6,4},{7,5},{8,10},{9,11},{10,... | collective-permute-start | bytes 442376 | tf_op jit(solution)/shard_map/ppermute | solution.py:407
  10.5 1.5 %collective-permute-start.12 = (bf16[128,1024]{1,0:T(8,128)(2,1)S(1)}, bf16[128,1024]{1,0:T(8,128)(2,1)S(1)}, u32[]{:S(2)}, u32[]{:S(2)}) collective-permute-start(bf16[128,1024]{1,0:T(8,128)(2,1)S(1)} %pad_maximum_fusion), channel_id=1, source_target_pairs={{0,1},{1,2},{2,3},{3,4},{4,5},{5,6},{6,7},{7,8},{8,9},{9,10},{10,1... | collective-permute-start | bytes 786440 | tf_op jit(solution)/shard_map/ppermute | solution.py:407
  12.0 0.0 copy-done.8
  12.0 0.2 convert_reduce_fusion
  12.3 0.0 copy-done.9
  12.3 0.7 %compare_reduce_fusion = pred[]{:T(512)} fusion(s32[6,16]{1,0:T(8,128)S(1)} %convert_reduce_fusion, s32[6]{0:T(128)S(1)} %copy-done.9), kind=kLoop, calls=%fused_computation.4 | loop fusion | flops 191 | bytes 409 | tf_op jit(solution)/shard_map/reduce_and | solution.py:420
  13.6 2.7 %collective-permute-done.9.refs_1_ = bf16[18,32,128]{2,1,0:T(8,128)(2,1)S(1)} collective-permute-done((bf16[18,32,128]{2,1,0:T(8,128)(2,1)S(1)}, bf16[18,32,128]{2,1,0:T(8,128)(2,1)S(1)}, u32[]{:S(2)}, u32[]{:S(2)}) %collective-permute-start.9) | collective-permute-done | bytes 147488 | tf_op jit(solution)/shard_map/ppermute | solution.py:407
  16.3 0.0 collective-permute-done.10.refs_3_
  16.3 1.0 %merge.6 = (bf16[28,32,128]{2,1,0:T(8,128)(2,1)S(1)}, bf16[28,16,128]{2,1,0:T(8,128)(2,1)S(1)}) custom-call(s32[4,16]{1,0:T(4,128)S(1)} %copy-done.6, bf16[18,32,128]{2,1,0:T(8,128)(2,1)S(1)} %get-tuple-element.82.refs_0_, bf16[18,32,128]{2,1,0:T(8,128)(2,1)S(1)} %collective-permute-done.9.refs_1_, bf16[18,32,128]{2,1,0:T(8,128)(2,1)S(1)} %get-tuple-element.86.refs_2_, ...), custom_call_target="tpu_custom_call" | custom-call | tf_op jit(solution)/shard_map/merge/pallas_call | solution.py:278
  17.4 0.8 %collective-permute-start.11 = (bf16[28,32,128]{2,1,0:T(8,128)(2,1)S(1)}, bf16[28,32,128]{2,1,0:T(8,128)(2,1)S(1)}, u32[]{:S(2)}, u32[]{:S(2)}) collective-permute-start(bf16[28,32,128]{2,1,0:T(8,128)(2,1)S(1)} %get-tuple-element.87.refs_0_), channel_id=1, source_target_pairs={{0,4},{1,5},{2,6},{3,7},{4,0},{5,1},{6,2},{7,3},{8,12},{9,13},{10,... | collective-permute-start | bytes 688136 | tf_op jit(solution)/shard_map/ppermute | solution.py:407
  18.1 0.0 collective-permute-done.12.refs_7_
  18.1 4.6 %collective-permute-start.13 = (bf16[28,16,128]{2,1,0:T(8,128)(2,1)S(1)}, bf16[28,16,128]{2,1,0:T(8,128)(2,1)S(1)}, u32[]{:S(2)}, u32[]{:S(2)}) collective-permute-start(bf16[28,16,128]{2,1,0:T(8,128)(2,1)S(1)} %get-tuple-element.90.refs_0_), channel_id=1, source_target_pairs={{0,8},{1,9},{2,10},{3,11},{4,12},{5,13},{6,14},{7,15},{8,0},{9,1},... | collective-permute-start | bytes 344072 | tf_op jit(solution)/shard_map/ppermute | solution.py:407
  22.8 4.2 %collective-permute-done.11.refs_1_ = bf16[28,32,128]{2,1,0:T(8,128)(2,1)S(1)} collective-permute-done((bf16[28,32,128]{2,1,0:T(8,128)(2,1)S(1)}, bf16[28,32,128]{2,1,0:T(8,128)(2,1)S(1)}, u32[]{:S(2)}, u32[]{:S(2)}) %collective-permute-start.11) | collective-permute-done | bytes 229408 | tf_op jit(solution)/shard_map/ppermute | solution.py:407
  27.0 0.0 collective-permute-done.13.refs_1_
  27.0 0.5 merge.7.refs_3_
  27.5 1.4 %collective-permute-start.14 = (bf16[46,32,128]{2,1,0:T(8,128)(2,1)S(1)}, bf16[46,32,128]{2,1,0:T(8,128)(2,1)S(1)}, u32[]{:S(2)}, u32[]{:S(2)}) collective-permute-start(bf16[46,32,128]{2,1,0:T(8,128)(2,1)S(1)} %merge.7.refs_3_), channel_id=1, source_target_pairs={{0,2},{1,3},{2,0},{3,1},{4,6},{5,7},{6,4},{7,5},{8,10},{9,11},{10,... | collective-permute-start | bytes 1130504 | tf_op jit(solution)/shard_map/ppermute | solution.py:407
  28.9 0.5 merge.8.refs_0_
  29.4 3.1 %collective-permute-start.15 = (bf16[46,16,128]{2,1,0:T(8,128)(2,1)S(1)}, bf16[46,16,128]{2,1,0:T(8,128)(2,1)S(1)}, u32[]{:S(2)}, u32[]{:S(2)}) collective-permute-start(bf16[46,16,128]{2,1,0:T(8,128)(2,1)S(1)} %merge.8.refs_0_), channel_id=1, source_target_pairs={{0,4},{1,5},{2,6},{3,7},{4,0},{5,1},{6,2},{7,3},{8,12},{9,13},{10,... | collective-permute-start | bytes 565256 | tf_op jit(solution)/shard_map/ppermute | solution.py:407
  32.5 0.0 collective-permute-start.16
  32.5 4.0 %collective-permute-done.15.refs_1_ = bf16[46,16,128]{2,1,0:T(8,128)(2,1)S(1)} collective-permute-done((bf16[46,16,128]{2,1,0:T(8,128)(2,1)S(1)}, bf16[46,16,128]{2,1,0:T(8,128)(2,1)S(1)}, u32[]{:S(2)}, u32[]{:S(2)}) %collective-permute-start.15) | collective-permute-done | bytes 188448 | tf_op jit(solution)/shard_map/ppermute | solution.py:407
  36.6 0.5 merge.9.refs_2_
  37.0 0.0 collective-permute-done.14.refs_4_
  37.1 0.1 collective-permute-start.17
  37.1 0.9 %collective-permute-start.18 = (bf16[64,16,128]{2,1,0:T(8,128)(2,1)S(1)}, bf16[64,16,128]{2,1,0:T(8,128)(2,1)S(1)}, u32[]{:S(2)}, u32[]{:S(2)}) collective-permute-start(bf16[64,16,128]{2,1,0:T(8,128)(2,1)S(1)} %merge.9.refs_2_), channel_id=1, source_target_pairs={{0,2},{1,3},{2,0},{3,1},{4,6},{5,7},{6,4},{7,5},{8,10},{9,11},{10,... | collective-permute-start | bytes 786440 | tf_op jit(solution)/shard_map/ppermute | solution.py:407
  38.0 0.2 collective-permute-start.19
  38.3 0.0 collective-permute-done.16.refs_5_
  38.3 0.6 %collective-permute-done.17.refs_6_ = bf16[46,32,128]{2,1,0:T(8,128)(2,1)S(1)} collective-permute-done((bf16[46,32,128]{2,1,0:T(8,128)(2,1)S(1)}, bf16[46,32,128]{2,1,0:T(8,128)(2,1)S(1)}, u32[]{:S(2)}, u32[]{:S(2)}) %collective-permute-start.17) | collective-permute-done | bytes 376864 | tf_op jit(solution)/shard_map/ppermute | solution.py:407
  38.8 0.0 copy-done.2
  38.8 0.0 copy-done.7
  38.8 4.9 %attend_first.1 = (f32[4096,128]{1,0:T(8,128)S(1)}, f32[4096,128]{1,0:T(8,128)S(1)}, f32[4096,128]{1,0:T(8,128)S(1)}) custom-call(s32[4,16]{1,0:T(4,128)S(1)} %copy-done.6, s32[4,64]{1,0:T(4,128)S(1)} %copy-done.7, bf16[128,4096]{1,0:T(8,128)(2,1)S(1)} %copy-done.2, bf16[46,32,128]{2,1,0:T(8,128)(2,1)S(1)} %merge.7.refs_3_, ...), custom_call_target="tpu_custom_call" | custom-call | flops 1048576 | bytes 1048576 | tf_op jit(solution)/shard_map/attend_first/pallas_call | solution.py:394
  43.8 2.1 %collective-permute-done.18.refs_3_ = bf16[64,16,128]{2,1,0:T(8,128)(2,1)S(1)} collective-permute-done((bf16[64,16,128]{2,1,0:T(8,128)(2,1)S(1)}, bf16[64,16,128]{2,1,0:T(8,128)(2,1)S(1)}, u32[]{:S(2)}, u32[]{:S(2)}) %collective-permute-start.18) | collective-permute-done | bytes 262176 | tf_op jit(solution)/shard_map/ppermute | solution.py:407
  45.9 0.0 collective-permute-start.20
  45.9 0.0 collective-permute-done.19.refs_4_
  45.9 1.5 %collective-permute-done.20.refs_5_ = bf16[64,16,128]{2,1,0:T(8,128)(2,1)S(1)} collective-permute-done((bf16[64,16,128]{2,1,0:T(8,128)(2,1)S(1)}, bf16[64,16,128]{2,1,0:T(8,128)(2,1)S(1)}, u32[]{:S(2)}, u32[]{:S(2)}) %collective-permute-start.20) | collective-permute-done | bytes 262176 | tf_op jit(solution)/shard_map/ppermute | solution.py:407
  47.4 4.0 %attend_last.1 = bf16[128,4096]{1,0:T(8,128)(2,1)} custom-call(s32[4,16]{1,0:T(4,128)S(1)} %copy-done.6, bf16[128,4096]{1,0:T(8,128)(2,1)S(1)} %copy-done.2, bf16[64,16,128]{2,1,0:T(8,128)(2,1)S(1)} %merge.9.refs_2_, bf16[64,16,128]{2,1,0:T(8,128)(2,1)S(1)} %collective-permute-done.18.refs_3_, bf16[64,16,128]{2,1,0:T(8,128)(2,1)S(1)} %collective-permute-done.19.refs_4_, ...), custom_call_target="tpu_custom_call" | custom-call | flops 1048576 | bytes 1048576 | tf_op jit(solution)/shard_map/attend_last/pallas_call | solution.py:394
  51.4 0.0 copy-done
  51.4 0.2 while.9
  (9 shorter events, 0.0 us)
Async XLA Ops:
  0.0 12.0 %copy-start.8 = (s32[6]{0:T(128)S(1)}, s32[6]{0:T(128)}, u32[]{:S(2)}) copy-start(s32[6]{0:T(128)} %constant.30) | copy-start | bytes 76
  0.0 12.3 %copy-start.9 = (s32[6]{0:T(128)S(1)}, s32[6]{0:T(128)}, u32[]{:S(2)}) copy-start(s32[6]{0:T(128)} %constant.29.clone) | copy-start | bytes 76
  0.0 3.3 %copy-start.6 = (s32[4,16]{1,0:T(4,128)S(1)}, s32[4,16]{1,0:T(4,128)}, u32[]{:S(2)}) copy-start(s32[4,16]{1,0:T(4,128)} %refs_0_.3) | copy-start | bytes 772
  0.0 3.4 %copy-start.3 = (bf16[128,512]{1,0:T(8,128)(2,1)S(1)}, bf16[128,512]{1,0:T(8,128)(2,1)}, u32[]{:S(2)}) copy-start(bf16[128,512]{1,0:T(8,128)(2,1)} %refs_9_.1) | copy-start | bytes 393220
  0.0 3.4 %copy-start.4 = (bf16[128,512]{1,0:T(8,128)(2,1)S(1)}, bf16[128,512]{1,0:T(8,128)(2,1)}, u32[]{:S(2)}) copy-start(bf16[128,512]{1,0:T(8,128)(2,1)} %refs_8_.1) | copy-start | bytes 393220
  2.8 36.1 %copy-start.2 = (bf16[128,4096]{1,0:T(8,128)(2,1)S(1)}, bf16[128,4096]{1,0:T(8,128)(2,1)}, u32[]{:S(2)}) copy-start(bf16[128,4096]{1,0:T(8,128)(2,1)} %refs_1_.3) | copy-start | bytes 3145732
  2.8 36.0 %copy-start.7 = (s32[4,64]{1,0:T(4,128)S(1)}, s32[4,64]{1,0:T(4,128)}, u32[]{:S(2)}) copy-start(s32[4,64]{1,0:T(4,128)} %refs_1_.2) | copy-start | bytes 3076
  2.8 1.6 %collective-permute-start.8 = (bf16[12,64,128]{2,1,0:T(8,128)(2,1)S(1)}, bf16[12,64,128]{2,1,0:T(8,128)(2,1)S(1)}, u32[]{:S(2)}, u32[]{:S(2)}) collective-permute-start(bf16[12,64,128]{2,1,0:T(8,128)(2,1)S(1)} %get-tuple-element.81), channel_id=1, source_target_pairs={{0,1},{1,0},{2,3},{3,2},{4,5},{5,4},{6,7},{7,6},{8,9},{9,8},{10,11... | collective-permute-start | bytes 589832 | tf_op jit(solution)/shard_map/ppermute | solution.py:407
  4.9 11.4 %collective-permute-start.9 = (bf16[18,32,128]{2,1,0:T(8,128)(2,1)S(1)}, bf16[18,32,128]{2,1,0:T(8,128)(2,1)S(1)}, u32[]{:S(2)}, u32[]{:S(2)}) collective-permute-start(bf16[18,32,128]{2,1,0:T(8,128)(2,1)S(1)} %get-tuple-element.82.refs_0_), channel_id=1, source_target_pairs={{0,8},{1,9},{2,10},{3,11},{4,12},{5,13},{6,14},{7,15},{8,0},{9,1},... | collective-permute-start | bytes 442376 | tf_op jit(solution)/shard_map/ppermute | solution.py:407
  9.0 7.3 %collective-permute-start.10 = (bf16[18,32,128]{2,1,0:T(8,128)(2,1)S(1)}, bf16[18,32,128]{2,1,0:T(8,128)(2,1)S(1)}, u32[]{:S(2)}, u32[]{:S(2)}) collective-permute-start(bf16[18,32,128]{2,1,0:T(8,128)(2,1)S(1)} %get-tuple-element.86.refs_2_), channel_id=1, source_target_pairs={{0,2},{1,3},{2,0},{3,1},{4,6},{5,7},{6,4},{7,5},{8,10},{9,11},{10,... | collective-permute-start | bytes 442376 | tf_op jit(solution)/shard_map/ppermute | solution.py:407
  10.5 7.6 %collective-permute-start.12 = (bf16[128,1024]{1,0:T(8,128)(2,1)S(1)}, bf16[128,1024]{1,0:T(8,128)(2,1)S(1)}, u32[]{:S(2)}, u32[]{:S(2)}) collective-permute-start(bf16[128,1024]{1,0:T(8,128)(2,1)S(1)} %pad_maximum_fusion), channel_id=1, source_target_pairs={{0,1},{1,2},{2,3},{3,4},{4,5},{5,6},{6,7},{7,8},{8,9},{9,10},{10,1... | collective-permute-start | bytes 786440 | tf_op jit(solution)/shard_map/ppermute | solution.py:407
  17.4 9.7 %collective-permute-start.11 = (bf16[28,32,128]{2,1,0:T(8,128)(2,1)S(1)}, bf16[28,32,128]{2,1,0:T(8,128)(2,1)S(1)}, u32[]{:S(2)}, u32[]{:S(2)}) collective-permute-start(bf16[28,32,128]{2,1,0:T(8,128)(2,1)S(1)} %get-tuple-element.87.refs_0_), channel_id=1, source_target_pairs={{0,4},{1,5},{2,6},{3,7},{4,0},{5,1},{6,2},{7,3},{8,12},{9,13},{10,... | collective-permute-start | bytes 688136 | tf_op jit(solution)/shard_map/ppermute | solution.py:407
  18.1 8.9 %collective-permute-start.13 = (bf16[28,16,128]{2,1,0:T(8,128)(2,1)S(1)}, bf16[28,16,128]{2,1,0:T(8,128)(2,1)S(1)}, u32[]{:S(2)}, u32[]{:S(2)}) collective-permute-start(bf16[28,16,128]{2,1,0:T(8,128)(2,1)S(1)} %get-tuple-element.90.refs_0_), channel_id=1, source_target_pairs={{0,8},{1,9},{2,10},{3,11},{4,12},{5,13},{6,14},{7,15},{8,0},{9,1},... | collective-permute-start | bytes 344072 | tf_op jit(solution)/shard_map/ppermute | solution.py:407
  27.5 9.5 %collective-permute-start.14 = (bf16[46,32,128]{2,1,0:T(8,128)(2,1)S(1)}, bf16[46,32,128]{2,1,0:T(8,128)(2,1)S(1)}, u32[]{:S(2)}, u32[]{:S(2)}) collective-permute-start(bf16[46,32,128]{2,1,0:T(8,128)(2,1)S(1)} %merge.7.refs_3_), channel_id=1, source_target_pairs={{0,2},{1,3},{2,0},{3,1},{4,6},{5,7},{6,4},{7,5},{8,10},{9,11},{10,... | collective-permute-start | bytes 1130504 | tf_op jit(solution)/shard_map/ppermute | solution.py:407
  29.4 7.1 %collective-permute-start.15 = (bf16[46,16,128]{2,1,0:T(8,128)(2,1)S(1)}, bf16[46,16,128]{2,1,0:T(8,128)(2,1)S(1)}, u32[]{:S(2)}, u32[]{:S(2)}) collective-permute-start(bf16[46,16,128]{2,1,0:T(8,128)(2,1)S(1)} %merge.8.refs_0_), channel_id=1, source_target_pairs={{0,4},{1,5},{2,6},{3,7},{4,0},{5,1},{6,2},{7,3},{8,12},{9,13},{10,... | collective-permute-start | bytes 565256 | tf_op jit(solution)/shard_map/ppermute | solution.py:407
  32.5 5.7 %collective-permute-start.16 = (bf16[46,32,128]{2,1,0:T(8,128)(2,1)S(1)}, bf16[46,32,128]{2,1,0:T(8,128)(2,1)S(1)}, u32[]{:S(2)}, u32[]{:S(2)}) collective-permute-start(bf16[46,32,128]{2,1,0:T(8,128)(2,1)S(1)} %merge.7.refs_3_), channel_id=1, source_target_pairs={{0,1},{1,0},{2,3},{3,2},{4,5},{5,4},{6,7},{7,6},{8,9},{9,8},{10,11... | collective-permute-start | bytes 1130504 | tf_op jit(solution)/shard_map/ppermute | solution.py:407
  37.1 1.8 %collective-permute-start.17 = (bf16[46,32,128]{2,1,0:T(8,128)(2,1)S(1)}, bf16[46,32,128]{2,1,0:T(8,128)(2,1)S(1)}, u32[]{:S(2)}, u32[]{:S(2)}) collective-permute-start(bf16[46,32,128]{2,1,0:T(8,128)(2,1)S(1)} %collective-permute-done.14.refs_4_), channel_id=1, source_target_pairs={{0,1},{1,0},{2,3},{3,2},{4,5},{5,4},{6,7},{7,6},{8,9},{9,8},{10,11... | collective-permute-start | bytes 1130504 | tf_op jit(solution)/shard_map/ppermute | solution.py:407
  37.1 8.7 %collective-permute-start.18 = (bf16[64,16,128]{2,1,0:T(8,128)(2,1)S(1)}, bf16[64,16,128]{2,1,0:T(8,128)(2,1)S(1)}, u32[]{:S(2)}, u32[]{:S(2)}) collective-permute-start(bf16[64,16,128]{2,1,0:T(8,128)(2,1)S(1)} %merge.9.refs_2_), channel_id=1, source_target_pairs={{0,2},{1,3},{2,0},{3,1},{4,6},{5,7},{6,4},{7,5},{8,10},{9,11},{10,... | collective-permute-start | bytes 786440 | tf_op jit(solution)/shard_map/ppermute | solution.py:407
  38.0 7.8 %collective-permute-start.19 = (bf16[64,16,128]{2,1,0:T(8,128)(2,1)S(1)}, bf16[64,16,128]{2,1,0:T(8,128)(2,1)S(1)}, u32[]{:S(2)}, u32[]{:S(2)}) collective-permute-start(bf16[64,16,128]{2,1,0:T(8,128)(2,1)S(1)} %merge.9.refs_2_), channel_id=1, source_target_pairs={{0,1},{1,0},{2,3},{3,2},{4,5},{5,4},{6,7},{7,6},{8,9},{9,8},{10,11... | collective-permute-start | bytes 786440 | tf_op jit(solution)/shard_map/ppermute | solution.py:407
  45.9 5.5 %copy-start = (bf16[2048,512]{1,0:T(8,128)(2,1)S(1)}, bf16[2048,512]{1,0:T(8,128)(2,1)}, u32[]{:S(2)}) copy-start(bf16[2048,512]{1,0:T(8,128)(2,1)} %cache_k.1) | copy-start | bytes 6291460
  45.9 1.5 %collective-permute-start.20 = (bf16[64,16,128]{2,1,0:T(8,128)(2,1)S(1)}, bf16[64,16,128]{2,1,0:T(8,128)(2,1)S(1)}, u32[]{:S(2)}, u32[]{:S(2)}) collective-permute-start(bf16[64,16,128]{2,1,0:T(8,128)(2,1)S(1)} %collective-permute-done.18.refs_3_), channel_id=1, source_target_pairs={{0,1},{1,0},{2,3},{3,2},{4,5},{5,4},{6,7},{7,6},{8,9},{9,8},{10,11... | collective-permute-start | bytes 786440 | tf_op jit(solution)/shard_map/ppermute | solution.py:407

commit v11 on v10

--- a/solution.py
+++ b/solution.py
@@ -188,10 +188,9 @@
     me = lax.axis_index("ctx")
     even = lax.rem(me, 2) == 0
     count = jnp.int32(0)
-    table = blocks[...]
     for entry in range(ENTRIES):
         head = entry // NV
-        block = table[head, entry % NV]
+        block = blocks[head, entry % NV]
         owner = owner_of(block, per_device)
         mine = owner == me
         local = block - owner * per_device
@@ -228,7 +227,7 @@
     return pl.pallas_call(
         functools.partial(pack_kernel, cache_k.shape[0] // VBLOCK, limit),
         out_shape=(shape, shape),
-        in_specs=[WHOLE, ANY, ANY],
+        in_specs=[SMEM, ANY, ANY],
         out_specs=(WHOLE, WHOLE),
         scratch_shapes=[pltpu.SemaphoreType.DMA((limit, 2))],
         compiler_params=pltpu.CompilerParams(vmem_limit_bytes=16 * 2**20),
@@ -465,14 +464,12 @@
         job_b = job(*steps_b[at], mine_b, other_b, halved=near if at == 0 else 0)
         if at < len(far) - 1:
             mine_a, mine_b = merge([job_a, job_b])
-            if at == 0:
-                mine_b, before = lax.optimization_barrier((mine_b, before))
         else:
             (mine_a,), (mine_b,) = merge([job_a]), merge([job_b])
         other_a = swapped(mine_a, (far + [near])[at + 1])
         other_b = swapped(mine_b, far[at])
         if at < len(far) - 1:
-            other_a, other_b = lax.optimization_barrier((other_a, other_b))
+            other_a, other_b, before = lax.optimization_barrier((other_a, other_b, before))
     (mine_b,) = merge([job(*steps_b[-1], mine_b, other_b)])
     other_a, mine_b = lax.optimization_barrier((other_a, mine_b))
     other_b = swapped(mine_b, near)

time: 52.6 us -> 52.2 us (level)
  waiting for transfers between devices: 16.1 us -> 17.3 us
  Pallas kernels: 14.7 us -> 13.6 us
  starting transfers between devices: 18.7 us -> 18.1 us
    ppermute x13, waiting for transfers between devices: 16.1 us -> 17.3 us  [permuted(): return lax.ppermute(array, 'ctx', pairs)]
    pallas_call x1, Pallas kernels: 2.74 us -> 1.66 us  [pack(): pl.pallas_call(functools.partial(pack_kernel, cache_k.shape[0] // VBLOCK,...]
    ppermute x13, starting transfers between devices: 18.7 us -> 18.1 us  [permuted(): return lax.ppermute(array, 'ctx', pairs)]
  transfers between devices with their start and end apart: 13 -> 13, of which waited for: 7 -> 8; matrix products, arithmetic and copies ran while one was open for 2% -> 2% of each run, Pallas kernels for 13% -> 14%
where the time goes in v11:
time: 52.2 us; the launch traced here: 51.3 us
  starting transfers between devices  18.1 us (35%)
  waiting for transfers between devices  17.3 us (33%)
  Pallas kernels  13.6 us (26%)
  other arithmetic  0.98 us (2%)
  between operations  0.98 us (2%)
    ppermute x13, starting transfers between devices, permuted(): return lax.ppermute(array, 'ctx', pairs)  18.1 us
    ppermute x13, waiting for transfers between devices, permuted(): return lax.ppermute(array, 'ctx', pairs)  17.3 us
    pallas_call x2, Pallas kernels, attend_stage(): pl.pallas_call(functools.partial(stage_kernel, per_device, known, bit, ba...  8.89 us
    pallas_call x5, Pallas kernels, merged(): pl.pallas_call(functools.partial(merge_kernel, per_device, [job[:4] for j...  3.1 us
    pallas_call x1, Pallas kernels, pack(): pl.pallas_call(functools.partial(pack_kernel, cache_k.shape[0] // VBLOCK,...  1.66 us
  transfers between devices with their start and end apart: 13, of which 8 were waited for; matrix products, arithmetic and copies ran while one was open for 2% of the time, Pallas kernels for 14%

profile of v11, /device:TPU:0, one launch (start us, length us, event | category | flops | bytes accessed | tf_op | source)
XLA Modules:
  0.0 51.3 jit_solution(15323738485057969226)
XLA Ops:
  0.0 1.7 %pack.1 = (bf16[12,64,128]{2,1,0:T(8,128)(2,1)S(1)}, bf16[12,64,128]{2,1,0:T(8,128)(2,1)S(1)}) custom-call(s32[4,16]{1,0:T(4,128)} %refs_0_.3, bf16[2048,512]{1,0:T(8,128)(2,1)} %cache_k.1, bf16[2048,512]{1,0:T(8,128)(2,1)} %cache_v.1), custom_call_target="tpu_custom_call" | custom-call | tf_op jit(solution)/shard_map/pack/pallas_call | solution.py:227
  1.7 0.0 copy-start.2
  1.7 0.0 copy-start.7
  1.7 1.1 %collective-permute-start.8 = (bf16[12,64,128]{2,1,0:T(8,128)(2,1)S(1)}, bf16[12,64,128]{2,1,0:T(8,128)(2,1)S(1)}, u32[]{:S(2)}, u32[]{:S(2)}) collective-permute-start(bf16[12,64,128]{2,1,0:T(8,128)(2,1)S(1)} %get-tuple-element.80), channel_id=1, source_target_pairs={{0,1},{1,0},{2,3},{3,2},{4,5},{5,4},{6,7},{7,6},{8,9},{9,8},{10,11... | collective-permute-start | bytes 589832 | tf_op jit(solution)/shard_map/ppermute | solution.py:406
  2.8 0.0 copy-done.6
  2.9 0.1 xor.20
  2.9 0.0 copy-done.3
  2.9 0.0 copy-done.4
  3.0 0.9 %collective-permute-done.8.refs_1_ = bf16[12,64,128]{2,1,0:T(8,128)(2,1)S(1)} collective-permute-done((bf16[12,64,128]{2,1,0:T(8,128)(2,1)S(1)}, bf16[12,64,128]{2,1,0:T(8,128)(2,1)S(1)}, u32[]{:S(2)}, u32[]{:S(2)}) %collective-permute-start.8) | collective-permute-done | bytes 196640 | tf_op jit(solution)/shard_map/ppermute | solution.py:406
  3.9 0.6 %merge.5 = (bf16[18,32,128]{2,1,0:T(8,128)(2,1)S(1)}, bf16[18,32,128]{2,1,0:T(8,128)(2,1)S(1)}) custom-call(s32[4,16]{1,0:T(4,128)S(1)} %copy-done.6, bf16[12,64,128]{2,1,0:T(8,128)(2,1)S(1)} %get-tuple-element.79.refs_0_, bf16[12,64,128]{2,1,0:T(8,128)(2,1)S(1)} %collective-permute-done.8.refs_1_), custom_call_target="tpu_custom_call" | custom-call | tf_op jit(solution)/shard_map/merge/pallas_call | solution.py:277
  4.5 4.1 %collective-permute-start.9 = (bf16[18,32,128]{2,1,0:T(8,128)(2,1)S(1)}, bf16[18,32,128]{2,1,0:T(8,128)(2,1)S(1)}, u32[]{:S(2)}, u32[]{:S(2)}) collective-permute-start(bf16[18,32,128]{2,1,0:T(8,128)(2,1)S(1)} %get-tuple-element.81.refs_0_), channel_id=1, source_target_pairs={{0,8},{1,9},{2,10},{3,11},{4,12},{5,13},{6,14},{7,15},{8,0},{9,1},... | collective-permute-start | bytes 442376 | tf_op jit(solution)/shard_map/ppermute | solution.py:406
  8.6 1.5 %collective-permute-start.10 = (bf16[18,32,128]{2,1,0:T(8,128)(2,1)S(1)}, bf16[18,32,128]{2,1,0:T(8,128)(2,1)S(1)}, u32[]{:S(2)}, u32[]{:S(2)}) collective-permute-start(bf16[18,32,128]{2,1,0:T(8,128)(2,1)S(1)} %get-tuple-element.85.refs_2_), channel_id=1, source_target_pairs={{0,2},{1,3},{2,0},{3,1},{4,6},{5,7},{6,4},{7,5},{8,10},{9,11},{10,... | collective-permute-start | bytes 442376 | tf_op jit(solution)/shard_map/ppermute | solution.py:406
  10.1 0.0 copy-done.8
  10.1 0.2 convert_reduce_fusion
  10.3 1.5 %collective-permute-start.13 = (bf16[128,1024]{1,0:T(8,128)(2,1)S(1)}, bf16[128,1024]{1,0:T(8,128)(2,1)S(1)}, u32[]{:S(2)}, u32[]{:S(2)}) collective-permute-start(bf16[128,1024]{1,0:T(8,128)(2,1)S(1)} %pad_maximum_fusion), channel_id=1, source_target_pairs={{0,1},{1,2},{2,3},{3,4},{4,5},{5,6},{6,7},{7,8},{8,9},{9,10},{10,1... | collective-permute-start | bytes 786440 | tf_op jit(solution)/shard_map/ppermute | solution.py:406
  11.8 0.0 copy-done.9
  11.8 0.7 %compare_reduce_fusion = pred[]{:T(512)} fusion(s32[6,16]{1,0:T(8,128)S(1)} %convert_reduce_fusion, s32[6]{0:T(128)S(1)} %copy-done.9), kind=kLoop, calls=%fused_computation.4 | loop fusion | flops 191 | bytes 409 | tf_op jit(solution)/shard_map/reduce_and | solution.py:419
  13.2 2.7 %collective-permute-done.9.refs_1_ = bf16[18,32,128]{2,1,0:T(8,128)(2,1)S(1)} collective-permute-done((bf16[18,32,128]{2,1,0:T(8,128)(2,1)S(1)}, bf16[18,32,128]{2,1,0:T(8,128)(2,1)S(1)}, u32[]{:S(2)}, u32[]{:S(2)}) %collective-permute-start.9) | collective-permute-done | bytes 147488 | tf_op jit(solution)/shard_map/ppermute | solution.py:406
  15.9 0.0 collective-permute-done.10.refs_3_
  15.9 1.0 %merge.6 = (bf16[28,32,128]{2,1,0:T(8,128)(2,1)S(1)}, bf16[28,16,128]{2,1,0:T(8,128)(2,1)S(1)}) custom-call(s32[4,16]{1,0:T(4,128)S(1)} %copy-done.6, bf16[18,32,128]{2,1,0:T(8,128)(2,1)S(1)} %get-tuple-element.81.refs_0_, bf16[18,32,128]{2,1,0:T(8,128)(2,1)S(1)} %collective-permute-done.9.refs_1_, bf16[18,32,128]{2,1,0:T(8,128)(2,1)S(1)} %get-tuple-element.85.refs_2_, ...), custom_call_target="tpu_custom_call" | custom-call | tf_op jit(solution)/shard_map/merge/pallas_call | solution.py:277
  16.9 0.8 %collective-permute-start.11 = (bf16[28,32,128]{2,1,0:T(8,128)(2,1)S(1)}, bf16[28,32,128]{2,1,0:T(8,128)(2,1)S(1)}, u32[]{:S(2)}, u32[]{:S(2)}) collective-permute-start(bf16[28,32,128]{2,1,0:T(8,128)(2,1)S(1)} %get-tuple-element.86.refs_0_), channel_id=1, source_target_pairs={{0,4},{1,5},{2,6},{3,7},{4,0},{5,1},{6,2},{7,3},{8,12},{9,13},{10,... | collective-permute-start | bytes 688136 | tf_op jit(solution)/shard_map/ppermute | solution.py:406
  17.7 3.4 %collective-permute-start.12 = (bf16[28,16,128]{2,1,0:T(8,128)(2,1)S(1)}, bf16[28,16,128]{2,1,0:T(8,128)(2,1)S(1)}, u32[]{:S(2)}, u32[]{:S(2)}) collective-permute-start(bf16[28,16,128]{2,1,0:T(8,128)(2,1)S(1)} %get-tuple-element.87.refs_0_), channel_id=1, source_target_pairs={{0,8},{1,9},{2,10},{3,11},{4,12},{5,13},{6,14},{7,15},{8,0},{9,1},... | collective-permute-start | bytes 344072 | tf_op jit(solution)/shard_map/ppermute | solution.py:406
  21.1 4.1 %collective-permute-done.12.refs_1_ = bf16[28,16,128]{2,1,0:T(8,128)(2,1)S(1)} collective-permute-done((bf16[28,16,128]{2,1,0:T(8,128)(2,1)S(1)}, bf16[28,16,128]{2,1,0:T(8,128)(2,1)S(1)}, u32[]{:S(2)}, u32[]{:S(2)}) %collective-permute-start.12) | collective-permute-done | bytes 114720 | tf_op jit(solution)/shard_map/ppermute | solution.py:406
  25.2 0.0 collective-permute-done.13.refs_7_
  25.2 1.3 %collective-permute-done.11.refs_1_ = bf16[28,32,128]{2,1,0:T(8,128)(2,1)S(1)} collective-permute-done((bf16[28,32,128]{2,1,0:T(8,128)(2,1)S(1)}, bf16[28,32,128]{2,1,0:T(8,128)(2,1)S(1)}, u32[]{:S(2)}, u32[]{:S(2)}) %collective-permute-start.11) | collective-permute-done | bytes 229408 | tf_op jit(solution)/shard_map/ppermute | solution.py:406
  26.6 0.5 %merge.7.refs_3_ = bf16[46,32,128]{2,1,0:T(8,128)(2,1)S(1)} custom-call(s32[4,16]{1,0:T(4,128)S(1)} %copy-done.6, bf16[28,32,128]{2,1,0:T(8,128)(2,1)S(1)} %get-tuple-element.86.refs_0_, bf16[28,32,128]{2,1,0:T(8,128)(2,1)S(1)} %collective-permute-done.11.refs_1_), custom_call_target="tpu_custom_call" | custom-call | tf_op jit(solution)/shard_map/merge/pallas_call | solution.py:277
  27.1 1.3 %collective-permute-start.14 = (bf16[46,32,128]{2,1,0:T(8,128)(2,1)S(1)}, bf16[46,32,128]{2,1,0:T(8,128)(2,1)S(1)}, u32[]{:S(2)}, u32[]{:S(2)}) collective-permute-start(bf16[46,32,128]{2,1,0:T(8,128)(2,1)S(1)} %merge.7.refs_3_), channel_id=1, source_target_pairs={{0,2},{1,3},{2,0},{3,1},{4,6},{5,7},{6,4},{7,5},{8,10},{9,11},{10,... | collective-permute-start | bytes 1130504 | tf_op jit(solution)/shard_map/ppermute | solution.py:406
  28.4 0.5 merge.8.refs_0_
  29.0 3.1 %collective-permute-start.15 = (bf16[46,16,128]{2,1,0:T(8,128)(2,1)S(1)}, bf16[46,16,128]{2,1,0:T(8,128)(2,1)S(1)}, u32[]{:S(2)}, u32[]{:S(2)}) collective-permute-start(bf16[46,16,128]{2,1,0:T(8,128)(2,1)S(1)} %merge.8.refs_0_), channel_id=1, source_target_pairs={{0,4},{1,5},{2,6},{3,7},{4,0},{5,1},{6,2},{7,3},{8,12},{9,13},{10,... | collective-permute-start | bytes 565256 | tf_op jit(solution)/shard_map/ppermute | solution.py:406
  32.1 0.0 collective-permute-start.16
  32.1 4.0 %collective-permute-done.15.refs_1_ = bf16[46,16,128]{2,1,0:T(8,128)(2,1)S(1)} collective-permute-done((bf16[46,16,128]{2,1,0:T(8,128)(2,1)S(1)}, bf16[46,16,128]{2,1,0:T(8,128)(2,1)S(1)}, u32[]{:S(2)}, u32[]{:S(2)}) %collective-permute-start.15) | collective-permute-done | bytes 188448 | tf_op jit(solution)/shard_map/ppermute | solution.py:406
  36.1 0.5 merge.9.refs_2_
  36.6 0.0 collective-permute-done.14.refs_4_
  36.6 0.1 collective-permute-start.17
  36.7 0.9 %collective-permute-start.18 = (bf16[64,16,128]{2,1,0:T(8,128)(2,1)S(1)}, bf16[64,16,128]{2,1,0:T(8,128)(2,1)S(1)}, u32[]{:S(2)}, u32[]{:S(2)}) collective-permute-start(bf16[64,16,128]{2,1,0:T(8,128)(2,1)S(1)} %merge.9.refs_2_), channel_id=1, source_target_pairs={{0,2},{1,3},{2,0},{3,1},{4,6},{5,7},{6,4},{7,5},{8,10},{9,11},{10,... | collective-permute-start | bytes 786440 | tf_op jit(solution)/shard_map/ppermute | solution.py:406
  37.6 0.2 collective-permute-start.19
  37.8 0.0 collective-permute-done.16.refs_5_
  37.8 0.6 %collective-permute-done.17.refs_6_ = bf16[46,32,128]{2,1,0:T(8,128)(2,1)S(1)} collective-permute-done((bf16[46,32,128]{2,1,0:T(8,128)(2,1)S(1)}, bf16[46,32,128]{2,1,0:T(8,128)(2,1)S(1)}, u32[]{:S(2)}, u32[]{:S(2)}) %collective-permute-start.17) | collective-permute-done | bytes 376864 | tf_op jit(solution)/shard_map/ppermute | solution.py:406
  38.4 0.0 copy-done.2
  38.4 0.0 copy-done.7
  38.4 4.9 %attend_first.1 = (f32[4096,128]{1,0:T(8,128)S(1)}, f32[4096,128]{1,0:T(8,128)S(1)}, f32[4096,128]{1,0:T(8,128)S(1)}) custom-call(s32[4,16]{1,0:T(4,128)S(1)} %copy-done.6, s32[4,64]{1,0:T(4,128)S(1)} %copy-done.7, bf16[128,4096]{1,0:T(8,128)(2,1)S(1)} %copy-done.2, bf16[46,32,128]{2,1,0:T(8,128)(2,1)S(1)} %merge.7.refs_3_, ...), custom_call_target="tpu_custom_call" | custom-call | flops 1048576 | bytes 1048576 | tf_op jit(solution)/shard_map/attend_first/pallas_call | solution.py:393
  43.3 2.1 %collective-permute-done.18.refs_3_ = bf16[64,16,128]{2,1,0:T(8,128)(2,1)S(1)} collective-permute-done((bf16[64,16,128]{2,1,0:T(8,128)(2,1)S(1)}, bf16[64,16,128]{2,1,0:T(8,128)(2,1)S(1)}, u32[]{:S(2)}, u32[]{:S(2)}) %collective-permute-start.18) | collective-permute-done | bytes 262176 | tf_op jit(solution)/shard_map/ppermute | solution.py:406
  45.4 0.0 collective-permute-start.20
  45.4 0.0 collective-permute-done.19.refs_4_
  45.4 1.5 %collective-permute-done.20.refs_5_ = bf16[64,16,128]{2,1,0:T(8,128)(2,1)S(1)} collective-permute-done((bf16[64,16,128]{2,1,0:T(8,128)(2,1)S(1)}, bf16[64,16,128]{2,1,0:T(8,128)(2,1)S(1)}, u32[]{:S(2)}, u32[]{:S(2)}) %collective-permute-start.20) | collective-permute-done | bytes 262176 | tf_op jit(solution)/shard_map/ppermute | solution.py:406
  47.0 4.0 %attend_last.1 = bf16[128,4096]{1,0:T(8,128)(2,1)} custom-call(s32[4,16]{1,0:T(4,128)S(1)} %copy-done.6, bf16[128,4096]{1,0:T(8,128)(2,1)S(1)} %copy-done.2, bf16[64,16,128]{2,1,0:T(8,128)(2,1)S(1)} %merge.9.refs_2_, bf16[64,16,128]{2,1,0:T(8,128)(2,1)S(1)} %collective-permute-done.18.refs_3_, bf16[64,16,128]{2,1,0:T(8,128)(2,1)S(1)} %collective-permute-done.19.refs_4_, ...), custom_call_target="tpu_custom_call" | custom-call | flops 1048576 | bytes 1048576 | tf_op jit(solution)/shard_map/attend_last/pallas_call | solution.py:393
  50.9 0.0 copy-done
  51.0 0.2 while.9
  (9 shorter events, 0.0 us)
Async XLA Ops:
  0.0 10.1 %copy-start.8 = (s32[6]{0:T(128)S(1)}, s32[6]{0:T(128)}, u32[]{:S(2)}) copy-start(s32[6]{0:T(128)} %constant.30) | copy-start | bytes 76
  0.0 11.8 %copy-start.9 = (s32[6]{0:T(128)S(1)}, s32[6]{0:T(128)}, u32[]{:S(2)}) copy-start(s32[6]{0:T(128)} %constant.29.clone) | copy-start | bytes 76
  0.0 2.8 %copy-start.6 = (s32[4,16]{1,0:T(4,128)S(1)}, s32[4,16]{1,0:T(4,128)}, u32[]{:S(2)}) copy-start(s32[4,16]{1,0:T(4,128)} %refs_0_.3) | copy-start | bytes 772
  0.0 2.9 %copy-start.3 = (bf16[128,512]{1,0:T(8,128)(2,1)S(1)}, bf16[128,512]{1,0:T(8,128)(2,1)}, u32[]{:S(2)}) copy-start(bf16[128,512]{1,0:T(8,128)(2,1)} %refs_9_.1) | copy-start | bytes 393220
  0.0 2.9 %copy-start.4 = (bf16[128,512]{1,0:T(8,128)(2,1)S(1)}, bf16[128,512]{1,0:T(8,128)(2,1)}, u32[]{:S(2)}) copy-start(bf16[128,512]{1,0:T(8,128)(2,1)} %refs_8_.1) | copy-start | bytes 393220
  1.7 36.7 %copy-start.2 = (bf16[128,4096]{1,0:T(8,128)(2,1)S(1)}, bf16[128,4096]{1,0:T(8,128)(2,1)}, u32[]{:S(2)}) copy-start(bf16[128,4096]{1,0:T(8,128)(2,1)} %refs_1_.3) | copy-start | bytes 3145732
  1.7 36.7 %copy-start.7 = (s32[4,64]{1,0:T(4,128)S(1)}, s32[4,64]{1,0:T(4,128)}, u32[]{:S(2)}) copy-start(s32[4,64]{1,0:T(4,128)} %refs_1_.2) | copy-start | bytes 3076
  1.7 2.2 %collective-permute-start.8 = (bf16[12,64,128]{2,1,0:T(8,128)(2,1)S(1)}, bf16[12,64,128]{2,1,0:T(8,128)(2,1)S(1)}, u32[]{:S(2)}, u32[]{:S(2)}) collective-permute-start(bf16[12,64,128]{2,1,0:T(8,128)(2,1)S(1)} %get-tuple-element.80), channel_id=1, source_target_pairs={{0,1},{1,0},{2,3},{3,2},{4,5},{5,4},{6,7},{7,6},{8,9},{9,8},{10,11... | collective-permute-start | bytes 589832 | tf_op jit(solution)/shard_map/ppermute | solution.py:406
  4.5 11.4 %collective-permute-start.9 = (bf16[18,32,128]{2,1,0:T(8,128)(2,1)S(1)}, bf16[18,32,128]{2,1,0:T(8,128)(2,1)S(1)}, u32[]{:S(2)}, u32[]{:S(2)}) collective-permute-start(bf16[18,32,128]{2,1,0:T(8,128)(2,1)S(1)} %get-tuple-element.81.refs_0_), channel_id=1, source_target_pairs={{0,8},{1,9},{2,10},{3,11},{4,12},{5,13},{6,14},{7,15},{8,0},{9,1},... | collective-permute-start | bytes 442376 | tf_op jit(solution)/shard_map/ppermute | solution.py:406
  8.6 7.3 %collective-permute-start.10 = (bf16[18,32,128]{2,1,0:T(8,128)(2,1)S(1)}, bf16[18,32,128]{2,1,0:T(8,128)(2,1)S(1)}, u32[]{:S(2)}, u32[]{:S(2)}) collective-permute-start(bf16[18,32,128]{2,1,0:T(8,128)(2,1)S(1)} %get-tuple-element.85.refs_2_), channel_id=1, source_target_pairs={{0,2},{1,3},{2,0},{3,1},{4,6},{5,7},{6,4},{7,5},{8,10},{9,11},{10,... | collective-permute-start | bytes 442376 | tf_op jit(solution)/shard_map/ppermute | solution.py:406
  10.3 14.9 %collective-permute-start.13 = (bf16[128,1024]{1,0:T(8,128)(2,1)S(1)}, bf16[128,1024]{1,0:T(8,128)(2,1)S(1)}, u32[]{:S(2)}, u32[]{:S(2)}) collective-permute-start(bf16[128,1024]{1,0:T(8,128)(2,1)S(1)} %pad_maximum_fusion), channel_id=1, source_target_pairs={{0,1},{1,2},{2,3},{3,4},{4,5},{5,6},{6,7},{7,8},{8,9},{9,10},{10,1... | collective-permute-start | bytes 786440 | tf_op jit(solution)/shard_map/ppermute | solution.py:406
  16.9 9.7 %collective-permute-start.11 = (bf16[28,32,128]{2,1,0:T(8,128)(2,1)S(1)}, bf16[28,32,128]{2,1,0:T(8,128)(2,1)S(1)}, u32[]{:S(2)}, u32[]{:S(2)}) collective-permute-start(bf16[28,32,128]{2,1,0:T(8,128)(2,1)S(1)} %get-tuple-element.86.refs_0_), channel_id=1, source_target_pairs={{0,4},{1,5},{2,6},{3,7},{4,0},{5,1},{6,2},{7,3},{8,12},{9,13},{10,... | collective-permute-start | bytes 688136 | tf_op jit(solution)/shard_map/ppermute | solution.py:406
  17.7 7.5 %collective-permute-start.12 = (bf16[28,16,128]{2,1,0:T(8,128)(2,1)S(1)}, bf16[28,16,128]{2,1,0:T(8,128)(2,1)S(1)}, u32[]{:S(2)}, u32[]{:S(2)}) collective-permute-start(bf16[28,16,128]{2,1,0:T(8,128)(2,1)S(1)} %get-tuple-element.87.refs_0_), channel_id=1, source_target_pairs={{0,8},{1,9},{2,10},{3,11},{4,12},{5,13},{6,14},{7,15},{8,0},{9,1},... | collective-permute-start | bytes 344072 | tf_op jit(solution)/shard_map/ppermute | solution.py:406
  27.1 9.5 %collective-permute-start.14 = (bf16[46,32,128]{2,1,0:T(8,128)(2,1)S(1)}, bf16[46,32,128]{2,1,0:T(8,128)(2,1)S(1)}, u32[]{:S(2)}, u32[]{:S(2)}) collective-permute-start(bf16[46,32,128]{2,1,0:T(8,128)(2,1)S(1)} %merge.7.refs_3_), channel_id=1, source_target_pairs={{0,2},{1,3},{2,0},{3,1},{4,6},{5,7},{6,4},{7,5},{8,10},{9,11},{10,... | collective-permute-start | bytes 1130504 | tf_op jit(solution)/shard_map/ppermute | solution.py:406
  29.0 7.2 %collective-permute-start.15 = (bf16[46,16,128]{2,1,0:T(8,128)(2,1)S(1)}, bf16[46,16,128]{2,1,0:T(8,128)(2,1)S(1)}, u32[]{:S(2)}, u32[]{:S(2)}) collective-permute-start(bf16[46,16,128]{2,1,0:T(8,128)(2,1)S(1)} %merge.8.refs_0_), channel_id=1, source_target_pairs={{0,4},{1,5},{2,6},{3,7},{4,0},{5,1},{6,2},{7,3},{8,12},{9,13},{10,... | collective-permute-start | bytes 565256 | tf_op jit(solution)/shard_map/ppermute | solution.py:406
  32.1 5.7 %collective-permute-start.16 = (bf16[46,32,128]{2,1,0:T(8,128)(2,1)S(1)}, bf16[46,32,128]{2,1,0:T(8,128)(2,1)S(1)}, u32[]{:S(2)}, u32[]{:S(2)}) collective-permute-start(bf16[46,32,128]{2,1,0:T(8,128)(2,1)S(1)} %merge.7.refs_3_), channel_id=1, source_target_pairs={{0,1},{1,0},{2,3},{3,2},{4,5},{5,4},{6,7},{7,6},{8,9},{9,8},{10,11... | collective-permute-start | bytes 1130504 | tf_op jit(solution)/shard_map/ppermute | solution.py:406
  36.6 1.8 %collective-permute-start.17 = (bf16[46,32,128]{2,1,0:T(8,128)(2,1)S(1)}, bf16[46,32,128]{2,1,0:T(8,128)(2,1)S(1)}, u32[]{:S(2)}, u32[]{:S(2)}) collective-permute-start(bf16[46,32,128]{2,1,0:T(8,128)(2,1)S(1)} %collective-permute-done.14.refs_4_), channel_id=1, source_target_pairs={{0,1},{1,0},{2,3},{3,2},{4,5},{5,4},{6,7},{7,6},{8,9},{9,8},{10,11... | collective-permute-start | bytes 1130504 | tf_op jit(solution)/shard_map/ppermute | solution.py:406
  36.7 8.7 %collective-permute-start.18 = (bf16[64,16,128]{2,1,0:T(8,128)(2,1)S(1)}, bf16[64,16,128]{2,1,0:T(8,128)(2,1)S(1)}, u32[]{:S(2)}, u32[]{:S(2)}) collective-permute-start(bf16[64,16,128]{2,1,0:T(8,128)(2,1)S(1)} %merge.9.refs_2_), channel_id=1, source_target_pairs={{0,2},{1,3},{2,0},{3,1},{4,6},{5,7},{6,4},{7,5},{8,10},{9,11},{10,... | collective-permute-start | bytes 786440 | tf_op jit(solution)/shard_map/ppermute | solution.py:406
  37.6 7.9 %collective-permute-start.19 = (bf16[64,16,128]{2,1,0:T(8,128)(2,1)S(1)}, bf16[64,16,128]{2,1,0:T(8,128)(2,1)S(1)}, u32[]{:S(2)}, u32[]{:S(2)}) collective-permute-start(bf16[64,16,128]{2,1,0:T(8,128)(2,1)S(1)} %merge.9.refs_2_), channel_id=1, source_target_pairs={{0,1},{1,0},{2,3},{3,2},{4,5},{5,4},{6,7},{7,6},{8,9},{9,8},{10,11... | collective-permute-start | bytes 786440 | tf_op jit(solution)/shard_map/ppermute | solution.py:406
  45.4 5.5 %copy-start = (bf16[2048,512]{1,0:T(8,128)(2,1)S(1)}, bf16[2048,512]{1,0:T(8,128)(2,1)}, u32[]{:S(2)}) copy-start(bf16[2048,512]{1,0:T(8,128)(2,1)} %cache_k.1) | copy-start | bytes 6291460
  45.4 1.5 %collective-permute-start.20 = (bf16[64,16,128]{2,1,0:T(8,128)(2,1)S(1)}, bf16[64,16,128]{2,1,0:T(8,128)(2,1)S(1)}, u32[]{:S(2)}, u32[]{:S(2)}) collective-permute-start(bf16[64,16,128]{2,1,0:T(8,128)(2,1)S(1)} %collective-permute-done.18.refs_3_), channel_id=1, source_target_pairs={{0,1},{1,0},{2,3},{3,2},{4,5},{5,4},{6,7},{7,6},{8,9},{9,8},{10,11... | collective-permute-start | bytes 786440 | tf_op jit(solution)/shard_map/ppermute | solution.py:406

commit v12 on v11

--- a/solution.py
+++ b/solution.py
@@ -174,7 +174,7 @@
 
 def room(share):
     mean = ENTRIES * share
-    wide = mean + 3.0 * math.sqrt(mean * (1.0 - share)) + 1.5
+    wide = mean + 3.2 * math.sqrt(mean * (1.0 - share)) + 2.0
     return min(ENTRIES + 1, math.ceil(wide))
 
 
@@ -421,8 +421,12 @@
 
 def general(queries, bands, cache_k, cache_v, blocks, offsets, bits):
     keys, values = owned_blocks(blocks, cache_k, cache_v)
-    for bit in bits:
-        keys, values = keys + swapped(keys, bit), values + swapped(values, bit)
+    even = lax.axis_index("ctx") % 2 == 0
+    mine = jnp.where(even, keys, values) + swapped(jnp.where(even, values, keys), 1)
+    for bit in bits[1:]:
+        mine = mine + swapped(mine, bit)
+    twin = swapped(mine, 1)
+    keys, values = jnp.where(even, mine, twin), jnp.where(even, twin, mine)
     keys = keys.reshape(KVH, NV * VBLOCK, HD)
     values = values.reshape(KVH, NV * VBLOCK, HD)
     before, own_k, own_v = bands

time: 52.2 us -> 53.3 us (1.021)
  the two profiles are of different devices: /device:TPU:0 before, /device:TPU:9 now
where the time goes in v12:
time: 53.3 us; the launch traced here: 53.1 us
  waiting for transfers between devices  19.4 us (36%)
  starting transfers between devices  17.2 us (32%)
  Pallas kernels  14.2 us (27%)
  other arithmetic  0.98 us (2%)
  between operations  0.98 us (2%)
    ppermute x13, waiting for transfers between devices, permuted(): return lax.ppermute(array, 'ctx', pairs)  19.4 us
    ppermute x13, starting transfers between devices, permuted(): return lax.ppermute(array, 'ctx', pairs)  17.2 us
    pallas_call x2, Pallas kernels, attend_stage(): pl.pallas_call(functools.partial(stage_kernel, per_device, known, bit, ba...  8.9 us
    pallas_call x5, Pallas kernels, merged(): pl.pallas_call(functools.partial(merge_kernel, per_device, [job[:4] for j...  3.09 us
    pallas_call x1, Pallas kernels, pack(): pl.pallas_call(functools.partial(pack_kernel, cache_k.shape[0] // VBLOCK,...  2.2 us
  transfers between devices with their start and end apart: 13, of which 8 were waited for; matrix products, arithmetic and copies ran while one was open for 2% of the time, Pallas kernels for 13%

profile of v12, /device:TPU:9, one launch (start us, length us, event | category | flops | bytes accessed | tf_op | source)
XLA Modules:
  0.0 53.1 jit_solution(13596343938681644727)
XLA Ops:
  0.0 0.0 copy-start.2
  0.0 0.0 copy-start.3
  0.0 2.2 %pack.1 = (bf16[13,64,128]{2,1,0:T(8,128)(2,1)S(1)}, bf16[13,64,128]{2,1,0:T(8,128)(2,1)S(1)}) custom-call(s32[4,16]{1,0:T(4,128)} %refs_0_.3, bf16[2048,512]{1,0:T(8,128)(2,1)} %cache_k.1, bf16[2048,512]{1,0:T(8,128)(2,1)} %cache_v.1), custom_call_target="tpu_custom_call" | custom-call | tf_op jit(solution)/shard_map/pack/pallas_call | solution.py:227
  2.2 0.0 copy-start.1
  2.3 0.0 copy-start.6
  2.3 0.9 %collective-permute-start.5 = (bf16[13,64,128]{2,1,0:T(8,128)(2,1)S(1)}, bf16[13,64,128]{2,1,0:T(8,128)(2,1)S(1)}, u32[]{:S(2)}, u32[]{:S(2)}) collective-permute-start(bf16[13,64,128]{2,1,0:T(8,128)(2,1)S(1)} %get-tuple-element.80), channel_id=1, source_target_pairs={{0,1},{1,0},{2,3},{3,2},{4,5},{5,4},{6,7},{7,6},{8,9},{9,8},{10,11... | collective-permute-start | bytes 638984 | tf_op jit(solution)/shard_map/ppermute | solution.py:406
  3.1 0.0 copy-done.5
  3.1 0.1 xor.20
  3.2 0.0 copy-done.2
  3.2 0.0 copy-done.3
  3.3 0.9 %collective-permute-done.5.refs_1_ = bf16[13,64,128]{2,1,0:T(8,128)(2,1)S(1)} collective-permute-done((bf16[13,64,128]{2,1,0:T(8,128)(2,1)S(1)}, bf16[13,64,128]{2,1,0:T(8,128)(2,1)S(1)}, u32[]{:S(2)}, u32[]{:S(2)}) %collective-permute-start.5) | collective-permute-done | bytes 213024 | tf_op jit(solution)/shard_map/ppermute | solution.py:406
  4.2 0.6 %merge.5 = (bf16[19,32,128]{2,1,0:T(8,128)(2,1)S(1)}, bf16[19,32,128]{2,1,0:T(8,128)(2,1)S(1)}) custom-call(s32[4,16]{1,0:T(4,128)S(1)} %copy-done.5, bf16[13,64,128]{2,1,0:T(8,128)(2,1)S(1)} %get-tuple-element.79.refs_0_, bf16[13,64,128]{2,1,0:T(8,128)(2,1)S(1)} %collective-permute-done.5.refs_1_), custom_call_target="tpu_custom_call" | custom-call | tf_op jit(solution)/shard_map/merge/pallas_call | solution.py:277
  4.8 2.4 %collective-permute-start.6 = (bf16[19,32,128]{2,1,0:T(8,128)(2,1)S(1)}, bf16[19,32,128]{2,1,0:T(8,128)(2,1)S(1)}, u32[]{:S(2)}, u32[]{:S(2)}) collective-permute-start(bf16[19,32,128]{2,1,0:T(8,128)(2,1)S(1)} %get-tuple-element.81.refs_0_), channel_id=1, source_target_pairs={{0,8},{1,9},{2,10},{3,11},{4,12},{5,13},{6,14},{7,15},{8,0},{9,1},... | collective-permute-start | bytes 466952 | tf_op jit(solution)/shard_map/ppermute | solution.py:406
  7.2 1.1 %collective-permute-start.7 = (bf16[19,32,128]{2,1,0:T(8,128)(2,1)S(1)}, bf16[19,32,128]{2,1,0:T(8,128)(2,1)S(1)}, u32[]{:S(2)}, u32[]{:S(2)}) collective-permute-start(bf16[19,32,128]{2,1,0:T(8,128)(2,1)S(1)} %get-tuple-element.85.refs_2_), channel_id=1, source_target_pairs={{0,2},{1,3},{2,0},{3,1},{4,6},{5,7},{6,4},{7,5},{8,10},{9,11},{10,... | collective-permute-start | bytes 466952 | tf_op jit(solution)/shard_map/ppermute | solution.py:406
  8.3 0.0 copy-done.7
  8.3 0.2 convert_reduce_fusion
  8.5 3.1 %collective-permute-start.10 = (bf16[128,1024]{1,0:T(8,128)(2,1)S(1)}, bf16[128,1024]{1,0:T(8,128)(2,1)S(1)}, u32[]{:S(2)}, u32[]{:S(2)}) collective-permute-start(bf16[128,1024]{1,0:T(8,128)(2,1)S(1)} %pad_maximum_fusion), channel_id=1, source_target_pairs={{0,1},{1,2},{2,3},{3,4},{4,5},{5,6},{6,7},{7,8},{8,9},{9,10},{10,1... | collective-permute-start | bytes 786440 | tf_op jit(solution)/shard_map/ppermute | solution.py:406
  11.6 0.0 copy-done.8
  11.6 0.7 %compare_reduce_fusion = pred[]{:T(512)} fusion(s32[6,16]{1,0:T(8,128)S(1)} %convert_reduce_fusion, s32[6]{0:T(128)S(1)} %copy-done.8), kind=kLoop, calls=%fused_computation.8 | loop fusion | flops 191 | bytes 409 | tf_op jit(solution)/shard_map/reduce_and | solution.py:419
  13.0 1.2 %collective-permute-done.6.refs_1_ = bf16[19,32,128]{2,1,0:T(8,128)(2,1)S(1)} collective-permute-done((bf16[19,32,128]{2,1,0:T(8,128)(2,1)S(1)}, bf16[19,32,128]{2,1,0:T(8,128)(2,1)S(1)}, u32[]{:S(2)}, u32[]{:S(2)}) %collective-permute-start.6) | collective-permute-done | bytes 155680 | tf_op jit(solution)/shard_map/ppermute | solution.py:406
  14.2 0.0 collective-permute-done.7.refs_3_
  14.2 1.0 %merge.6 = (bf16[30,32,128]{2,1,0:T(8,128)(2,1)S(1)}, bf16[30,16,128]{2,1,0:T(8,128)(2,1)S(1)}) custom-call(s32[4,16]{1,0:T(4,128)S(1)} %copy-done.5, bf16[19,32,128]{2,1,0:T(8,128)(2,1)S(1)} %get-tuple-element.81.refs_0_, bf16[19,32,128]{2,1,0:T(8,128)(2,1)S(1)} %collective-permute-done.6.refs_1_, bf16[19,32,128]{2,1,0:T(8,128)(2,1)S(1)} %get-tuple-element.85.refs_2_, ...), custom_call_target="tpu_custom_call" | custom-call | tf_op jit(solution)/shard_map/merge/pallas_call | solution.py:277
  15.2 0.7 %collective-permute-start.8 = (bf16[30,32,128]{2,1,0:T(8,128)(2,1)S(1)}, bf16[30,32,128]{2,1,0:T(8,128)(2,1)S(1)}, u32[]{:S(2)}, u32[]{:S(2)}) collective-permute-start(bf16[30,32,128]{2,1,0:T(8,128)(2,1)S(1)} %get-tuple-element.86.refs_0_), channel_id=1, source_target_pairs={{0,4},{1,5},{2,6},{3,7},{4,0},{5,1},{6,2},{7,3},{8,12},{9,13},{10,... | collective-permute-start | bytes 737288 | tf_op jit(solution)/shard_map/ppermute | solution.py:406
  15.9 2.6 %collective-permute-start.9 = (bf16[30,16,128]{2,1,0:T(8,128)(2,1)S(1)}, bf16[30,16,128]{2,1,0:T(8,128)(2,1)S(1)}, u32[]{:S(2)}, u32[]{:S(2)}) collective-permute-start(bf16[30,16,128]{2,1,0:T(8,128)(2,1)S(1)} %get-tuple-element.87.refs_0_), channel_id=1, source_target_pairs={{0,8},{1,9},{2,10},{3,11},{4,12},{5,13},{6,14},{7,15},{8,0},{9,1},... | collective-permute-start | bytes 368648 | tf_op jit(solution)/shard_map/ppermute | solution.py:406
  18.5 0.0 collective-permute-done.10.refs_7_
  18.5 8.5 %collective-permute-done.9.refs_1_ = bf16[30,16,128]{2,1,0:T(8,128)(2,1)S(1)} collective-permute-done((bf16[30,16,128]{2,1,0:T(8,128)(2,1)S(1)}, bf16[30,16,128]{2,1,0:T(8,128)(2,1)S(1)}, u32[]{:S(2)}, u32[]{:S(2)}) %collective-permute-start.9) | collective-permute-done | bytes 122912 | tf_op jit(solution)/shard_map/ppermute | solution.py:406
  26.9 0.0 collective-permute-done.8.refs_1_
  26.9 0.5 merge.7.refs_3_
  27.4 0.9 %collective-permute-start.11 = (bf16[47,32,128]{2,1,0:T(8,128)(2,1)S(1)}, bf16[47,32,128]{2,1,0:T(8,128)(2,1)S(1)}, u32[]{:S(2)}, u32[]{:S(2)}) collective-permute-start(bf16[47,32,128]{2,1,0:T(8,128)(2,1)S(1)} %merge.7.refs_3_), channel_id=1, source_target_pairs={{0,2},{1,3},{2,0},{3,1},{4,6},{5,7},{6,4},{7,5},{8,10},{9,11},{10,... | collective-permute-start | bytes 1155080 | tf_op jit(solution)/shard_map/ppermute | solution.py:406
  28.4 0.5 merge.8.refs_0_
  28.9 0.1 collective-permute-start.12
  29.0 1.6 %collective-permute-start.13 = (bf16[47,32,128]{2,1,0:T(8,128)(2,1)S(1)}, bf16[47,32,128]{2,1,0:T(8,128)(2,1)S(1)}, u32[]{:S(2)}, u32[]{:S(2)}) collective-permute-start(bf16[47,32,128]{2,1,0:T(8,128)(2,1)S(1)} %merge.7.refs_3_), channel_id=1, source_target_pairs={{0,1},{1,0},{2,3},{3,2},{4,5},{5,4},{6,7},{7,6},{8,9},{9,8},{10,11... | collective-permute-start | bytes 1155080 | tf_op jit(solution)/shard_map/ppermute | solution.py:406
  30.6 3.1 %collective-permute-done.12.refs_1_ = bf16[47,16,128]{2,1,0:T(8,128)(2,1)S(1)} collective-permute-done((bf16[47,16,128]{2,1,0:T(8,128)(2,1)S(1)}, bf16[47,16,128]{2,1,0:T(8,128)(2,1)S(1)}, u32[]{:S(2)}, u32[]{:S(2)}) %collective-permute-start.12) | collective-permute-done | bytes 192544 | tf_op jit(solution)/shard_map/ppermute | solution.py:406
  33.7 0.5 merge.9.refs_2_
  34.2 2.7 %collective-permute-done.11.refs_4_ = bf16[47,32,128]{2,1,0:T(8,128)(2,1)S(1)} collective-permute-done((bf16[47,32,128]{2,1,0:T(8,128)(2,1)S(1)}, bf16[47,32,128]{2,1,0:T(8,128)(2,1)S(1)}, u32[]{:S(2)}, u32[]{:S(2)}) %collective-permute-start.11) | collective-permute-done | bytes 385056 | tf_op jit(solution)/shard_map/ppermute | solution.py:406
  36.9 1.9 %collective-permute-start.14 = (bf16[47,32,128]{2,1,0:T(8,128)(2,1)S(1)}, bf16[47,32,128]{2,1,0:T(8,128)(2,1)S(1)}, u32[]{:S(2)}, u32[]{:S(2)}) collective-permute-start(bf16[47,32,128]{2,1,0:T(8,128)(2,1)S(1)} %collective-permute-done.11.refs_4_), channel_id=1, source_target_pairs={{0,1},{1,0},{2,3},{3,2},{4,5},{5,4},{6,7},{7,6},{8,9},{9,8},{10,11... | collective-permute-start | bytes 1155080 | tf_op jit(solution)/shard_map/ppermute | solution.py:406
  38.9 0.9 %collective-permute-start.15 = (bf16[64,16,128]{2,1,0:T(8,128)(2,1)S(1)}, bf16[64,16,128]{2,1,0:T(8,128)(2,1)S(1)}, u32[]{:S(2)}, u32[]{:S(2)}) collective-permute-start(bf16[64,16,128]{2,1,0:T(8,128)(2,1)S(1)} %merge.9.refs_2_), channel_id=1, source_target_pairs={{0,2},{1,3},{2,0},{3,1},{4,6},{5,7},{6,4},{7,5},{8,10},{9,11},{10,... | collective-permute-start | bytes 786440 | tf_op jit(solution)/shard_map/ppermute | solution.py:406
  39.7 0.3 collective-permute-start.16
  40.0 0.0 collective-permute-done.13.refs_5_
  40.0 0.2 collective-permute-done.14.refs_6_
  40.2 0.0 copy-done.1
  40.2 4.9 %attend_first.1 = (f32[4096,128]{1,0:T(8,128)S(1)}, f32[4096,128]{1,0:T(8,128)S(1)}, f32[4096,128]{1,0:T(8,128)S(1)}) custom-call(s32[4,16]{1,0:T(4,128)S(1)} %copy-done.5, s32[4,64]{1,0:T(4,128)S(1)} %copy-done.6, bf16[128,4096]{1,0:T(8,128)(2,1)S(1)} %copy-done.1, bf16[47,32,128]{2,1,0:T(8,128)(2,1)S(1)} %merge.7.refs_3_, ...), custom_call_target="tpu_custom_call" | custom-call | flops 1048576 | bytes 1048576 | tf_op jit(solution)/shard_map/attend_first/pallas_call | solution.py:393
  45.1 1.7 %collective-permute-done.15.refs_3_ = bf16[64,16,128]{2,1,0:T(8,128)(2,1)S(1)} collective-permute-done((bf16[64,16,128]{2,1,0:T(8,128)(2,1)S(1)}, bf16[64,16,128]{2,1,0:T(8,128)(2,1)S(1)}, u32[]{:S(2)}, u32[]{:S(2)}) %collective-permute-start.15) | collective-permute-done | bytes 262176 | tf_op jit(solution)/shard_map/ppermute | solution.py:406
  46.8 0.8 %collective-permute-start.17 = (bf16[64,16,128]{2,1,0:T(8,128)(2,1)S(1)}, bf16[64,16,128]{2,1,0:T(8,128)(2,1)S(1)}, u32[]{:S(2)}, u32[]{:S(2)}) collective-permute-start(bf16[64,16,128]{2,1,0:T(8,128)(2,1)S(1)} %collective-permute-done.15.refs_3_), channel_id=1, source_target_pairs={{0,1},{1,0},{2,3},{3,2},{4,5},{5,4},{6,7},{7,6},{8,9},{9,8},{10,11... | collective-permute-start | bytes 786440 | tf_op jit(solution)/shard_map/ppermute | solution.py:406
  47.6 0.0 collective-permute-done.16.refs_4_
  47.6 1.2 %collective-permute-done.17.refs_5_ = bf16[64,16,128]{2,1,0:T(8,128)(2,1)S(1)} collective-permute-done((bf16[64,16,128]{2,1,0:T(8,128)(2,1)S(1)}, bf16[64,16,128]{2,1,0:T(8,128)(2,1)S(1)}, u32[]{:S(2)}, u32[]{:S(2)}) %collective-permute-start.17) | collective-permute-done | bytes 262176 | tf_op jit(solution)/shard_map/ppermute | solution.py:406
  48.8 4.0 %attend_last.1 = bf16[128,4096]{1,0:T(8,128)(2,1)} custom-call(s32[4,16]{1,0:T(4,128)S(1)} %copy-done.5, bf16[128,4096]{1,0:T(8,128)(2,1)S(1)} %copy-done.1, bf16[64,16,128]{2,1,0:T(8,128)(2,1)S(1)} %merge.9.refs_2_, bf16[64,16,128]{2,1,0:T(8,128)(2,1)S(1)} %collective-permute-done.15.refs_3_, bf16[64,16,128]{2,1,0:T(8,128)(2,1)S(1)} %collective-permute-done.16.refs_4_, ...), custom_call_target="tpu_custom_call" | custom-call | flops 1048576 | bytes 1048576 | tf_op jit(solution)/shard_map/attend_last/pallas_call | solution.py:393
  52.7 0.2 while.9
  (9 shorter events, 0.0 us)
Async XLA Ops:
  0.0 8.3 %copy-start.7 = (s32[6]{0:T(128)S(1)}, s32[6]{0:T(128)}, u32[]{:S(2)}) copy-start(s32[6]{0:T(128)} %constant.46) | copy-start | bytes 76
  0.0 11.6 %copy-start.8 = (s32[6]{0:T(128)S(1)}, s32[6]{0:T(128)}, u32[]{:S(2)}) copy-start(s32[6]{0:T(128)} %constant.45.clone) | copy-start | bytes 76
  0.0 3.1 %copy-start.5 = (s32[4,16]{1,0:T(4,128)S(1)}, s32[4,16]{1,0:T(4,128)}, u32[]{:S(2)}) copy-start(s32[4,16]{1,0:T(4,128)} %refs_0_.3) | copy-start | bytes 772
  0.0 3.2 %copy-start.2 = (bf16[128,512]{1,0:T(8,128)(2,1)S(1)}, bf16[128,512]{1,0:T(8,128)(2,1)}, u32[]{:S(2)}) copy-start(bf16[128,512]{1,0:T(8,128)(2,1)} %refs_9_.1) | copy-start | bytes 393220
  0.0 3.2 %copy-start.3 = (bf16[128,512]{1,0:T(8,128)(2,1)S(1)}, bf16[128,512]{1,0:T(8,128)(2,1)}, u32[]{:S(2)}) copy-start(bf16[128,512]{1,0:T(8,128)(2,1)} %refs_8_.1) | copy-start | bytes 393220
  2.2 38.0 %copy-start.1 = (bf16[128,4096]{1,0:T(8,128)(2,1)S(1)}, bf16[128,4096]{1,0:T(8,128)(2,1)}, u32[]{:S(2)}) copy-start(bf16[128,4096]{1,0:T(8,128)(2,1)} %refs_1_.3) | copy-start | bytes 3145732
  2.3 38.0 %copy-start.6 = (s32[4,64]{1,0:T(4,128)S(1)}, s32[4,64]{1,0:T(4,128)}, u32[]{:S(2)}) copy-start(s32[4,64]{1,0:T(4,128)} %refs_1_.2) | copy-start | bytes 3076
  2.3 2.0 %collective-permute-start.5 = (bf16[13,64,128]{2,1,0:T(8,128)(2,1)S(1)}, bf16[13,64,128]{2,1,0:T(8,128)(2,1)S(1)}, u32[]{:S(2)}, u32[]{:S(2)}) collective-permute-start(bf16[13,64,128]{2,1,0:T(8,128)(2,1)S(1)} %get-tuple-element.80), channel_id=1, source_target_pairs={{0,1},{1,0},{2,3},{3,2},{4,5},{5,4},{6,7},{7,6},{8,9},{9,8},{10,11... | collective-permute-start | bytes 638984 | tf_op jit(solution)/shard_map/ppermute | solution.py:406
  4.8 9.4 %collective-permute-start.6 = (bf16[19,32,128]{2,1,0:T(8,128)(2,1)S(1)}, bf16[19,32,128]{2,1,0:T(8,128)(2,1)S(1)}, u32[]{:S(2)}, u32[]{:S(2)}) collective-permute-start(bf16[19,32,128]{2,1,0:T(8,128)(2,1)S(1)} %get-tuple-element.81.refs_0_), channel_id=1, source_target_pairs={{0,8},{1,9},{2,10},{3,11},{4,12},{5,13},{6,14},{7,15},{8,0},{9,1},... | collective-permute-start | bytes 466952 | tf_op jit(solution)/shard_map/ppermute | solution.py:406
  7.2 7.0 %collective-permute-start.7 = (bf16[19,32,128]{2,1,0:T(8,128)(2,1)S(1)}, bf16[19,32,128]{2,1,0:T(8,128)(2,1)S(1)}, u32[]{:S(2)}, u32[]{:S(2)}) collective-permute-start(bf16[19,32,128]{2,1,0:T(8,128)(2,1)S(1)} %get-tuple-element.85.refs_2_), channel_id=1, source_target_pairs={{0,2},{1,3},{2,0},{3,1},{4,6},{5,7},{6,4},{7,5},{8,10},{9,11},{10,... | collective-permute-start | bytes 466952 | tf_op jit(solution)/shard_map/ppermute | solution.py:406
  8.5 9.9 %collective-permute-start.10 = (bf16[128,1024]{1,0:T(8,128)(2,1)S(1)}, bf16[128,1024]{1,0:T(8,128)(2,1)S(1)}, u32[]{:S(2)}, u32[]{:S(2)}) collective-permute-start(bf16[128,1024]{1,0:T(8,128)(2,1)S(1)} %pad_maximum_fusion), channel_id=1, source_target_pairs={{0,1},{1,2},{2,3},{3,4},{4,5},{5,6},{6,7},{7,8},{8,9},{9,10},{10,1... | collective-permute-start | bytes 786440 | tf_op jit(solution)/shard_map/ppermute | solution.py:406
  15.2 11.7 %collective-permute-start.8 = (bf16[30,32,128]{2,1,0:T(8,128)(2,1)S(1)}, bf16[30,32,128]{2,1,0:T(8,128)(2,1)S(1)}, u32[]{:S(2)}, u32[]{:S(2)}) collective-permute-start(bf16[30,32,128]{2,1,0:T(8,128)(2,1)S(1)} %get-tuple-element.86.refs_0_), channel_id=1, source_target_pairs={{0,4},{1,5},{2,6},{3,7},{4,0},{5,1},{6,2},{7,3},{8,12},{9,13},{10,... | collective-permute-start | bytes 737288 | tf_op jit(solution)/shard_map/ppermute | solution.py:406
  15.9 11.0 %collective-permute-start.9 = (bf16[30,16,128]{2,1,0:T(8,128)(2,1)S(1)}, bf16[30,16,128]{2,1,0:T(8,128)(2,1)S(1)}, u32[]{:S(2)}, u32[]{:S(2)}) collective-permute-start(bf16[30,16,128]{2,1,0:T(8,128)(2,1)S(1)} %get-tuple-element.87.refs_0_), channel_id=1, source_target_pairs={{0,8},{1,9},{2,10},{3,11},{4,12},{5,13},{6,14},{7,15},{8,0},{9,1},... | collective-permute-start | bytes 368648 | tf_op jit(solution)/shard_map/ppermute | solution.py:406
  27.4 9.5 %collective-permute-start.11 = (bf16[47,32,128]{2,1,0:T(8,128)(2,1)S(1)}, bf16[47,32,128]{2,1,0:T(8,128)(2,1)S(1)}, u32[]{:S(2)}, u32[]{:S(2)}) collective-permute-start(bf16[47,32,128]{2,1,0:T(8,128)(2,1)S(1)} %merge.7.refs_3_), channel_id=1, source_target_pairs={{0,2},{1,3},{2,0},{3,1},{4,6},{5,7},{6,4},{7,5},{8,10},{9,11},{10,... | collective-permute-start | bytes 1155080 | tf_op jit(solution)/shard_map/ppermute | solution.py:406
  28.9 4.8 %collective-permute-start.12 = (bf16[47,16,128]{2,1,0:T(8,128)(2,1)S(1)}, bf16[47,16,128]{2,1,0:T(8,128)(2,1)S(1)}, u32[]{:S(2)}, u32[]{:S(2)}) collective-permute-start(bf16[47,16,128]{2,1,0:T(8,128)(2,1)S(1)} %merge.8.refs_0_), channel_id=1, source_target_pairs={{0,4},{1,5},{2,6},{3,7},{4,0},{5,1},{6,2},{7,3},{8,12},{9,13},{10,... | collective-permute-start | bytes 577544 | tf_op jit(solution)/shard_map/ppermute | solution.py:406
  29.0 11.0 %collective-permute-start.13 = (bf16[47,32,128]{2,1,0:T(8,128)(2,1)S(1)}, bf16[47,32,128]{2,1,0:T(8,128)(2,1)S(1)}, u32[]{:S(2)}, u32[]{:S(2)}) collective-permute-start(bf16[47,32,128]{2,1,0:T(8,128)(2,1)S(1)} %merge.7.refs_3_), channel_id=1, source_target_pairs={{0,1},{1,0},{2,3},{3,2},{4,5},{5,4},{6,7},{7,6},{8,9},{9,8},{10,11... | collective-permute-start | bytes 1155080 | tf_op jit(solution)/shard_map/ppermute | solution.py:406
  36.9 3.3 %collective-permute-start.14 = (bf16[47,32,128]{2,1,0:T(8,128)(2,1)S(1)}, bf16[47,32,128]{2,1,0:T(8,128)(2,1)S(1)}, u32[]{:S(2)}, u32[]{:S(2)}) collective-permute-start(bf16[47,32,128]{2,1,0:T(8,128)(2,1)S(1)} %collective-permute-done.11.refs_4_), channel_id=1, source_target_pairs={{0,1},{1,0},{2,3},{3,2},{4,5},{5,4},{6,7},{7,6},{8,9},{9,8},{10,11... | collective-permute-start | bytes 1155080 | tf_op jit(solution)/shard_map/ppermute | solution.py:406
  38.9 7.9 %collective-permute-start.15 = (bf16[64,16,128]{2,1,0:T(8,128)(2,1)S(1)}, bf16[64,16,128]{2,1,0:T(8,128)(2,1)S(1)}, u32[]{:S(2)}, u32[]{:S(2)}) collective-permute-start(bf16[64,16,128]{2,1,0:T(8,128)(2,1)S(1)} %merge.9.refs_2_), channel_id=1, source_target_pairs={{0,2},{1,3},{2,0},{3,1},{4,6},{5,7},{6,4},{7,5},{8,10},{9,11},{10,... | collective-permute-start | bytes 786440 | tf_op jit(solution)/shard_map/ppermute | solution.py:406
  39.7 7.9 %collective-permute-start.16 = (bf16[64,16,128]{2,1,0:T(8,128)(2,1)S(1)}, bf16[64,16,128]{2,1,0:T(8,128)(2,1)S(1)}, u32[]{:S(2)}, u32[]{:S(2)}) collective-permute-start(bf16[64,16,128]{2,1,0:T(8,128)(2,1)S(1)} %merge.9.refs_2_), channel_id=1, source_target_pairs={{0,1},{1,0},{2,3},{3,2},{4,5},{5,4},{6,7},{7,6},{8,9},{9,8},{10,11... | collective-permute-start | bytes 786440 | tf_op jit(solution)/shard_map/ppermute | solution.py:406
  46.8 5.9 %copy-start = (bf16[2048,512]{1,0:T(8,128)(2,1)S(1)}, bf16[2048,512]{1,0:T(8,128)(2,1)}, u32[]{:S(2)}) copy-start(bf16[2048,512]{1,0:T(8,128)(2,1)} %cache_k.1) | copy-start | bytes 6291460
  46.8 1.9 %collective-permute-start.17 = (bf16[64,16,128]{2,1,0:T(8,128)(2,1)S(1)}, bf16[64,16,128]{2,1,0:T(8,128)(2,1)S(1)}, u32[]{:S(2)}, u32[]{:S(2)}) collective-permute-start(bf16[64,16,128]{2,1,0:T(8,128)(2,1)S(1)} %collective-permute-done.15.refs_3_), channel_id=1, source_target_pairs={{0,1},{1,0},{2,3},{3,2},{4,5},{5,4},{6,7},{7,6},{8,9},{9,8},{10,11... | collective-permute-start | bytes 786440 | tf_op jit(solution)/shard_map/ppermute | solution.py:406

commit v13 on v12

--- a/solution.py
+++ b/solution.py
@@ -174,7 +174,7 @@
 
 def room(share):
     mean = ENTRIES * share
-    wide = mean + 3.2 * math.sqrt(mean * (1.0 - share)) + 2.0
+    wide = mean + 3.0 * math.sqrt(mean * (1.0 - share)) + 1.5
     return min(ENTRIES + 1, math.ceil(wide))
 
 
@@ -411,7 +411,7 @@
 
 
 def fits(blocks, per_device, peers, masks):
-    most = [room((1 << mask.bit_count()) / peers) - (mask > 0) for mask in masks]
+    most = [room((1 << mask.bit_count()) / peers) + (-1 if mask else 1) for mask in masks]
     owners = (blocks // per_device).reshape(1, 1, ENTRIES)
     ids = jnp.arange(peers, dtype=jnp.int32)[None, :, None]
     away = (owners ^ ids) & ~jnp.array(masks, jnp.int32)[:, None, None]
@@ -452,7 +452,7 @@
         return known, bit, halved, parts, mine, other, size
 
     merge = functools.partial(merged, blocks, per_device)
-    kept, sent = pack(blocks, cache_k, cache_v, room(1 / peers))
+    kept, sent = pack(blocks, cache_k, cache_v, room(1 / peers) + 1)
     mine_a, mine_b = merge([job(0, 1, kept, swapped(sent, 1), parts=STAGES)])
     spans, mine_b = lax.optimization_barrier((jnp.concatenate([span_k, span_v], axis=1), mine_b))
     before = permuted(spans, ahead)

time: 53.3 us -> 52.3 us (0.981)
  starting transfers between devices: 17.2 us -> 16.4 us
    ppermute x13, starting transfers between devices: 17.2 us -> 16.4 us  [permuted(): return lax.ppermute(array, 'ctx', pairs)]
where the time goes in v13:
time: 52.3 us; the launch traced here: 52 us
  waiting for transfers between devices  19 us (36%)
  starting transfers between devices  16.4 us (31%)
  Pallas kernels  14.3 us (27%)
  other arithmetic  0.98 us (2%)
  between operations  0.98 us (2%)
    ppermute x13, waiting for transfers between devices, permuted(): return lax.ppermute(array, 'ctx', pairs)  19 us
    ppermute x13, starting transfers between devices, permuted(): return lax.ppermute(array, 'ctx', pairs)  16.4 us
    pallas_call x2, Pallas kernels, attend_stage(): pl.pallas_call(functools.partial(stage_kernel, per_device, known, bit, ba...  8.89 us
    pallas_call x5, Pallas kernels, merged(): pl.pallas_call(functools.partial(merge_kernel, per_device, [job[:4] for j...  3.1 us
    pallas_call x1, Pallas kernels, pack(): pl.pallas_call(functools.partial(pack_kernel, cache_k.shape[0] // VBLOCK,...  2.35 us
  transfers between devices with their start and end apart: 13, of which 8 were waited for; matrix products, arithmetic and copies ran while one was open for 2% of the time, Pallas kernels for 13%

profile of v13, /device:TPU:9, one launch (start us, length us, event | category | flops | bytes accessed | tf_op | source)
XLA Modules:
  0.0 52.0 jit_solution(16622480400795376607)
XLA Ops:
  0.0 0.0 copy-start.2
  0.0 0.0 copy-start.3
  0.0 2.3 %pack.1 = (bf16[13,64,128]{2,1,0:T(8,128)(2,1)S(1)}, bf16[13,64,128]{2,1,0:T(8,128)(2,1)S(1)}) custom-call(s32[4,16]{1,0:T(4,128)} %refs_0_.3, bf16[2048,512]{1,0:T(8,128)(2,1)} %cache_k.1, bf16[2048,512]{1,0:T(8,128)(2,1)} %cache_v.1), custom_call_target="tpu_custom_call" | custom-call | tf_op jit(solution)/shard_map/pack/pallas_call | solution.py:227
  2.4 0.0 copy-start.1
  2.4 0.0 copy-start.6
  2.4 0.7 %collective-permute-start.5 = (bf16[13,64,128]{2,1,0:T(8,128)(2,1)S(1)}, bf16[13,64,128]{2,1,0:T(8,128)(2,1)S(1)}, u32[]{:S(2)}, u32[]{:S(2)}) collective-permute-start(bf16[13,64,128]{2,1,0:T(8,128)(2,1)S(1)} %get-tuple-element.80), channel_id=1, source_target_pairs={{0,1},{1,0},{2,3},{3,2},{4,5},{5,4},{6,7},{7,6},{8,9},{9,8},{10,11... | collective-permute-start | bytes 638984 | tf_op jit(solution)/shard_map/ppermute | solution.py:406
  3.1 0.0 copy-done.5
  3.1 0.1 xor.20
  3.2 0.0 copy-done.2
  3.2 0.0 copy-done.3
  3.2 0.9 %collective-permute-done.5.refs_1_ = bf16[13,64,128]{2,1,0:T(8,128)(2,1)S(1)} collective-permute-done((bf16[13,64,128]{2,1,0:T(8,128)(2,1)S(1)}, bf16[13,64,128]{2,1,0:T(8,128)(2,1)S(1)}, u32[]{:S(2)}, u32[]{:S(2)}) %collective-permute-start.5) | collective-permute-done | bytes 213024 | tf_op jit(solution)/shard_map/ppermute | solution.py:406
  4.2 0.6 %merge.5 = (bf16[18,32,128]{2,1,0:T(8,128)(2,1)S(1)}, bf16[18,32,128]{2,1,0:T(8,128)(2,1)S(1)}) custom-call(s32[4,16]{1,0:T(4,128)S(1)} %copy-done.5, bf16[13,64,128]{2,1,0:T(8,128)(2,1)S(1)} %get-tuple-element.79.refs_0_, bf16[13,64,128]{2,1,0:T(8,128)(2,1)S(1)} %collective-permute-done.5.refs_1_), custom_call_target="tpu_custom_call" | custom-call | tf_op jit(solution)/shard_map/merge/pallas_call | solution.py:277
  4.7 2.4 %collective-permute-start.6 = (bf16[18,32,128]{2,1,0:T(8,128)(2,1)S(1)}, bf16[18,32,128]{2,1,0:T(8,128)(2,1)S(1)}, u32[]{:S(2)}, u32[]{:S(2)}) collective-permute-start(bf16[18,32,128]{2,1,0:T(8,128)(2,1)S(1)} %get-tuple-element.81.refs_0_), channel_id=1, source_target_pairs={{0,8},{1,9},{2,10},{3,11},{4,12},{5,13},{6,14},{7,15},{8,0},{9,1},... | collective-permute-start | bytes 442376 | tf_op jit(solution)/shard_map/ppermute | solution.py:406
  7.2 1.0 %collective-permute-start.7 = (bf16[18,32,128]{2,1,0:T(8,128)(2,1)S(1)}, bf16[18,32,128]{2,1,0:T(8,128)(2,1)S(1)}, u32[]{:S(2)}, u32[]{:S(2)}) collective-permute-start(bf16[18,32,128]{2,1,0:T(8,128)(2,1)S(1)} %get-tuple-element.85.refs_2_), channel_id=1, source_target_pairs={{0,2},{1,3},{2,0},{3,1},{4,6},{5,7},{6,4},{7,5},{8,10},{9,11},{10,... | collective-permute-start | bytes 442376 | tf_op jit(solution)/shard_map/ppermute | solution.py:406
  8.1 0.0 copy-done.7
  8.1 0.2 convert_reduce_fusion
  8.4 3.2 %collective-permute-start.10 = (bf16[128,1024]{1,0:T(8,128)(2,1)S(1)}, bf16[128,1024]{1,0:T(8,128)(2,1)S(1)}, u32[]{:S(2)}, u32[]{:S(2)}) collective-permute-start(bf16[128,1024]{1,0:T(8,128)(2,1)S(1)} %pad_maximum_fusion), channel_id=1, source_target_pairs={{0,1},{1,2},{2,3},{3,4},{4,5},{5,6},{6,7},{7,8},{8,9},{9,10},{10,1... | collective-permute-start | bytes 786440 | tf_op jit(solution)/shard_map/ppermute | solution.py:406
  11.6 0.0 copy-done.8
  11.6 0.7 %compare_reduce_fusion = pred[]{:T(512)} fusion(s32[6,16]{1,0:T(8,128)S(1)} %convert_reduce_fusion, s32[6]{0:T(128)S(1)} %copy-done.8), kind=kLoop, calls=%fused_computation.8 | loop fusion | flops 191 | bytes 409 | tf_op jit(solution)/shard_map/reduce_and | solution.py:419
  13.0 0.8 %collective-permute-done.6.refs_1_ = bf16[18,32,128]{2,1,0:T(8,128)(2,1)S(1)} collective-permute-done((bf16[18,32,128]{2,1,0:T(8,128)(2,1)S(1)}, bf16[18,32,128]{2,1,0:T(8,128)(2,1)S(1)}, u32[]{:S(2)}, u32[]{:S(2)}) %collective-permute-start.6) | collective-permute-done | bytes 147488 | tf_op jit(solution)/shard_map/ppermute | solution.py:406
  13.8 0.0 collective-permute-done.7.refs_3_
  13.8 1.0 %merge.6 = (bf16[28,32,128]{2,1,0:T(8,128)(2,1)S(1)}, bf16[28,16,128]{2,1,0:T(8,128)(2,1)S(1)}) custom-call(s32[4,16]{1,0:T(4,128)S(1)} %copy-done.5, bf16[18,32,128]{2,1,0:T(8,128)(2,1)S(1)} %get-tuple-element.81.refs_0_, bf16[18,32,128]{2,1,0:T(8,128)(2,1)S(1)} %collective-permute-done.6.refs_1_, bf16[18,32,128]{2,1,0:T(8,128)(2,1)S(1)} %get-tuple-element.85.refs_2_, ...), custom_call_target="tpu_custom_call" | custom-call | tf_op jit(solution)/shard_map/merge/pallas_call | solution.py:277
  14.8 0.7 %collective-permute-start.8 = (bf16[28,32,128]{2,1,0:T(8,128)(2,1)S(1)}, bf16[28,32,128]{2,1,0:T(8,128)(2,1)S(1)}, u32[]{:S(2)}, u32[]{:S(2)}) collective-permute-start(bf16[28,32,128]{2,1,0:T(8,128)(2,1)S(1)} %get-tuple-element.86.refs_0_), channel_id=1, source_target_pairs={{0,4},{1,5},{2,6},{3,7},{4,0},{5,1},{6,2},{7,3},{8,12},{9,13},{10,... | collective-permute-start | bytes 688136 | tf_op jit(solution)/shard_map/ppermute | solution.py:406
  15.5 2.6 %collective-permute-start.9 = (bf16[28,16,128]{2,1,0:T(8,128)(2,1)S(1)}, bf16[28,16,128]{2,1,0:T(8,128)(2,1)S(1)}, u32[]{:S(2)}, u32[]{:S(2)}) collective-permute-start(bf16[28,16,128]{2,1,0:T(8,128)(2,1)S(1)} %get-tuple-element.87.refs_0_), channel_id=1, source_target_pairs={{0,8},{1,9},{2,10},{3,11},{4,12},{5,13},{6,14},{7,15},{8,0},{9,1},... | collective-permute-start | bytes 344072 | tf_op jit(solution)/shard_map/ppermute | solution.py:406
  18.1 7.9 %collective-permute-done.9.refs_1_ = bf16[28,16,128]{2,1,0:T(8,128)(2,1)S(1)} collective-permute-done((bf16[28,16,128]{2,1,0:T(8,128)(2,1)S(1)}, bf16[28,16,128]{2,1,0:T(8,128)(2,1)S(1)}, u32[]{:S(2)}, u32[]{:S(2)}) %collective-permute-start.9) | collective-permute-done | bytes 114720 | tf_op jit(solution)/shard_map/ppermute | solution.py:406
  26.0 0.0 collective-permute-done.10.refs_7_
  26.0 0.0 collective-permute-done.8.refs_1_
  26.0 0.5 merge.7.refs_3_
  26.5 0.5 %collective-permute-start.11 = (bf16[46,32,128]{2,1,0:T(8,128)(2,1)S(1)}, bf16[46,32,128]{2,1,0:T(8,128)(2,1)S(1)}, u32[]{:S(2)}, u32[]{:S(2)}) collective-permute-start(bf16[46,32,128]{2,1,0:T(8,128)(2,1)S(1)} %merge.7.refs_3_), channel_id=1, source_target_pairs={{0,2},{1,3},{2,0},{3,1},{4,6},{5,7},{6,4},{7,5},{8,10},{9,11},{10,... | collective-permute-start | bytes 1130504 | tf_op jit(solution)/shard_map/ppermute | solution.py:406
  27.1 0.5 merge.8.refs_0_
  27.6 0.1 collective-permute-start.12
  27.7 1.8 %collective-permute-start.13 = (bf16[46,32,128]{2,1,0:T(8,128)(2,1)S(1)}, bf16[46,32,128]{2,1,0:T(8,128)(2,1)S(1)}, u32[]{:S(2)}, u32[]{:S(2)}) collective-permute-start(bf16[46,32,128]{2,1,0:T(8,128)(2,1)S(1)} %merge.7.refs_3_), channel_id=1, source_target_pairs={{0,1},{1,0},{2,3},{3,2},{4,5},{5,4},{6,7},{7,6},{8,9},{9,8},{10,11... | collective-permute-start | bytes 1130504 | tf_op jit(solution)/shard_map/ppermute | solution.py:406
  29.5 2.9 %collective-permute-done.12.refs_1_ = bf16[46,16,128]{2,1,0:T(8,128)(2,1)S(1)} collective-permute-done((bf16[46,16,128]{2,1,0:T(8,128)(2,1)S(1)}, bf16[46,16,128]{2,1,0:T(8,128)(2,1)S(1)}, u32[]{:S(2)}, u32[]{:S(2)}) %collective-permute-start.12) | collective-permute-done | bytes 188448 | tf_op jit(solution)/shard_map/ppermute | solution.py:406
  32.4 0.5 merge.9.refs_2_
  32.9 3.0 %collective-permute-done.11.refs_4_ = bf16[46,32,128]{2,1,0:T(8,128)(2,1)S(1)} collective-permute-done((bf16[46,32,128]{2,1,0:T(8,128)(2,1)S(1)}, bf16[46,32,128]{2,1,0:T(8,128)(2,1)S(1)}, u32[]{:S(2)}, u32[]{:S(2)}) %collective-permute-start.11) | collective-permute-done | bytes 376864 | tf_op jit(solution)/shard_map/ppermute | solution.py:406
  35.9 1.9 %collective-permute-start.14 = (bf16[46,32,128]{2,1,0:T(8,128)(2,1)S(1)}, bf16[46,32,128]{2,1,0:T(8,128)(2,1)S(1)}, u32[]{:S(2)}, u32[]{:S(2)}) collective-permute-start(bf16[46,32,128]{2,1,0:T(8,128)(2,1)S(1)} %collective-permute-done.11.refs_4_), channel_id=1, source_target_pairs={{0,1},{1,0},{2,3},{3,2},{4,5},{5,4},{6,7},{7,6},{8,9},{9,8},{10,11... | collective-permute-start | bytes 1130504 | tf_op jit(solution)/shard_map/ppermute | solution.py:406
  37.8 0.5 collective-permute-start.15
  38.3 0.3 collective-permute-start.16
  38.6 0.0 collective-permute-done.13.refs_5_
  38.6 0.6 %collective-permute-done.14.refs_6_ = bf16[46,32,128]{2,1,0:T(8,128)(2,1)S(1)} collective-permute-done((bf16[46,32,128]{2,1,0:T(8,128)(2,1)S(1)}, bf16[46,32,128]{2,1,0:T(8,128)(2,1)S(1)}, u32[]{:S(2)}, u32[]{:S(2)}) %collective-permute-start.14) | collective-permute-done | bytes 376864 | tf_op jit(solution)/shard_map/ppermute | solution.py:406
  39.1 0.0 copy-done.1
  39.1 4.9 %attend_first.1 = (f32[4096,128]{1,0:T(8,128)S(1)}, f32[4096,128]{1,0:T(8,128)S(1)}, f32[4096,128]{1,0:T(8,128)S(1)}) custom-call(s32[4,16]{1,0:T(4,128)S(1)} %copy-done.5, s32[4,64]{1,0:T(4,128)S(1)} %copy-done.6, bf16[128,4096]{1,0:T(8,128)(2,1)S(1)} %copy-done.1, bf16[46,32,128]{2,1,0:T(8,128)(2,1)S(1)} %merge.7.refs_3_, ...), custom_call_target="tpu_custom_call" | custom-call | flops 1048576 | bytes 1048576 | tf_op jit(solution)/shard_map/attend_first/pallas_call | solution.py:393
  44.0 1.7 %collective-permute-done.15.refs_3_ = bf16[64,16,128]{2,1,0:T(8,128)(2,1)S(1)} collective-permute-done((bf16[64,16,128]{2,1,0:T(8,128)(2,1)S(1)}, bf16[64,16,128]{2,1,0:T(8,128)(2,1)S(1)}, u32[]{:S(2)}, u32[]{:S(2)}) %collective-permute-start.15) | collective-permute-done | bytes 262176 | tf_op jit(solution)/shard_map/ppermute | solution.py:406
  45.7 0.8 %collective-permute-start.17 = (bf16[64,16,128]{2,1,0:T(8,128)(2,1)S(1)}, bf16[64,16,128]{2,1,0:T(8,128)(2,1)S(1)}, u32[]{:S(2)}, u32[]{:S(2)}) collective-permute-start(bf16[64,16,128]{2,1,0:T(8,128)(2,1)S(1)} %collective-permute-done.15.refs_3_), channel_id=1, source_target_pairs={{0,1},{1,0},{2,3},{3,2},{4,5},{5,4},{6,7},{7,6},{8,9},{9,8},{10,11... | collective-permute-start | bytes 786440 | tf_op jit(solution)/shard_map/ppermute | solution.py:406
  46.5 0.0 collective-permute-done.16.refs_4_
  46.5 1.2 %collective-permute-done.17.refs_5_ = bf16[64,16,128]{2,1,0:T(8,128)(2,1)S(1)} collective-permute-done((bf16[64,16,128]{2,1,0:T(8,128)(2,1)S(1)}, bf16[64,16,128]{2,1,0:T(8,128)(2,1)S(1)}, u32[]{:S(2)}, u32[]{:S(2)}) %collective-permute-start.17) | collective-permute-done | bytes 262176 | tf_op jit(solution)/shard_map/ppermute | solution.py:406
  47.7 4.0 %attend_last.1 = bf16[128,4096]{1,0:T(8,128)(2,1)} custom-call(s32[4,16]{1,0:T(4,128)S(1)} %copy-done.5, bf16[128,4096]{1,0:T(8,128)(2,1)S(1)} %copy-done.1, bf16[64,16,128]{2,1,0:T(8,128)(2,1)S(1)} %merge.9.refs_2_, bf16[64,16,128]{2,1,0:T(8,128)(2,1)S(1)} %collective-permute-done.15.refs_3_, bf16[64,16,128]{2,1,0:T(8,128)(2,1)S(1)} %collective-permute-done.16.refs_4_, ...), custom_call_target="tpu_custom_call" | custom-call | flops 1048576 | bytes 1048576 | tf_op jit(solution)/shard_map/attend_last/pallas_call | solution.py:393
  51.7 0.2 while.9
  (9 shorter events, 0.0 us)
Async XLA Ops:
  0.0 8.1 %copy-start.7 = (s32[6]{0:T(128)S(1)}, s32[6]{0:T(128)}, u32[]{:S(2)}) copy-start(s32[6]{0:T(128)} %constant.46) | copy-start | bytes 76
  0.0 11.6 %copy-start.8 = (s32[6]{0:T(128)S(1)}, s32[6]{0:T(128)}, u32[]{:S(2)}) copy-start(s32[6]{0:T(128)} %constant.45.clone) | copy-start | bytes 76
  0.0 3.1 %copy-start.5 = (s32[4,16]{1,0:T(4,128)S(1)}, s32[4,16]{1,0:T(4,128)}, u32[]{:S(2)}) copy-start(s32[4,16]{1,0:T(4,128)} %refs_0_.3) | copy-start | bytes 772
  0.0 3.2 %copy-start.2 = (bf16[128,512]{1,0:T(8,128)(2,1)S(1)}, bf16[128,512]{1,0:T(8,128)(2,1)}, u32[]{:S(2)}) copy-start(bf16[128,512]{1,0:T(8,128)(2,1)} %refs_9_.1) | copy-start | bytes 393220
  0.0 3.1 %copy-start.3 = (bf16[128,512]{1,0:T(8,128)(2,1)S(1)}, bf16[128,512]{1,0:T(8,128)(2,1)}, u32[]{:S(2)}) copy-start(bf16[128,512]{1,0:T(8,128)(2,1)} %refs_8_.1) | copy-start | bytes 393220
  2.4 36.7 %copy-start.1 = (bf16[128,4096]{1,0:T(8,128)(2,1)S(1)}, bf16[128,4096]{1,0:T(8,128)(2,1)}, u32[]{:S(2)}) copy-start(bf16[128,4096]{1,0:T(8,128)(2,1)} %refs_1_.3) | copy-start | bytes 3145732
  2.4 36.7 %copy-start.6 = (s32[4,64]{1,0:T(4,128)S(1)}, s32[4,64]{1,0:T(4,128)}, u32[]{:S(2)}) copy-start(s32[4,64]{1,0:T(4,128)} %refs_1_.2) | copy-start | bytes 3076
  2.4 1.7 %collective-permute-start.5 = (bf16[13,64,128]{2,1,0:T(8,128)(2,1)S(1)}, bf16[13,64,128]{2,1,0:T(8,128)(2,1)S(1)}, u32[]{:S(2)}, u32[]{:S(2)}) collective-permute-start(bf16[13,64,128]{2,1,0:T(8,128)(2,1)S(1)} %get-tuple-element.80), channel_id=1, source_target_pairs={{0,1},{1,0},{2,3},{3,2},{4,5},{5,4},{6,7},{7,6},{8,9},{9,8},{10,11... | collective-permute-start | bytes 638984 | tf_op jit(solution)/shard_map/ppermute | solution.py:406
  4.7 9.1 %collective-permute-start.6 = (bf16[18,32,128]{2,1,0:T(8,128)(2,1)S(1)}, bf16[18,32,128]{2,1,0:T(8,128)(2,1)S(1)}, u32[]{:S(2)}, u32[]{:S(2)}) collective-permute-start(bf16[18,32,128]{2,1,0:T(8,128)(2,1)S(1)} %get-tuple-element.81.refs_0_), channel_id=1, source_target_pairs={{0,8},{1,9},{2,10},{3,11},{4,12},{5,13},{6,14},{7,15},{8,0},{9,1},... | collective-permute-start | bytes 442376 | tf_op jit(solution)/shard_map/ppermute | solution.py:406
  7.2 6.6 %collective-permute-start.7 = (bf16[18,32,128]{2,1,0:T(8,128)(2,1)S(1)}, bf16[18,32,128]{2,1,0:T(8,128)(2,1)S(1)}, u32[]{:S(2)}, u32[]{:S(2)}) collective-permute-start(bf16[18,32,128]{2,1,0:T(8,128)(2,1)S(1)} %get-tuple-element.85.refs_2_), channel_id=1, source_target_pairs={{0,2},{1,3},{2,0},{3,1},{4,6},{5,7},{6,4},{7,5},{8,10},{9,11},{10,... | collective-permute-start | bytes 442376 | tf_op jit(solution)/shard_map/ppermute | solution.py:406
  8.4 17.6 %collective-permute-start.10 = (bf16[128,1024]{1,0:T(8,128)(2,1)S(1)}, bf16[128,1024]{1,0:T(8,128)(2,1)S(1)}, u32[]{:S(2)}, u32[]{:S(2)}) collective-permute-start(bf16[128,1024]{1,0:T(8,128)(2,1)S(1)} %pad_maximum_fusion), channel_id=1, source_target_pairs={{0,1},{1,2},{2,3},{3,4},{4,5},{5,6},{6,7},{7,8},{8,9},{9,10},{10,1... | collective-permute-start | bytes 786440 | tf_op jit(solution)/shard_map/ppermute | solution.py:406
  14.8 11.2 %collective-permute-start.8 = (bf16[28,32,128]{2,1,0:T(8,128)(2,1)S(1)}, bf16[28,32,128]{2,1,0:T(8,128)(2,1)S(1)}, u32[]{:S(2)}, u32[]{:S(2)}) collective-permute-start(bf16[28,32,128]{2,1,0:T(8,128)(2,1)S(1)} %get-tuple-element.86.refs_0_), channel_id=1, source_target_pairs={{0,4},{1,5},{2,6},{3,7},{4,0},{5,1},{6,2},{7,3},{8,12},{9,13},{10,... | collective-permute-start | bytes 688136 | tf_op jit(solution)/shard_map/ppermute | solution.py:406
  15.5 10.5 %collective-permute-start.9 = (bf16[28,16,128]{2,1,0:T(8,128)(2,1)S(1)}, bf16[28,16,128]{2,1,0:T(8,128)(2,1)S(1)}, u32[]{:S(2)}, u32[]{:S(2)}) collective-permute-start(bf16[28,16,128]{2,1,0:T(8,128)(2,1)S(1)} %get-tuple-element.87.refs_0_), channel_id=1, source_target_pairs={{0,8},{1,9},{2,10},{3,11},{4,12},{5,13},{6,14},{7,15},{8,0},{9,1},... | collective-permute-start | bytes 344072 | tf_op jit(solution)/shard_map/ppermute | solution.py:406
  26.5 9.3 %collective-permute-start.11 = (bf16[46,32,128]{2,1,0:T(8,128)(2,1)S(1)}, bf16[46,32,128]{2,1,0:T(8,128)(2,1)S(1)}, u32[]{:S(2)}, u32[]{:S(2)}) collective-permute-start(bf16[46,32,128]{2,1,0:T(8,128)(2,1)S(1)} %merge.7.refs_3_), channel_id=1, source_target_pairs={{0,2},{1,3},{2,0},{3,1},{4,6},{5,7},{6,4},{7,5},{8,10},{9,11},{10,... | collective-permute-start | bytes 1130504 | tf_op jit(solution)/shard_map/ppermute | solution.py:406
  27.6 4.8 %collective-permute-start.12 = (bf16[46,16,128]{2,1,0:T(8,128)(2,1)S(1)}, bf16[46,16,128]{2,1,0:T(8,128)(2,1)S(1)}, u32[]{:S(2)}, u32[]{:S(2)}) collective-permute-start(bf16[46,16,128]{2,1,0:T(8,128)(2,1)S(1)} %merge.8.refs_0_), channel_id=1, source_target_pairs={{0,4},{1,5},{2,6},{3,7},{4,0},{5,1},{6,2},{7,3},{8,12},{9,13},{10,... | collective-permute-start | bytes 565256 | tf_op jit(solution)/shard_map/ppermute | solution.py:406
  27.7 10.9 %collective-permute-start.13 = (bf16[46,32,128]{2,1,0:T(8,128)(2,1)S(1)}, bf16[46,32,128]{2,1,0:T(8,128)(2,1)S(1)}, u32[]{:S(2)}, u32[]{:S(2)}) collective-permute-start(bf16[46,32,128]{2,1,0:T(8,128)(2,1)S(1)} %merge.7.refs_3_), channel_id=1, source_target_pairs={{0,1},{1,0},{2,3},{3,2},{4,5},{5,4},{6,7},{7,6},{8,9},{9,8},{10,11... | collective-permute-start | bytes 1130504 | tf_op jit(solution)/shard_map/ppermute | solution.py:406
  35.9 3.2 %collective-permute-start.14 = (bf16[46,32,128]{2,1,0:T(8,128)(2,1)S(1)}, bf16[46,32,128]{2,1,0:T(8,128)(2,1)S(1)}, u32[]{:S(2)}, u32[]{:S(2)}) collective-permute-start(bf16[46,32,128]{2,1,0:T(8,128)(2,1)S(1)} %collective-permute-done.11.refs_4_), channel_id=1, source_target_pairs={{0,1},{1,0},{2,3},{3,2},{4,5},{5,4},{6,7},{7,6},{8,9},{9,8},{10,11... | collective-permute-start | bytes 1130504 | tf_op jit(solution)/shard_map/ppermute | solution.py:406
  37.8 7.9 %collective-permute-start.15 = (bf16[64,16,128]{2,1,0:T(8,128)(2,1)S(1)}, bf16[64,16,128]{2,1,0:T(8,128)(2,1)S(1)}, u32[]{:S(2)}, u32[]{:S(2)}) collective-permute-start(bf16[64,16,128]{2,1,0:T(8,128)(2,1)S(1)} %merge.9.refs_2_), channel_id=1, source_target_pairs={{0,2},{1,3},{2,0},{3,1},{4,6},{5,7},{6,4},{7,5},{8,10},{9,11},{10,... | collective-permute-start | bytes 786440 | tf_op jit(solution)/shard_map/ppermute | solution.py:406
  38.3 8.2 %collective-permute-start.16 = (bf16[64,16,128]{2,1,0:T(8,128)(2,1)S(1)}, bf16[64,16,128]{2,1,0:T(8,128)(2,1)S(1)}, u32[]{:S(2)}, u32[]{:S(2)}) collective-permute-start(bf16[64,16,128]{2,1,0:T(8,128)(2,1)S(1)} %merge.9.refs_2_), channel_id=1, source_target_pairs={{0,1},{1,0},{2,3},{3,2},{4,5},{5,4},{6,7},{7,6},{8,9},{9,8},{10,11... | collective-permute-start | bytes 786440 | tf_op jit(solution)/shard_map/ppermute | solution.py:406
  45.7 5.9 %copy-start = (bf16[2048,512]{1,0:T(8,128)(2,1)S(1)}, bf16[2048,512]{1,0:T(8,128)(2,1)}, u32[]{:S(2)}) copy-start(bf16[2048,512]{1,0:T(8,128)(2,1)} %cache_k.1) | copy-start | bytes 6291460
  45.7 1.9 %collective-permute-start.17 = (bf16[64,16,128]{2,1,0:T(8,128)(2,1)S(1)}, bf16[64,16,128]{2,1,0:T(8,128)(2,1)S(1)}, u32[]{:S(2)}, u32[]{:S(2)}) collective-permute-start(bf16[64,16,128]{2,1,0:T(8,128)(2,1)S(1)} %collective-permute-done.15.refs_3_), channel_id=1, source_target_pairs={{0,1},{1,0},{2,3},{3,2},{4,5},{5,4},{6,7},{7,6},{8,9},{9,8},{10,11... | collective-permute-start | bytes 786440 | tf_op jit(solution)/shard_map/ppermute | solution.py:406

commit v14 on v13

--- a/solution.py
+++ b/solution.py
@@ -473,7 +473,7 @@
         other_a = swapped(mine_a, (far + [near])[at + 1])
         other_b = swapped(mine_b, far[at])
         if at < len(far) - 1:
-            other_a, other_b, before = lax.optimization_barrier((other_a, other_b, before))
+            other_a, before = lax.optimization_barrier((other_a, before))
     (mine_b,) = merge([job(*steps_b[-1], mine_b, other_b)])
     other_a, mine_b = lax.optimization_barrier((other_a, mine_b))
     other_b = swapped(mine_b, near)

time: 52.3 us -> 55.5 us (1.061)
  the two profiles are of different devices: /device:TPU:9 before, /device:TPU:0 now
where the time goes in v14:
time: 55.5 us; the launch traced here: 55.2 us
  waiting for transfers between devices  24.9 us (45%)
  Pallas kernels  14.3 us (26%)
  starting transfers between devices  13.7 us (25%)
  other arithmetic  0.98 us (2%)
  between operations  0.98 us (2%)
    ppermute x13, waiting for transfers between devices, permuted(): return lax.ppermute(array, 'ctx', pairs)  24.9 us
    ppermute x13, starting transfers between devices, permuted(): return lax.ppermute(array, 'ctx', pairs)  13.7 us
    pallas_call x2, Pallas kernels, attend_stage(): pl.pallas_call(functools.partial(stage_kernel, per_device, known, bit, ba...  8.89 us
    pallas_call x5, Pallas kernels, merged(): pl.pallas_call(functools.partial(merge_kernel, per_device, [job[:4] for j...  3.1 us
    pallas_call x1, Pallas kernels, pack(): pl.pallas_call(functools.partial(pack_kernel, cache_k.shape[0] // VBLOCK,...  2.34 us
  transfers between devices with their start and end apart: 13, of which 8 were waited for; matrix products, arithmetic and copies ran while one was open for 2% of the time, Pallas kernels for 13%

profile of v14, /device:TPU:0, one launch (start us, length us, event | category | flops | bytes accessed | tf_op | source)
XLA Modules:
  0.0 55.2 jit_solution(3918199149848082135)
XLA Ops:
  0.0 2.3 %pack.1 = (bf16[13,64,128]{2,1,0:T(8,128)(2,1)S(1)}, bf16[13,64,128]{2,1,0:T(8,128)(2,1)S(1)}) custom-call(s32[4,16]{1,0:T(4,128)} %refs_0_.3, bf16[2048,512]{1,0:T(8,128)(2,1)} %cache_k.1, bf16[2048,512]{1,0:T(8,128)(2,1)} %cache_v.1), custom_call_target="tpu_custom_call" | custom-call | tf_op jit(solution)/shard_map/pack/pallas_call | solution.py:227
  2.4 0.0 copy-start.1
  2.4 0.0 copy-start.6
  2.4 0.6 %collective-permute-start.5 = (bf16[13,64,128]{2,1,0:T(8,128)(2,1)S(1)}, bf16[13,64,128]{2,1,0:T(8,128)(2,1)S(1)}, u32[]{:S(2)}, u32[]{:S(2)}) collective-permute-start(bf16[13,64,128]{2,1,0:T(8,128)(2,1)S(1)} %get-tuple-element.79), channel_id=1, source_target_pairs={{0,1},{1,0},{2,3},{3,2},{4,5},{5,4},{6,7},{7,6},{8,9},{9,8},{10,11... | collective-permute-start | bytes 638984 | tf_op jit(solution)/shard_map/ppermute | solution.py:406
  3.0 0.0 copy-done.5
  3.0 0.1 xor.20
  3.0 0.0 copy-done.2
  3.1 0.0 copy-done.3
  3.1 0.9 %collective-permute-done.5.refs_1_ = bf16[13,64,128]{2,1,0:T(8,128)(2,1)S(1)} collective-permute-done((bf16[13,64,128]{2,1,0:T(8,128)(2,1)S(1)}, bf16[13,64,128]{2,1,0:T(8,128)(2,1)S(1)}, u32[]{:S(2)}, u32[]{:S(2)}) %collective-permute-start.5) | collective-permute-done | bytes 213024 | tf_op jit(solution)/shard_map/ppermute | solution.py:406
  4.0 0.6 %merge.5 = (bf16[18,32,128]{2,1,0:T(8,128)(2,1)S(1)}, bf16[18,32,128]{2,1,0:T(8,128)(2,1)S(1)}) custom-call(s32[4,16]{1,0:T(4,128)S(1)} %copy-done.5, bf16[13,64,128]{2,1,0:T(8,128)(2,1)S(1)} %get-tuple-element.78.refs_0_, bf16[13,64,128]{2,1,0:T(8,128)(2,1)S(1)} %collective-permute-done.5.refs_1_), custom_call_target="tpu_custom_call" | custom-call | tf_op jit(solution)/shard_map/merge/pallas_call | solution.py:277
  4.6 4.1 %collective-permute-start.6 = (bf16[18,32,128]{2,1,0:T(8,128)(2,1)S(1)}, bf16[18,32,128]{2,1,0:T(8,128)(2,1)S(1)}, u32[]{:S(2)}, u32[]{:S(2)}) collective-permute-start(bf16[18,32,128]{2,1,0:T(8,128)(2,1)S(1)} %get-tuple-element.80.refs_0_), channel_id=1, source_target_pairs={{0,8},{1,9},{2,10},{3,11},{4,12},{5,13},{6,14},{7,15},{8,0},{9,1},... | collective-permute-start | bytes 442376 | tf_op jit(solution)/shard_map/ppermute | solution.py:406
  8.7 1.3 %collective-permute-start.7 = (bf16[18,32,128]{2,1,0:T(8,128)(2,1)S(1)}, bf16[18,32,128]{2,1,0:T(8,128)(2,1)S(1)}, u32[]{:S(2)}, u32[]{:S(2)}) collective-permute-start(bf16[18,32,128]{2,1,0:T(8,128)(2,1)S(1)} %get-tuple-element.84.refs_2_), channel_id=1, source_target_pairs={{0,2},{1,3},{2,0},{3,1},{4,6},{5,7},{6,4},{7,5},{8,10},{9,11},{10,... | collective-permute-start | bytes 442376 | tf_op jit(solution)/shard_map/ppermute | solution.py:406
  10.0 0.0 copy-done.7
  10.0 0.2 convert_reduce_fusion
  10.2 1.5 %collective-permute-start.9 = (bf16[128,1024]{1,0:T(8,128)(2,1)S(1)}, bf16[128,1024]{1,0:T(8,128)(2,1)S(1)}, u32[]{:S(2)}, u32[]{:S(2)}) collective-permute-start(bf16[128,1024]{1,0:T(8,128)(2,1)S(1)} %pad_maximum_fusion), channel_id=1, source_target_pairs={{0,1},{1,2},{2,3},{3,4},{4,5},{5,6},{6,7},{7,8},{8,9},{9,10},{10,1... | collective-permute-start | bytes 786440 | tf_op jit(solution)/shard_map/ppermute | solution.py:406
  11.7 0.0 copy-done.8
  11.7 0.7 %compare_reduce_fusion = pred[]{:T(512)} fusion(s32[6,16]{1,0:T(8,128)S(1)} %convert_reduce_fusion, s32[6]{0:T(128)S(1)} %copy-done.8), kind=kLoop, calls=%fused_computation.8 | loop fusion | flops 191 | bytes 409 | tf_op jit(solution)/shard_map/reduce_and | solution.py:419
  13.1 2.9 %collective-permute-done.6.refs_1_ = bf16[18,32,128]{2,1,0:T(8,128)(2,1)S(1)} collective-permute-done((bf16[18,32,128]{2,1,0:T(8,128)(2,1)S(1)}, bf16[18,32,128]{2,1,0:T(8,128)(2,1)S(1)}, u32[]{:S(2)}, u32[]{:S(2)}) %collective-permute-start.6) | collective-permute-done | bytes 147488 | tf_op jit(solution)/shard_map/ppermute | solution.py:406
  16.0 0.0 collective-permute-done.7.refs_3_
  16.0 1.0 %merge.6 = (bf16[28,32,128]{2,1,0:T(8,128)(2,1)S(1)}, bf16[28,16,128]{2,1,0:T(8,128)(2,1)S(1)}) custom-call(s32[4,16]{1,0:T(4,128)S(1)} %copy-done.5, bf16[18,32,128]{2,1,0:T(8,128)(2,1)S(1)} %get-tuple-element.80.refs_0_, bf16[18,32,128]{2,1,0:T(8,128)(2,1)S(1)} %collective-permute-done.6.refs_1_, bf16[18,32,128]{2,1,0:T(8,128)(2,1)S(1)} %get-tuple-element.84.refs_2_, ...), custom_call_target="tpu_custom_call" | custom-call | tf_op jit(solution)/shard_map/merge/pallas_call | solution.py:277
  17.1 0.6 %collective-permute-start.8 = (bf16[28,32,128]{2,1,0:T(8,128)(2,1)S(1)}, bf16[28,32,128]{2,1,0:T(8,128)(2,1)S(1)}, u32[]{:S(2)}, u32[]{:S(2)}) collective-permute-start(bf16[28,32,128]{2,1,0:T(8,128)(2,1)S(1)} %get-tuple-element.85.refs_0_), channel_id=1, source_target_pairs={{0,4},{1,5},{2,6},{3,7},{4,0},{5,1},{6,2},{7,3},{8,12},{9,13},{10,... | collective-permute-start | bytes 688136 | tf_op jit(solution)/shard_map/ppermute | solution.py:406
  17.6 0.0 collective-permute-done.9.refs_7_
  17.6 6.6 %collective-permute-done.8.refs_1_ = bf16[28,32,128]{2,1,0:T(8,128)(2,1)S(1)} collective-permute-done((bf16[28,32,128]{2,1,0:T(8,128)(2,1)S(1)}, bf16[28,32,128]{2,1,0:T(8,128)(2,1)S(1)}, u32[]{:S(2)}, u32[]{:S(2)}) %collective-permute-start.8) | collective-permute-done | bytes 229408 | tf_op jit(solution)/shard_map/ppermute | solution.py:406
  24.3 0.5 merge.7.refs_3_
  24.8 1.1 %collective-permute-start.10 = (bf16[46,32,128]{2,1,0:T(8,128)(2,1)S(1)}, bf16[46,32,128]{2,1,0:T(8,128)(2,1)S(1)}, u32[]{:S(2)}, u32[]{:S(2)}) collective-permute-start(bf16[46,32,128]{2,1,0:T(8,128)(2,1)S(1)} %merge.7.refs_3_), channel_id=1, source_target_pairs={{0,2},{1,3},{2,0},{3,1},{4,6},{5,7},{6,4},{7,5},{8,10},{9,11},{10,... | collective-permute-start | bytes 1130504 | tf_op jit(solution)/shard_map/ppermute | solution.py:406
  25.9 3.0 %collective-permute-start.11 = (bf16[28,16,128]{2,1,0:T(8,128)(2,1)S(1)}, bf16[28,16,128]{2,1,0:T(8,128)(2,1)S(1)}, u32[]{:S(2)}, u32[]{:S(2)}) collective-permute-start(bf16[28,16,128]{2,1,0:T(8,128)(2,1)S(1)} %get-tuple-element.88.refs_0_), channel_id=1, source_target_pairs={{0,8},{1,9},{2,10},{3,11},{4,12},{5,13},{6,14},{7,15},{8,0},{9,1},... | collective-permute-start | bytes 344072 | tf_op jit(solution)/shard_map/ppermute | solution.py:406
  28.9 4.9 %collective-permute-done.11.refs_1_ = bf16[28,16,128]{2,1,0:T(8,128)(2,1)S(1)} collective-permute-done((bf16[28,16,128]{2,1,0:T(8,128)(2,1)S(1)}, bf16[28,16,128]{2,1,0:T(8,128)(2,1)S(1)}, u32[]{:S(2)}, u32[]{:S(2)}) %collective-permute-start.11) | collective-permute-done | bytes 114720 | tf_op jit(solution)/shard_map/ppermute | solution.py:406
  33.8 0.5 merge.8.refs_0_
  34.4 0.7 %collective-permute-start.12 = (bf16[46,16,128]{2,1,0:T(8,128)(2,1)S(1)}, bf16[46,16,128]{2,1,0:T(8,128)(2,1)S(1)}, u32[]{:S(2)}, u32[]{:S(2)}) collective-permute-start(bf16[46,16,128]{2,1,0:T(8,128)(2,1)S(1)} %merge.8.refs_0_), channel_id=1, source_target_pairs={{0,4},{1,5},{2,6},{3,7},{4,0},{5,1},{6,2},{7,3},{8,12},{9,13},{10,... | collective-permute-start | bytes 565256 | tf_op jit(solution)/shard_map/ppermute | solution.py:406
  35.1 0.0 collective-permute-start.13
  35.1 4.9 %collective-permute-done.12.refs_1_ = bf16[46,16,128]{2,1,0:T(8,128)(2,1)S(1)} collective-permute-done((bf16[46,16,128]{2,1,0:T(8,128)(2,1)S(1)}, bf16[46,16,128]{2,1,0:T(8,128)(2,1)S(1)}, u32[]{:S(2)}, u32[]{:S(2)}) %collective-permute-start.12) | collective-permute-done | bytes 188448 | tf_op jit(solution)/shard_map/ppermute | solution.py:406
  40.0 0.5 merge.9.refs_2_
  40.5 0.0 collective-permute-done.10.refs_4_
  40.5 0.1 collective-permute-start.14
  40.6 0.6 %collective-permute-start.15 = (bf16[64,16,128]{2,1,0:T(8,128)(2,1)S(1)}, bf16[64,16,128]{2,1,0:T(8,128)(2,1)S(1)}, u32[]{:S(2)}, u32[]{:S(2)}) collective-permute-start(bf16[64,16,128]{2,1,0:T(8,128)(2,1)S(1)} %merge.9.refs_2_), channel_id=1, source_target_pairs={{0,2},{1,3},{2,0},{3,1},{4,6},{5,7},{6,4},{7,5},{8,10},{9,11},{10,... | collective-permute-start | bytes 786440 | tf_op jit(solution)/shard_map/ppermute | solution.py:406
  41.2 0.2 collective-permute-start.16
  41.3 0.0 collective-permute-done.13.refs_5_
  41.3 1.0 %collective-permute-done.14.refs_6_ = bf16[46,32,128]{2,1,0:T(8,128)(2,1)S(1)} collective-permute-done((bf16[46,32,128]{2,1,0:T(8,128)(2,1)S(1)}, bf16[46,32,128]{2,1,0:T(8,128)(2,1)S(1)}, u32[]{:S(2)}, u32[]{:S(2)}) %collective-permute-start.14) | collective-permute-done | bytes 376864 | tf_op jit(solution)/shard_map/ppermute | solution.py:406
  42.3 0.0 copy-done.1
  42.3 0.0 copy-done.6
  42.3 4.9 %attend_first.1 = (f32[4096,128]{1,0:T(8,128)S(1)}, f32[4096,128]{1,0:T(8,128)S(1)}, f32[4096,128]{1,0:T(8,128)S(1)}) custom-call(s32[4,16]{1,0:T(4,128)S(1)} %copy-done.5, s32[4,64]{1,0:T(4,128)S(1)} %copy-done.6, bf16[128,4096]{1,0:T(8,128)(2,1)S(1)} %copy-done.1, bf16[46,32,128]{2,1,0:T(8,128)(2,1)S(1)} %merge.7.refs_3_, ...), custom_call_target="tpu_custom_call" | custom-call | flops 1048576 | bytes 1048576 | tf_op jit(solution)/shard_map/attend_first/pallas_call | solution.py:393
  47.2 2.1 %collective-permute-done.15.refs_3_ = bf16[64,16,128]{2,1,0:T(8,128)(2,1)S(1)} collective-permute-done((bf16[64,16,128]{2,1,0:T(8,128)(2,1)S(1)}, bf16[64,16,128]{2,1,0:T(8,128)(2,1)S(1)}, u32[]{:S(2)}, u32[]{:S(2)}) %collective-permute-start.15) | collective-permute-done | bytes 262176 | tf_op jit(solution)/shard_map/ppermute | solution.py:406
  49.3 0.0 collective-permute-start.17
  49.3 0.0 collective-permute-done.16.refs_4_
  49.3 1.5 %collective-permute-done.17.refs_5_ = bf16[64,16,128]{2,1,0:T(8,128)(2,1)S(1)} collective-permute-done((bf16[64,16,128]{2,1,0:T(8,128)(2,1)S(1)}, bf16[64,16,128]{2,1,0:T(8,128)(2,1)S(1)}, u32[]{:S(2)}, u32[]{:S(2)}) %collective-permute-start.17) | collective-permute-done | bytes 262176 | tf_op jit(solution)/shard_map/ppermute | solution.py:406
  50.8 4.0 %attend_last.1 = bf16[128,4096]{1,0:T(8,128)(2,1)} custom-call(s32[4,16]{1,0:T(4,128)S(1)} %copy-done.5, bf16[128,4096]{1,0:T(8,128)(2,1)S(1)} %copy-done.1, bf16[64,16,128]{2,1,0:T(8,128)(2,1)S(1)} %merge.9.refs_2_, bf16[64,16,128]{2,1,0:T(8,128)(2,1)S(1)} %collective-permute-done.15.refs_3_, bf16[64,16,128]{2,1,0:T(8,128)(2,1)S(1)} %collective-permute-done.16.refs_4_, ...), custom_call_target="tpu_custom_call" | custom-call | flops 1048576 | bytes 1048576 | tf_op jit(solution)/shard_map/attend_last/pallas_call | solution.py:393
  54.8 0.0 copy-done
  54.8 0.2 while.9
  (9 shorter events, 0.0 us)
Async XLA Ops:
  0.0 10.0 %copy-start.7 = (s32[6]{0:T(128)S(1)}, s32[6]{0:T(128)}, u32[]{:S(2)}) copy-start(s32[6]{0:T(128)} %constant.46) | copy-start | bytes 76
  0.0 11.7 %copy-start.8 = (s32[6]{0:T(128)S(1)}, s32[6]{0:T(128)}, u32[]{:S(2)}) copy-start(s32[6]{0:T(128)} %constant.45.clone) | copy-start | bytes 76
  0.0 2.9 %copy-start.5 = (s32[4,16]{1,0:T(4,128)S(1)}, s32[4,16]{1,0:T(4,128)}, u32[]{:S(2)}) copy-start(s32[4,16]{1,0:T(4,128)} %refs_0_.3) | copy-start | bytes 772
  0.0 3.0 %copy-start.2 = (bf16[128,512]{1,0:T(8,128)(2,1)S(1)}, bf16[128,512]{1,0:T(8,128)(2,1)}, u32[]{:S(2)}) copy-start(bf16[128,512]{1,0:T(8,128)(2,1)} %refs_9_.1) | copy-start | bytes 393220
  0.0 3.0 %copy-start.3 = (bf16[128,512]{1,0:T(8,128)(2,1)S(1)}, bf16[128,512]{1,0:T(8,128)(2,1)}, u32[]{:S(2)}) copy-start(bf16[128,512]{1,0:T(8,128)(2,1)} %refs_8_.1) | copy-start | bytes 393220
  2.4 39.9 %copy-start.1 = (bf16[128,4096]{1,0:T(8,128)(2,1)S(1)}, bf16[128,4096]{1,0:T(8,128)(2,1)}, u32[]{:S(2)}) copy-start(bf16[128,4096]{1,0:T(8,128)(2,1)} %refs_1_.3) | copy-start | bytes 3145732
  2.4 39.9 %copy-start.6 = (s32[4,64]{1,0:T(4,128)S(1)}, s32[4,64]{1,0:T(4,128)}, u32[]{:S(2)}) copy-start(s32[4,64]{1,0:T(4,128)} %refs_1_.2) | copy-start | bytes 3076
  2.4 1.7 %collective-permute-start.5 = (bf16[13,64,128]{2,1,0:T(8,128)(2,1)S(1)}, bf16[13,64,128]{2,1,0:T(8,128)(2,1)S(1)}, u32[]{:S(2)}, u32[]{:S(2)}) collective-permute-start(bf16[13,64,128]{2,1,0:T(8,128)(2,1)S(1)} %get-tuple-element.79), channel_id=1, source_target_pairs={{0,1},{1,0},{2,3},{3,2},{4,5},{5,4},{6,7},{7,6},{8,9},{9,8},{10,11... | collective-permute-start | bytes 638984 | tf_op jit(solution)/shard_map/ppermute | solution.py:406
  4.6 11.4 %collective-permute-start.6 = (bf16[18,32,128]{2,1,0:T(8,128)(2,1)S(1)}, bf16[18,32,128]{2,1,0:T(8,128)(2,1)S(1)}, u32[]{:S(2)}, u32[]{:S(2)}) collective-permute-start(bf16[18,32,128]{2,1,0:T(8,128)(2,1)S(1)} %get-tuple-element.80.refs_0_), channel_id=1, source_target_pairs={{0,8},{1,9},{2,10},{3,11},{4,12},{5,13},{6,14},{7,15},{8,0},{9,1},... | collective-permute-start | bytes 442376 | tf_op jit(solution)/shard_map/ppermute | solution.py:406
  8.7 7.3 %collective-permute-start.7 = (bf16[18,32,128]{2,1,0:T(8,128)(2,1)S(1)}, bf16[18,32,128]{2,1,0:T(8,128)(2,1)S(1)}, u32[]{:S(2)}, u32[]{:S(2)}) collective-permute-start(bf16[18,32,128]{2,1,0:T(8,128)(2,1)S(1)} %get-tuple-element.84.refs_2_), channel_id=1, source_target_pairs={{0,2},{1,3},{2,0},{3,1},{4,6},{5,7},{6,4},{7,5},{8,10},{9,11},{10,... | collective-permute-start | bytes 442376 | tf_op jit(solution)/shard_map/ppermute | solution.py:406
  10.2 7.4 %collective-permute-start.9 = (bf16[128,1024]{1,0:T(8,128)(2,1)S(1)}, bf16[128,1024]{1,0:T(8,128)(2,1)S(1)}, u32[]{:S(2)}, u32[]{:S(2)}) collective-permute-start(bf16[128,1024]{1,0:T(8,128)(2,1)S(1)} %pad_maximum_fusion), channel_id=1, source_target_pairs={{0,1},{1,2},{2,3},{3,4},{4,5},{5,6},{6,7},{7,8},{8,9},{9,10},{10,1... | collective-permute-start | bytes 786440 | tf_op jit(solution)/shard_map/ppermute | solution.py:406
  17.1 7.2 %collective-permute-start.8 = (bf16[28,32,128]{2,1,0:T(8,128)(2,1)S(1)}, bf16[28,32,128]{2,1,0:T(8,128)(2,1)S(1)}, u32[]{:S(2)}, u32[]{:S(2)}) collective-permute-start(bf16[28,32,128]{2,1,0:T(8,128)(2,1)S(1)} %get-tuple-element.85.refs_0_), channel_id=1, source_target_pairs={{0,4},{1,5},{2,6},{3,7},{4,0},{5,1},{6,2},{7,3},{8,12},{9,13},{10,... | collective-permute-start | bytes 688136 | tf_op jit(solution)/shard_map/ppermute | solution.py:406
  24.8 15.7 %collective-permute-start.10 = (bf16[46,32,128]{2,1,0:T(8,128)(2,1)S(1)}, bf16[46,32,128]{2,1,0:T(8,128)(2,1)S(1)}, u32[]{:S(2)}, u32[]{:S(2)}) collective-permute-start(bf16[46,32,128]{2,1,0:T(8,128)(2,1)S(1)} %merge.7.refs_3_), channel_id=1, source_target_pairs={{0,2},{1,3},{2,0},{3,1},{4,6},{5,7},{6,4},{7,5},{8,10},{9,11},{10,... | collective-permute-start | bytes 1130504 | tf_op jit(solution)/shard_map/ppermute | solution.py:406
  25.9 8.0 %collective-permute-start.11 = (bf16[28,16,128]{2,1,0:T(8,128)(2,1)S(1)}, bf16[28,16,128]{2,1,0:T(8,128)(2,1)S(1)}, u32[]{:S(2)}, u32[]{:S(2)}) collective-permute-start(bf16[28,16,128]{2,1,0:T(8,128)(2,1)S(1)} %get-tuple-element.88.refs_0_), channel_id=1, source_target_pairs={{0,8},{1,9},{2,10},{3,11},{4,12},{5,13},{6,14},{7,15},{8,0},{9,1},... | collective-permute-start | bytes 344072 | tf_op jit(solution)/shard_map/ppermute | solution.py:406
  34.4 5.6 %collective-permute-start.12 = (bf16[46,16,128]{2,1,0:T(8,128)(2,1)S(1)}, bf16[46,16,128]{2,1,0:T(8,128)(2,1)S(1)}, u32[]{:S(2)}, u32[]{:S(2)}) collective-permute-start(bf16[46,16,128]{2,1,0:T(8,128)(2,1)S(1)} %merge.8.refs_0_), channel_id=1, source_target_pairs={{0,4},{1,5},{2,6},{3,7},{4,0},{5,1},{6,2},{7,3},{8,12},{9,13},{10,... | collective-permute-start | bytes 565256 | tf_op jit(solution)/shard_map/ppermute | solution.py:406
  35.1 6.2 %collective-permute-start.13 = (bf16[46,32,128]{2,1,0:T(8,128)(2,1)S(1)}, bf16[46,32,128]{2,1,0:T(8,128)(2,1)S(1)}, u32[]{:S(2)}, u32[]{:S(2)}) collective-permute-start(bf16[46,32,128]{2,1,0:T(8,128)(2,1)S(1)} %merge.7.refs_3_), channel_id=1, source_target_pairs={{0,1},{1,0},{2,3},{3,2},{4,5},{5,4},{6,7},{7,6},{8,9},{9,8},{10,11... | collective-permute-start | bytes 1130504 | tf_op jit(solution)/shard_map/ppermute | solution.py:406
  40.5 1.8 %collective-permute-start.14 = (bf16[46,32,128]{2,1,0:T(8,128)(2,1)S(1)}, bf16[46,32,128]{2,1,0:T(8,128)(2,1)S(1)}, u32[]{:S(2)}, u32[]{:S(2)}) collective-permute-start(bf16[46,32,128]{2,1,0:T(8,128)(2,1)S(1)} %collective-permute-done.10.refs_4_), channel_id=1, source_target_pairs={{0,1},{1,0},{2,3},{3,2},{4,5},{5,4},{6,7},{7,6},{8,9},{9,8},{10,11... | collective-permute-start | bytes 1130504 | tf_op jit(solution)/shard_map/ppermute | solution.py:406
  40.6 8.7 %collective-permute-start.15 = (bf16[64,16,128]{2,1,0:T(8,128)(2,1)S(1)}, bf16[64,16,128]{2,1,0:T(8,128)(2,1)S(1)}, u32[]{:S(2)}, u32[]{:S(2)}) collective-permute-start(bf16[64,16,128]{2,1,0:T(8,128)(2,1)S(1)} %merge.9.refs_2_), channel_id=1, source_target_pairs={{0,2},{1,3},{2,0},{3,1},{4,6},{5,7},{6,4},{7,5},{8,10},{9,11},{10,... | collective-permute-start | bytes 786440 | tf_op jit(solution)/shard_map/ppermute | solution.py:406
  41.2 8.2 %collective-permute-start.16 = (bf16[64,16,128]{2,1,0:T(8,128)(2,1)S(1)}, bf16[64,16,128]{2,1,0:T(8,128)(2,1)S(1)}, u32[]{:S(2)}, u32[]{:S(2)}) collective-permute-start(bf16[64,16,128]{2,1,0:T(8,128)(2,1)S(1)} %merge.9.refs_2_), channel_id=1, source_target_pairs={{0,1},{1,0},{2,3},{3,2},{4,5},{5,4},{6,7},{7,6},{8,9},{9,8},{10,11... | collective-permute-start | bytes 786440 | tf_op jit(solution)/shard_map/ppermute | solution.py:406
  49.3 5.5 %copy-start = (bf16[2048,512]{1,0:T(8,128)(2,1)S(1)}, bf16[2048,512]{1,0:T(8,128)(2,1)}, u32[]{:S(2)}) copy-start(bf16[2048,512]{1,0:T(8,128)(2,1)} %cache_k.1) | copy-start | bytes 6291460
  49.3 1.5 %collective-permute-start.17 = (bf16[64,16,128]{2,1,0:T(8,128)(2,1)S(1)}, bf16[64,16,128]{2,1,0:T(8,128)(2,1)S(1)}, u32[]{:S(2)}, u32[]{:S(2)}) collective-permute-start(bf16[64,16,128]{2,1,0:T(8,128)(2,1)S(1)} %collective-permute-done.15.refs_3_), channel_id=1, source_target_pairs={{0,1},{1,0},{2,3},{3,2},{4,5},{5,4},{6,7},{7,6},{8,9},{9,8},{10,11... | collective-permute-start | bytes 786440 | tf_op jit(solution)/shard_map/ppermute | solution.py:406

commit v15 on v13

--- a/solution.py
+++ b/solution.py
@@ -462,12 +462,14 @@
     steps_b = list(zip([1] + masks_b, [near] + far))
     other_a = swapped(mine_a, far[0])
     other_b = swapped(mine_b, near)
-    other_a, short = lax.optimization_barrier((other_a, short))
+    other_b, short = lax.optimization_barrier((other_b, short))
     for at in range(len(far)):
         job_a = job(*steps_a[at], mine_a, other_a)
         job_b = job(*steps_b[at], mine_b, other_b, halved=near if at == 0 else 0)
         if at < len(far) - 1:
-            mine_a, mine_b = merge([job_a, job_b])
+            (mine_b,) = merge([job_b])
+            other_a, mine_b = lax.optimization_barrier((other_a, mine_b))
+            (mine_a,) = merge([job(*steps_a[at], mine_a, other_a)])
         else:
             (mine_a,), (mine_b,) = merge([job_a]), merge([job_b])
         other_a = swapped(mine_a, (far + [near])[at + 1])

time: 52.3 us -> 53 us (1.013)
  waiting for transfers between devices: 19 us -> 20.6 us
    ppermute x13, waiting for transfers between devices: 19 us -> 20.6 us  [permuted(): return lax.ppermute(array, 'ctx', pairs)]
    pallas_call x5 -> x6, Pallas kernels: 3.1 us -> 3.2 us  [merged(): pl.pallas_call(functools.partial(merge_kernel, per_device, [job[:4] for j...]
where the time goes in v15:
time: 53 us; the launch traced here: 52.8 us
  waiting for transfers between devices  20.6 us (39%)
  starting transfers between devices  16 us (30%)
  Pallas kernels  14 us (26%)
  between operations  1 us (2%)
  other arithmetic  0.98 us (2%)
    ppermute x13, waiting for transfers between devices, permuted(): return lax.ppermute(array, 'ctx', pairs)  20.6 us
    ppermute x13, starting transfers between devices, permuted(): return lax.ppermute(array, 'ctx', pairs)  16 us
    pallas_call x2, Pallas kernels, attend_stage(): pl.pallas_call(functools.partial(stage_kernel, per_device, known, bit, ba...  8.89 us
    pallas_call x6, Pallas kernels, merged(): pl.pallas_call(functools.partial(merge_kernel, per_device, [job[:4] for j...  3.2 us
    pallas_call x1, Pallas kernels, pack(): pl.pallas_call(functools.partial(pack_kernel, cache_k.shape[0] // VBLOCK,...  1.88 us
  transfers between devices with their start and end apart: 13, of which 8 were waited for; matrix products, arithmetic and copies ran while one was open for 2% of the time, Pallas kernels for 13%

profile of v15, /device:TPU:9, one launch (start us, length us, event | category | flops | bytes accessed | tf_op | source)
XLA Modules:
  0.0 52.8 jit_solution(1016177958273382941)
XLA Ops:
  0.0 0.0 copy-start.2
  0.0 0.0 copy-start.3
  0.0 1.9 %pack.1 = (bf16[13,64,128]{2,1,0:T(8,128)(2,1)S(1)}, bf16[13,64,128]{2,1,0:T(8,128)(2,1)S(1)}) custom-call(s32[4,16]{1,0:T(4,128)} %refs_0_.3, bf16[2048,512]{1,0:T(8,128)(2,1)} %cache_k.1, bf16[2048,512]{1,0:T(8,128)(2,1)} %cache_v.1), custom_call_target="tpu_custom_call" | custom-call | tf_op jit(solution)/shard_map/pack/pallas_call | solution.py:227
  1.9 0.0 copy-start.1
  1.9 0.0 copy-start.6
  1.9 1.2 %collective-permute-start.5 = (bf16[13,64,128]{2,1,0:T(8,128)(2,1)S(1)}, bf16[13,64,128]{2,1,0:T(8,128)(2,1)S(1)}, u32[]{:S(2)}, u32[]{:S(2)}) collective-permute-start(bf16[13,64,128]{2,1,0:T(8,128)(2,1)S(1)} %get-tuple-element.80), channel_id=1, source_target_pairs={{0,1},{1,0},{2,3},{3,2},{4,5},{5,4},{6,7},{7,6},{8,9},{9,8},{10,11... | collective-permute-start | bytes 638984 | tf_op jit(solution)/shard_map/ppermute | solution.py:406
  3.1 0.0 copy-done.5
  3.1 0.1 xor.20
  3.2 0.0 copy-done.2
  3.2 0.0 copy-done.3
  3.3 0.9 %collective-permute-done.5.refs_1_ = bf16[13,64,128]{2,1,0:T(8,128)(2,1)S(1)} collective-permute-done((bf16[13,64,128]{2,1,0:T(8,128)(2,1)S(1)}, bf16[13,64,128]{2,1,0:T(8,128)(2,1)S(1)}, u32[]{:S(2)}, u32[]{:S(2)}) %collective-permute-start.5) | collective-permute-done | bytes 213024 | tf_op jit(solution)/shard_map/ppermute | solution.py:406
  4.2 0.6 %merge.6 = (bf16[18,32,128]{2,1,0:T(8,128)(2,1)S(1)}, bf16[18,32,128]{2,1,0:T(8,128)(2,1)S(1)}) custom-call(s32[4,16]{1,0:T(4,128)S(1)} %copy-done.5, bf16[13,64,128]{2,1,0:T(8,128)(2,1)S(1)} %get-tuple-element.79.refs_0_, bf16[13,64,128]{2,1,0:T(8,128)(2,1)S(1)} %collective-permute-done.5.refs_1_), custom_call_target="tpu_custom_call" | custom-call | tf_op jit(solution)/shard_map/merge/pallas_call | solution.py:277
  4.8 1.3 %collective-permute-start.6 = (bf16[18,32,128]{2,1,0:T(8,128)(2,1)S(1)}, bf16[18,32,128]{2,1,0:T(8,128)(2,1)S(1)}, u32[]{:S(2)}, u32[]{:S(2)}) collective-permute-start(bf16[18,32,128]{2,1,0:T(8,128)(2,1)S(1)} %get-tuple-element.82.refs_0_), channel_id=1, source_target_pairs={{0,2},{1,3},{2,0},{3,1},{4,6},{5,7},{6,4},{7,5},{8,10},{9,11},{10,... | collective-permute-start | bytes 442376 | tf_op jit(solution)/shard_map/ppermute | solution.py:406
  6.1 2.3 %collective-permute-start.7 = (bf16[18,32,128]{2,1,0:T(8,128)(2,1)S(1)}, bf16[18,32,128]{2,1,0:T(8,128)(2,1)S(1)}, u32[]{:S(2)}, u32[]{:S(2)}) collective-permute-start(bf16[18,32,128]{2,1,0:T(8,128)(2,1)S(1)} %get-tuple-element.84.refs_0_), channel_id=1, source_target_pairs={{0,8},{1,9},{2,10},{3,11},{4,12},{5,13},{6,14},{7,15},{8,0},{9,1},... | collective-permute-start | bytes 442376 | tf_op jit(solution)/shard_map/ppermute | solution.py:406
  8.4 0.2 convert_reduce_fusion
  8.7 2.9 %collective-permute-start.10 = (bf16[128,1024]{1,0:T(8,128)(2,1)S(1)}, bf16[128,1024]{1,0:T(8,128)(2,1)S(1)}, u32[]{:S(2)}, u32[]{:S(2)}) collective-permute-start(bf16[128,1024]{1,0:T(8,128)(2,1)S(1)} %pad_maximum_fusion), channel_id=1, source_target_pairs={{0,1},{1,2},{2,3},{3,4},{4,5},{5,6},{6,7},{7,8},{8,9},{9,10},{10,1... | collective-permute-start | bytes 786440 | tf_op jit(solution)/shard_map/ppermute | solution.py:406
  11.6 0.7 %compare_reduce_fusion = pred[]{:T(512)} fusion(s32[6,16]{1,0:T(8,128)S(1)} %convert_reduce_fusion, s32[6]{0:T(128)S(1)} %copy-done.8), kind=kLoop, calls=%fused_computation.8 | loop fusion | flops 191 | bytes 409 | tf_op jit(solution)/shard_map/reduce_and | solution.py:419
  13.0 0.0 collective-permute-done.6.refs_1_
  13.0 0.6 %merge.7.refs_0_ = bf16[28,16,128]{2,1,0:T(8,128)(2,1)S(1)} custom-call(s32[4,16]{1,0:T(4,128)S(1)} %copy-done.5, bf16[18,32,128]{2,1,0:T(8,128)(2,1)S(1)} %get-tuple-element.82.refs_0_, bf16[18,32,128]{2,1,0:T(8,128)(2,1)S(1)} %collective-permute-done.6.refs_1_), custom_call_target="tpu_custom_call" | custom-call | tf_op jit(solution)/shard_map/merge/pallas_call | solution.py:277
  13.6 1.5 %collective-permute-done.7.refs_1_ = bf16[18,32,128]{2,1,0:T(8,128)(2,1)S(1)} collective-permute-done((bf16[18,32,128]{2,1,0:T(8,128)(2,1)S(1)}, bf16[18,32,128]{2,1,0:T(8,128)(2,1)S(1)}, u32[]{:S(2)}, u32[]{:S(2)}) %collective-permute-start.7) | collective-permute-done | bytes 147488 | tf_op jit(solution)/shard_map/ppermute | solution.py:406
  15.1 0.5 %merge.8.refs_0_ = bf16[28,32,128]{2,1,0:T(8,128)(2,1)S(1)} custom-call(s32[4,16]{1,0:T(4,128)S(1)} %copy-done.5, bf16[18,32,128]{2,1,0:T(8,128)(2,1)S(1)} %get-tuple-element.84.refs_0_, bf16[18,32,128]{2,1,0:T(8,128)(2,1)S(1)} %collective-permute-done.7.refs_1_), custom_call_target="tpu_custom_call" | custom-call | tf_op jit(solution)/shard_map/merge/pallas_call | solution.py:277
  15.6 0.2 collective-permute-start.8
  15.8 3.1 %collective-permute-start.9 = (bf16[28,16,128]{2,1,0:T(8,128)(2,1)S(1)}, bf16[28,16,128]{2,1,0:T(8,128)(2,1)S(1)}, u32[]{:S(2)}, u32[]{:S(2)}) collective-permute-start(bf16[28,16,128]{2,1,0:T(8,128)(2,1)S(1)} %merge.7.refs_0_), channel_id=1, source_target_pairs={{0,8},{1,9},{2,10},{3,11},{4,12},{5,13},{6,14},{7,15},{8,0},{9,1},... | collective-permute-start | bytes 344072 | tf_op jit(solution)/shard_map/ppermute | solution.py:406
  18.9 7.9 %collective-permute-done.9.refs_1_ = bf16[28,16,128]{2,1,0:T(8,128)(2,1)S(1)} collective-permute-done((bf16[28,16,128]{2,1,0:T(8,128)(2,1)S(1)}, bf16[28,16,128]{2,1,0:T(8,128)(2,1)S(1)}, u32[]{:S(2)}, u32[]{:S(2)}) %collective-permute-start.9) | collective-permute-done | bytes 114720 | tf_op jit(solution)/shard_map/ppermute | solution.py:406
  26.8 0.0 collective-permute-done.10.refs_7_
  26.8 0.0 collective-permute-done.8.refs_1_
  26.8 0.5 merge.9.refs_3_
  27.3 0.2 collective-permute-start.11
  27.5 0.5 merge.10.refs_0_
  28.1 0.1 collective-permute-start.12
  28.1 1.5 %collective-permute-start.13 = (bf16[46,32,128]{2,1,0:T(8,128)(2,1)S(1)}, bf16[46,32,128]{2,1,0:T(8,128)(2,1)S(1)}, u32[]{:S(2)}, u32[]{:S(2)}) collective-permute-start(bf16[46,32,128]{2,1,0:T(8,128)(2,1)S(1)} %merge.9.refs_3_), channel_id=1, source_target_pairs={{0,1},{1,0},{2,3},{3,2},{4,5},{5,4},{6,7},{7,6},{8,9},{9,8},{10,11... | collective-permute-start | bytes 1130504 | tf_op jit(solution)/shard_map/ppermute | solution.py:406
  29.6 3.3 %collective-permute-done.12.refs_1_ = bf16[46,16,128]{2,1,0:T(8,128)(2,1)S(1)} collective-permute-done((bf16[46,16,128]{2,1,0:T(8,128)(2,1)S(1)}, bf16[46,16,128]{2,1,0:T(8,128)(2,1)S(1)}, u32[]{:S(2)}, u32[]{:S(2)}) %collective-permute-start.12) | collective-permute-done | bytes 188448 | tf_op jit(solution)/shard_map/ppermute | solution.py:406
  32.9 0.5 merge.11.refs_2_
  33.4 3.2 %collective-permute-done.11.refs_4_ = bf16[46,32,128]{2,1,0:T(8,128)(2,1)S(1)} collective-permute-done((bf16[46,32,128]{2,1,0:T(8,128)(2,1)S(1)}, bf16[46,32,128]{2,1,0:T(8,128)(2,1)S(1)}, u32[]{:S(2)}, u32[]{:S(2)}) %collective-permute-start.11) | collective-permute-done | bytes 376864 | tf_op jit(solution)/shard_map/ppermute | solution.py:406
  36.6 1.9 %collective-permute-start.14 = (bf16[46,32,128]{2,1,0:T(8,128)(2,1)S(1)}, bf16[46,32,128]{2,1,0:T(8,128)(2,1)S(1)}, u32[]{:S(2)}, u32[]{:S(2)}) collective-permute-start(bf16[46,32,128]{2,1,0:T(8,128)(2,1)S(1)} %collective-permute-done.11.refs_4_), channel_id=1, source_target_pairs={{0,1},{1,0},{2,3},{3,2},{4,5},{5,4},{6,7},{7,6},{8,9},{9,8},{10,11... | collective-permute-start | bytes 1130504 | tf_op jit(solution)/shard_map/ppermute | solution.py:406
  38.6 0.2 collective-permute-start.15
  38.7 0.3 collective-permute-start.16
  39.0 0.0 collective-permute-done.13.refs_5_
  39.0 0.9 %collective-permute-done.14.refs_6_ = bf16[46,32,128]{2,1,0:T(8,128)(2,1)S(1)} collective-permute-done((bf16[46,32,128]{2,1,0:T(8,128)(2,1)S(1)}, bf16[46,32,128]{2,1,0:T(8,128)(2,1)S(1)}, u32[]{:S(2)}, u32[]{:S(2)}) %collective-permute-start.14) | collective-permute-done | bytes 376864 | tf_op jit(solution)/shard_map/ppermute | solution.py:406
  39.9 0.0 copy-done.6
  39.9 4.9 %attend_first.1 = (f32[4096,128]{1,0:T(8,128)S(1)}, f32[4096,128]{1,0:T(8,128)S(1)}, f32[4096,128]{1,0:T(8,128)S(1)}) custom-call(s32[4,16]{1,0:T(4,128)S(1)} %copy-done.5, s32[4,64]{1,0:T(4,128)S(1)} %copy-done.6, bf16[128,4096]{1,0:T(8,128)(2,1)S(1)} %copy-done.1, bf16[46,32,128]{2,1,0:T(8,128)(2,1)S(1)} %merge.9.refs_3_, ...), custom_call_target="tpu_custom_call" | custom-call | flops 1048576 | bytes 1048576 | tf_op jit(solution)/shard_map/attend_first/pallas_call | solution.py:393
  44.8 1.7 %collective-permute-done.15.refs_3_ = bf16[64,16,128]{2,1,0:T(8,128)(2,1)S(1)} collective-permute-done((bf16[64,16,128]{2,1,0:T(8,128)(2,1)S(1)}, bf16[64,16,128]{2,1,0:T(8,128)(2,1)S(1)}, u32[]{:S(2)}, u32[]{:S(2)}) %collective-permute-start.15) | collective-permute-done | bytes 262176 | tf_op jit(solution)/shard_map/ppermute | solution.py:406
  46.5 0.8 %collective-permute-start.17 = (bf16[64,16,128]{2,1,0:T(8,128)(2,1)S(1)}, bf16[64,16,128]{2,1,0:T(8,128)(2,1)S(1)}, u32[]{:S(2)}, u32[]{:S(2)}) collective-permute-start(bf16[64,16,128]{2,1,0:T(8,128)(2,1)S(1)} %collective-permute-done.15.refs_3_), channel_id=1, source_target_pairs={{0,1},{1,0},{2,3},{3,2},{4,5},{5,4},{6,7},{7,6},{8,9},{9,8},{10,11... | collective-permute-start | bytes 786440 | tf_op jit(solution)/shard_map/ppermute | solution.py:406
  47.3 0.0 collective-permute-done.16.refs_4_
  47.3 1.2 %collective-permute-done.17.refs_5_ = bf16[64,16,128]{2,1,0:T(8,128)(2,1)S(1)} collective-permute-done((bf16[64,16,128]{2,1,0:T(8,128)(2,1)S(1)}, bf16[64,16,128]{2,1,0:T(8,128)(2,1)S(1)}, u32[]{:S(2)}, u32[]{:S(2)}) %collective-permute-start.17) | collective-permute-done | bytes 262176 | tf_op jit(solution)/shard_map/ppermute | solution.py:406
  48.4 4.0 %attend_last.1 = bf16[128,4096]{1,0:T(8,128)(2,1)} custom-call(s32[4,16]{1,0:T(4,128)S(1)} %copy-done.5, bf16[128,4096]{1,0:T(8,128)(2,1)S(1)} %copy-done.1, bf16[64,16,128]{2,1,0:T(8,128)(2,1)S(1)} %merge.11.refs_2_, bf16[64,16,128]{2,1,0:T(8,128)(2,1)S(1)} %collective-permute-done.15.refs_3_, bf16[64,16,128]{2,1,0:T(8,128)(2,1)S(1)} %collective-permute-done.16.refs_4_, ...), custom_call_target="tpu_custom_call" | custom-call | flops 1048576 | bytes 1048576 | tf_op jit(solution)/shard_map/attend_last/pallas_call | solution.py:393
  52.4 0.0 copy-done
  52.4 0.2 while.9
  (10 shorter events, 0.0 us)
Async XLA Ops:
  0.0 8.4 %copy-start.7 = (s32[6]{0:T(128)S(1)}, s32[6]{0:T(128)}, u32[]{:S(2)}) copy-start(s32[6]{0:T(128)} %constant.46) | copy-start | bytes 76
  0.0 11.6 %copy-start.8 = (s32[6]{0:T(128)S(1)}, s32[6]{0:T(128)}, u32[]{:S(2)}) copy-start(s32[6]{0:T(128)} %constant.45.clone) | copy-start | bytes 76
  0.0 3.1 %copy-start.5 = (s32[4,16]{1,0:T(4,128)S(1)}, s32[4,16]{1,0:T(4,128)}, u32[]{:S(2)}) copy-start(s32[4,16]{1,0:T(4,128)} %refs_0_.3) | copy-start | bytes 772
  0.0 3.2 %copy-start.2 = (bf16[128,512]{1,0:T(8,128)(2,1)S(1)}, bf16[128,512]{1,0:T(8,128)(2,1)}, u32[]{:S(2)}) copy-start(bf16[128,512]{1,0:T(8,128)(2,1)} %refs_9_.1) | copy-start | bytes 393220
  0.0 3.2 %copy-start.3 = (bf16[128,512]{1,0:T(8,128)(2,1)S(1)}, bf16[128,512]{1,0:T(8,128)(2,1)}, u32[]{:S(2)}) copy-start(bf16[128,512]{1,0:T(8,128)(2,1)} %refs_8_.1) | copy-start | bytes 393220
  1.9 38.0 %copy-start.1 = (bf16[128,4096]{1,0:T(8,128)(2,1)S(1)}, bf16[128,4096]{1,0:T(8,128)(2,1)}, u32[]{:S(2)}) copy-start(bf16[128,4096]{1,0:T(8,128)(2,1)} %refs_1_.3) | copy-start | bytes 3145732
  1.9 37.9 %copy-start.6 = (s32[4,64]{1,0:T(4,128)S(1)}, s32[4,64]{1,0:T(4,128)}, u32[]{:S(2)}) copy-start(s32[4,64]{1,0:T(4,128)} %refs_1_.2) | copy-start | bytes 3076
  1.9 2.3 %collective-permute-start.5 = (bf16[13,64,128]{2,1,0:T(8,128)(2,1)S(1)}, bf16[13,64,128]{2,1,0:T(8,128)(2,1)S(1)}, u32[]{:S(2)}, u32[]{:S(2)}) collective-permute-start(bf16[13,64,128]{2,1,0:T(8,128)(2,1)S(1)} %get-tuple-element.80), channel_id=1, source_target_pairs={{0,1},{1,0},{2,3},{3,2},{4,5},{5,4},{6,7},{7,6},{8,9},{9,8},{10,11... | collective-permute-start | bytes 638984 | tf_op jit(solution)/shard_map/ppermute | solution.py:406
  4.8 8.2 %collective-permute-start.6 = (bf16[18,32,128]{2,1,0:T(8,128)(2,1)S(1)}, bf16[18,32,128]{2,1,0:T(8,128)(2,1)S(1)}, u32[]{:S(2)}, u32[]{:S(2)}) collective-permute-start(bf16[18,32,128]{2,1,0:T(8,128)(2,1)S(1)} %get-tuple-element.82.refs_0_), channel_id=1, source_target_pairs={{0,2},{1,3},{2,0},{3,1},{4,6},{5,7},{6,4},{7,5},{8,10},{9,11},{10,... | collective-permute-start | bytes 442376 | tf_op jit(solution)/shard_map/ppermute | solution.py:406
  6.1 9.0 %collective-permute-start.7 = (bf16[18,32,128]{2,1,0:T(8,128)(2,1)S(1)}, bf16[18,32,128]{2,1,0:T(8,128)(2,1)S(1)}, u32[]{:S(2)}, u32[]{:S(2)}) collective-permute-start(bf16[18,32,128]{2,1,0:T(8,128)(2,1)S(1)} %get-tuple-element.84.refs_0_), channel_id=1, source_target_pairs={{0,8},{1,9},{2,10},{3,11},{4,12},{5,13},{6,14},{7,15},{8,0},{9,1},... | collective-permute-start | bytes 442376 | tf_op jit(solution)/shard_map/ppermute | solution.py:406
  8.7 18.1 %collective-permute-start.10 = (bf16[128,1024]{1,0:T(8,128)(2,1)S(1)}, bf16[128,1024]{1,0:T(8,128)(2,1)S(1)}, u32[]{:S(2)}, u32[]{:S(2)}) collective-permute-start(bf16[128,1024]{1,0:T(8,128)(2,1)S(1)} %pad_maximum_fusion), channel_id=1, source_target_pairs={{0,1},{1,2},{2,3},{3,4},{4,5},{5,6},{6,7},{7,8},{8,9},{9,10},{10,1... | collective-permute-start | bytes 786440 | tf_op jit(solution)/shard_map/ppermute | solution.py:406
  15.6 11.2 %collective-permute-start.8 = (bf16[28,32,128]{2,1,0:T(8,128)(2,1)S(1)}, bf16[28,32,128]{2,1,0:T(8,128)(2,1)S(1)}, u32[]{:S(2)}, u32[]{:S(2)}) collective-permute-start(bf16[28,32,128]{2,1,0:T(8,128)(2,1)S(1)} %merge.8.refs_0_), channel_id=1, source_target_pairs={{0,4},{1,5},{2,6},{3,7},{4,0},{5,1},{6,2},{7,3},{8,12},{9,13},{10,... | collective-permute-start | bytes 688136 | tf_op jit(solution)/shard_map/ppermute | solution.py:406
  15.8 11.0 %collective-permute-start.9 = (bf16[28,16,128]{2,1,0:T(8,128)(2,1)S(1)}, bf16[28,16,128]{2,1,0:T(8,128)(2,1)S(1)}, u32[]{:S(2)}, u32[]{:S(2)}) collective-permute-start(bf16[28,16,128]{2,1,0:T(8,128)(2,1)S(1)} %merge.7.refs_0_), channel_id=1, source_target_pairs={{0,8},{1,9},{2,10},{3,11},{4,12},{5,13},{6,14},{7,15},{8,0},{9,1},... | collective-permute-start | bytes 344072 | tf_op jit(solution)/shard_map/ppermute | solution.py:406
  27.3 9.3 %collective-permute-start.11 = (bf16[46,32,128]{2,1,0:T(8,128)(2,1)S(1)}, bf16[46,32,128]{2,1,0:T(8,128)(2,1)S(1)}, u32[]{:S(2)}, u32[]{:S(2)}) collective-permute-start(bf16[46,32,128]{2,1,0:T(8,128)(2,1)S(1)} %merge.9.refs_3_), channel_id=1, source_target_pairs={{0,2},{1,3},{2,0},{3,1},{4,6},{5,7},{6,4},{7,5},{8,10},{9,11},{10,... | collective-permute-start | bytes 1130504 | tf_op jit(solution)/shard_map/ppermute | solution.py:406
  28.1 4.9 %collective-permute-start.12 = (bf16[46,16,128]{2,1,0:T(8,128)(2,1)S(1)}, bf16[46,16,128]{2,1,0:T(8,128)(2,1)S(1)}, u32[]{:S(2)}, u32[]{:S(2)}) collective-permute-start(bf16[46,16,128]{2,1,0:T(8,128)(2,1)S(1)} %merge.10.refs_0_), channel_id=1, source_target_pairs={{0,4},{1,5},{2,6},{3,7},{4,0},{5,1},{6,2},{7,3},{8,12},{9,13},{10,... | collective-permute-start | bytes 565256 | tf_op jit(solution)/shard_map/ppermute | solution.py:406
  28.1 10.9 %collective-permute-start.13 = (bf16[46,32,128]{2,1,0:T(8,128)(2,1)S(1)}, bf16[46,32,128]{2,1,0:T(8,128)(2,1)S(1)}, u32[]{:S(2)}, u32[]{:S(2)}) collective-permute-start(bf16[46,32,128]{2,1,0:T(8,128)(2,1)S(1)} %merge.9.refs_3_), channel_id=1, source_target_pairs={{0,1},{1,0},{2,3},{3,2},{4,5},{5,4},{6,7},{7,6},{8,9},{9,8},{10,11... | collective-permute-start | bytes 1130504 | tf_op jit(solution)/shard_map/ppermute | solution.py:406
  36.6 3.3 %collective-permute-start.14 = (bf16[46,32,128]{2,1,0:T(8,128)(2,1)S(1)}, bf16[46,32,128]{2,1,0:T(8,128)(2,1)S(1)}, u32[]{:S(2)}, u32[]{:S(2)}) collective-permute-start(bf16[46,32,128]{2,1,0:T(8,128)(2,1)S(1)} %collective-permute-done.11.refs_4_), channel_id=1, source_target_pairs={{0,1},{1,0},{2,3},{3,2},{4,5},{5,4},{6,7},{7,6},{8,9},{9,8},{10,11... | collective-permute-start | bytes 1130504 | tf_op jit(solution)/shard_map/ppermute | solution.py:406
  38.6 7.9 %collective-permute-start.15 = (bf16[64,16,128]{2,1,0:T(8,128)(2,1)S(1)}, bf16[64,16,128]{2,1,0:T(8,128)(2,1)S(1)}, u32[]{:S(2)}, u32[]{:S(2)}) collective-permute-start(bf16[64,16,128]{2,1,0:T(8,128)(2,1)S(1)} %merge.11.refs_2_), channel_id=1, source_target_pairs={{0,2},{1,3},{2,0},{3,1},{4,6},{5,7},{6,4},{7,5},{8,10},{9,11},{10,... | collective-permute-start | bytes 786440 | tf_op jit(solution)/shard_map/ppermute | solution.py:406
  38.7 8.6 %collective-permute-start.16 = (bf16[64,16,128]{2,1,0:T(8,128)(2,1)S(1)}, bf16[64,16,128]{2,1,0:T(8,128)(2,1)S(1)}, u32[]{:S(2)}, u32[]{:S(2)}) collective-permute-start(bf16[64,16,128]{2,1,0:T(8,128)(2,1)S(1)} %merge.11.refs_2_), channel_id=1, source_target_pairs={{0,1},{1,0},{2,3},{3,2},{4,5},{5,4},{6,7},{7,6},{8,9},{9,8},{10,11... | collective-permute-start | bytes 786440 | tf_op jit(solution)/shard_map/ppermute | solution.py:406
  46.5 5.9 %copy-start = (bf16[2048,512]{1,0:T(8,128)(2,1)S(1)}, bf16[2048,512]{1,0:T(8,128)(2,1)}, u32[]{:S(2)}) copy-start(bf16[2048,512]{1,0:T(8,128)(2,1)} %cache_k.1) | copy-start | bytes 6291460
  46.5 1.9 %collective-permute-start.17 = (bf16[64,16,128]{2,1,0:T(8,128)(2,1)S(1)}, bf16[64,16,128]{2,1,0:T(8,128)(2,1)S(1)}, u32[]{:S(2)}, u32[]{:S(2)}) collective-permute-start(bf16[64,16,128]{2,1,0:T(8,128)(2,1)S(1)} %collective-permute-done.15.refs_3_), channel_id=1, source_target_pairs={{0,1},{1,0},{2,3},{3,2},{4,5},{5,4},{6,7},{7,6},{8,9},{9,8},{10,11... | collective-permute-start | bytes 786440 | tf_op jit(solution)/shard_map/ppermute | solution.py:406
